TPU v7x, 128 devices: a whole 4x4x4 slice. The times are simulated.
128 devices in a mesh: seq: 32 (over y, z, core), mp: 4 (over x).
Axes of the slice: x: 4, y: 4, z: 4, core: 2. Of those that a mesh axis runs over, the one named last changes fastest.
Arguments:
- byte_states: bfloat16 [8192, 1024], P('seq'), may hold values from -6 to 6
- patch_lengths: int32 [32, 32], P('seq'), may hold values from 1 to 16, 256 in all within a row
- patch_owner: int32 [1024, 1], P('seq'), may hold values from 0 to 31; in each aligned block of 32 rows (0 to 31, 32 to 63, ...) at most 2 rows name the same one
- w_enc: bfloat16 [1024, 4096], P(None, 'mp'), may hold values from -0.5 to 0.5
- w_gate: bfloat16 [4096, 14336], P('mp', 'seq'), may hold values from -0.09375 to 0.09375
- w_lift: bfloat16 [4096, 14336], P('mp', 'seq'), may hold values from -0.09375 to 0.09375
- w_down: bfloat16 [14336, 4096], P('seq', 'mp'), may hold values from -0.046875 to 0.046875
- w_dec: bfloat16 [4096, 1024], P('mp'), may hold values from -0.09375 to 0.09375
- byte_cot: bfloat16 [8192, 1024], P('seq'), may hold values from -6 to 6
Outputs:
- byte_out: bfloat16 [8192, 1024], P('seq')
- byte_grad: bfloat16 [8192, 1024], P('seq')
- latent_states: bfloat16 [2048, 4096], P('seq', 'mp')
Inputs may be any that keep to these rules, and one draw needn't show every extreme that they name: `patch_lengths`: each row sums to 256; the longest patch has exactly 16 bytes. `patch_owner`: among the patches of one byte shard (aligned blocks of 32 rows) no owner is named more than 2 times, a bound that some block reaches.
All inputs are finite; a program needn't handle non-finite values.
Results may differ from a plain program's by a relative error of at most 0.008.
Values may be sent and summed in bfloat16 or wider, within the bound.
No kernel may reach another device: no remote copies, remote signals or barrier semaphores. Data moves between devices by JAX's collectives and lax.ppermute only.
A program may use at most 128 MiB of HBM per device.

v0:
```python
import jax
import jax.numpy as jnp
from jax import lax
from jax.sharding import PartitionSpec as P


def on_device(
    byte_states, patch_lengths, patch_owner, w_enc, w_gate, w_lift, w_down, w_dec, byte_cot
):
    seq_count = lax.axis_size("seq")
    patch_count = patch_lengths.shape[1]
    slot_count = 2 * patch_count // seq_count
    own_rows = seq_count * slot_count
    hidden_width = w_gate.shape[1]
    patch_ends = jnp.cumsum(patch_lengths[0])
    positions = jnp.arange(byte_states.shape[0], dtype=jnp.int32)
    local_patch = jnp.sum((patch_ends[None, :] <= positions[:, None]).astype(jnp.int32), axis=1)
    patch_index = jnp.arange(patch_count, dtype=jnp.int32)
    pooling = (patch_index[:, None] == local_patch[None, :]).astype(jnp.bfloat16)
    lengths = patch_lengths[0].astype(jnp.float32)[:, None]
    owners = patch_owner[:, 0]
    onehot = (owners[:, None] == jnp.arange(seq_count, dtype=jnp.int32)[None, :]).astype(jnp.int32)
    ranks = jnp.sum((jnp.cumsum(onehot, axis=0) - 1) * onehot, axis=1)
    targets = owners * slot_count + ranks
    routing = (jnp.arange(own_rows, dtype=jnp.int32)[:, None] == targets[None, :]).astype(
        jnp.bfloat16
    )
    pooled = (jnp.dot(pooling, byte_states, preferred_element_type=jnp.float32) / lengths).astype(
        jnp.bfloat16
    )
    patch_rep = jnp.dot(pooled, w_enc, preferred_element_type=jnp.float32).astype(jnp.bfloat16)
    outgoing = jnp.dot(routing, patch_rep, preferred_element_type=jnp.float32).astype(jnp.bfloat16)
    rows_in = lax.all_to_all(outgoing, "seq", split_axis=0, concat_axis=0, tiled=True)
    piece = lax.all_gather(rows_in, "seq", axis=0, tiled=True)
    combined = jnp.concatenate(
        [
            jnp.dot(piece, w_gate, preferred_element_type=jnp.float32),
            jnp.dot(piece, w_lift, preferred_element_type=jnp.float32),
        ],
        axis=1,
    )
    combined = lax.psum(combined, "mp")
    gate_value = combined[:, :hidden_width]
    lift_value = combined[:, hidden_width:]
    hidden = (jax.nn.silu(gate_value) * lift_value).astype(jnp.bfloat16)
    latent_sum = lax.psum_scatter(
        jnp.dot(hidden, w_down, preferred_element_type=jnp.float32),
        "seq",
        scatter_dimension=0,
        tiled=True,
    )
    row_states = (rows_in.astype(jnp.float32) + latent_sum).astype(jnp.bfloat16)
    arrived = lax.all_to_all(row_states, "seq", split_axis=0, concat_axis=0, tiled=True)
    patch_back = jnp.dot(routing.T, arrived, preferred_element_type=jnp.float32).astype(
        jnp.bfloat16
    )
    decoded = lax.psum(jnp.dot(patch_back, w_dec, preferred_element_type=jnp.float32), "mp")
    byte_out = (byte_states.astype(jnp.float32) + jnp.take(decoded, local_patch, axis=0)).astype(
        jnp.bfloat16
    )
    patch_cot = jnp.dot(pooling, byte_cot, preferred_element_type=jnp.float32).astype(jnp.bfloat16)
    grad_back = jnp.dot(patch_cot, w_dec.T, preferred_element_type=jnp.float32).astype(jnp.bfloat16)
    grad_out_rows = jnp.dot(routing, grad_back, preferred_element_type=jnp.float32).astype(
        jnp.bfloat16
    )
    grad_own = lax.all_to_all(grad_out_rows, "seq", split_axis=0, concat_axis=0, tiled=True)
    grad_hidden = jnp.dot(
        lax.all_gather(grad_own, "seq", axis=0, tiled=True),
        w_down.T,
        preferred_element_type=jnp.float32,
    )
    grad_hidden = lax.psum(grad_hidden, "mp")
    sigma = jax.nn.sigmoid(gate_value)
    grad_gate = (grad_hidden * lift_value * sigma * (1.0 + gate_value * (1.0 - sigma))).astype(
        jnp.bfloat16
    )
    grad_lift = (grad_hidden * gate_value * sigma).astype(jnp.bfloat16)
    grad_sum = lax.psum_scatter(
        jnp.dot(grad_gate, w_gate.T, preferred_element_type=jnp.float32)
        + jnp.dot(grad_lift, w_lift.T, preferred_element_type=jnp.float32),
        "seq",
        scatter_dimension=0,
        tiled=True,
    )
    grad_in = (grad_own.astype(jnp.float32) + grad_sum).astype(jnp.bfloat16)
    grad_arrived = lax.all_to_all(grad_in, "seq", split_axis=0, concat_axis=0, tiled=True)
    grad_rep = jnp.dot(routing.T, grad_arrived, preferred_element_type=jnp.float32).astype(
        jnp.bfloat16
    )
    grad_pool = (
        lax.psum(jnp.dot(grad_rep, w_enc.T, preferred_element_type=jnp.float32), "mp") / lengths
    )
    byte_grad = (byte_cot.astype(jnp.float32) + jnp.take(grad_pool, local_patch, axis=0)).astype(
        jnp.bfloat16
    )
    return (byte_out, byte_grad, row_states)


def solution(mesh):
    return jax.shard_map(
        on_device,
        mesh=mesh,
        in_specs=(
            P("seq", None),
            P("seq", None),
            P("seq", None),
            P(None, "mp"),
            P("mp", "seq"),
            P("mp", "seq"),
            P("seq", "mp"),
            P("mp", None),
            P("seq", None),
        ),
        out_specs=(P("seq", None), P("seq", None), P("seq", "mp")),
        check_vma=False,
    )
```

profile of v0, /device:TPU:1, one launch (start us, length us, event | category | flops | bytes accessed | tf_op | source)
XLA Modules:
  0.0 603.1 jit_solution(17027190598067921183)
XLA Ops:
  11.4 2.4 convolution_convert_fusion.6
  13.9 17.1 %all_to_all.48 = bf16[32,2,1024]{2,1,0:T(2,128)(2,1)S(1)} all-to-all(bf16[32,2,1024]{2,1,0:T(2,128)(2,1)S(1)} %all_to_all.32), channel_id=1, replica_groups=mesh['seq'=32,'mp'=4] {'seq'}, dimensions={0} | all-to-all | bytes 262144 | tf_op jit(solution)/shard_map/all_to_all | solution.py:33
  33.0 11.3 %all_to_all.49 = bf16[32,2,1024]{2,1,0:T(2,128)(2,1)S(1)} all-to-all(bf16[32,2,1024]{2,1,0:T(2,128)(2,1)S(1)} %all_to_all.38), channel_id=1, replica_groups=mesh['seq'=32,'mp'=4] {'seq'}, dimensions={0} | all-to-all | bytes 262144 | tf_op jit(solution)/shard_map/all_to_all | solution.py:66
  45.0 31.1 %all-gather.3.cloned.1.call-done = bf16[2048,1024]{1,0:T(8,128)(2,1)} async-done(((bf16[64,1024]{1,0:T(8,128)(2,1)}), bf16[2048,1024]{1,0:T(8,128)(2,1)}) %all-gather.3.cloned.1.call-update) | async-done | bytes 4194320 | tf_op jit(solution)/shard_map/all_gather | solution.py:34
  76.2 4.7 fusion.23
  80.9 3.3 fusion.24
  84.1 3.4 pad_maximum_fusion
  87.6 37.1 %all-gather.5.cloned.1.call-done = bf16[2048,1024]{1,0:T(8,128)(2,1)} async-done(((bf16[64,1024]{1,0:T(8,128)(2,1)}), bf16[2048,1024]{1,0:T(8,128)(2,1)}) %all-gather.5.cloned.1.call-update) | async-done | bytes 4194320 | tf_op jit(solution)/shard_map/all_gather | solution.py:68
  124.7 6.4 %fusion.25 = f32[2048,448]{0,1:T(8,128)} fusion(bf16[2048,1024]{1,0:T(8,128)(2,1)} %all-gather.5.cloned.1.call-done, bf16[448,1024]{1,0:T(8,128)(2,1)} %param.17), kind=kOutput, calls=%fused_computation.54 | convolution fusion | flops 1879048192 | bytes 8781824 | tf_op jit(solution)/shard_map/dot_general | solution.py:67
  131.4 201.6 %all-reduce.7.cloned.1.call-done = (f32[2048,896]{0,1:T(8,128)}, f32[2048,448]{0,1:T(8,128)}) async-done(((f32[2048,896]{0,1:T(8,128)}, f32[2048,448]{0,1:T(8,128)}), (f32[2048,896]{0,1:T(8,128)}, f32[2048,448]{0,1:T(8,128)})) %all-reduce.7.cloned.1.call-update) | async-done | bytes 11010064 | tf_op jit(solution)/shard_map/psum | solution.py:42
  333.0 7.8 %fusion.3 = f32[2048,1024]{1,0:T(8,128)S(1)} fusion(bf16[1024,448]{0,1:T(8,128)(2,1)} %param.15, f32[2048,448]{0,1:T(8,128)} %get-tuple-element.7, f32[2048,896]{0,1:T(8,128)} %get-tuple-element.6), kind=kOutput, calls=%fused_computation.11 | convolution fusion | flops 1888223232 | bytes 20316160 | tf_op jit(solution)/shard_map/dot_general | solution.py:79
  340.8 5.9 convolution_add_fusion
  346.8 9.0 %fusion = f32[2048,1024]{1,0:T(8,128)} fusion(bf16[448,1024]{1,0:T(8,128)(2,1)} %param.17, f32[2048,896]{0,1:T(8,128)} %get-tuple-element.6), kind=kOutput, calls=%fused_computation.8 | convolution fusion | flops 1884553216 | bytes 16646144 | tf_op jit(solution)/shard_map/dot_general | solution.py:47
  355.8 82.2 %reduce-scatter.5.cloned.1.call-done = f32[64,1024]{1,0:T(8,128)} async-done(((f32[2048,1024]{1,0:T(8,128)}), f32[64,1024]{1,0:T(8,128)}) %reduce-scatter.5.cloned.1.call-update) | async-done | bytes 262160 | tf_op jit(solution)/shard_map/reduce_scatter | solution.py:78
  439.7 7.3 %all-to-all-start.3 = ((bf16[32,2,1024]{2,1,0:T(2,128)(2,1)}), bf16[32,2,1024]{2,1,0:T(2,128)(2,1)S(1)}, u32[]{:S(2)}, u32[]{:S(2)}) async-start(bf16[32,2,1024]{2,1,0:T(2,128)(2,1)} %all_to_all.41), calls=%async_computation.5 | async-start | bytes 262144 | tf_op jit(solution)/shard_map/all_to_all | solution.py:86
  447.1 87.1 %reduce-scatter.3.cloned.1.call-done = f32[64,1024]{1,0:T(8,128)} async-done(((f32[2048,1024]{1,0:T(8,128)}), f32[64,1024]{1,0:T(8,128)}) %reduce-scatter.3.cloned.1.call-update) | async-done | bytes 262160 | tf_op jit(solution)/shard_map/reduce_scatter | solution.py:46
  535.9 7.3 %all-to-all-start.1 = ((bf16[32,2,1024]{2,1,0:T(2,128)(2,1)}), bf16[32,2,1024]{2,1,0:T(2,128)(2,1)S(1)}, u32[]{:S(2)}, u32[]{:S(2)}) async-start(bf16[32,2,1024]{2,1,0:T(2,128)(2,1)} %all_to_all.35), calls=%async_computation.2 | async-start | bytes 262144 | tf_op jit(solution)/shard_map/all_to_all | solution.py:53
  543.3 3.1 fusion.6
  546.4 4.5 all-to-all-done.1
  551.0 1.3 fusion.5
  552.3 37.0 %all-reduce.5.cloned.1.call-done = (f32[32,1024]{1,0:T(8,128)}, f32[32,1024]{1,0:T(8,128)}) async-done(((f32[32,1024]{1,0:T(8,128)}, f32[32,1024]{1,0:T(8,128)}), (f32[32,1024]{1,0:T(8,128)}, f32[32,1024]{1,0:T(8,128)})) %all-reduce.5.cloned.1.call-update) | async-done | bytes 262160 | tf_op jit(solution)/shard_map/psum | solution.py:57
  590.4 1.1 gather_fusion.1
  591.5 2.0 gather_fusion
  593.5 2.8 fusion.7
  (59 shorter events, 11.9 us)
Async XLA Ops:
  7.2 24.9 %copy-start = (bf16[1024,1024]{1,0:T(8,128)(2,1)S(1)}, bf16[1024,1024]{1,0:T(8,128)(2,1)}, u32[]{:S(2)}) copy-start(bf16[1024,1024]{1,0:T(8,128)(2,1)} %param.18) | copy-start | bytes 6291460
  7.2 24.7 %copy-start.2 = (bf16[256,1024]{1,0:T(8,128)(2,1)S(1)}, bf16[256,1024]{1,0:T(8,128)(2,1)}, u32[]{:S(2)}) copy-start(bf16[256,1024]{1,0:T(8,128)(2,1)} %param.19) | copy-start | bytes 1572868
  7.2 69.0 %all-gather.3.cloned.1.call-start = ((), (), s32[]{:S(2)}) async-start(), calls=%async_computation.6 | async-start | bytes 4325376 | tf_op jit(solution)/shard_map/all_gather | solution.py:34
  31.8 92.9 %all-gather.5.cloned.1.call-start = ((), (), s32[]{:S(2)}) async-start(), calls=%async_computation.8 | async-start | bytes 4325376 | tf_op jit(solution)/shard_map/all_gather | solution.py:68
  45.0 288.0 %all-reduce.7.cloned.1.call-start = ((), (), s32[]{:S(2)}) async-start(), calls=%async_computation.11 | async-start | bytes 22020096 | tf_op jit(solution)/shard_map/psum | solution.py:42
  76.2 4.7 copy-start.7
  131.2 306.9 %reduce-scatter.5.cloned.1.call-start = ((), (), s32[]{:S(2)}) async-start(), calls=%async_computation.9 | async-start | bytes 8650752 | tf_op jit(solution)/shard_map/reduce_scatter | solution.py:78
  333.0 7.8 %copy-start.6 = (f32[2048,896]{0,1:T(8,128)S(1)}, f32[2048,896]{0,1:T(8,128)}, u32[]{:S(2)}) copy-start(f32[2048,896]{0,1:T(8,128)} %get-tuple-element.6) | copy-start | bytes 22020100
  333.0 7.8 %copy-start.8 = (f32[2048,448]{0,1:T(8,128)S(1)}, f32[2048,448]{0,1:T(8,128)}, u32[]{:S(2)}) copy-start(f32[2048,448]{0,1:T(8,128)} %get-tuple-element.7) | copy-start | bytes 11010052
  333.0 7.9 %copy-start.9 = (bf16[1024,448]{0,1:T(8,128)(2,1)S(1)}, bf16[1024,448]{0,1:T(8,128)(2,1)}, u32[]{:S(2)}) copy-start(bf16[1024,448]{0,1:T(8,128)(2,1)} %param.16) | copy-start | bytes 2752516
  346.8 187.4 %reduce-scatter.3.cloned.1.call-start = ((), (), s32[]{:S(2)}) async-start(), calls=%async_computation.7 | async-start | bytes 8650752 | tf_op jit(solution)/shard_map/reduce_scatter | solution.py:46
  355.8 82.2 %copy-start.4 = (bf16[64,1024]{1,0:T(8,128)(2,1)S(1)}, bf16[64,1024]{1,0:T(8,128)(2,1)}, u32[]{:S(2)}) copy-start(bf16[64,1024]{1,0:T(8,128)(2,1)} %all_to_all.40) | copy-start | bytes 393220
  355.8 178.4 %copy-start.3 = (bf16[64,1024]{1,0:T(8,128)(2,1)S(1)}, bf16[64,1024]{1,0:T(8,128)(2,1)}, u32[]{:S(2)}) copy-start(bf16[64,1024]{1,0:T(8,128)(2,1)} %all_to_all.34) | copy-start | bytes 393220
  439.7 96.1 %all-to-all-start.3 = ((bf16[32,2,1024]{2,1,0:T(2,128)(2,1)}), bf16[32,2,1024]{2,1,0:T(2,128)(2,1)S(1)}, u32[]{:S(2)}, u32[]{:S(2)}) async-start(bf16[32,2,1024]{2,1,0:T(2,128)(2,1)} %all_to_all.41), calls=%async_computation.5 | async-start | bytes 262144 | tf_op jit(solution)/shard_map/all_to_all | solution.py:86
  535.1 56.3 %copy-start.5 = (bf16[64,1024]{1,0:T(8,128)(2,1)}, bf16[64,1024]{1,0:T(8,128)(2,1)S(1)}, u32[]{:S(2)}) copy-start(bf16[64,1024]{1,0:T(8,128)(2,1)S(1)} %add_convert_fusion.1) | copy-start | bytes 393220
  535.9 15.1 %all-to-all-start.1 = ((bf16[32,2,1024]{2,1,0:T(2,128)(2,1)}), bf16[32,2,1024]{2,1,0:T(2,128)(2,1)S(1)}, u32[]{:S(2)}, u32[]{:S(2)}) async-start(bf16[32,2,1024]{2,1,0:T(2,128)(2,1)} %all_to_all.35), calls=%async_computation.2 | async-start | bytes 262144 | tf_op jit(solution)/shard_map/all_to_all | solution.py:53
  543.2 46.1 %all-reduce.5.cloned.1.call-start = ((), (), s32[]{:S(2)}) async-start(), calls=%async_computation.10 | async-start | bytes 524288 | tf_op jit(solution)/shard_map/psum | solution.py:57
  590.4 1.1 copy-start.1
Sparse Core Ops, SparseCore 0:
  31.9 44.2 all-gather.2
  79.0 45.6 all-gather.4
  131.3 201.6 all-reduce.6
  346.9 91.1 reduce-scatter.4
  442.1 92.0 reduce-scatter.2
  552.4 36.9 all-reduce.4
where the time goes:
time: 605 us; the launch traced here: 603 us
  waiting for transfers between devices  481 us (80%)
  matrix products  45.1 us (7%)
  blocking collectives  28.4 us (5%)
  starting transfers between devices  15.1 us (2%)
  between operations  14.3 us (2%)
  other arithmetic  12.6 us (2%)
  local copies, waits for them, and re-layouts  6.91 us (1%)
    psum x1, waiting for transfers between devices, on_device(): combined = lax.psum(combined, 'mp')  202 us
    reduce_scatter x1, waiting for transfers between devices, on_device(): lax.psum_scatter(jnp.dot(hidden, w_down, preferred_element_type=jnp.float...  87.1 us
    reduce_scatter x1, waiting for transfers between devices, on_device(): lax.psum_scatter(jnp.dot(grad_gate, w_gate.T, preferred_element_type=jnp....  82.2 us
    all_gather x1, waiting for transfers between devices, on_device(): lax.all_gather(grad_own, 'seq', axis=0, tiled=True)  37.1 us
    psum x1, waiting for transfers between devices, on_device(): lax.psum(jnp.dot(patch_back, w_dec, preferred_element_type=jnp.float32),...  37 us
    all_gather x1, waiting for transfers between devices, on_device(): piece = lax.all_gather(rows_in, 'seq', axis=0, tiled=True)  31.1 us
    all_to_all x1, blocking collectives, on_device(): lax.all_to_all(outgoing, 'seq', split_axis=0, concat_axis=0, tiled=True)  17.1 us
  transfers between devices with their start and end apart: 8, of which 7 were waited for; matrix products, arithmetic and copies ran while one was open for 4% of the time, Pallas kernels for 0%

commit v1 on v0

v1 whole, which is shorter than its diff:
```python
import functools

import jax
import jax.numpy as jnp
from jax import lax
from jax.experimental import pallas as pl
from jax.experimental.pallas import tpu as pltpu
from jax.sharding import Mesh
from jax.sharding import PartitionSpec as P

F32 = jnp.float32
BF16 = jnp.bfloat16
SEQ = ("y", "z", "c")
VMEM_LIMIT = 48 * 1024 * 1024


def swap_core(value):
    return lax.ppermute(value, "c", [(0, 1), (1, 0)])


def swap_x(value, k):
    return lax.ppermute(value, "x", [(i, i ^ k) for i in range(4)])


def swap_near(value, first):
    steps = (1, 3) if first else (3, 1)
    return lax.ppermute(
        value, ("c", "x"), [(c * 4 + x, c * 4 + (x ^ steps[c])) for c in range(2) for x in range(4)]
    )


def dot(a, b):
    return jnp.dot(a, b, preferred_element_type=F32)


def dot_t(a, b):
    return lax.dot_general(a, b, (((1,), (1,)), ((), ())), preferred_element_type=F32)


def call(body, outs, inputs, scalars=(), flops=0):
    specs = [pl.BlockSpec(memory_space=pltpu.SMEM)] * len(scalars)
    specs += [pl.BlockSpec(memory_space=pltpu.VMEM)] * len(inputs)
    moved = sum(v.size * v.dtype.itemsize for v in list(inputs) + list(outs))
    return pl.pallas_call(
        body,
        out_shape=outs,
        in_specs=specs,
        out_specs=[pl.BlockSpec(memory_space=pltpu.VMEM)] * len(outs),
        compiler_params=pltpu.CompilerParams(vmem_limit_bytes=VMEM_LIMIT),
        cost_estimate=pl.CostEstimate(flops=flops, bytes_accessed=moved, transcendentals=0),
    )(*scalars, *inputs)


def shape(dims, dtype):
    return jax.ShapeDtypeStruct(dims, dtype)


def bounds(lengths):
    count = lengths.shape[1]
    row = lax.broadcasted_iota(jnp.int32, (count, count), 0)
    column = lax.broadcasted_iota(jnp.int32, (count, count), 1)
    wide = jnp.broadcast_to(lengths, (count, count)).astype(F32)
    ends = jnp.sum(jnp.where(column <= row, wide, 0.0), axis=1, keepdims=True)
    size = jnp.sum(jnp.where(column == row, wide, 0.0), axis=1, keepdims=True)
    return ends - size, ends, size


def membership(lengths, length):
    starts, ends, size = bounds(lengths)
    count = lengths.shape[1]
    position = lax.broadcasted_iota(jnp.int32, (count, length), 1).astype(F32)
    inside = (position >= starts) & (position < ends)
    return jnp.where(inside, 1.0, 0.0).astype(BF16), size


def encode_kernel(forward, lengths, values, weight, rep, repeated):
    pooling, size = membership(lengths[...], values.shape[0])
    pooled = dot(pooling, values[...])
    if forward:
        result = dot((pooled / size).astype(BF16), weight[...])
    else:
        result = dot_t(pooled.astype(BF16), weight[...])
    result = result.astype(BF16)
    rep[...] = result
    for i in range(repeated.shape[0]):
        repeated[i] = result


def spread_kernel(transposed, offsets, near, far, weight, keep, send):
    multiply = dot_t if transposed else dot
    span = near.shape[0] // 4

    @pl.loop(0, 2)
    def _(t):
        off = pl.multiple_of(offsets[t], span)
        keep[t, 0] = multiply(near[pl.ds(off, span), :], weight[...])
        keep[t, 1] = multiply(far[pl.ds(off, span), :], weight[...])

    @pl.loop(0, 2)
    def _(t):
        off = pl.multiple_of(offsets[t + 2], span)
        send[t, 0] = multiply(near[pl.ds(off, span), :], weight[...]).astype(BF16)
        send[t, 1] = multiply(far[pl.ds(off, span), :], weight[...]).astype(BF16)


def down_kernel(transposed, offsets, own, second, others, weight, near, far):
    multiply = dot_t if transposed else dot
    span = near.shape[0] // 4
    blocks = [own, second, others.at[0], others.at[1]]
    for t, block in enumerate(blocks):
        off = pl.multiple_of(offsets[t], span)
        near[pl.ds(off, span), :] = multiply(block[0], weight[...]).astype(BF16)
        far[pl.ds(off, span), :] = multiply(block[1], weight[...]).astype(BF16)


def decode_kernel(forward, arrived, rep, weight, owners, *outs):
    total = rep[...].astype(F32)
    for i in range(arrived.shape[0]):
        total = total + arrived[i].astype(F32)
    states = total.astype(BF16)
    if forward:
        partial, outgoing = outs
        partial[...] = dot(states, weight[...]).astype(BF16)
        count = rep.shape[0]
        own_row = jnp.broadcast_to(owners[...], (count, count))
        row = lax.broadcasted_iota(jnp.int32, (count, count), 0)
        column = lax.broadcasted_iota(jnp.int32, (count, count), 1)
        own_column = jnp.sum(jnp.where(row == column, own_row, 0), axis=1, keepdims=True)
        same = jnp.where((own_column == own_row) & (row < column), 1, 0)
        targets = 2 * owners[...] + jnp.sum(same, axis=0, keepdims=True)
        slots = lax.broadcasted_iota(jnp.int32, (2 * count, count), 0)
        routing = jnp.where(slots == targets, 1.0, 0.0).astype(BF16)
        outgoing[...] = dot(routing, states).astype(BF16)
    else:
        (partial,) = outs
        partial[...] = dot_t(states, weight[...]).astype(BF16)


def finish_kernel(forward, lengths, values, own, one, two, three, out):
    total = (
        own[...].astype(F32) + one[...].astype(F32) + two[...].astype(F32) + three[...].astype(F32)
    )
    pooling, size = membership(lengths[...], values.shape[0])
    if not forward:
        total = total / size
    high = total.astype(BF16)
    low = (total - high.astype(F32)).astype(BF16)
    pick = (((0,), (0,)), ((), ()))
    spread = lax.dot_general(pooling, high, pick, preferred_element_type=F32)
    spread = spread + lax.dot_general(pooling, low, pick, preferred_element_type=F32)
    out[...] = (values[...].astype(F32) + spread).astype(BF16)


def gather_seq(repeated):
    near = lax.all_to_all(repeated, ("y", "z"), split_axis=0, concat_axis=0, tiled=True)
    near = near.reshape(-1, near.shape[2])
    return near, swap_core(near)


def scatter_x(keep, send):
    first = swap_near(send, True)
    second = swap_near((keep[1] + first[1].astype(F32)).astype(BF16), False)
    return keep[0] + first[0].astype(F32) + second.astype(F32)


def gather_x(block):
    second = swap_near(block, False)
    others = swap_near(jnp.stack([block, second]), True)
    return block, second, others


def scatter_seq(near, far):
    total = (near.astype(F32) + swap_core(far).astype(F32)).astype(BF16)
    total = total.reshape(16, -1, total.shape[1])
    return lax.all_to_all(total, ("y", "z"), split_axis=0, concat_axis=0, tiled=True)


def on_device(
    byte_states, patch_lengths, patch_owner, w_enc, w_gate, w_lift, w_down, w_dec, byte_cot
):
    patches = patch_lengths.shape[1]
    width = w_enc.shape[1]
    hid = w_gate.shape[1]
    span = 4 * patches
    x = lax.axis_index("x")
    core = lax.axis_index("c")
    step = jnp.where(core == 0, 1, 3)
    offsets = (jnp.stack([x, x ^ step ^ 2, x ^ step, x ^ 2]) * span).astype(jnp.int32)
    owners = patch_owner.reshape(1, patches)
    pair = jnp.concatenate([w_gate, w_lift], axis=1)
    enc_out = [shape((patches, width), BF16), shape((16, patches, width), BF16)]
    flops = 2 * patches * width * width

    patch_rep, repeated = call(
        functools.partial(encode_kernel, True), enc_out, [patch_lengths, byte_states, w_enc], flops=flops
    )
    near, far = gather_seq(repeated)

    def spread(transposed, near, far, weight, columns):
        return call(
            functools.partial(spread_kernel, transposed),
            [shape((2, 2, span, columns), F32), shape((2, 2, span, columns), BF16)],
            [near, far, weight],
            [offsets],
            flops=2 * 8 * span * width * columns,
        )

    def down(transposed, blocks, weight, columns):
        return call(
            functools.partial(down_kernel, transposed),
            [shape((4 * span, width), BF16)] * 2,
            [*blocks, weight],
            [offsets],
            flops=2 * 8 * span * width * columns,
        )

    keep, send = spread(False, near, far, pair, 2 * hid)
    byte_cot_in, send = lax.optimization_barrier((byte_cot, send))
    grad_back, repeated = call(
        functools.partial(encode_kernel, False), enc_out, [patch_lengths, byte_cot_in, w_dec], flops=flops
    )
    gates = scatter_x(keep, send)
    near, far = gather_seq(repeated)
    keep, send = spread(True, near, far, w_down, hid)

    gate, lift = gates[:, :, :hid], gates[:, :, hid:]
    sig = jax.nn.sigmoid(gate)
    silu = gate * sig
    hidden = (silu * lift).astype(BF16)
    hiddens = gather_x(hidden)
    grad_hidden = scatter_x(keep, send)
    grads = jnp.concatenate(
        [grad_hidden * lift * sig * (1.0 + gate * (1.0 - sig)), grad_hidden * silu], axis=2
    ).astype(BF16)
    grads = gather_x(grads)
    near, far = down(False, hiddens, w_down, hid)
    arrived = scatter_seq(near, far)
    decoded, outgoing = call(
        functools.partial(decode_kernel, True),
        [shape((patches, width), BF16), shape((2 * patches, width), BF16)],
        [arrived, patch_rep, w_dec, owners],
        flops=flops,
    )
    near, far = down(True, grads, pair, 2 * hid)
    arrived = scatter_seq(near, far)
    (grad_pool,) = call(
        functools.partial(decode_kernel, False),
        [shape((patches, width), BF16)],
        [arrived, grad_back, w_enc, owners],
        flops=flops,
    )
    latent = lax.all_to_all(outgoing, SEQ, split_axis=0, concat_axis=0, tiled=True)

    def finish(forward, values, partial):
        return call(
            functools.partial(finish_kernel, forward),
            [shape(values.shape, BF16)],
            [patch_lengths, values, partial] + [swap_x(partial, k) for k in (1, 2, 3)],
            flops=4 * patches * values.size,
        )[0]

    return finish(True, byte_states, decoded), finish(False, byte_cot, grad_pool), latent


def solution(mesh):
    fine = Mesh(mesh.devices.reshape(4, 4, 2, 4), ("y", "z", "c", "x"))
    return jax.shard_map(
        on_device,
        mesh=fine,
        in_specs=(
            P(SEQ, None),
            P(SEQ, None),
            P(SEQ, None),
            P(None, "x"),
            P("x", SEQ),
            P("x", SEQ),
            P(SEQ, "x"),
            P("x", None),
            P(SEQ, None),
        ),
        out_specs=(P(SEQ, None), P(SEQ, None), P(SEQ, "x")),
        check_vma=False,
    )
```

time: 605 us -> 195 us (0.32)
  waiting for transfers between devices: 481 us -> 67.1 us
  matrix products: 45.1 us -> 0 us
  starting transfers between devices: 15.1 us -> 41.9 us
  Pallas kernels: 0 us -> 21.8 us
  blocking collectives: 28.4 us -> 43.4 us
  between operations: 14.3 us -> 0.88 us
    psum x2 -> x0, waiting for transfers between devices: 239 us -> none  [the longest x1 202 us: on_device(): combined = lax.psum(combined, 'mp')]
    reduce_scatter x2 -> x0, waiting for transfers between devices: 169 us -> none  [the longest x1 87.1 us: on_device(): lax.psum_scatter(jnp.dot(hidden, w_down, preferred_element_type=jnp.float...]
    all_gather x2 -> x0, waiting for transfers between devices: 68.2 us -> none  [the longest x1 37.1 us: on_device(): lax.all_gather(grad_own, 'seq', axis=0, tiled=True)]
    dot_general x12 -> x0, matrix products: 45.1 us -> none  [the longest x1 9 us: on_device(): jnp.dot(hidden, w_down, preferred_element_type=jnp.float32)]
    ppermute x0 -> x18, waiting for transfers between devices: none -> 39.4 us  [the longest x8 37.6 us: swap_near(): lax.ppermute(value, ('c', 'x'), [(c * 4 + x, c * 4 + (x ^ steps[c])) for...]
    ppermute x0 -> x18, starting transfers between devices: none -> 28 us  [the longest x8 12 us: swap_near(): lax.ppermute(value, ('c', 'x'), [(c * 4 + x, c * 4 + (x ^ steps[c])) for...]
    all_to_all x2 -> x3, waiting for transfers between devices: 4.49 us -> 27.7 us  [the longest x2 27.7 us: scatter_seq(): lax.all_to_all(total, ('y', 'z'), split_axis=0, concat_axis=0, tiled=True)]
    pallas_call x0 -> x10, Pallas kernels: none -> 21.8 us  [call(): pl.pallas_call(body, out_shape=outs, in_specs=specs, out_specs=[pl.BlockS...]
  transfers between devices with their start and end apart: 8 -> 21, of which waited for: 7 -> 11; matrix products, arithmetic and copies ran while one was open for 4% -> 5% of each run, Pallas kernels for 0% -> 7%
where the time goes in v1:
time: 195 us; the launch traced here: 193 us
  waiting for transfers between devices  67.1 us (34%)
  blocking collectives  43.4 us (22%)
  starting transfers between devices  41.9 us (21%)
  Pallas kernels  21.8 us (11%)
  local copies, waits for them, and re-layouts  10.5 us (5%)
  other arithmetic  7.35 us (4%)
    all_to_all x2, blocking collectives, gather_seq(): lax.all_to_all(repeated, ('y', 'z'), split_axis=0, concat_axis=0, tiled=T...  43.4 us
    ppermute x8, waiting for transfers between devices, swap_near(): lax.ppermute(value, ('c', 'x'), [(c * 4 + x, c * 4 + (x ^ steps[c])) for...  37.6 us
    all_to_all x2, waiting for transfers between devices, scatter_seq(): lax.all_to_all(total, ('y', 'z'), split_axis=0, concat_axis=0, tiled=True)  27.7 us
    pallas_call x10, Pallas kernels, call(): pl.pallas_call(body, out_shape=outs, in_specs=specs, out_specs=[pl.BlockS...  21.8 us
    ppermute x8, starting transfers between devices, swap_near(): lax.ppermute(value, ('c', 'x'), [(c * 4 + x, c * 4 + (x ^ steps[c])) for...  12 us
    ppermute x4, starting transfers between devices, swap_core(): return lax.ppermute(value, 'c', [(0, 1), (1, 0)])  9.39 us
    unnamed x34, local copies, waits for them, and re-layouts  9.1 us
    all_to_all x2, starting transfers between devices, scatter_seq(): lax.all_to_all(total, ('y', 'z'), split_axis=0, concat_axis=0, tiled=True)  7.31 us
  transfers between devices with their start and end apart: 21, of which 11 were waited for; matrix products, arithmetic and copies ran while one was open for 5% of the time, Pallas kernels for 7%

profile of v1, /device:TPU:1, one launch (start us, length us, event | category | flops | bytes accessed | tf_op | source)
XLA Modules:
  0.0 193.0 jit_solution(18330901541398295118)
XLA Ops:
  4.6 24.3 %all_to_all.32 = bf16[16,32,1024]{2,1,0:T(8,128)(2,1)S(1)} all-to-all(bf16[16,32,1024]{2,1,0:T(8,128)(2,1)S(1)} %get-tuple-element.19), channel_id=1, replica_groups=mesh['y'=4,'z'=4,'c'=2,'x'=4] {'y','z'}, dimensions={0} | all-to-all | bytes 2097152 | tf_op jit(solution)/shard_map/all_to_all | solution.py:155
  34.8 4.9 %shard_map.113 = (f32[2,2,128,896]{3,2,1,0:T(8,128)S(1)}, bf16[2,2,128,896]{3,2,1,0:T(8,128)(2,1)S(1)}) custom-call(s32[4]{0:T(128)S(1)} %add_multiply_fusion.offsets, bf16[512,1024]{1,0:T(8,128)(2,1)S(1)} %bitcast.27, bf16[512,1024]{1,0:T(8,128)(2,1)} %collective-permute-done.far, bf16[1024,896]{1,0:T(8,128)(2,1)} %pad_maximum_fusion.weight), custom_call_target="tpu_custom_call" | custom-call | flops 1879048192 | bytes 6684672 | tf_op jit(solution)/shard_map/pallas_call | solution.py:44
  40.6 19.1 %all_to_all.33 = bf16[16,32,1024]{2,1,0:T(8,128)(2,1)S(1)} all-to-all(bf16[16,32,1024]{2,1,0:T(8,128)(2,1)S(1)} %get-tuple-element.28), channel_id=1, replica_groups=mesh['y'=4,'z'=4,'c'=2,'x'=4] {'y','z'}, dimensions={0} | all-to-all | bytes 2097152 | tf_op jit(solution)/shard_map/all_to_all | solution.py:155
  62.1 2.5 %collective-permute-start.1 = (bf16[2,2,128,896]{3,2,1,0:T(8,128)(2,1)S(1)}, bf16[2,2,128,896]{3,2,1,0:T(8,128)(2,1)S(1)}, u32[]{:S(2)}, u32[]{:S(2)}) collective-permute-start(bf16[2,2,128,896]{3,2,1,0:T(8,128)(2,1)S(1)} %get-tuple-element.22), channel_id=1, source_target_pairs={{0,1},{1,0},{2,3},{3,2},{4,7},{5,6},{6,5},{7,4},{8,9},{9,8},{10,11... | collective-permute-start | bytes 2752520 | tf_op jit(solution)/shard_map/ppermute | solution.py:27
  64.5 3.3 %shard_map.118 = (f32[2,2,128,448]{3,2,1,0:T(8,128)S(1)}, bf16[2,2,128,448]{3,2,1,0:T(8,128)(2,1)S(1)}) custom-call(s32[4]{0:T(128)S(1)} %add_multiply_fusion.offsets, bf16[512,1024]{1,0:T(8,128)(2,1)S(1)} %bitcast.29, bf16[512,1024]{1,0:T(8,128)(2,1)S(1)} %collective-permute-done.9.far, bf16[448,1024]{1,0:T(8,128)(2,1)S(1)} %copy-done.14), custom_call_target="tpu_custom_call" | custom-call | flops 939524096 | bytes 4390912 | tf_op jit(solution)/shard_map/pallas_call | solution.py:44
  70.2 5.4 %collective-permute-done.1 = bf16[2,2,128,896]{3,2,1,0:T(8,128)(2,1)S(1)} collective-permute-done((bf16[2,2,128,896]{3,2,1,0:T(8,128)(2,1)S(1)}, bf16[2,2,128,896]{3,2,1,0:T(8,128)(2,1)S(1)}, u32[]{:S(2)}, u32[]{:S(2)}) %collective-permute-start.1) | collective-permute-done | bytes 917536 | tf_op jit(solution)/shard_map/ppermute | solution.py:27
  76.0 6.8 %collective-permute-done.10 = bf16[2,2,128,448]{3,2,1,0:T(8,128)(2,1)S(1)} collective-permute-done((bf16[2,2,128,448]{3,2,1,0:T(8,128)(2,1)S(1)}, bf16[2,2,128,448]{3,2,1,0:T(8,128)(2,1)S(1)}, u32[]{:S(2)}, u32[]{:S(2)}) %collective-permute-start.10) | collective-permute-done | bytes 458784 | tf_op jit(solution)/shard_map/ppermute | solution.py:27
  82.9 2.6 %collective-permute-done.2 = bf16[2,128,896]{2,1,0:T(8,128)(2,1)S(1)} collective-permute-done((bf16[2,128,896]{2,1,0:T(8,128)(2,1)S(1)}, bf16[2,128,896]{2,1,0:T(8,128)(2,1)S(1)}, u32[]{:S(2)}, u32[]{:S(2)}) %collective-permute-start.2) | collective-permute-done | bytes 458784 | tf_op jit(solution)/shard_map/ppermute | solution.py:27
  85.7 2.7 %collective-permute-done.11 = bf16[2,128,448]{2,1,0:T(8,128)(2,1)S(1)} collective-permute-done((bf16[2,128,448]{2,1,0:T(8,128)(2,1)S(1)}, bf16[2,128,448]{2,1,0:T(8,128)(2,1)S(1)}, u32[]{:S(2)}, u32[]{:S(2)}) %collective-permute-start.11) | collective-permute-done | bytes 229408 | tf_op jit(solution)/shard_map/ppermute | solution.py:27
  90.6 3.5 %collective-permute-done.3.second = bf16[2,128,448]{2,1,0:T(8,128)(2,1)S(1)} collective-permute-done((bf16[2,128,448]{2,1,0:T(8,128)(2,1)S(1)}, bf16[2,128,448]{2,1,0:T(8,128)(2,1)S(1)}, u32[]{:S(2)}, u32[]{:S(2)}) %collective-permute-start.3) | collective-permute-done | bytes 229408 | tf_op jit(solution)/shard_map/ppermute | solution.py:27
  94.2 2.6 %collective-permute-start.4 = (bf16[2,2,128,448]{3,2,1,0:T(8,128)(2,1)S(1)}, bf16[2,2,128,448]{3,2,1,0:T(8,128)(2,1)S(1)}, u32[]{:S(2)}, u32[]{:S(2)}) collective-permute-start(bf16[2,2,128,448]{3,2,1,0:T(8,128)(2,1)S(1)} %pad_maximum_fusion.2), channel_id=1, source_target_pairs={{0,1},{1,0},{2,3},{3,2},{4,7},{5,6},{6,5},{7,4},{8,9},{9,8},{10,11... | collective-permute-start | bytes 1376264 | tf_op jit(solution)/shard_map/ppermute | solution.py:27
  96.8 2.6 %collective-permute-done.12.second = bf16[2,128,896]{2,1,0:T(8,128)(2,1)S(1)} collective-permute-done((bf16[2,128,896]{2,1,0:T(8,128)(2,1)S(1)}, bf16[2,128,896]{2,1,0:T(8,128)(2,1)S(1)}, u32[]{:S(2)}, u32[]{:S(2)}) %collective-permute-start.12) | collective-permute-done | bytes 458784 | tf_op jit(solution)/shard_map/ppermute | solution.py:27
  99.6 2.6 %collective-permute-start.13 = (bf16[2,2,128,896]{3,2,1,0:T(8,128)(2,1)S(1)}, bf16[2,2,128,896]{3,2,1,0:T(8,128)(2,1)S(1)}, u32[]{:S(2)}, u32[]{:S(2)}) collective-permute-start(bf16[2,2,128,896]{3,2,1,0:T(8,128)(2,1)S(1)} %pad_maximum_fusion.1), channel_id=1, source_target_pairs={{0,1},{1,0},{2,3},{3,2},{4,7},{5,6},{6,5},{7,4},{8,9},{9,8},{10,11... | collective-permute-start | bytes 2752520 | tf_op jit(solution)/shard_map/ppermute | solution.py:27
  102.1 6.9 %collective-permute-done.4.others = bf16[2,2,128,448]{3,2,1,0:T(8,128)(2,1)S(1)} collective-permute-done((bf16[2,2,128,448]{3,2,1,0:T(8,128)(2,1)S(1)}, bf16[2,2,128,448]{3,2,1,0:T(8,128)(2,1)S(1)}, u32[]{:S(2)}, u32[]{:S(2)}) %collective-permute-start.4) | collective-permute-done | bytes 458784 | tf_op jit(solution)/shard_map/ppermute | solution.py:27
  111.7 7.1 %collective-permute-done.13.others = bf16[2,2,128,896]{3,2,1,0:T(8,128)(2,1)S(1)} collective-permute-done((bf16[2,2,128,896]{3,2,1,0:T(8,128)(2,1)S(1)}, bf16[2,2,128,896]{3,2,1,0:T(8,128)(2,1)S(1)}, u32[]{:S(2)}, u32[]{:S(2)}) %collective-permute-start.13) | collective-permute-done | bytes 917536 | tf_op jit(solution)/shard_map/ppermute | solution.py:27
  118.8 6.3 %shard_map.119 = (bf16[512,1024]{1,0:T(8,128)(2,1)S(1)}, bf16[512,1024]{1,0:T(8,128)(2,1)}) custom-call(s32[4]{0:T(128)S(1)} %add_multiply_fusion.offsets, bf16[2,128,896]{2,1,0:T(8,128)(2,1)S(1)} %pad_maximum_fusion.3.own, bf16[2,128,896]{2,1,0:T(8,128)(2,1)S(1)} %collective-permute-done.12.second, ...), custom_call_target="tpu_custom_call" | custom-call | flops 1879048192 | bytes 5767168 | tf_op jit(solution)/shard_map/pallas_call | solution.py:44
  125.1 4.2 %collective-permute-start.14 = (bf16[512,1024]{1,0:T(8,128)(2,1)}, bf16[512,1024]{1,0:T(8,128)(2,1)}, u32[]{:S(2)}, u32[]{:S(2)}) collective-permute-start(bf16[512,1024]{1,0:T(8,128)(2,1)} %get-tuple-element.32), channel_id=1, source_target_pairs={{0,4},{4,0},{1,5},{5,1},{2,6},{6,2},{3,7},{7,3},{8,12},{12,8},{9,1... | collective-permute-start | bytes 3145736 | tf_op jit(solution)/shard_map/ppermute | solution.py:18
  130.7 3.7 %all-to-all-start.1 = ((bf16[16,32,1024]{2,1,0:T(8,128)(2,1)}), bf16[16,32,1024]{2,1,0:T(8,128)(2,1)S(1)}, u32[]{:S(2)}, u32[]{:S(2)}) async-start(bf16[16,32,1024]{2,1,0:T(8,128)(2,1)} %bitcast.36), calls=%async_computation.1 | async-start | bytes 2097152 | tf_op jit(solution)/shard_map/all_to_all | solution.py:175
  134.4 3.0 %add_convert_fusion = bf16[512,1024]{1,0:T(8,128)(2,1)} fusion(bf16[512,1024]{1,0:T(8,128)(2,1)} %collective-permute-done.14, bf16[512,1024]{1,0:T(8,128)(2,1)} %copy-done.10), kind=kLoop, calls=%fused_computation | loop fusion | flops 2097152 | bytes 3145728 | tf_op jit(solution)/shard_map/convert_element_type | solution.py:173
  137.4 14.9 %all-to-all-done.1.arrived = bf16[16,32,1024]{2,1,0:T(8,128)(2,1)S(1)} async-done(((bf16[16,32,1024]{2,1,0:T(8,128)(2,1)}), bf16[16,32,1024]{2,1,0:T(8,128)(2,1)S(1)}, u32[]{:S(2)}, u32[]{:S(2)}) %all-to-all-start.1) | async-done | bytes 1048608 | tf_op jit(solution)/shard_map/all_to_all | solution.py:175
  153.3 3.7 %all-to-all-start.3 = ((bf16[16,32,1024]{2,1,0:T(8,128)(2,1)}), bf16[16,32,1024]{2,1,0:T(8,128)(2,1)S(1)}, u32[]{:S(2)}, u32[]{:S(2)}) async-start(bf16[16,32,1024]{2,1,0:T(8,128)(2,1)} %bitcast.35), calls=%async_computation.3 | async-start | bytes 2097152 | tf_op jit(solution)/shard_map/all_to_all | solution.py:175
  159.6 12.8 %all-to-all-done.3.arrived = bf16[16,32,1024]{2,1,0:T(8,128)(2,1)S(1)} async-done(((bf16[16,32,1024]{2,1,0:T(8,128)(2,1)}), bf16[16,32,1024]{2,1,0:T(8,128)(2,1)S(1)}, u32[]{:S(2)}, u32[]{:S(2)}) %all-to-all-start.3) | async-done | bytes 1048608 | tf_op jit(solution)/shard_map/all_to_all | solution.py:175
  172.4 6.6 %all-to-all-start.4 = ((bf16[32,2,1024]{2,1,0:T(2,128)(2,1)}), bf16[32,2,1024]{2,1,0:T(2,128)(2,1)S(1)}, u32[]{:S(2)}, u32[]{:S(2)}) async-start(bf16[32,2,1024]{2,1,0:T(2,128)(2,1)} %all_to_all.24), calls=%async_computation.4 | async-start | bytes 262144 | tf_op jit(solution)/shard_map/all_to_all | solution.py:252
  184.4 2.7 %collective-permute-start.16 = (bf16[32,1024]{1,0:T(8,128)(2,1)S(1)}, bf16[32,1024]{1,0:T(8,128)(2,1)S(1)}, u32[]{:S(2)}, u32[]{:S(2)}) collective-permute-start(bf16[32,1024]{1,0:T(8,128)(2,1)S(1)} %shard_map.120.own), channel_id=1, source_target_pairs={{0,2},{1,3},{2,0},{3,1},{4,6},{5,7},{6,4},{7,5},{8,10},{9,11},{10,... | collective-permute-start | bytes 196616 | tf_op jit(solution)/shard_map/ppermute | solution.py:22
  (77 shorter events, 37.6 us)
Async XLA Ops:
  3.9 26.9 %copy-start.15 = (bf16[1024,448]{0,1:T(8,128)(2,1)S(1)}, bf16[1024,448]{0,1:T(8,128)(2,1)}, u32[]{:S(2)}) copy-start(bf16[1024,448]{0,1:T(8,128)(2,1)} %param.14) | copy-start | bytes 2752516
  28.9 5.9 %collective-permute-start = (bf16[512,1024]{1,0:T(8,128)(2,1)S(1)}, bf16[512,1024]{1,0:T(8,128)(2,1)}, u32[]{:S(2)}, u32[]{:S(2)}) collective-permute-start(bf16[512,1024]{1,0:T(8,128)(2,1)S(1)} %bitcast.26), channel_id=1, source_target_pairs={{0,4},{4,0},{1,5},{5,1},{2,6},{6,2},{3,7},{7,3},{8,12},{12,8},{9,1... | collective-permute-start | bytes 3145736 | tf_op jit(solution)/shard_map/ppermute | solution.py:18
  39.7 24.9 %copy-start.14 = (bf16[448,1024]{1,0:T(8,128)(2,1)S(1)}, bf16[448,1024]{1,0:T(8,128)(2,1)}, u32[]{:S(2)}) copy-start(bf16[448,1024]{1,0:T(8,128)(2,1)} %weight.10) | copy-start | bytes 2752516
  59.8 4.8 %collective-permute-start.9 = (bf16[512,1024]{1,0:T(8,128)(2,1)S(1)}, bf16[512,1024]{1,0:T(8,128)(2,1)S(1)}, u32[]{:S(2)}, u32[]{:S(2)}) collective-permute-start(bf16[512,1024]{1,0:T(8,128)(2,1)S(1)} %bitcast.28), channel_id=1, source_target_pairs={{0,4},{4,0},{1,5},{5,1},{2,6},{6,2},{3,7},{7,3},{8,12},{12,8},{9,1... | collective-permute-start | bytes 3145736 | tf_op jit(solution)/shard_map/ppermute | solution.py:18
  62.1 13.5 %collective-permute-start.1 = (bf16[2,2,128,896]{3,2,1,0:T(8,128)(2,1)S(1)}, bf16[2,2,128,896]{3,2,1,0:T(8,128)(2,1)S(1)}, u32[]{:S(2)}, u32[]{:S(2)}) collective-permute-start(bf16[2,2,128,896]{3,2,1,0:T(8,128)(2,1)S(1)} %get-tuple-element.22), channel_id=1, source_target_pairs={{0,1},{1,0},{2,3},{3,2},{4,7},{5,6},{6,5},{7,4},{8,9},{9,8},{10,11... | collective-permute-start | bytes 2752520 | tf_op jit(solution)/shard_map/ppermute | solution.py:27
  67.8 15.0 %collective-permute-start.10 = (bf16[2,2,128,448]{3,2,1,0:T(8,128)(2,1)S(1)}, bf16[2,2,128,448]{3,2,1,0:T(8,128)(2,1)S(1)}, u32[]{:S(2)}, u32[]{:S(2)}) collective-permute-start(bf16[2,2,128,448]{3,2,1,0:T(8,128)(2,1)S(1)} %get-tuple-element.30), channel_id=1, source_target_pairs={{0,1},{1,0},{2,3},{3,2},{4,7},{5,6},{6,5},{7,4},{8,9},{9,8},{10,11... | collective-permute-start | bytes 1376264 | tf_op jit(solution)/shard_map/ppermute | solution.py:27
  75.6 10.0 %collective-permute-start.2 = (bf16[2,128,896]{2,1,0:T(8,128)(2,1)S(1)}, bf16[2,128,896]{2,1,0:T(8,128)(2,1)S(1)}, u32[]{:S(2)}, u32[]{:S(2)}) collective-permute-start(bf16[2,128,896]{2,1,0:T(8,128)(2,1)S(1)} %fusion.1), channel_id=1, source_target_pairs={{0,3},{1,2},{2,1},{3,0},{4,5},{5,4},{6,7},{7,6},{8,11},{9,10},{10,... | collective-permute-start | bytes 1376264 | tf_op jit(solution)/shard_map/ppermute | solution.py:27
  82.9 5.6 %collective-permute-start.11 = (bf16[2,128,448]{2,1,0:T(8,128)(2,1)S(1)}, bf16[2,128,448]{2,1,0:T(8,128)(2,1)S(1)}, u32[]{:S(2)}, u32[]{:S(2)}) collective-permute-start(bf16[2,128,448]{2,1,0:T(8,128)(2,1)S(1)} %fusion.2), channel_id=1, source_target_pairs={{0,3},{1,2},{2,1},{3,0},{4,5},{5,4},{6,7},{7,6},{8,11},{9,10},{10,... | collective-permute-start | bytes 688136 | tf_op jit(solution)/shard_map/ppermute | solution.py:27
  88.9 5.3 %collective-permute-start.3 = (bf16[2,128,448]{2,1,0:T(8,128)(2,1)S(1)}, bf16[2,128,448]{2,1,0:T(8,128)(2,1)S(1)}, u32[]{:S(2)}, u32[]{:S(2)}) collective-permute-start(bf16[2,128,448]{2,1,0:T(8,128)(2,1)S(1)} %get-tuple-element.37.own), channel_id=1, source_target_pairs={{0,3},{1,2},{2,1},{3,0},{4,5},{5,4},{6,7},{7,6},{8,11},{9,10},{10,... | collective-permute-start | bytes 688136 | tf_op jit(solution)/shard_map/ppermute | solution.py:27
  90.3 9.1 %collective-permute-start.12 = (bf16[2,128,896]{2,1,0:T(8,128)(2,1)S(1)}, bf16[2,128,896]{2,1,0:T(8,128)(2,1)S(1)}, u32[]{:S(2)}, u32[]{:S(2)}) collective-permute-start(bf16[2,128,896]{2,1,0:T(8,128)(2,1)S(1)} %pad_maximum_fusion.3.own), channel_id=1, source_target_pairs={{0,3},{1,2},{2,1},{3,0},{4,5},{5,4},{6,7},{7,6},{8,11},{9,10},{10,... | collective-permute-start | bytes 1376264 | tf_op jit(solution)/shard_map/ppermute | solution.py:27
  94.2 14.7 %collective-permute-start.4 = (bf16[2,2,128,448]{3,2,1,0:T(8,128)(2,1)S(1)}, bf16[2,2,128,448]{3,2,1,0:T(8,128)(2,1)S(1)}, u32[]{:S(2)}, u32[]{:S(2)}) collective-permute-start(bf16[2,2,128,448]{3,2,1,0:T(8,128)(2,1)S(1)} %pad_maximum_fusion.2), channel_id=1, source_target_pairs={{0,1},{1,0},{2,3},{3,2},{4,7},{5,6},{6,5},{7,4},{8,9},{9,8},{10,11... | collective-permute-start | bytes 1376264 | tf_op jit(solution)/shard_map/ppermute | solution.py:27
  99.6 19.2 %collective-permute-start.13 = (bf16[2,2,128,896]{3,2,1,0:T(8,128)(2,1)S(1)}, bf16[2,2,128,896]{3,2,1,0:T(8,128)(2,1)S(1)}, u32[]{:S(2)}, u32[]{:S(2)}) collective-permute-start(bf16[2,2,128,896]{3,2,1,0:T(8,128)(2,1)S(1)} %pad_maximum_fusion.1), channel_id=1, source_target_pairs={{0,1},{1,0},{2,3},{3,2},{4,7},{5,6},{6,5},{7,4},{8,9},{9,8},{10,11... | collective-permute-start | bytes 2752520 | tf_op jit(solution)/shard_map/ppermute | solution.py:27
  110.8 18.6 %collective-permute-start.5 = (bf16[512,1024]{1,0:T(8,128)(2,1)S(1)}, bf16[512,1024]{1,0:T(8,128)(2,1)S(1)}, u32[]{:S(2)}, u32[]{:S(2)}) collective-permute-start(bf16[512,1024]{1,0:T(8,128)(2,1)S(1)} %get-tuple-element.24), channel_id=1, source_target_pairs={{0,4},{4,0},{1,5},{5,1},{2,6},{6,2},{3,7},{7,3},{8,12},{12,8},{9,1... | collective-permute-start | bytes 3145736 | tf_op jit(solution)/shard_map/ppermute | solution.py:18
  125.1 9.3 %collective-permute-start.14 = (bf16[512,1024]{1,0:T(8,128)(2,1)}, bf16[512,1024]{1,0:T(8,128)(2,1)}, u32[]{:S(2)}, u32[]{:S(2)}) collective-permute-start(bf16[512,1024]{1,0:T(8,128)(2,1)} %get-tuple-element.32), channel_id=1, source_target_pairs={{0,4},{4,0},{1,5},{5,1},{2,6},{6,2},{3,7},{7,3},{8,12},{12,8},{9,1... | collective-permute-start | bytes 3145736 | tf_op jit(solution)/shard_map/ppermute | solution.py:18
  130.7 21.5 %all-to-all-start.1 = ((bf16[16,32,1024]{2,1,0:T(8,128)(2,1)}), bf16[16,32,1024]{2,1,0:T(8,128)(2,1)S(1)}, u32[]{:S(2)}, u32[]{:S(2)}) async-start(bf16[16,32,1024]{2,1,0:T(8,128)(2,1)} %bitcast.36), calls=%async_computation.1 | async-start | bytes 2097152 | tf_op jit(solution)/shard_map/all_to_all | solution.py:175
  153.3 19.1 %all-to-all-start.3 = ((bf16[16,32,1024]{2,1,0:T(8,128)(2,1)}), bf16[16,32,1024]{2,1,0:T(8,128)(2,1)S(1)}, u32[]{:S(2)}, u32[]{:S(2)}) async-start(bf16[16,32,1024]{2,1,0:T(8,128)(2,1)} %bitcast.35), calls=%async_computation.3 | async-start | bytes 2097152 | tf_op jit(solution)/shard_map/all_to_all | solution.py:175
  158.7 28.4 %collective-permute-start.6 = (bf16[32,1024]{1,0:T(8,128)(2,1)S(1)}, bf16[32,1024]{1,0:T(8,128)(2,1)S(1)}, u32[]{:S(2)}, u32[]{:S(2)}) collective-permute-start(bf16[32,1024]{1,0:T(8,128)(2,1)S(1)} %get-tuple-element.26.own), channel_id=1, source_target_pairs={{0,1},{1,0},{2,3},{3,2},{4,5},{5,4},{6,7},{7,6},{8,9},{9,8},{10,11... | collective-permute-start | bytes 196616 | tf_op jit(solution)/shard_map/ppermute | solution.py:22
  158.8 29.0 %copy-start.6 = (bf16[256,1024]{1,0:T(8,128)(2,1)S(1)}, bf16[256,1024]{1,0:T(8,128)(2,1)}, u32[]{:S(2)}) copy-start(bf16[256,1024]{1,0:T(8,128)(2,1)} %values.4) | copy-start | bytes 1572868
  172.4 16.8 %all-to-all-start.4 = ((bf16[32,2,1024]{2,1,0:T(2,128)(2,1)}), bf16[32,2,1024]{2,1,0:T(2,128)(2,1)S(1)}, u32[]{:S(2)}, u32[]{:S(2)}) async-start(bf16[32,2,1024]{2,1,0:T(2,128)(2,1)} %all_to_all.24), calls=%async_computation.4 | async-start | bytes 262144 | tf_op jit(solution)/shard_map/all_to_all | solution.py:252
  179.0 8.8 %collective-permute-start.7 = (bf16[32,1024]{1,0:T(8,128)(2,1)S(1)}, bf16[32,1024]{1,0:T(8,128)(2,1)S(1)}, u32[]{:S(2)}, u32[]{:S(2)}) collective-permute-start(bf16[32,1024]{1,0:T(8,128)(2,1)S(1)} %get-tuple-element.26.own), channel_id=1, source_target_pairs={{0,2},{1,3},{2,0},{3,1},{4,6},{5,7},{6,4},{7,5},{8,10},{9,11},{10,... | collective-permute-start | bytes 196616 | tf_op jit(solution)/shard_map/ppermute | solution.py:22
  181.0 6.9 %collective-permute-start.8 = (bf16[32,1024]{1,0:T(8,128)(2,1)S(1)}, bf16[32,1024]{1,0:T(8,128)(2,1)S(1)}, u32[]{:S(2)}, u32[]{:S(2)}) collective-permute-start(bf16[32,1024]{1,0:T(8,128)(2,1)S(1)} %get-tuple-element.26.own), channel_id=1, source_target_pairs={{0,3},{1,2},{2,1},{3,0},{4,7},{5,6},{6,5},{7,4},{8,11},{9,10},{10,... | collective-permute-start | bytes 196616 | tf_op jit(solution)/shard_map/ppermute | solution.py:22
  183.9 5.9 %collective-permute-start.15 = (bf16[32,1024]{1,0:T(8,128)(2,1)S(1)}, bf16[32,1024]{1,0:T(8,128)(2,1)S(1)}, u32[]{:S(2)}, u32[]{:S(2)}) collective-permute-start(bf16[32,1024]{1,0:T(8,128)(2,1)S(1)} %shard_map.120.own), channel_id=1, source_target_pairs={{0,1},{1,0},{2,3},{3,2},{4,5},{5,4},{6,7},{7,6},{8,9},{9,8},{10,11... | collective-permute-start | bytes 196616 | tf_op jit(solution)/shard_map/ppermute | solution.py:22
  184.4 5.4 %collective-permute-start.16 = (bf16[32,1024]{1,0:T(8,128)(2,1)S(1)}, bf16[32,1024]{1,0:T(8,128)(2,1)S(1)}, u32[]{:S(2)}, u32[]{:S(2)}) collective-permute-start(bf16[32,1024]{1,0:T(8,128)(2,1)S(1)} %shard_map.120.own), channel_id=1, source_target_pairs={{0,2},{1,3},{2,0},{3,1},{4,6},{5,7},{6,4},{7,5},{8,10},{9,11},{10,... | collective-permute-start | bytes 196616 | tf_op jit(solution)/shard_map/ppermute | solution.py:22
  187.2 4.5 %collective-permute-start.17 = (bf16[32,1024]{1,0:T(8,128)(2,1)S(1)}, bf16[32,1024]{1,0:T(8,128)(2,1)S(1)}, u32[]{:S(2)}, u32[]{:S(2)}) collective-permute-start(bf16[32,1024]{1,0:T(8,128)(2,1)S(1)} %shard_map.120.own), channel_id=1, source_target_pairs={{0,3},{1,2},{2,1},{3,0},{4,7},{5,6},{6,5},{7,4},{8,11},{9,10},{10,... | collective-permute-start | bytes 196616 | tf_op jit(solution)/shard_map/ppermute | solution.py:22
  (13 other events, 74.6 us)

commit v2 on v1

v2 whole, which is shorter than its diff:
```python
import functools

import jax
import jax.numpy as jnp
from jax import lax
from jax.experimental import pallas as pl
from jax.experimental.pallas import tpu as pltpu
from jax.sharding import Mesh
from jax.sharding import PartitionSpec as P

F32 = jnp.float32
BF16 = jnp.bfloat16
SEQ = ("y", "z", "c")
VMEM_LIMIT = 48 * 1024 * 1024


def swap_core(value):
    return lax.ppermute(value, "c", [(0, 1), (1, 0)])


def swap_x(value, k):
    return lax.ppermute(value, "x", [(i, i ^ k) for i in range(4)])


def swap_near(value, first):
    steps = (1, 3) if first else (3, 1)
    return lax.ppermute(
        value, ("c", "x"), [(c * 4 + x, c * 4 + (x ^ steps[c])) for c in range(2) for x in range(4)]
    )


def swap_axis(axis, value, k):
    return lax.ppermute(value, axis, [(i, i ^ k) for i in range(4)])


def dot(a, b):
    return jnp.dot(a, b, preferred_element_type=F32)


def dot_t(a, b):
    return lax.dot_general(a, b, (((1,), (1,)), ((), ())), preferred_element_type=F32)


def call(body, outs, inputs, scalars=(), flops=0, scratch=()):
    specs = [pl.BlockSpec(memory_space=pltpu.SMEM)] * len(scalars)
    specs += [pl.BlockSpec(memory_space=pltpu.VMEM)] * len(inputs)
    moved = sum(v.size * v.dtype.itemsize for v in list(inputs) + list(outs))
    return pl.pallas_call(
        body,
        out_shape=outs,
        in_specs=specs,
        out_specs=[pl.BlockSpec(memory_space=pltpu.VMEM)] * len(outs),
        scratch_shapes=list(scratch),
        compiler_params=pltpu.CompilerParams(vmem_limit_bytes=VMEM_LIMIT),
        cost_estimate=pl.CostEstimate(flops=flops, bytes_accessed=moved, transcendentals=0),
    )(*scalars, *inputs)


def shape(dims, dtype):
    return jax.ShapeDtypeStruct(dims, dtype)


def bounds(lengths):
    count = lengths.shape[1]
    row = lax.broadcasted_iota(jnp.int32, (count, count), 0)
    column = lax.broadcasted_iota(jnp.int32, (count, count), 1)
    wide = jnp.broadcast_to(lengths, (count, count)).astype(F32)
    ends = jnp.sum(jnp.where(column <= row, wide, 0.0), axis=1, keepdims=True)
    size = jnp.sum(jnp.where(column == row, wide, 0.0), axis=1, keepdims=True)
    return ends - size, ends, size


def membership(lengths, length):
    starts, ends, size = bounds(lengths)
    count = lengths.shape[1]
    position = lax.broadcasted_iota(jnp.int32, (count, length), 1).astype(F32)
    inside = (position >= starts) & (position < ends)
    return jnp.where(inside, 1.0, 0.0).astype(BF16), size


def pool_kernel(lengths, states, cots, repeated, pooled, pooled_cot):
    pooling, size = membership(lengths[...], states.shape[0])
    width = states.shape[1]
    pooled[...] = (dot(pooling, states[...]) / size).astype(BF16)
    pooled_cot[...] = dot(pooling, cots[...]).astype(BF16)
    for i in range(repeated.shape[0]):
        repeated[i, :, :width] = pooled[...]
        repeated[i, :, width:] = pooled_cot[...]


def product_kernel(offsets, w_enc, w_gate, w_lift, w_down, w_dec, keep, send, whole):
    hid = w_gate.shape[0]
    part = hid // 4
    whole[:hid] = dot_t(w_gate[...], w_enc[...]).astype(BF16)
    whole[hid : 2 * hid] = dot_t(w_lift[...], w_enc[...]).astype(BF16)
    whole[2 * hid :] = dot(w_down[...], w_dec[...]).astype(BF16)
    for k in range(4):
        out = keep if k < 2 else send
        for i in range(3):
            place = pl.multiple_of(offsets[k] + i * hid, 16)
            to = (k % 2) * 3 * part + i * part
            out[to : to + part] = whole[pl.ds(place, part), :]


def encode_kernel(pooled, cot, w_enc, w_dec, rep, back):
    rep[...] = dot(pooled[...], w_enc[...]).astype(BF16)
    back[...] = dot_t(dot_t(cot[...], w_dec[...]).astype(BF16), w_enc[...])


def hidden_rows(rows, products):
    part = products.shape[0] // 3
    width = products.shape[1]
    both = dot_t(products[: 2 * part], rows[:, :width])
    gate, lift = both[:part], both[part:]
    grad_hidden = dot_t(products[2 * part :], rows[:, width:])
    sig = 1.0 / (1.0 + jnp.exp(-gate))
    silu = gate * sig
    grad_gate = grad_hidden * lift * sig * (1.0 + gate * (1.0 - sig))
    grads = jnp.concatenate([grad_gate, grad_hidden * silu], axis=0).astype(BF16)
    return (silu * lift).astype(BF16), grads


def near_kernel(rows, products, hidden, grads):
    hidden[...], grads[...] = hidden_rows(rows[...], products[...])


def far_kernel(rows, products, near_hidden, hidden, partial):
    half = near_hidden.shape[1]
    part = products.shape[0] // 3
    hidden[:, :half] = near_hidden[...]
    hidden[:, half:], grads = hidden_rows(rows[...], products[...])
    partial[...] = dot(grads.T, products[: 2 * part]).astype(BF16)


def place_blocks(blocks, whole, outs):
    patches = whole.shape[0] // 16
    for k, out in enumerate(outs):
        for i in range(4):
            place = pl.multiple_of(blocks[4 * k + i], patches)
            out[i * patches : (i + 1) * patches] = whole[pl.ds(place, patches), :]


def near_grad_kernel(blocks, grads, products, other, *rest):
    whole = rest[-1]
    total = dot(grads[...].T, products[: grads.shape[0]]) + other[...].astype(F32)
    whole[...] = total.astype(BF16)
    place_blocks(blocks, whole, rest[:-1])


def down_far_kernel(offsets, own, one, two, three, w_down, out, stack):
    part, span = own.shape[0], out.shape[0]
    for k, block in enumerate((own, one, two, three)):
        stack[pl.ds(pl.multiple_of(offsets[k], 16), part), :] = block[:, span:]
    out[...] = dot(stack[...].T, w_down[...]).astype(BF16)


def down_near_kernel(offsets, blocks, own, one, two, three, w_down, other, *rest):
    stack, whole = rest[-2:]
    part, span = own.shape[0], other.shape[0]
    for k, block in enumerate((own, one, two, three)):
        stack[pl.ds(pl.multiple_of(offsets[k], 16), part), :] = block[:, :span]
    total = dot(stack[...].T, w_down[...]) + other[...].astype(F32)
    whole[...] = total.astype(BF16)
    place_blocks(blocks, whole, rest[:-2])


def add_kernel(own, one, two, three, *outs):
    total = (
        own[...].astype(F32) + one[...].astype(F32) + two[...].astype(F32) + three[...].astype(F32)
    )
    patches = own.shape[0] // 4
    for i, out in enumerate(outs):
        out[...] = total[i * patches : (i + 1) * patches].astype(out.dtype)


def decode_kernel(own, one, two, three, rep, weight, owners, partial, outgoing):
    total = own[...] + one[...].astype(F32) + two[...].astype(F32) + three[...].astype(F32)
    total = total + rep[...].astype(F32)
    states = total.astype(BF16)
    partial[...] = dot(states, weight[...]).astype(BF16)
    count = rep.shape[0]
    own_row = jnp.broadcast_to(owners[...], (count, count))
    row = lax.broadcasted_iota(jnp.int32, (count, count), 0)
    column = lax.broadcasted_iota(jnp.int32, (count, count), 1)
    own_column = jnp.sum(jnp.where(row == column, own_row, 0), axis=1, keepdims=True)
    same = jnp.where((own_column == own_row) & (row < column), 1, 0)
    targets = 2 * owners[...] + jnp.sum(same, axis=0, keepdims=True)
    slots = lax.broadcasted_iota(jnp.int32, (2 * count, count), 0)
    routing = jnp.where(slots == targets, 1.0, 0.0).astype(BF16)
    outgoing[...] = dot(routing, states).astype(BF16)


def grad_kernel(own, one, two, three, back, partial):
    total = own[...] + one[...].astype(F32) + two[...].astype(F32) + three[...].astype(F32)
    partial[...] = (total + back[...]).astype(BF16)


def finish_kernel(forward, lengths, values, own, one, two, three, out):
    total = (
        own[...].astype(F32) + one[...].astype(F32) + two[...].astype(F32) + three[...].astype(F32)
    )
    pooling, size = membership(lengths[...], values.shape[0])
    if not forward:
        total = total / size
    high = total.astype(BF16)
    low = (total - high.astype(F32)).astype(BF16)
    pick = (((0,), (0,)), ((), ()))
    spread = lax.dot_general(pooling, high, pick, preferred_element_type=F32)
    spread = spread + lax.dot_general(pooling, low, pick, preferred_element_type=F32)
    out[...] = (values[...].astype(F32) + spread).astype(BF16)


def on_device(
    byte_states, patch_lengths, patch_owner, w_enc, w_gate, w_lift, w_down, w_dec, byte_cot
):
    patches = patch_lengths.shape[1]
    width = byte_states.shape[1]
    latent = w_enc.shape[1]
    hid = w_gate.shape[1]
    part = hid // 4
    group = 16 * patches
    x, y, z = lax.axis_index("x"), lax.axis_index("y"), lax.axis_index("z")
    step = jnp.where(lax.axis_index("c") == 0, 1, 3)
    halving = (jnp.stack([x, x ^ step ^ 2, x ^ step, x ^ 2]) * part).astype(jnp.int32)
    offsets = (jnp.stack([x, x ^ 1, x ^ 2, x ^ 3]) * part).astype(jnp.int32)
    near_z, near_y = z ^ jnp.arange(4), y ^ jnp.arange(4)
    blocks = ((near_y[None, :] * 4 + near_z[:, None]) * patches).reshape(16).astype(jnp.int32)
    owners = patch_owner.reshape(1, patches)
    w_gate, w_lift = w_gate.T, w_lift.T

    repeated, pooled, pooled_cot = call(
        pool_kernel,
        [shape((16, patches, 2 * width), BF16)] + [shape((patches, width), BF16)] * 2,
        [patch_lengths, byte_states, byte_cot],
        flops=4 * patches * byte_states.size,
    )
    near = lax.all_to_all(repeated, ("y", "z"), split_axis=0, concat_axis=0, tiled=True)
    near = near.reshape(group, 2 * width)
    pooled, w_gate = lax.optimization_barrier((pooled, w_gate))
    keep, send = call(
        product_kernel,
        [shape((6 * part, width), BF16)] * 2,
        [w_enc, w_gate, w_lift, w_down, w_dec],
        [halving],
        flops=6 * hid * width * latent,
        scratch=[pltpu.VMEM((3 * hid, width), BF16)],
    )
    patch_rep, back = call(
        encode_kernel,
        [shape((patches, latent), BF16), shape((patches, width), F32)],
        [pooled, pooled_cot, w_enc, w_dec],
        flops=6 * patches * width * latent,
    )
    first = swap_near(send, True)
    half = 3 * part
    second = swap_near((keep[half:].astype(F32) + first[half:].astype(F32)).astype(BF16), False)
    products = (keep[:half].astype(F32) + first[:half].astype(F32) + second.astype(F32)).astype(BF16)
    far = swap_core(near)
    flops = 2 * group * width * 3 * part
    near_hidden, near_grads = call(
        near_kernel,
        [shape((part, group), BF16), shape((2 * part, group), BF16)],
        [near, products],
        flops=flops,
    )
    hidden, far_partial = call(
        far_kernel,
        [shape((part, 2 * group), BF16), shape((group, width), BF16)],
        [far, products, near_hidden],
        flops=flops + 4 * group * width * part,
    )
    hiddens = [hidden] + [swap_x(hidden, k) for k in (1, 2, 3)]
    pieces = [shape((4 * patches, width), BF16)] * 4

    def over_z(own, *sends):
        return [own] + [swap_axis("z", send, k + 1) for k, send in enumerate(sends)]

    def over_y(terms):
        own, *sends = call(
            add_kernel,
            [shape((patches, width), F32)] + [shape((patches, width), BF16)] * 3,
            terms,
            flops=4 * terms[0].size,
        )
        return [own] + [swap_axis("y", send, k + 1) for k, send in enumerate(sends)]

    terms = call(
        near_grad_kernel,
        pieces,
        [near_grads, products, swap_core(far_partial)],
        [blocks],
        flops=4 * group * width * part,
        scratch=[pltpu.VMEM((group, width), BF16)],
    )
    terms = over_z(*terms)
    hiddens, terms = lax.optimization_barrier((hiddens, terms))
    terms = over_y(terms)
    (far,) = call(
        down_far_kernel,
        [shape((group, latent), BF16)],
        [*hiddens, w_down],
        [offsets],
        flops=2 * group * latent * hid,
        scratch=[pltpu.VMEM((hid, group), BF16)],
    )
    (grad_pool,) = call(
        grad_kernel, [shape((patches, width), BF16)], [*terms, back], flops=4 * back.size
    )
    terms = call(
        down_near_kernel,
        pieces,
        [*hiddens, w_down, swap_core(far)],
        [offsets, blocks],
        flops=2 * group * latent * hid,
        scratch=[pltpu.VMEM((hid, group), BF16), pltpu.VMEM((group, latent), BF16)],
    )
    terms = over_y(over_z(*terms))
    decoded, outgoing = call(
        decode_kernel,
        [shape((patches, width), BF16), shape((2 * patches, latent), BF16)],
        [*terms, patch_rep, w_dec, owners],
        flops=2 * patches * width * latent,
    )
    latent_states = lax.all_to_all(outgoing, SEQ, split_axis=0, concat_axis=0, tiled=True)

    def finish(forward, values, partial):
        return call(
            functools.partial(finish_kernel, forward),
            [shape(values.shape, BF16)],
            [patch_lengths, values, partial] + [swap_x(partial, k) for k in (1, 2, 3)],
            flops=4 * patches * values.size,
        )[0]

    byte_out = finish(True, byte_states, decoded)
    return byte_out, finish(False, byte_cot, grad_pool), latent_states


def solution(mesh):
    fine = Mesh(mesh.devices.reshape(4, 4, 2, 4), ("y", "z", "c", "x"))
    return jax.shard_map(
        on_device,
        mesh=fine,
        in_specs=(
            P(SEQ, None),
            P(SEQ, None),
            P(SEQ, None),
            P(None, "x"),
            P("x", SEQ),
            P("x", SEQ),
            P(SEQ, "x"),
            P("x", None),
            P(SEQ, None),
        ),
        out_specs=(P(SEQ, None), P(SEQ, None), P(SEQ, "x")),
        check_vma=False,
    )
```

time: 195 us -> 138 us (0.71)
  blocking collectives: 43.4 us -> 0 us
  waiting for transfers between devices: 67.1 us -> 52.6 us
  starting transfers between devices: 41.9 us -> 51.2 us
  other arithmetic: 7.35 us -> 3.16 us
  Pallas kernels: 21.8 us -> 19.1 us
    all_to_all x2 -> x0, blocking collectives: 43.4 us -> none  [gather_seq(): lax.all_to_all(repeated, ('y', 'z'), split_axis=0, concat_axis=0, tiled=T...]
    ppermute x8 -> x2, waiting for transfers between devices: 37.6 us -> 8.87 us  [swap_near(): lax.ppermute(value, ('c', 'x'), [(c * 4 + x, c * 4 + (x ^ steps[c])) for...]
    ppermute x0 -> x12, starting transfers between devices: none -> 17.4 us  [swap_axis(): return lax.ppermute(value, axis, [(i, i ^ k) for i in range(4)])]
    ppermute x6 -> x9, waiting for transfers between devices: 1.75 us -> 14.4 us  [swap_x(): return lax.ppermute(value, 'x', [(i, i ^ k) for i in range(4)])]
    all_to_all x2 -> x1, waiting for transfers between devices: 27.7 us -> 15.2 us  [on_device(): lax.all_to_all(repeated, ('y', 'z'), split_axis=0, concat_axis=0, tiled=T...]
    ppermute x0 -> x12, waiting for transfers between devices: none -> 9.58 us  [swap_axis(): return lax.ppermute(value, axis, [(i, i ^ k) for i in range(4)])]
    ppermute x8 -> x2, starting transfers between devices: 12 us -> 3.77 us  [swap_near(): lax.ppermute(value, ('c', 'x'), [(c * 4 + x, c * 4 + (x ^ steps[c])) for...]
    ppermute x4 -> x3, waiting for transfers between devices: 0.01 us -> 4.61 us  [swap_core(): return lax.ppermute(value, 'c', [(0, 1), (1, 0)])]
  transfers between devices with their start and end apart: 21 -> 28, of which waited for: 11 -> 14; matrix products, arithmetic and copies ran while one was open for 5% -> 2% of each run, Pallas kernels for 7% -> 10%
where the time goes in v2:
time: 138 us; the launch traced here: 137 us
  waiting for transfers between devices  52.6 us (38%)
  starting transfers between devices  51.2 us (37%)
  Pallas kernels  19.1 us (14%)
  local copies, waits for them, and re-layouts  9.77 us (7%)
  other arithmetic  3.16 us (2%)
    pallas_call x14, Pallas kernels, call(): pl.pallas_call(body, out_shape=outs, in_specs=specs, out_specs=[pl.BlockS...  19.1 us
    ppermute x12, starting transfers between devices, swap_axis(): return lax.ppermute(value, axis, [(i, i ^ k) for i in range(4)])  17.4 us
    all_to_all x1, waiting for transfers between devices, on_device(): lax.all_to_all(repeated, ('y', 'z'), split_axis=0, concat_axis=0, tiled=T...  15.2 us
    ppermute x9, waiting for transfers between devices, swap_x(): return lax.ppermute(value, 'x', [(i, i ^ k) for i in range(4)])  14.4 us
    ppermute x12, waiting for transfers between devices, swap_axis(): return lax.ppermute(value, axis, [(i, i ^ k) for i in range(4)])  9.58 us
    ppermute x9, starting transfers between devices, swap_x(): return lax.ppermute(value, 'x', [(i, i ^ k) for i in range(4)])  9.1 us
    ppermute x2, waiting for transfers between devices, swap_near(): lax.ppermute(value, ('c', 'x'), [(c * 4 + x, c * 4 + (x ^ steps[c])) for...  8.87 us
    all_to_all x1, starting transfers between devices, on_device(): lax.all_to_all(repeated, ('y', 'z'), split_axis=0, concat_axis=0, tiled=T...  8.6 us
  transfers between devices with their start and end apart: 28, of which 14 were waited for; matrix products, arithmetic and copies ran while one was open for 2% of the time, Pallas kernels for 10%

profile of v2, /device:TPU:1, one launch (start us, length us, event | category | flops | bytes accessed | tf_op | source)
XLA Modules:
  0.0 136.7 jit_solution(997377478651106485)
XLA Ops:
  5.8 8.6 %all-to-all-start = ((bf16[16,32,2048]{2,1,0:T(8,128)(2,1)}), bf16[16,32,2048]{2,1,0:T(8,128)(2,1)S(1)}, u32[]{:S(2)}, u32[]{:S(2)}) async-start(bf16[16,32,2048]{2,1,0:T(8,128)(2,1)} %copy-done.8), calls=%async_computation | async-start | bytes 4194304 | tf_op jit(solution)/shard_map/all_to_all | solution.py:237
  18.0 6.6 %shard_map.113 = (bf16[672,1024]{1,0:T(8,128)(2,1)S(1)}, bf16[672,1024]{1,0:T(8,128)(2,1)}) custom-call(s32[4]{0:T(128)S(1)} %get-tuple-element.82.offsets, bf16[1024,1024]{1,0:T(8,128)(2,1)} %w_enc.3, bf16[448,1024]{1,0:T(8,128)(2,1)S(1)} %bitcast.13, bf16[448,1024]{1,0:T(8,128)(2,1)S(1)} %bitcast.14, bf16[448,1024]{1,0:T(8,128)(2,1)S(1)} %copy-done.1, ...), custom_call_target="tpu_custom_call" | custom-call | flops 2818572288 | bytes 9699328 | tf_op jit(solution)/shard_map/pallas_call | solution.py:48
  24.7 2.5 %collective-permute-start.1 = (bf16[672,1024]{1,0:T(8,128)(2,1)}, bf16[672,1024]{1,0:T(8,128)(2,1)}, u32[]{:S(2)}, u32[]{:S(2)}) collective-permute-start(bf16[672,1024]{1,0:T(8,128)(2,1)} %get-tuple-element.46), channel_id=1, source_target_pairs={{0,1},{1,0},{2,3},{3,2},{4,7},{5,6},{6,5},{7,4},{8,9},{9,8},{10,11... | collective-permute-start | bytes 4128776 | tf_op jit(solution)/shard_map/ppermute | solution.py:27
  27.1 15.2 %all-to-all-done = bf16[16,32,2048]{2,1,0:T(8,128)(2,1)S(1)} async-done(((bf16[16,32,2048]{2,1,0:T(8,128)(2,1)}), bf16[16,32,2048]{2,1,0:T(8,128)(2,1)S(1)}, u32[]{:S(2)}, u32[]{:S(2)}) %all-to-all-start) | async-done | bytes 2097184 | tf_op jit(solution)/shard_map/all_to_all | solution.py:237
  42.3 3.5 %collective-permute-start = (bf16[512,2048]{1,0:T(8,128)(2,1)S(1)}, bf16[512,2048]{1,0:T(8,128)(2,1)S(1)}, u32[]{:S(2)}, u32[]{:S(2)}) collective-permute-start(bf16[512,2048]{1,0:T(8,128)(2,1)S(1)} %bitcast.10), channel_id=1, source_target_pairs={{0,4},{4,0},{1,5},{5,1},{2,6},{6,2},{3,7},{7,3},{8,12},{12,8},{9,1... | collective-permute-start | bytes 6291464 | tf_op jit(solution)/shard_map/ppermute | solution.py:18
  48.4 8.9 %collective-permute-done.2 = bf16[336,1024]{1,0:T(8,128)(2,1)S(1)} collective-permute-done((bf16[336,1024]{1,0:T(8,128)(2,1)S(1)}, bf16[336,1024]{1,0:T(8,128)(2,1)S(1)}, u32[]{:S(2)}, u32[]{:S(2)}) %collective-permute-start.2) | collective-permute-done | bytes 688160 | tf_op jit(solution)/shard_map/ppermute | solution.py:27
  59.8 2.3 %shard_map.115 = (bf16[112,1024]{1,0:T(8,128)(2,1)S(1)}, bf16[512,1024]{1,0:T(8,128)(2,1)}) custom-call(bf16[512,2048]{1,0:T(8,128)(2,1)S(1)} %collective-permute-done.rows, bf16[336,1024]{1,0:T(8,128)(2,1)S(1)} %add_convert_fusion.products, bf16[112,512]{1,0:T(8,128)(2,1)S(1)} %get-tuple-element.47.near_hidden), custom_call_target="tpu_custom_call" | custom-call | flops 587202560 | bytes 4177920 | tf_op jit(solution)/shard_map/pallas_call | solution.py:48
  62.1 2.1 %collective-permute-start.6 = (bf16[512,1024]{1,0:T(8,128)(2,1)}, bf16[512,1024]{1,0:T(8,128)(2,1)S(1)}, u32[]{:S(2)}, u32[]{:S(2)}) collective-permute-start(bf16[512,1024]{1,0:T(8,128)(2,1)} %get-tuple-element.50), channel_id=1, source_target_pairs={{0,4},{4,0},{1,5},{5,1},{2,6},{6,2},{3,7},{7,3},{8,12},{12,8},{9,1... | collective-permute-start | bytes 3145736 | tf_op jit(solution)/shard_map/ppermute | solution.py:18
  64.3 2.3 %collective-permute-done.6.other = bf16[512,1024]{1,0:T(8,128)(2,1)S(1)} collective-permute-done((bf16[512,1024]{1,0:T(8,128)(2,1)}, bf16[512,1024]{1,0:T(8,128)(2,1)S(1)}, u32[]{:S(2)}, u32[]{:S(2)}) %collective-permute-start.6) | collective-permute-done | bytes 1048608 | tf_op jit(solution)/shard_map/ppermute | solution.py:18
  68.1 2.2 %collective-permute-start.8 = (bf16[128,1024]{1,0:T(8,128)(2,1)S(1)}, bf16[128,1024]{1,0:T(8,128)(2,1)S(1)}, u32[]{:S(2)}, u32[]{:S(2)}) collective-permute-start(bf16[128,1024]{1,0:T(8,128)(2,1)S(1)} %get-tuple-element.53), channel_id=1, source_target_pairs={{0,16},{8,24},{16,0},{24,8},{1,17},{9,25},{17,1},{25,9},{2,18},{10... | collective-permute-start | bytes 786440 | tf_op jit(solution)/shard_map/ppermute | solution.py:33
  74.1 4.9 %collective-permute-done.4.two = bf16[112,1024]{1,0:T(8,128)(2,1)S(1)} collective-permute-done((bf16[112,1024]{1,0:T(8,128)(2,1)S(1)}, bf16[112,1024]{1,0:T(8,128)(2,1)S(1)}, u32[]{:S(2)}, u32[]{:S(2)}) %collective-permute-start.4) | collective-permute-done | bytes 229408 | tf_op jit(solution)/shard_map/ppermute | solution.py:22
  79.1 6.5 %collective-permute-done.5.three = bf16[112,1024]{1,0:T(8,128)(2,1)S(1)} collective-permute-done((bf16[112,1024]{1,0:T(8,128)(2,1)S(1)}, bf16[112,1024]{1,0:T(8,128)(2,1)S(1)}, u32[]{:S(2)}, u32[]{:S(2)}) %collective-permute-start.5) | collective-permute-done | bytes 229408 | tf_op jit(solution)/shard_map/ppermute | solution.py:22
  87.5 2.3 %collective-permute-done.10.other = bf16[512,1024]{1,0:T(8,128)(2,1)S(1)} collective-permute-done((bf16[512,1024]{1,0:T(8,128)(2,1)S(1)}, bf16[512,1024]{1,0:T(8,128)(2,1)S(1)}, u32[]{:S(2)}, u32[]{:S(2)}) %collective-permute-start.10) | collective-permute-done | bytes 1048608 | tf_op jit(solution)/shard_map/ppermute | solution.py:18
  91.3 2.5 %collective-permute-start.12 = (bf16[128,1024]{1,0:T(8,128)(2,1)S(1)}, bf16[128,1024]{1,0:T(8,128)(2,1)S(1)}, u32[]{:S(2)}, u32[]{:S(2)}) collective-permute-start(bf16[128,1024]{1,0:T(8,128)(2,1)S(1)} %get-tuple-element.61), channel_id=1, source_target_pairs={{0,16},{8,24},{16,0},{24,8},{1,17},{9,25},{17,1},{25,9},{2,18},{10... | collective-permute-start | bytes 786440 | tf_op jit(solution)/shard_map/ppermute | solution.py:33
  96.3 2.4 %collective-permute-start.21 = (bf16[32,1024]{1,0:T(8,128)(2,1)S(1)}, bf16[32,1024]{1,0:T(8,128)(2,1)S(1)}, u32[]{:S(2)}, u32[]{:S(2)}) collective-permute-start(bf16[32,1024]{1,0:T(8,128)(2,1)S(1)} %get-tuple-element.77), channel_id=1, source_target_pairs={{0,64},{32,96},{64,0},{96,32},{1,65},{33,97},{65,1},{97,33},{2,66}... | collective-permute-start | bytes 196616 | tf_op jit(solution)/shard_map/ppermute | solution.py:33
  98.8 2.2 %collective-permute-start.22 = (bf16[32,1024]{1,0:T(8,128)(2,1)S(1)}, bf16[32,1024]{1,0:T(8,128)(2,1)S(1)}, u32[]{:S(2)}, u32[]{:S(2)}) collective-permute-start(bf16[32,1024]{1,0:T(8,128)(2,1)S(1)} %get-tuple-element.78), channel_id=1, source_target_pairs={{0,96},{32,64},{64,32},{96,0},{1,97},{33,65},{65,33},{97,1},{2,98}... | collective-permute-start | bytes 196616 | tf_op jit(solution)/shard_map/ppermute | solution.py:33
  100.9 4.6 %collective-permute-done.12.two = bf16[128,1024]{1,0:T(8,128)(2,1)S(1)} collective-permute-done((bf16[128,1024]{1,0:T(8,128)(2,1)S(1)}, bf16[128,1024]{1,0:T(8,128)(2,1)S(1)}, u32[]{:S(2)}, u32[]{:S(2)}) %collective-permute-start.12) | collective-permute-done | bytes 262176 | tf_op jit(solution)/shard_map/ppermute | solution.py:33
  105.5 2.0 %collective-permute-done.13.three = bf16[128,1024]{1,0:T(8,128)(2,1)S(1)} collective-permute-done((bf16[128,1024]{1,0:T(8,128)(2,1)S(1)}, bf16[128,1024]{1,0:T(8,128)(2,1)S(1)}, u32[]{:S(2)}, u32[]{:S(2)}) %collective-permute-start.13) | collective-permute-done | bytes 262176 | tf_op jit(solution)/shard_map/ppermute | solution.py:33
  108.9 2.4 %collective-permute-start.15 = (bf16[32,1024]{1,0:T(8,128)(2,1)S(1)}, bf16[32,1024]{1,0:T(8,128)(2,1)S(1)}, u32[]{:S(2)}, u32[]{:S(2)}) collective-permute-start(bf16[32,1024]{1,0:T(8,128)(2,1)S(1)} %get-tuple-element.65), channel_id=1, source_target_pairs={{0,64},{32,96},{64,0},{96,32},{1,65},{33,97},{65,1},{97,33},{2,66}... | collective-permute-start | bytes 196616 | tf_op jit(solution)/shard_map/ppermute | solution.py:33
  113.6 2.7 %collective-permute-done.16.three = bf16[32,1024]{1,0:T(8,128)(2,1)S(1)} collective-permute-done((bf16[32,1024]{1,0:T(8,128)(2,1)S(1)}, bf16[32,1024]{1,0:T(8,128)(2,1)S(1)}, u32[]{:S(2)}, u32[]{:S(2)}) %collective-permute-start.16) | collective-permute-done | bytes 65568 | tf_op jit(solution)/shard_map/ppermute | solution.py:33
  117.6 6.3 %all-to-all-start.1 = ((bf16[32,2,1024]{2,1,0:T(2,128)(2,1)}), bf16[32,2,1024]{2,1,0:T(2,128)(2,1)S(1)}, u32[]{:S(2)}, u32[]{:S(2)}) async-start(bf16[32,2,1024]{2,1,0:T(2,128)(2,1)} %all_to_all.12), calls=%async_computation.1 | async-start | bytes 262144 | tf_op jit(solution)/shard_map/all_to_all | solution.py:324
  124.0 2.4 %collective-permute-start.24 = (bf16[32,1024]{1,0:T(8,128)(2,1)S(1)}, bf16[32,1024]{1,0:T(8,128)(2,1)S(1)}, u32[]{:S(2)}, u32[]{:S(2)}) collective-permute-start(bf16[32,1024]{1,0:T(8,128)(2,1)S(1)} %shard_map.124.own), channel_id=1, source_target_pairs={{0,2},{1,3},{2,0},{3,1},{4,6},{5,7},{6,4},{7,5},{8,10},{9,11},{10,... | collective-permute-start | bytes 196616 | tf_op jit(solution)/shard_map/ppermute | solution.py:22
  126.8 3.4 %collective-permute-start.18 = (bf16[32,1024]{1,0:T(8,128)(2,1)S(1)}, bf16[32,1024]{1,0:T(8,128)(2,1)S(1)}, u32[]{:S(2)}, u32[]{:S(2)}) collective-permute-start(bf16[32,1024]{1,0:T(8,128)(2,1)S(1)} %get-tuple-element.70.own), channel_id=1, source_target_pairs={{0,2},{1,3},{2,0},{3,1},{4,6},{5,7},{6,4},{7,5},{8,10},{9,11},{10,... | collective-permute-start | bytes 196616 | tf_op jit(solution)/shard_map/ppermute | solution.py:22
  132.7 2.0 %collective-permute-done.19.three = bf16[32,1024]{1,0:T(8,128)(2,1)S(1)} collective-permute-done((bf16[32,1024]{1,0:T(8,128)(2,1)S(1)}, bf16[32,1024]{1,0:T(8,128)(2,1)S(1)}, u32[]{:S(2)}, u32[]{:S(2)}) %collective-permute-start.19) | collective-permute-done | bytes 65568 | tf_op jit(solution)/shard_map/ppermute | solution.py:22
  (88 shorter events, 35.2 us)
Async XLA Ops:
  5.8 36.5 %all-to-all-start = ((bf16[16,32,2048]{2,1,0:T(8,128)(2,1)}), bf16[16,32,2048]{2,1,0:T(8,128)(2,1)S(1)}, u32[]{:S(2)}, u32[]{:S(2)}) async-start(bf16[16,32,2048]{2,1,0:T(8,128)(2,1)} %copy-done.8), calls=%async_computation | async-start | bytes 4194304 | tf_op jit(solution)/shard_map/all_to_all | solution.py:237
  24.7 21.1 %collective-permute-start.1 = (bf16[672,1024]{1,0:T(8,128)(2,1)}, bf16[672,1024]{1,0:T(8,128)(2,1)}, u32[]{:S(2)}, u32[]{:S(2)}) collective-permute-start(bf16[672,1024]{1,0:T(8,128)(2,1)} %get-tuple-element.46), channel_id=1, source_target_pairs={{0,1},{1,0},{2,3},{3,2},{4,7},{5,6},{6,5},{7,4},{8,9},{9,8},{10,11... | collective-permute-start | bytes 4128776 | tf_op jit(solution)/shard_map/ppermute | solution.py:27
  42.3 17.5 %collective-permute-start = (bf16[512,2048]{1,0:T(8,128)(2,1)S(1)}, bf16[512,2048]{1,0:T(8,128)(2,1)S(1)}, u32[]{:S(2)}, u32[]{:S(2)}) collective-permute-start(bf16[512,2048]{1,0:T(8,128)(2,1)S(1)} %bitcast.10), channel_id=1, source_target_pairs={{0,4},{4,0},{1,5},{5,1},{2,6},{6,2},{3,7},{7,3},{8,12},{12,8},{9,1... | collective-permute-start | bytes 6291464 | tf_op jit(solution)/shard_map/ppermute | solution.py:18
  47.1 10.2 %collective-permute-start.2 = (bf16[336,1024]{1,0:T(8,128)(2,1)S(1)}, bf16[336,1024]{1,0:T(8,128)(2,1)S(1)}, u32[]{:S(2)}, u32[]{:S(2)}) collective-permute-start(bf16[336,1024]{1,0:T(8,128)(2,1)S(1)} %add_convert_fusion.1), channel_id=1, source_target_pairs={{0,3},{1,2},{2,1},{3,0},{4,5},{5,4},{6,7},{7,6},{8,11},{9,10},{10,... | collective-permute-start | bytes 2064392 | tf_op jit(solution)/shard_map/ppermute | solution.py:27
  64.1 9.1 %collective-permute-start.3 = (bf16[112,1024]{1,0:T(8,128)(2,1)S(1)}, bf16[112,1024]{1,0:T(8,128)(2,1)S(1)}, u32[]{:S(2)}, u32[]{:S(2)}) collective-permute-start(bf16[112,1024]{1,0:T(8,128)(2,1)S(1)} %get-tuple-element.55.own), channel_id=1, source_target_pairs={{0,1},{1,0},{2,3},{3,2},{4,5},{5,4},{6,7},{7,6},{8,9},{9,8},{10,11... | collective-permute-start | bytes 688136 | tf_op jit(solution)/shard_map/ppermute | solution.py:22
  67.7 17.9 %collective-permute-start.7 = (bf16[128,1024]{1,0:T(8,128)(2,1)S(1)}, bf16[128,1024]{1,0:T(8,128)(2,1)S(1)}, u32[]{:S(2)}, u32[]{:S(2)}) collective-permute-start(bf16[128,1024]{1,0:T(8,128)(2,1)S(1)} %get-tuple-element.52), channel_id=1, source_target_pairs={{0,8},{8,0},{16,24},{24,16},{1,9},{9,1},{17,25},{25,17},{2,10},{10... | collective-permute-start | bytes 786440 | tf_op jit(solution)/shard_map/ppermute | solution.py:33
  68.1 17.5 %collective-permute-start.8 = (bf16[128,1024]{1,0:T(8,128)(2,1)S(1)}, bf16[128,1024]{1,0:T(8,128)(2,1)S(1)}, u32[]{:S(2)}, u32[]{:S(2)}) collective-permute-start(bf16[128,1024]{1,0:T(8,128)(2,1)S(1)} %get-tuple-element.53), channel_id=1, source_target_pairs={{0,16},{8,24},{16,0},{24,8},{1,17},{9,25},{17,1},{25,9},{2,18},{10... | collective-permute-start | bytes 786440 | tf_op jit(solution)/shard_map/ppermute | solution.py:33
  70.3 15.3 %collective-permute-start.9 = (bf16[128,1024]{1,0:T(8,128)(2,1)S(1)}, bf16[128,1024]{1,0:T(8,128)(2,1)S(1)}, u32[]{:S(2)}, u32[]{:S(2)}) collective-permute-start(bf16[128,1024]{1,0:T(8,128)(2,1)S(1)} %get-tuple-element.54), channel_id=1, source_target_pairs={{0,24},{8,16},{16,8},{24,0},{1,25},{9,17},{17,9},{25,1},{2,26},{10... | collective-permute-start | bytes 786440 | tf_op jit(solution)/shard_map/ppermute | solution.py:33
  71.6 7.4 %collective-permute-start.4 = (bf16[112,1024]{1,0:T(8,128)(2,1)S(1)}, bf16[112,1024]{1,0:T(8,128)(2,1)S(1)}, u32[]{:S(2)}, u32[]{:S(2)}) collective-permute-start(bf16[112,1024]{1,0:T(8,128)(2,1)S(1)} %get-tuple-element.55.own), channel_id=1, source_target_pairs={{0,2},{1,3},{2,0},{3,1},{4,6},{5,7},{6,4},{7,5},{8,10},{9,11},{10,... | collective-permute-start | bytes 688136 | tf_op jit(solution)/shard_map/ppermute | solution.py:22
  73.2 12.4 %collective-permute-start.5 = (bf16[112,1024]{1,0:T(8,128)(2,1)S(1)}, bf16[112,1024]{1,0:T(8,128)(2,1)S(1)}, u32[]{:S(2)}, u32[]{:S(2)}) collective-permute-start(bf16[112,1024]{1,0:T(8,128)(2,1)S(1)} %get-tuple-element.55.own), channel_id=1, source_target_pairs={{0,3},{1,2},{2,1},{3,0},{4,7},{5,6},{6,5},{7,4},{8,11},{9,10},{10,... | collective-permute-start | bytes 688136 | tf_op jit(solution)/shard_map/ppermute | solution.py:22
  91.2 7.6 %collective-permute-start.11 = (bf16[128,1024]{1,0:T(8,128)(2,1)S(1)}, bf16[128,1024]{1,0:T(8,128)(2,1)S(1)}, u32[]{:S(2)}, u32[]{:S(2)}) collective-permute-start(bf16[128,1024]{1,0:T(8,128)(2,1)S(1)} %get-tuple-element.60), channel_id=1, source_target_pairs={{0,8},{8,0},{16,24},{24,16},{1,9},{9,1},{17,25},{25,17},{2,10},{10... | collective-permute-start | bytes 786440 | tf_op jit(solution)/shard_map/ppermute | solution.py:33
  91.3 14.2 %collective-permute-start.12 = (bf16[128,1024]{1,0:T(8,128)(2,1)S(1)}, bf16[128,1024]{1,0:T(8,128)(2,1)S(1)}, u32[]{:S(2)}, u32[]{:S(2)}) collective-permute-start(bf16[128,1024]{1,0:T(8,128)(2,1)S(1)} %get-tuple-element.61), channel_id=1, source_target_pairs={{0,16},{8,24},{16,0},{24,8},{1,17},{9,25},{17,1},{25,9},{2,18},{10... | collective-permute-start | bytes 786440 | tf_op jit(solution)/shard_map/ppermute | solution.py:33
  93.8 13.7 %collective-permute-start.13 = (bf16[128,1024]{1,0:T(8,128)(2,1)S(1)}, bf16[128,1024]{1,0:T(8,128)(2,1)S(1)}, u32[]{:S(2)}, u32[]{:S(2)}) collective-permute-start(bf16[128,1024]{1,0:T(8,128)(2,1)S(1)} %get-tuple-element.62), channel_id=1, source_target_pairs={{0,24},{8,16},{16,8},{24,0},{1,25},{9,17},{17,9},{25,1},{2,26},{10... | collective-permute-start | bytes 786440 | tf_op jit(solution)/shard_map/ppermute | solution.py:33
  95.3 16.0 %collective-permute-start.20 = (bf16[32,1024]{1,0:T(8,128)(2,1)S(1)}, bf16[32,1024]{1,0:T(8,128)(2,1)S(1)}, u32[]{:S(2)}, u32[]{:S(2)}) collective-permute-start(bf16[32,1024]{1,0:T(8,128)(2,1)S(1)} %get-tuple-element.76), channel_id=1, source_target_pairs={{0,32},{32,0},{64,96},{96,64},{1,33},{33,1},{65,97},{97,65},{2,34}... | collective-permute-start | bytes 196616 | tf_op jit(solution)/shard_map/ppermute | solution.py:33
  96.3 17.0 %collective-permute-start.21 = (bf16[32,1024]{1,0:T(8,128)(2,1)S(1)}, bf16[32,1024]{1,0:T(8,128)(2,1)S(1)}, u32[]{:S(2)}, u32[]{:S(2)}) collective-permute-start(bf16[32,1024]{1,0:T(8,128)(2,1)S(1)} %get-tuple-element.77), channel_id=1, source_target_pairs={{0,64},{32,96},{64,0},{96,32},{1,65},{33,97},{65,1},{97,33},{2,66}... | collective-permute-start | bytes 196616 | tf_op jit(solution)/shard_map/ppermute | solution.py:33
  98.8 14.5 %collective-permute-start.22 = (bf16[32,1024]{1,0:T(8,128)(2,1)S(1)}, bf16[32,1024]{1,0:T(8,128)(2,1)S(1)}, u32[]{:S(2)}, u32[]{:S(2)}) collective-permute-start(bf16[32,1024]{1,0:T(8,128)(2,1)S(1)} %get-tuple-element.78), channel_id=1, source_target_pairs={{0,96},{32,64},{64,32},{96,0},{1,97},{33,65},{65,33},{97,1},{2,98}... | collective-permute-start | bytes 196616 | tf_op jit(solution)/shard_map/ppermute | solution.py:33
  107.6 5.9 %collective-permute-start.14 = (bf16[32,1024]{1,0:T(8,128)(2,1)S(1)}, bf16[32,1024]{1,0:T(8,128)(2,1)S(1)}, u32[]{:S(2)}, u32[]{:S(2)}) collective-permute-start(bf16[32,1024]{1,0:T(8,128)(2,1)S(1)} %get-tuple-element.64), channel_id=1, source_target_pairs={{0,32},{32,0},{64,96},{96,64},{1,33},{33,1},{65,97},{97,65},{2,34}... | collective-permute-start | bytes 196616 | tf_op jit(solution)/shard_map/ppermute | solution.py:33
  108.9 4.8 %collective-permute-start.15 = (bf16[32,1024]{1,0:T(8,128)(2,1)S(1)}, bf16[32,1024]{1,0:T(8,128)(2,1)S(1)}, u32[]{:S(2)}, u32[]{:S(2)}) collective-permute-start(bf16[32,1024]{1,0:T(8,128)(2,1)S(1)} %get-tuple-element.65), channel_id=1, source_target_pairs={{0,64},{32,96},{64,0},{96,32},{1,65},{33,97},{65,1},{97,33},{2,66}... | collective-permute-start | bytes 196616 | tf_op jit(solution)/shard_map/ppermute | solution.py:33
  111.3 5.1 %collective-permute-start.16 = (bf16[32,1024]{1,0:T(8,128)(2,1)S(1)}, bf16[32,1024]{1,0:T(8,128)(2,1)S(1)}, u32[]{:S(2)}, u32[]{:S(2)}) collective-permute-start(bf16[32,1024]{1,0:T(8,128)(2,1)S(1)} %get-tuple-element.66), channel_id=1, source_target_pairs={{0,96},{32,64},{64,32},{96,0},{1,97},{33,65},{65,33},{97,1},{2,98}... | collective-permute-start | bytes 196616 | tf_op jit(solution)/shard_map/ppermute | solution.py:33
  113.3 16.9 %collective-permute-start.23 = (bf16[32,1024]{1,0:T(8,128)(2,1)S(1)}, bf16[32,1024]{1,0:T(8,128)(2,1)S(1)}, u32[]{:S(2)}, u32[]{:S(2)}) collective-permute-start(bf16[32,1024]{1,0:T(8,128)(2,1)S(1)} %shard_map.124.own), channel_id=1, source_target_pairs={{0,1},{1,0},{2,3},{3,2},{4,5},{5,4},{6,7},{7,6},{8,9},{9,8},{10,11... | collective-permute-start | bytes 196616 | tf_op jit(solution)/shard_map/ppermute | solution.py:22
  117.6 18.4 %all-to-all-start.1 = ((bf16[32,2,1024]{2,1,0:T(2,128)(2,1)}), bf16[32,2,1024]{2,1,0:T(2,128)(2,1)S(1)}, u32[]{:S(2)}, u32[]{:S(2)}) async-start(bf16[32,2,1024]{2,1,0:T(2,128)(2,1)} %all_to_all.12), calls=%async_computation.1 | async-start | bytes 262144 | tf_op jit(solution)/shard_map/all_to_all | solution.py:324
  124.0 6.5 %collective-permute-start.24 = (bf16[32,1024]{1,0:T(8,128)(2,1)S(1)}, bf16[32,1024]{1,0:T(8,128)(2,1)S(1)}, u32[]{:S(2)}, u32[]{:S(2)}) collective-permute-start(bf16[32,1024]{1,0:T(8,128)(2,1)S(1)} %shard_map.124.own), channel_id=1, source_target_pairs={{0,2},{1,3},{2,0},{3,1},{4,6},{5,7},{6,4},{7,5},{8,10},{9,11},{10,... | collective-permute-start | bytes 196616 | tf_op jit(solution)/shard_map/ppermute | solution.py:22
  126.5 5.8 %collective-permute-start.17 = (bf16[32,1024]{1,0:T(8,128)(2,1)S(1)}, bf16[32,1024]{1,0:T(8,128)(2,1)S(1)}, u32[]{:S(2)}, u32[]{:S(2)}) collective-permute-start(bf16[32,1024]{1,0:T(8,128)(2,1)S(1)} %get-tuple-element.70.own), channel_id=1, source_target_pairs={{0,1},{1,0},{2,3},{3,2},{4,5},{5,4},{6,7},{7,6},{8,9},{9,8},{10,11... | collective-permute-start | bytes 196616 | tf_op jit(solution)/shard_map/ppermute | solution.py:22
  126.8 5.9 %collective-permute-start.18 = (bf16[32,1024]{1,0:T(8,128)(2,1)S(1)}, bf16[32,1024]{1,0:T(8,128)(2,1)S(1)}, u32[]{:S(2)}, u32[]{:S(2)}) collective-permute-start(bf16[32,1024]{1,0:T(8,128)(2,1)S(1)} %get-tuple-element.70.own), channel_id=1, source_target_pairs={{0,2},{1,3},{2,0},{3,1},{4,6},{5,7},{6,4},{7,5},{8,10},{9,11},{10,... | collective-permute-start | bytes 196616 | tf_op jit(solution)/shard_map/ppermute | solution.py:22
  (21 other events, 187.7 us)

commit v3 on v2

v3 whole, which is shorter than its diff:
```python
import functools

import jax
import jax.numpy as jnp
from jax import lax
from jax.experimental import pallas as pl
from jax.experimental.pallas import tpu as pltpu
from jax.sharding import Mesh
from jax.sharding import PartitionSpec as P

F32 = jnp.float32
BF16 = jnp.bfloat16
SEQ = ("y", "z", "c")
VMEM_LIMIT = 20 * 1024 * 1024


def swap_core(value):
    return lax.ppermute(value, "c", [(0, 1), (1, 0)])


def swap_x(value, k):
    return lax.ppermute(value, "x", [(i, i ^ k) for i in range(4)])


def swap_near(value, first):
    steps = (1, 3) if first else (3, 1)
    return lax.ppermute(
        value, ("c", "x"), [(c * 4 + x, c * 4 + (x ^ steps[c])) for c in range(2) for x in range(4)]
    )


def swap_axis(axis, value, k):
    return lax.ppermute(value, axis, [(i, i ^ k) for i in range(4)])


def dot(a, b):
    return jnp.dot(a, b, preferred_element_type=F32)


def dot_t(a, b):
    return lax.dot_general(a, b, (((1,), (1,)), ((), ())), preferred_element_type=F32)


def call(body, outs, inputs, scalars=(), flops=0, scratch=(), outside=False):
    specs = [pl.BlockSpec(memory_space=pltpu.SMEM)] * len(scalars)
    specs += [pl.BlockSpec(memory_space=pl.ANY if outside else pltpu.VMEM)] * len(inputs)
    moved = sum(v.size * v.dtype.itemsize for v in list(inputs) + list(outs))
    return pl.pallas_call(
        body,
        out_shape=outs,
        in_specs=specs,
        out_specs=[pl.BlockSpec(memory_space=pltpu.VMEM)] * len(outs),
        scratch_shapes=list(scratch),
        compiler_params=pltpu.CompilerParams(vmem_limit_bytes=VMEM_LIMIT),
        cost_estimate=pl.CostEstimate(flops=flops, bytes_accessed=moved, transcendentals=0),
    )(*scalars, *inputs)


def shape(dims, dtype):
    return jax.ShapeDtypeStruct(dims, dtype)


def bounds(lengths):
    count = lengths.shape[1]
    row = lax.broadcasted_iota(jnp.int32, (count, count), 0)
    column = lax.broadcasted_iota(jnp.int32, (count, count), 1)
    wide = jnp.broadcast_to(lengths, (count, count)).astype(F32)
    ends = jnp.sum(jnp.where(column <= row, wide, 0.0), axis=1, keepdims=True)
    size = jnp.sum(jnp.where(column == row, wide, 0.0), axis=1, keepdims=True)
    return ends - size, ends, size


def membership(lengths, length):
    starts, ends, size = bounds(lengths)
    count = lengths.shape[1]
    position = lax.broadcasted_iota(jnp.int32, (count, length), 1).astype(F32)
    inside = (position >= starts) & (position < ends)
    return jnp.where(inside, 1.0, 0.0).astype(BF16), size


def pool_kernel(lengths, states, pooled):
    pooling, size = membership(lengths[...], states.shape[0])
    pooled[...] = (dot(pooling, states[...]) / size).astype(BF16)


def pool_cot_kernel(lengths, cots, pooled):
    pooling, _ = membership(lengths[...], cots.shape[0])
    pooled[...] = dot(pooling, cots[...]).astype(BF16)


def stack_kernel(own, one, two, three, out):
    span = own.shape[0]
    for k, block in enumerate((own, one, two, three)):
        out[k * span : (k + 1) * span] = block[...]


def cut_products(count, offsets, whole, keep, send):
    part = keep.shape[0] // (2 * count)
    for k in range(4):
        out = keep if k < 2 else send
        for i in range(count):
            place = pl.multiple_of(offsets[k] + i * 4 * part, 16)
            to = (k % 2) * count * part + i * part
            out[to : to + part] = whole[pl.ds(place, part), :]


def gate_product_kernel(
    offsets, enc_hbm, gate_hbm, lift_hbm, keep, send, w_enc, w_gate, w_lift, whole, sems
):
    copies = [
        pltpu.make_async_copy(source, target, sems.at[i])
        for i, (source, target) in enumerate(
            ((enc_hbm, w_enc), (gate_hbm, w_gate), (lift_hbm, w_lift))
        )
    ]
    for copy in copies:
        copy.start()
    hid = w_gate.shape[0]
    copies[0].wait()
    copies[1].wait()
    whole[:hid] = dot_t(w_gate[...], w_enc[...]).astype(BF16)
    copies[2].wait()
    whole[hid:] = dot_t(w_lift[...], w_enc[...]).astype(BF16)
    cut_products(2, offsets, whole, keep, send)


def down_product_kernel(offsets, down_hbm, dec_hbm, keep, send, w_down, w_dec, whole, sems):
    copies = [
        pltpu.make_async_copy(down_hbm, w_down, sems.at[0]),
        pltpu.make_async_copy(dec_hbm, w_dec, sems.at[1]),
    ]
    for copy in copies:
        copy.start()
    for copy in copies:
        copy.wait()
    whole[...] = dot(w_down[...], w_dec[...]).astype(BF16)
    cut_products(1, offsets, whole, keep, send)


def halve_kernel(keep, first, own, send):
    half = own.shape[0]
    own[...] = keep[:half].astype(F32) + first[:half].astype(F32)
    send[...] = (keep[half:].astype(F32) + first[half:].astype(F32)).astype(BF16)


def encode_kernel(pooled, cot, w_enc, w_dec, rep, back):
    rep[...] = dot(pooled[...], w_enc[...]).astype(BF16)
    back[...] = dot_t(dot_t(cot[...], w_dec[...]).astype(BF16), w_enc[...])


def hidden_rows(rows, products):
    both = dot_t(products[...], jnp.concatenate([block[...] for block in rows], axis=0))
    part = both.shape[0] // 2
    gate, lift = both[:part], both[part:]
    hidden = gate * (1.0 / (1.0 + jnp.exp(-gate))) * lift
    return both, hidden.astype(BF16)


def near_kernel(r0, r1, r2, r3, own, second, products, gates, hidden):
    products[...] = (own[...] + second[...].astype(F32)).astype(BF16)
    gates[...], hidden[...] = hidden_rows((r0, r1, r2, r3), products)


def far_kernel(r0, r1, r2, r3, products, near_hidden, gates, hidden):
    half = near_hidden.shape[1]
    hidden[:, :half] = near_hidden[...]
    gates[...], hidden[:, half:] = hidden_rows((r0, r1, r2, r3), products)


def grad_rows(rows, down, gates):
    patches = rows[0].shape[0] // 4
    pieces = [rows[z][y * patches : (y + 1) * patches, :] for y in range(4) for z in range(4)]
    grad_hidden = dot_t(down, jnp.concatenate(pieces, axis=0))
    part = gates.shape[0] // 2
    gate, lift = gates[:part], gates[part:]
    sig = 1.0 / (1.0 + jnp.exp(-gate))
    grad_gate = grad_hidden * lift * sig * (1.0 + gate * (1.0 - sig))
    return jnp.concatenate([grad_gate, grad_hidden * (gate * sig)], axis=0).astype(BF16)


def grad_far_kernel(r0, r1, r2, r3, own, second, products, gates, down, partial):
    down[...] = (own[...] + second[...].astype(F32)).astype(BF16)
    grads = grad_rows((r0, r1, r2, r3), down[...], gates)
    partial[...] = dot(grads.T, products[...]).astype(BF16)


def place_blocks(total, outs):
    patches = total.shape[0] // 16
    for z, out in enumerate(outs):
        for y in range(4):
            place = (4 * y + z) * patches
            out[y * patches : (y + 1) * patches] = total[place : place + patches].astype(BF16)


def grad_near_kernel(r0, r1, r2, r3, down, products, gates, other, *outs):
    grads = grad_rows((r0, r1, r2, r3), down[...], gates)
    place_blocks(dot(grads.T, products[...]) + other[...].astype(F32), outs)


def down_far_kernel(offsets, own, one, two, three, w_down, out, stack):
    part, span = own.shape[0], out.shape[0]
    for k, block in enumerate((own, one, two, three)):
        stack[pl.ds(pl.multiple_of(offsets[k], 16), part), :] = block[:, span:]
    out[...] = dot(stack[...].T, w_down[...]).astype(BF16)


def down_near_kernel(offsets, own, one, two, three, w_down, other, *rest):
    stack = rest[-1]
    part, span = own.shape[0], other.shape[0]
    for k, block in enumerate((own, one, two, three)):
        stack[pl.ds(pl.multiple_of(offsets[k], 16), part), :] = block[:, :span]
    place_blocks(dot(stack[...].T, w_down[...]) + other[...].astype(F32), rest[:-1])


def add_kernel(own, one, two, three, *outs):
    total = (
        own[...].astype(F32) + one[...].astype(F32) + two[...].astype(F32) + three[...].astype(F32)
    )
    patches = own.shape[0] // 4
    for i, out in enumerate(outs):
        out[...] = total[i * patches : (i + 1) * patches].astype(out.dtype)


def decode_kernel(me, own, one, two, three, rep, weight, owners, partial, *outs):
    total = own[...] + one[...].astype(F32) + two[...].astype(F32) + three[...].astype(F32)
    states = (total + rep[...].astype(F32)).astype(BF16)
    partial[...] = dot(states, weight[...]).astype(BF16)
    count = rep.shape[0]
    own_row = jnp.broadcast_to(owners[...], (count, count))
    row = lax.broadcasted_iota(jnp.int32, (count, count), 0)
    column = lax.broadcasted_iota(jnp.int32, (count, count), 1)
    own_column = jnp.sum(jnp.where(row == column, own_row, 0), axis=1, keepdims=True)
    same = jnp.where((own_column == own_row) & (row < column), 1, 0)
    rank = jnp.sum(same, axis=0, keepdims=True)
    owner = owners[...]
    owner_y, owner_z, owner_c = owner >> 3, (owner >> 1) & 3, owner & 1
    targets = (((owner_z ^ me[1]) * 4 + (owner_y ^ me[0])) * 2 + (owner_c ^ me[2])) * 2 + rank
    slots = lax.broadcasted_iota(jnp.int32, (2 * count, count), 0)
    routing = jnp.where(slots == targets, 1.0, 0.0).astype(BF16)
    outgoing = dot(routing, states).astype(BF16)
    for k, out in enumerate(outs):
        out[...] = outgoing[k * count // 2 : (k + 1) * count // 2]


def move_rows(source_of, blocks):
    rows = jnp.concatenate([block[...] for block in blocks], axis=0)
    count = rows.shape[0]
    to = lax.broadcasted_iota(jnp.int32, (count, count), 0)
    source = lax.broadcasted_iota(jnp.int32, (count, count), 1)
    moved = jnp.where(source == source_of(to), 1.0, 0.0).astype(BF16)
    return dot(moved, rows).astype(BF16)


def route_y_kernel(own, one, two, three, *outs):
    moved = move_rows(
        lambda d: ((d >> 2) & 3) * 16 + (d >> 4) * 4 + (d & 3), (own, one, two, three)
    )
    for k, out in enumerate(outs):
        out[...] = moved[k * 16 : (k + 1) * 16]


def route_core_kernel(own, one, two, three, *outs):
    moved = move_rows(
        lambda d: ((d >> 1) & 15) * 4 + (d >> 5) * 2 + (d & 1), (own, one, two, three)
    )
    for k, out in enumerate(outs):
        out[...] = moved[k * 32 : (k + 1) * 32]


def route_end_kernel(me, own, other, out):
    out[...] = move_rows(
        lambda d: (((d >> 1) & 1) ^ me[2]) * 32
        + ((d >> 4) ^ me[0]) * 8
        + (((d >> 2) & 3) ^ me[1]) * 2
        + (d & 1),
        (own, other),
    )


def grad_kernel(own, one, two, three, back, partial):
    total = own[...] + one[...].astype(F32) + two[...].astype(F32) + three[...].astype(F32)
    partial[...] = (total + back[...]).astype(BF16)


def finish_kernel(forward, lengths, values, own, one, two, three, out):
    total = (
        own[...].astype(F32) + one[...].astype(F32) + two[...].astype(F32) + three[...].astype(F32)
    )
    pooling, size = membership(lengths[...], values.shape[0])
    if not forward:
        total = total / size
    high = total.astype(BF16)
    low = (total - high.astype(F32)).astype(BF16)
    pick = (((0,), (0,)), ((), ()))
    spread = lax.dot_general(pooling, high, pick, preferred_element_type=F32)
    spread = spread + lax.dot_general(pooling, low, pick, preferred_element_type=F32)
    out[...] = (values[...].astype(F32) + spread).astype(BF16)


def on_device(
    byte_states, patch_lengths, patch_owner, w_enc, w_gate, w_lift, w_down, w_dec, byte_cot
):
    patches = patch_lengths.shape[1]
    width = byte_states.shape[1]
    latent = w_enc.shape[1]
    hid = w_gate.shape[1]
    part = hid // 4
    group = 16 * patches
    x, y, z, core = [lax.axis_index(axis) for axis in ("x", "y", "z", "c")]
    step = jnp.where(core == 0, 1, 3)
    halving = (jnp.stack([x, x ^ step ^ 2, x ^ step, x ^ 2]) * part).astype(jnp.int32)
    offsets = (jnp.stack([x, x ^ 1, x ^ 2, x ^ 3]) * part).astype(jnp.int32)
    me = jnp.stack([y, z, core]).astype(jnp.int32)
    owners = patch_owner.reshape(1, patches)
    w_gate, w_lift = w_gate.T, w_lift.T

    def after(value, token):
        return lax.optimization_barrier((value, token))[0]

    def over(axis, own, *sends):
        sends = sends or (own,) * 3
        return [own] + [swap_axis(axis, send, k + 1) for k, send in enumerate(sends)]

    def products_of(body, weights, count):
        return call(
            body,
            [shape((2 * count * part, width), BF16)] * 2,
            weights,
            [halving],
            flops=2 * count * hid * width * latent,
            scratch=[pltpu.VMEM(w.shape, BF16) for w in weights]
            + [pltpu.VMEM((count * hid, width), BF16), pltpu.SemaphoreType.DMA((len(weights),))],
            outside=True,
        )

    def halve(keep, first):
        own, send = call(
            halve_kernel,
            [shape((keep.shape[0] // 2, width), F32), shape((keep.shape[0] // 2, width), BF16)],
            [keep, first],
            flops=2 * keep.size,
        )
        return own, swap_near(send, False)

    def pool(body, values):
        return call(
            body,
            [shape((patches, width), BF16)],
            [patch_lengths, values],
            flops=2 * patches * values.size,
        )[0]

    def gather(rows, first_axis, second_axis):
        (group,) = call(
            stack_kernel,
            [shape((4 * patches, width), BF16)],
            over(first_axis, rows),
            flops=4 * rows.size,
        )
        near = over(second_axis, group)
        return group, near, [swap_core(block) for block in near]

    keep, send = products_of(gate_product_kernel, [w_enc, w_gate, w_lift], 2)
    first = swap_near(send, True)
    pooled = pool(pool_kernel, after(byte_states, send))
    z_rows, near, far = gather(pooled, "z", "y")
    pooled_cot = pool(pool_cot_kernel, after(byte_cot, pooled))
    _, near_cot, far_cot = gather(after(pooled_cot, z_rows), "y", "z")
    down_keep, down_send = products_of(down_product_kernel, [w_down, w_dec], 1)
    own, second = halve(keep, first)
    down_first = swap_near(after(down_send, second), True)
    flops = 4 * group * width * part
    products, near_gates, near_hidden = call(
        near_kernel,
        [
            shape((2 * part, width), BF16),
            shape((2 * part, group), F32),
            shape((part, group), BF16),
        ],
        [*near, own, second],
        flops=flops,
    )
    far_gates, hidden = call(
        far_kernel,
        [shape((2 * part, group), F32), shape((part, 2 * group), BF16)],
        [*far, products, near_hidden],
        flops=flops,
    )
    hiddens = [hidden] + [swap_x(hidden, k) for k in (1, 2, 3)]
    patch_rep, back = call(
        encode_kernel,
        [shape((patches, latent), BF16), shape((patches, width), F32)],
        [pooled, pooled_cot, w_enc, w_dec],
        flops=6 * patches * width * latent,
    )
    hiddens, patch_rep, back = lax.optimization_barrier((hiddens, patch_rep, back))
    down_own, down_second = halve(down_keep, down_first)
    down, far_partial = call(
        grad_far_kernel,
        [shape((part, width), BF16), shape((group, width), BF16)],
        [*far_cot, down_own, down_second, products, far_gates],
        flops=flops,
    )
    pieces = [shape((4 * patches, width), BF16)] * 4

    def sum_seq(terms):
        own, *sends = call(
            add_kernel,
            [shape((patches, width), F32)] + [shape((patches, width), BF16)] * 3,
            over("z", *terms),
            flops=16 * patches * width,
        )
        return over("y", own, *sends)

    (far_rows,) = call(
        down_far_kernel,
        [shape((group, latent), BF16)],
        [*hiddens, w_down],
        [offsets],
        flops=2 * group * latent * hid,
        scratch=[pltpu.VMEM((hid, group), BF16)],
    )
    terms = call(
        down_near_kernel,
        pieces,
        [*hiddens, w_down, swap_core(far_rows)],
        [offsets],
        flops=2 * group * latent * hid,
        scratch=[pltpu.VMEM((hid, group), BF16)],
    )
    decoded, *outgoing = call(
        decode_kernel,
        [shape((patches, width), BF16)] + [shape((patches // 2, latent), BF16)] * 4,
        [*sum_seq(terms), patch_rep, w_dec, owners],
        [me],
        flops=2 * patches * width * latent,
    )
    terms = call(
        grad_near_kernel,
        pieces,
        [*near_cot, down, products, near_gates, swap_core(far_partial)],
        flops=flops,
    )
    (grad_pool,) = call(
        grad_kernel, [shape((patches, width), BF16)], [*sum_seq(terms), back], flops=4 * back.size
    )
    quarter, half = shape((patches // 2, latent), BF16), shape((patches, latent), BF16)
    outgoing = call(route_y_kernel, [quarter] * 4, over("z", *outgoing), flops=8 * patch_rep.size)
    mine, others = call(route_core_kernel, [half] * 2, over("y", *outgoing), flops=8 * patch_rep.size)
    (latent_states,) = call(
        route_end_kernel,
        [shape((2 * patches, latent), BF16)],
        [mine, swap_core(others)],
        [me],
        flops=8 * patch_rep.size,
    )

    def finish(forward, values, partial):
        return call(
            functools.partial(finish_kernel, forward),
            [shape(values.shape, BF16)],
            [patch_lengths, values, partial] + [swap_x(partial, k) for k in (1, 2, 3)],
            flops=4 * patches * values.size,
        )[0]

    byte_out = finish(True, byte_states, decoded)
    return byte_out, finish(False, byte_cot, grad_pool), latent_states


def solution(mesh):
    fine = Mesh(mesh.devices.reshape(4, 4, 2, 4), ("y", "z", "c", "x"))
    return jax.shard_map(
        on_device,
        mesh=fine,
        in_specs=(
            P(SEQ, None),
            P(SEQ, None),
            P(SEQ, None),
            P(None, "x"),
            P("x", SEQ),
            P("x", SEQ),
            P(SEQ, "x"),
            P("x", None),
            P(SEQ, None),
        ),
        out_specs=(P(SEQ, None), P(SEQ, None), P(SEQ, "x")),
        check_vma=False,
    )
```

time: 138 us -> 156 us (1.13)
  starting transfers between devices: 51.2 us -> 77.5 us
  waiting for transfers between devices: 52.6 us -> 47.7 us
  Pallas kernels: 19.1 us -> 22.2 us
  local copies, waits for them, and re-layouts: 9.77 us -> 6.74 us
  other arithmetic: 3.16 us -> 0.15 us
    ppermute x12 -> x30, waiting for transfers between devices: 9.58 us -> 40.3 us  [swap_axis(): return lax.ppermute(value, axis, [(i, i ^ k) for i in range(4)])]
    ppermute x12 -> x30, starting transfers between devices: 17.4 us -> 38.4 us  [swap_axis(): return lax.ppermute(value, axis, [(i, i ^ k) for i in range(4)])]
    ppermute x3 -> x11, starting transfers between devices: 6.09 us -> 23.8 us  [swap_core(): return lax.ppermute(value, 'c', [(0, 1), (1, 0)])]
    all_to_all x2 -> x0, waiting for transfers between devices: 15.2 us -> none  [the longest x1 15.2 us: on_device(): lax.all_to_all(repeated, ('y', 'z'), split_axis=0, concat_axis=0, tiled=T...]
    all_to_all x2 -> x0, starting transfers between devices: 14.9 us -> none  [the longest x1 8.6 us: on_device(): lax.all_to_all(repeated, ('y', 'z'), split_axis=0, concat_axis=0, tiled=T...]
    ppermute x9, waiting for transfers between devices: 14.4 us -> 2.23 us  [swap_x(): return lax.ppermute(value, 'x', [(i, i ^ k) for i in range(4)])]
    ppermute x3 -> x11, waiting for transfers between devices: 4.61 us -> 0.03 us  [swap_core(): return lax.ppermute(value, 'c', [(0, 1), (1, 0)])]
    ppermute x2 -> x4, waiting for transfers between devices: 8.87 us -> 5.13 us  [swap_near(): lax.ppermute(value, ('c', 'x'), [(c * 4 + x, c * 4 + (x ^ steps[c])) for...]
  transfers between devices with their start and end apart: 28 -> 54, of which waited for: 14 -> 19; matrix products, arithmetic and copies ran while one was open for 2% -> 0% of each run, Pallas kernels for 10% -> 11%
where the time goes in v3:
time: 156 us; the launch traced here: 155 us
  starting transfers between devices  77.5 us (50%)
  waiting for transfers between devices  47.7 us (31%)
  Pallas kernels  22.2 us (14%)
  local copies, waits for them, and re-layouts  6.74 us (4%)
    ppermute x30, waiting for transfers between devices, swap_axis(): return lax.ppermute(value, axis, [(i, i ^ k) for i in range(4)])  40.3 us
    ppermute x30, starting transfers between devices, swap_axis(): return lax.ppermute(value, axis, [(i, i ^ k) for i in range(4)])  38.4 us
    ppermute x11, starting transfers between devices, swap_core(): return lax.ppermute(value, 'c', [(0, 1), (1, 0)])  23.8 us
    pallas_call x24, Pallas kernels, call(): pl.pallas_call(body, out_shape=outs, in_specs=specs, out_specs=[pl.BlockS...  22.2 us
    ppermute x9, starting transfers between devices, swap_x(): return lax.ppermute(value, 'x', [(i, i ^ k) for i in range(4)])  11.7 us
    unnamed x32, local copies, waits for them, and re-layouts  6.74 us
    ppermute x4, waiting for transfers between devices, swap_near(): lax.ppermute(value, ('c', 'x'), [(c * 4 + x, c * 4 + (x ^ steps[c])) for...  5.13 us
    ppermute x4, starting transfers between devices, swap_near(): lax.ppermute(value, ('c', 'x'), [(c * 4 + x, c * 4 + (x ^ steps[c])) for...  3.65 us
  transfers between devices with their start and end apart: 54, of which 19 were waited for; matrix products, arithmetic and copies ran while one was open for 0% of the time, Pallas kernels for 11%

profile of v3, /device:TPU:1, one launch (start us, length us, event | category | flops | bytes accessed | tf_op | source)
XLA Modules:
  0.0 155.3 jit_solution(11581406309866136999)
XLA Ops:
  4.7 3.6 %shard_map.112 = (bf16[448,1024]{1,0:T(8,128)(2,1)S(1)}, bf16[448,1024]{1,0:T(8,128)(2,1)S(1)}) custom-call(s32[4]{0:T(128)S(1)} %get-tuple-element.112.offsets, bf16[1024,1024]{1,0:T(8,128)(2,1)S(1)} %copy-done.4, bf16[448,1024]{1,0:T(8,128)(2,1)S(1)} %bitcast.13, bf16[448,1024]{1,0:T(8,128)(2,1)S(1)} %bitcast.14), custom_call_target="tpu_custom_call" | custom-call | flops 1879048192 | bytes 5767168 | tf_op jit(solution)/shard_map/pallas_call | solution.py:48
  8.3 3.4 %collective-permute-start.10 = (bf16[448,1024]{1,0:T(8,128)(2,1)S(1)}, bf16[448,1024]{1,0:T(8,128)(2,1)S(1)}, u32[]{:S(2)}, u32[]{:S(2)}) collective-permute-start(bf16[448,1024]{1,0:T(8,128)(2,1)S(1)} %get-tuple-element.57), channel_id=1, source_target_pairs={{0,1},{1,0},{2,3},{3,2},{4,7},{5,6},{6,5},{7,4},{8,9},{9,8},{10,11... | collective-permute-start | bytes 2752520 | tf_op jit(solution)/shard_map/ppermute | solution.py:27
  13.6 3.3 %collective-permute-start.1 = (bf16[32,1024]{1,0:T(8,128)(2,1)S(1)}, bf16[32,1024]{1,0:T(8,128)(2,1)S(1)}, u32[]{:S(2)}, u32[]{:S(2)}) collective-permute-start(bf16[32,1024]{1,0:T(8,128)(2,1)S(1)} %shard_map.113.own.pooled), channel_id=1, source_target_pairs={{0,16},{8,24},{16,0},{24,8},{1,17},{9,25},{17,1},{25,9},{2,18},{10... | collective-permute-start | bytes 196616 | tf_op jit(solution)/shard_map/ppermute | solution.py:33
  16.9 3.9 %collective-permute-done.1.two = bf16[32,1024]{1,0:T(8,128)(2,1)S(1)} collective-permute-done((bf16[32,1024]{1,0:T(8,128)(2,1)S(1)}, bf16[32,1024]{1,0:T(8,128)(2,1)S(1)}, u32[]{:S(2)}, u32[]{:S(2)}) %collective-permute-start.1) | collective-permute-done | bytes 65568 | tf_op jit(solution)/shard_map/ppermute | solution.py:33
  23.5 2.7 %collective-permute-start.6 = (bf16[128,1024]{1,0:T(8,128)(2,1)S(1)}, bf16[128,1024]{1,0:T(8,128)(2,1)S(1)}, u32[]{:S(2)}, u32[]{:S(2)}) collective-permute-start(bf16[128,1024]{1,0:T(8,128)(2,1)S(1)} %shard_map.114.r0), channel_id=1, source_target_pairs={{0,64},{32,96},{64,0},{96,32},{1,65},{33,97},{65,1},{97,33},{2,66}... | collective-permute-start | bytes 786440 | tf_op jit(solution)/shard_map/ppermute | solution.py:33
  28.4 7.5 %collective-permute-done.25.one = bf16[32,1024]{1,0:T(8,128)(2,1)S(1)} collective-permute-done((bf16[32,1024]{1,0:T(8,128)(2,1)S(1)}, bf16[32,1024]{1,0:T(8,128)(2,1)S(1)}, u32[]{:S(2)}, u32[]{:S(2)}) %collective-permute-start.25) | collective-permute-done | bytes 65568 | tf_op jit(solution)/shard_map/ppermute | solution.py:33
  35.9 2.7 %collective-permute-start.27 = (bf16[32,1024]{1,0:T(8,128)(2,1)S(1)}, bf16[32,1024]{1,0:T(8,128)(2,1)S(1)}, u32[]{:S(2)}, u32[]{:S(2)}) collective-permute-start(bf16[32,1024]{1,0:T(8,128)(2,1)S(1)} %shard_map.118.cot.own), channel_id=1, source_target_pairs={{0,96},{32,64},{64,32},{96,0},{1,97},{33,65},{65,33},{97,1},{2,98}... | collective-permute-start | bytes 196616 | tf_op jit(solution)/shard_map/ppermute | solution.py:33
  40.6 3.4 %collective-permute-start.3 = (bf16[128,1024]{1,0:T(8,128)(2,1)S(1)}, bf16[128,1024]{1,0:T(8,128)(2,1)S(1)}, u32[]{:S(2)}, u32[]{:S(2)}) collective-permute-start(bf16[128,1024]{1,0:T(8,128)(2,1)S(1)} %shard_map.114.r0), channel_id=1, source_target_pairs={{0,4},{4,0},{1,5},{5,1},{2,6},{6,2},{3,7},{7,3},{8,12},{12,8},{9,1... | collective-permute-start | bytes 786440 | tf_op jit(solution)/shard_map/ppermute | solution.py:18
  44.5 2.3 %collective-permute-done.8.r3 = bf16[128,1024]{1,0:T(8,128)(2,1)S(1)} collective-permute-done((bf16[128,1024]{1,0:T(8,128)(2,1)S(1)}, bf16[128,1024]{1,0:T(8,128)(2,1)S(1)}, u32[]{:S(2)}, u32[]{:S(2)}) %collective-permute-start.8) | collective-permute-done | bytes 262176 | tf_op jit(solution)/shard_map/ppermute | solution.py:33
  46.8 2.8 %collective-permute-start.9 = (bf16[128,1024]{1,0:T(8,128)(2,1)S(1)}, bf16[128,1024]{1,0:T(8,128)(2,1)S(1)}, u32[]{:S(2)}, u32[]{:S(2)}) collective-permute-start(bf16[128,1024]{1,0:T(8,128)(2,1)S(1)} %collective-permute-done.8.r3), channel_id=1, source_target_pairs={{0,4},{4,0},{1,5},{5,1},{2,6},{6,2},{3,7},{7,3},{8,12},{12,8},{9,1... | collective-permute-start | bytes 786440 | tf_op jit(solution)/shard_map/ppermute | solution.py:18
  49.8 2.3 %collective-permute-start.29 = (bf16[128,1024]{1,0:T(8,128)(2,1)S(1)}, bf16[128,1024]{1,0:T(8,128)(2,1)S(1)}, u32[]{:S(2)}, u32[]{:S(2)}) collective-permute-start(bf16[128,1024]{1,0:T(8,128)(2,1)S(1)} %shard_map.125.r0), channel_id=1, source_target_pairs={{0,16},{8,24},{16,0},{24,8},{1,17},{9,25},{17,1},{25,9},{2,18},{10... | collective-permute-start | bytes 786440 | tf_op jit(solution)/shard_map/ppermute | solution.py:33
  57.7 3.1 %collective-permute-start.13 = (bf16[112,1024]{1,0:T(8,128)(2,1)S(1)}, bf16[112,1024]{1,0:T(8,128)(2,1)S(1)}, u32[]{:S(2)}, u32[]{:S(2)}) collective-permute-start(bf16[112,1024]{1,0:T(8,128)(2,1)S(1)} %get-tuple-element.68.own), channel_id=1, source_target_pairs={{0,2},{1,3},{2,0},{3,1},{4,6},{5,7},{6,4},{7,5},{8,10},{9,11},{10,... | collective-permute-start | bytes 688136 | tf_op jit(solution)/shard_map/ppermute | solution.py:22
  60.8 3.4 %collective-permute-done.29.r2 = bf16[128,1024]{1,0:T(8,128)(2,1)S(1)} collective-permute-done((bf16[128,1024]{1,0:T(8,128)(2,1)S(1)}, bf16[128,1024]{1,0:T(8,128)(2,1)S(1)}, u32[]{:S(2)}, u32[]{:S(2)}) %collective-permute-start.29) | collective-permute-done | bytes 262176 | tf_op jit(solution)/shard_map/ppermute | solution.py:33
  70.0 2.4 %collective-permute-start.32 = (bf16[128,1024]{1,0:T(8,128)(2,1)S(1)}, bf16[128,1024]{1,0:T(8,128)(2,1)S(1)}, u32[]{:S(2)}, u32[]{:S(2)}) collective-permute-start(bf16[128,1024]{1,0:T(8,128)(2,1)S(1)} %collective-permute-done.28.r1), channel_id=1, source_target_pairs={{0,4},{4,0},{1,5},{5,1},{2,6},{6,2},{3,7},{7,3},{8,12},{12,8},{9,1... | collective-permute-start | bytes 786440 | tf_op jit(solution)/shard_map/ppermute | solution.py:18
  79.5 5.1 %collective-permute-done.36.second = bf16[112,1024]{1,0:T(8,128)(2,1)S(1)} collective-permute-done((bf16[112,1024]{1,0:T(8,128)(2,1)S(1)}, bf16[112,1024]{1,0:T(8,128)(2,1)S(1)}, u32[]{:S(2)}, u32[]{:S(2)}) %collective-permute-start.36) | collective-permute-done | bytes 229408 | tf_op jit(solution)/shard_map/ppermute | solution.py:27
  85.5 2.6 %collective-permute-start.37 = (bf16[512,1024]{1,0:T(8,128)(2,1)S(1)}, bf16[512,1024]{1,0:T(8,128)(2,1)S(1)}, u32[]{:S(2)}, u32[]{:S(2)}) collective-permute-start(bf16[512,1024]{1,0:T(8,128)(2,1)S(1)} %get-tuple-element.91), channel_id=1, source_target_pairs={{0,4},{4,0},{1,5},{5,1},{2,6},{6,2},{3,7},{7,3},{8,12},{12,8},{9,1... | collective-permute-start | bytes 3145736 | tf_op jit(solution)/shard_map/ppermute | solution.py:18
  89.6 2.5 %collective-permute-start.17 = (bf16[128,1024]{1,0:T(8,128)(2,1)S(1)}, bf16[128,1024]{1,0:T(8,128)(2,1)S(1)}, u32[]{:S(2)}, u32[]{:S(2)}) collective-permute-start(bf16[128,1024]{1,0:T(8,128)(2,1)S(1)} %get-tuple-element.74), channel_id=1, source_target_pairs={{0,16},{8,24},{16,0},{24,8},{1,17},{9,25},{17,1},{25,9},{2,18},{10... | collective-permute-start | bytes 786440 | tf_op jit(solution)/shard_map/ppermute | solution.py:33
  97.5 6.7 %collective-permute-done.17.two = bf16[128,1024]{1,0:T(8,128)(2,1)S(1)} collective-permute-done((bf16[128,1024]{1,0:T(8,128)(2,1)S(1)}, bf16[128,1024]{1,0:T(8,128)(2,1)S(1)}, u32[]{:S(2)}, u32[]{:S(2)}) %collective-permute-start.17) | collective-permute-done | bytes 262176 | tf_op jit(solution)/shard_map/ppermute | solution.py:33
  114.8 2.4 %collective-permute-done.21.three = bf16[32,1024]{1,0:T(8,128)(2,1)S(1)} collective-permute-done((bf16[32,1024]{1,0:T(8,128)(2,1)}, bf16[32,1024]{1,0:T(8,128)(2,1)S(1)}, u32[]{:S(2)}, u32[]{:S(2)}) %collective-permute-start.21) | collective-permute-done | bytes 65568 | tf_op jit(solution)/shard_map/ppermute | solution.py:33
  119.6 2.5 %collective-permute-start.48 = (bf16[16,1024]{1,0:T(8,128)(2,1)S(1)}, bf16[16,1024]{1,0:T(8,128)(2,1)S(1)}, u32[]{:S(2)}, u32[]{:S(2)}) collective-permute-start(bf16[16,1024]{1,0:T(8,128)(2,1)S(1)} %get-tuple-element.103), channel_id=1, source_target_pairs={{0,16},{8,24},{16,0},{24,8},{1,17},{9,25},{17,1},{25,9},{2,18},{10... | collective-permute-start | bytes 98312 | tf_op jit(solution)/shard_map/ppermute | solution.py:33
  124.0 2.6 %collective-permute-done.49.three = bf16[16,1024]{1,0:T(8,128)(2,1)S(1)} collective-permute-done((bf16[16,1024]{1,0:T(8,128)(2,1)S(1)}, bf16[16,1024]{1,0:T(8,128)(2,1)S(1)}, u32[]{:S(2)}, u32[]{:S(2)}) %collective-permute-start.49) | collective-permute-done | bytes 32800 | tf_op jit(solution)/shard_map/ppermute | solution.py:33
  126.9 2.4 %collective-permute-start.51 = (bf16[16,1024]{1,0:T(8,128)(2,1)S(1)}, bf16[16,1024]{1,0:T(8,128)(2,1)S(1)}, u32[]{:S(2)}, u32[]{:S(2)}) collective-permute-start(bf16[16,1024]{1,0:T(8,128)(2,1)S(1)} %get-tuple-element.107), channel_id=1, source_target_pairs={{0,64},{32,96},{64,0},{96,32},{1,65},{33,97},{65,1},{97,33},{2,66}... | collective-permute-start | bytes 98312 | tf_op jit(solution)/shard_map/ppermute | solution.py:33
  132.1 2.4 %collective-permute-start.42 = (bf16[32,1024]{1,0:T(8,128)(2,1)S(1)}, bf16[32,1024]{1,0:T(8,128)(2,1)S(1)}, u32[]{:S(2)}, u32[]{:S(2)}) collective-permute-start(bf16[32,1024]{1,0:T(8,128)(2,1)S(1)} %get-tuple-element.98), channel_id=1, source_target_pairs={{0,64},{32,96},{64,0},{96,32},{1,65},{33,97},{65,1},{97,33},{2,66}... | collective-permute-start | bytes 196616 | tf_op jit(solution)/shard_map/ppermute | solution.py:33
  140.0 7.3 %collective-permute-start.53 = (bf16[32,1024]{1,0:T(8,128)(2,1)S(1)}, bf16[32,1024]{1,0:T(8,128)(2,1)S(1)}, u32[]{:S(2)}, u32[]{:S(2)}) collective-permute-start(bf16[32,1024]{1,0:T(8,128)(2,1)S(1)} %get-tuple-element.110), channel_id=1, source_target_pairs={{0,4},{4,0},{1,5},{5,1},{2,6},{6,2},{3,7},{7,3},{8,12},{12,8},{9,1... | collective-permute-start | bytes 196616 | tf_op jit(solution)/shard_map/ppermute | solution.py:18
  (142 shorter events, 70.9 us)
Async XLA Ops:
  8.3 15.0 %collective-permute-start.10 = (bf16[448,1024]{1,0:T(8,128)(2,1)S(1)}, bf16[448,1024]{1,0:T(8,128)(2,1)S(1)}, u32[]{:S(2)}, u32[]{:S(2)}) collective-permute-start(bf16[448,1024]{1,0:T(8,128)(2,1)S(1)} %get-tuple-element.57), channel_id=1, source_target_pairs={{0,1},{1,0},{2,3},{3,2},{4,7},{5,6},{6,5},{7,4},{8,9},{9,8},{10,11... | collective-permute-start | bytes 2752520 | tf_op jit(solution)/shard_map/ppermute | solution.py:27
  21.9 22.1 %collective-permute-start.4 = (bf16[128,1024]{1,0:T(8,128)(2,1)S(1)}, bf16[128,1024]{1,0:T(8,128)(2,1)S(1)}, u32[]{:S(2)}, u32[]{:S(2)}) collective-permute-start(bf16[128,1024]{1,0:T(8,128)(2,1)S(1)} %shard_map.114.r0), channel_id=1, source_target_pairs={{0,32},{32,0},{64,96},{96,64},{1,33},{33,1},{65,97},{97,65},{2,34}... | collective-permute-start | bytes 786440 | tf_op jit(solution)/shard_map/ppermute | solution.py:33
  23.4 28.6 %collective-permute-start.11 = (bf16[224,1024]{1,0:T(8,128)(2,1)S(1)}, bf16[224,1024]{1,0:T(8,128)(2,1)S(1)}, u32[]{:S(2)}, u32[]{:S(2)}) collective-permute-start(bf16[224,1024]{1,0:T(8,128)(2,1)S(1)} %get-tuple-element.61), channel_id=1, source_target_pairs={{0,3},{1,2},{2,1},{3,0},{4,5},{5,4},{6,7},{7,6},{8,11},{9,10},{10,... | collective-permute-start | bytes 1376264 | tf_op jit(solution)/shard_map/ppermute | solution.py:27
  23.5 20.4 %collective-permute-start.6 = (bf16[128,1024]{1,0:T(8,128)(2,1)S(1)}, bf16[128,1024]{1,0:T(8,128)(2,1)S(1)}, u32[]{:S(2)}, u32[]{:S(2)}) collective-permute-start(bf16[128,1024]{1,0:T(8,128)(2,1)S(1)} %shard_map.114.r0), channel_id=1, source_target_pairs={{0,64},{32,96},{64,0},{96,32},{1,65},{33,97},{65,1},{97,33},{2,66}... | collective-permute-start | bytes 786440 | tf_op jit(solution)/shard_map/ppermute | solution.py:33
  26.8 12.9 %collective-permute-start.26 = (bf16[32,1024]{1,0:T(8,128)(2,1)S(1)}, bf16[32,1024]{1,0:T(8,128)(2,1)S(1)}, u32[]{:S(2)}, u32[]{:S(2)}) collective-permute-start(bf16[32,1024]{1,0:T(8,128)(2,1)S(1)} %shard_map.118.cot.own), channel_id=1, source_target_pairs={{0,64},{32,96},{64,0},{96,32},{1,65},{33,97},{65,1},{97,33},{2,66}... | collective-permute-start | bytes 196616 | tf_op jit(solution)/shard_map/ppermute | solution.py:33
  44.0 11.8 %collective-permute-start.7 = (bf16[128,1024]{1,0:T(8,128)(2,1)S(1)}, bf16[128,1024]{1,0:T(8,128)(2,1)S(1)}, u32[]{:S(2)}, u32[]{:S(2)}) collective-permute-start(bf16[128,1024]{1,0:T(8,128)(2,1)S(1)} %collective-permute-done.6.r2), channel_id=1, source_target_pairs={{0,4},{4,0},{1,5},{5,1},{2,6},{6,2},{3,7},{7,3},{8,12},{12,8},{9,1... | collective-permute-start | bytes 786440 | tf_op jit(solution)/shard_map/ppermute | solution.py:18
  46.8 9.6 %collective-permute-start.9 = (bf16[128,1024]{1,0:T(8,128)(2,1)S(1)}, bf16[128,1024]{1,0:T(8,128)(2,1)S(1)}, u32[]{:S(2)}, u32[]{:S(2)}) collective-permute-start(bf16[128,1024]{1,0:T(8,128)(2,1)S(1)} %collective-permute-done.8.r3), channel_id=1, source_target_pairs={{0,4},{4,0},{1,5},{5,1},{2,6},{6,2},{3,7},{7,3},{8,12},{12,8},{9,1... | collective-permute-start | bytes 786440 | tf_op jit(solution)/shard_map/ppermute | solution.py:18
  49.8 14.4 %collective-permute-start.29 = (bf16[128,1024]{1,0:T(8,128)(2,1)S(1)}, bf16[128,1024]{1,0:T(8,128)(2,1)S(1)}, u32[]{:S(2)}, u32[]{:S(2)}) collective-permute-start(bf16[128,1024]{1,0:T(8,128)(2,1)S(1)} %shard_map.125.r0), channel_id=1, source_target_pairs={{0,16},{8,24},{16,0},{24,8},{1,17},{9,25},{17,1},{25,9},{2,18},{10... | collective-permute-start | bytes 786440 | tf_op jit(solution)/shard_map/ppermute | solution.py:33
  52.1 14.1 %collective-permute-start.30 = (bf16[128,1024]{1,0:T(8,128)(2,1)S(1)}, bf16[128,1024]{1,0:T(8,128)(2,1)S(1)}, u32[]{:S(2)}, u32[]{:S(2)}) collective-permute-start(bf16[128,1024]{1,0:T(8,128)(2,1)S(1)} %shard_map.125.r0), channel_id=1, source_target_pairs={{0,24},{8,16},{16,8},{24,0},{1,25},{9,17},{17,9},{25,1},{2,26},{10... | collective-permute-start | bytes 786440 | tf_op jit(solution)/shard_map/ppermute | solution.py:33
  55.8 23.4 %collective-permute-start.35 = (bf16[224,1024]{1,0:T(8,128)(2,1)S(1)}, bf16[224,1024]{1,0:T(8,128)(2,1)S(1)}, u32[]{:S(2)}, u32[]{:S(2)}) collective-permute-start(bf16[224,1024]{1,0:T(8,128)(2,1)S(1)} %get-tuple-element.85), channel_id=1, source_target_pairs={{0,1},{1,0},{2,3},{3,2},{4,7},{5,6},{6,5},{7,4},{8,9},{9,8},{10,11... | collective-permute-start | bytes 1376264 | tf_op jit(solution)/shard_map/ppermute | solution.py:27
  56.9 13.1 %collective-permute-start.12 = (bf16[112,1024]{1,0:T(8,128)(2,1)S(1)}, bf16[112,1024]{1,0:T(8,128)(2,1)S(1)}, u32[]{:S(2)}, u32[]{:S(2)}) collective-permute-start(bf16[112,1024]{1,0:T(8,128)(2,1)S(1)} %get-tuple-element.68.own), channel_id=1, source_target_pairs={{0,1},{1,0},{2,3},{3,2},{4,5},{5,4},{6,7},{7,6},{8,9},{9,8},{10,11... | collective-permute-start | bytes 688136 | tf_op jit(solution)/shard_map/ppermute | solution.py:22
  57.7 14.7 %collective-permute-start.13 = (bf16[112,1024]{1,0:T(8,128)(2,1)S(1)}, bf16[112,1024]{1,0:T(8,128)(2,1)S(1)}, u32[]{:S(2)}, u32[]{:S(2)}) collective-permute-start(bf16[112,1024]{1,0:T(8,128)(2,1)S(1)} %get-tuple-element.68.own), channel_id=1, source_target_pairs={{0,2},{1,3},{2,0},{3,1},{4,6},{5,7},{6,4},{7,5},{8,10},{9,11},{10,... | collective-permute-start | bytes 688136 | tf_op jit(solution)/shard_map/ppermute | solution.py:22
  64.2 12.5 %collective-permute-start.14 = (bf16[112,1024]{1,0:T(8,128)(2,1)S(1)}, bf16[112,1024]{1,0:T(8,128)(2,1)S(1)}, u32[]{:S(2)}, u32[]{:S(2)}) collective-permute-start(bf16[112,1024]{1,0:T(8,128)(2,1)S(1)} %get-tuple-element.68.own), channel_id=1, source_target_pairs={{0,3},{1,2},{2,1},{3,0},{4,7},{5,6},{6,5},{7,4},{8,11},{9,10},{10,... | collective-permute-start | bytes 688136 | tf_op jit(solution)/shard_map/ppermute | solution.py:22
  66.2 13.1 %collective-permute-start.31 = (bf16[128,1024]{1,0:T(8,128)(2,1)S(1)}, bf16[128,1024]{1,0:T(8,128)(2,1)S(1)}, u32[]{:S(2)}, u32[]{:S(2)}) collective-permute-start(bf16[128,1024]{1,0:T(8,128)(2,1)S(1)} %shard_map.125.r0), channel_id=1, source_target_pairs={{0,4},{4,0},{1,5},{5,1},{2,6},{6,2},{3,7},{7,3},{8,12},{12,8},{9,1... | collective-permute-start | bytes 786440 | tf_op jit(solution)/shard_map/ppermute | solution.py:18
  89.6 14.6 %collective-permute-start.17 = (bf16[128,1024]{1,0:T(8,128)(2,1)S(1)}, bf16[128,1024]{1,0:T(8,128)(2,1)S(1)}, u32[]{:S(2)}, u32[]{:S(2)}) collective-permute-start(bf16[128,1024]{1,0:T(8,128)(2,1)S(1)} %get-tuple-element.74), channel_id=1, source_target_pairs={{0,16},{8,24},{16,0},{24,8},{1,17},{9,25},{17,1},{25,9},{2,18},{10... | collective-permute-start | bytes 786440 | tf_op jit(solution)/shard_map/ppermute | solution.py:33
  92.1 14.1 %collective-permute-start.18 = (bf16[128,1024]{1,0:T(8,128)(2,1)S(1)}, bf16[128,1024]{1,0:T(8,128)(2,1)S(1)}, u32[]{:S(2)}, u32[]{:S(2)}) collective-permute-start(bf16[128,1024]{1,0:T(8,128)(2,1)S(1)} %get-tuple-element.75), channel_id=1, source_target_pairs={{0,24},{8,16},{16,8},{24,0},{1,25},{9,17},{17,9},{25,1},{2,26},{10... | collective-permute-start | bytes 786440 | tf_op jit(solution)/shard_map/ppermute | solution.py:33
  95.3 34.1 %collective-permute-start.38 = (bf16[128,1024]{1,0:T(8,128)(2,1)}, bf16[128,1024]{1,0:T(8,128)(2,1)}, u32[]{:S(2)}, u32[]{:S(2)}) collective-permute-start(bf16[128,1024]{1,0:T(8,128)(2,1)} %get-tuple-element.93), channel_id=1, source_target_pairs={{0,8},{8,0},{16,24},{24,16},{1,9},{9,1},{17,25},{25,17},{2,10},{10... | collective-permute-start | bytes 786440 | tf_op jit(solution)/shard_map/ppermute | solution.py:33
  108.1 22.6 %collective-permute-start.39 = (bf16[128,1024]{1,0:T(8,128)(2,1)}, bf16[128,1024]{1,0:T(8,128)(2,1)}, u32[]{:S(2)}, u32[]{:S(2)}) collective-permute-start(bf16[128,1024]{1,0:T(8,128)(2,1)} %get-tuple-element.94), channel_id=1, source_target_pairs={{0,16},{8,24},{16,0},{24,8},{1,17},{9,25},{17,1},{25,9},{2,18},{10... | collective-permute-start | bytes 786440 | tf_op jit(solution)/shard_map/ppermute | solution.py:33
  108.1 22.6 %collective-permute-start.40 = (bf16[128,1024]{1,0:T(8,128)(2,1)}, bf16[128,1024]{1,0:T(8,128)(2,1)}, u32[]{:S(2)}, u32[]{:S(2)}) collective-permute-start(bf16[128,1024]{1,0:T(8,128)(2,1)} %get-tuple-element.95), channel_id=1, source_target_pairs={{0,24},{8,16},{16,8},{24,0},{1,25},{9,17},{17,9},{25,1},{2,26},{10... | collective-permute-start | bytes 786440 | tf_op jit(solution)/shard_map/ppermute | solution.py:33
  134.6 12.7 %collective-permute-start.43 = (bf16[32,1024]{1,0:T(8,128)(2,1)S(1)}, bf16[32,1024]{1,0:T(8,128)(2,1)S(1)}, u32[]{:S(2)}, u32[]{:S(2)}) collective-permute-start(bf16[32,1024]{1,0:T(8,128)(2,1)S(1)} %get-tuple-element.99), channel_id=1, source_target_pairs={{0,96},{32,64},{64,32},{96,0},{1,97},{33,65},{65,33},{97,1},{2,98}... | collective-permute-start | bytes 196616 | tf_op jit(solution)/shard_map/ppermute | solution.py:33
  136.0 11.5 %collective-permute-start.22 = (bf16[32,1024]{1,0:T(8,128)(2,1)S(1)}, bf16[32,1024]{1,0:T(8,128)(2,1)S(1)}, u32[]{:S(2)}, u32[]{:S(2)}) collective-permute-start(bf16[32,1024]{1,0:T(8,128)(2,1)S(1)} %get-tuple-element.81.own), channel_id=1, source_target_pairs={{0,1},{1,0},{2,3},{3,2},{4,5},{5,4},{6,7},{7,6},{8,9},{9,8},{10,11... | collective-permute-start | bytes 196616 | tf_op jit(solution)/shard_map/ppermute | solution.py:22
  136.0 13.3 %collective-permute-start.23 = (bf16[32,1024]{1,0:T(8,128)(2,1)S(1)}, bf16[32,1024]{1,0:T(8,128)(2,1)S(1)}, u32[]{:S(2)}, u32[]{:S(2)}) collective-permute-start(bf16[32,1024]{1,0:T(8,128)(2,1)S(1)} %get-tuple-element.81.own), channel_id=1, source_target_pairs={{0,2},{1,3},{2,0},{3,1},{4,6},{5,7},{6,4},{7,5},{8,10},{9,11},{10,... | collective-permute-start | bytes 196616 | tf_op jit(solution)/shard_map/ppermute | solution.py:22
  137.6 13.7 %collective-permute-start.24 = (bf16[32,1024]{1,0:T(8,128)(2,1)S(1)}, bf16[32,1024]{1,0:T(8,128)(2,1)S(1)}, u32[]{:S(2)}, u32[]{:S(2)}) collective-permute-start(bf16[32,1024]{1,0:T(8,128)(2,1)S(1)} %get-tuple-element.81.own), channel_id=1, source_target_pairs={{0,3},{1,2},{2,1},{3,0},{4,7},{5,6},{6,5},{7,4},{8,11},{9,10},{10,... | collective-permute-start | bytes 196616 | tf_op jit(solution)/shard_map/ppermute | solution.py:22
  140.0 12.6 %collective-permute-start.53 = (bf16[32,1024]{1,0:T(8,128)(2,1)S(1)}, bf16[32,1024]{1,0:T(8,128)(2,1)S(1)}, u32[]{:S(2)}, u32[]{:S(2)}) collective-permute-start(bf16[32,1024]{1,0:T(8,128)(2,1)S(1)} %get-tuple-element.110), channel_id=1, source_target_pairs={{0,4},{4,0},{1,5},{5,1},{2,6},{6,2},{3,7},{7,3},{8,12},{12,8},{9,1... | collective-permute-start | bytes 196616 | tf_op jit(solution)/shard_map/ppermute | solution.py:18
  (46 other events, 413.6 us)

commit v4 on v3

v4 whole, which is shorter than its diff:
```python
import functools

import jax
import jax.numpy as jnp
from jax import lax
from jax.experimental import pallas as pl
from jax.experimental.pallas import tpu as pltpu
from jax.sharding import Mesh
from jax.sharding import PartitionSpec as P

F32 = jnp.float32
BF16 = jnp.bfloat16
SEQ = ("y", "z", "c")
VMEM_LIMIT = 16 * 1024 * 1024


def swap_core(value):
    return lax.ppermute(value, "c", [(0, 1), (1, 0)])


def swap_x(value, k):
    return lax.ppermute(value, "x", [(i, i ^ k) for i in range(4)])


def swap_near(value, first):
    steps = (1, 3) if first else (3, 1)
    return lax.ppermute(
        value, ("c", "x"), [(c * 4 + x, c * 4 + (x ^ steps[c])) for c in range(2) for x in range(4)]
    )


def swap_first(value, k, first=True):
    pairs = []
    for index in range(32):
        along_z = (index % 2 == 0) == first
        pairs.append((index, index ^ (2 * k if along_z else 8 * k)))
    return lax.ppermute(value, SEQ, pairs)


def swap_second(value, k):
    return swap_first(value, k, False)


def dot(a, b):
    return jnp.dot(a, b, preferred_element_type=F32)


def dot_t(a, b):
    return lax.dot_general(a, b, (((1,), (1,)), ((), ())), preferred_element_type=F32)


def call(body, outs, inputs, scalars=(), flops=0, scratch=(), outside=False):
    specs = [pl.BlockSpec(memory_space=pltpu.SMEM)] * len(scalars)
    specs += [pl.BlockSpec(memory_space=pltpu.HBM if outside else pltpu.VMEM)] * len(inputs)
    moved = sum(v.size * v.dtype.itemsize for v in list(inputs) + list(outs))
    return pl.pallas_call(
        body,
        out_shape=outs,
        in_specs=specs,
        out_specs=[pl.BlockSpec(memory_space=pltpu.VMEM)] * len(outs),
        scratch_shapes=list(scratch),
        compiler_params=pltpu.CompilerParams(vmem_limit_bytes=60 * 1024 * 1024 if outside else VMEM_LIMIT),
        cost_estimate=pl.CostEstimate(flops=flops, bytes_accessed=moved, transcendentals=0),
    )(*scalars, *inputs)


def shape(dims, dtype):
    return jax.ShapeDtypeStruct(dims, dtype)


def bounds(lengths):
    count = lengths.shape[1]
    row = lax.broadcasted_iota(jnp.int32, (count, count), 0)
    column = lax.broadcasted_iota(jnp.int32, (count, count), 1)
    wide = jnp.broadcast_to(lengths, (count, count)).astype(F32)
    ends = jnp.sum(jnp.where(column <= row, wide, 0.0), axis=1, keepdims=True)
    size = jnp.sum(jnp.where(column == row, wide, 0.0), axis=1, keepdims=True)
    return ends - size, ends, size


def membership(lengths, length):
    starts, ends, size = bounds(lengths)
    count = lengths.shape[1]
    position = lax.broadcasted_iota(jnp.int32, (count, length), 1).astype(F32)
    inside = (position >= starts) & (position < ends)
    return jnp.where(inside, 1.0, 0.0).astype(BF16), size


def pool_kernel(lengths, states, cots, pooled):
    pooling, size = membership(lengths[...], states.shape[0])
    width = states.shape[1]
    pooled[:, :width] = (dot(pooling, states[...]) / size).astype(BF16)
    pooled[:, width:] = dot(pooling, cots[...]).astype(BF16)


def stack_kernel(own, one, two, three, out):
    span = own.shape[0]
    for k, block in enumerate((own, one, two, three)):
        out[k * span : (k + 1) * span] = block[...]


def cut_products(count, offsets, whole, keep, send):
    part = keep.shape[0] // (2 * count)
    for k in range(4):
        out = keep if k < 2 else send
        for i in range(count):
            place = pl.multiple_of(offsets[k] + i * 4 * part, 16)
            to = (k % 2) * count * part + i * part
            out[to : to + part] = whole[pl.ds(place, part), :]


def gate_product_kernel(
    offsets, enc_hbm, gate_hbm, lift_hbm, keep, send, w_enc, w_gate, w_lift, whole, sems
):
    copies = [
        pltpu.make_async_copy(source, target, sems.at[i])
        for i, (source, target) in enumerate(
            ((enc_hbm, w_enc), (gate_hbm, w_gate), (lift_hbm, w_lift))
        )
    ]
    for copy in copies:
        copy.start()
    hid = w_gate.shape[0]
    copies[0].wait()
    copies[1].wait()
    whole[:hid] = dot_t(w_gate[...], w_enc[...]).astype(BF16)
    copies[2].wait()
    whole[hid:] = dot_t(w_lift[...], w_enc[...]).astype(BF16)
    cut_products(2, offsets, whole, keep, send)


def down_product_kernel(offsets, w_down, w_dec, w_enc, pooled, keep, send, rep, back, whole):
    whole[...] = dot(w_down[...], w_dec[...]).astype(BF16)
    cut_products(1, offsets, whole, keep, send)
    width = w_enc.shape[0]
    rep[...] = dot(pooled[:, :width], w_enc[...]).astype(BF16)
    back[...] = dot_t(dot_t(pooled[:, width:], w_dec[...]).astype(BF16), w_enc[...])


def halve_kernel(keep, first, own, send):
    half = own.shape[0]
    own[...] = keep[:half].astype(F32) + first[:half].astype(F32)
    send[...] = (keep[half:].astype(F32) + first[half:].astype(F32)).astype(BF16)


def gate_rows(rows, products):
    width = products.shape[1]
    both = dot_t(products[...], jnp.concatenate([block[:, :width] for block in rows], axis=0))
    part = both.shape[0] // 2
    return both[:part], both[part:]


def hidden_rows(rows, products):
    gate, lift = gate_rows(rows, products)
    return (gate * (1.0 / (1.0 + jnp.exp(-gate))) * lift).astype(BF16)


def near_kernel(r0, r1, r2, r3, own, second, products, hidden):
    products[...] = (own[...] + second[...].astype(F32)).astype(BF16)
    hidden[...] = hidden_rows((r0, r1, r2, r3), products)


def far_kernel(r0, r1, r2, r3, products, near_hidden, hidden):
    half = near_hidden.shape[1]
    hidden[:, :half] = near_hidden[...]
    hidden[:, half:] = hidden_rows((r0, r1, r2, r3), products)


def grad_rows(rows, down, products):
    width = down.shape[1]
    grad_hidden = dot_t(down, jnp.concatenate([block[:, width:] for block in rows], axis=0))
    gate, lift = gate_rows(rows, products)
    sig = 1.0 / (1.0 + jnp.exp(-gate))
    grad_gate = grad_hidden * lift * sig * (1.0 + gate * (1.0 - sig))
    return jnp.concatenate([grad_gate, grad_hidden * (gate * sig)], axis=0).astype(BF16)


def grad_far_kernel(r0, r1, r2, r3, own, second, products, down, partial):
    down[...] = (own[...] + second[...].astype(F32)).astype(BF16)
    grads = grad_rows((r0, r1, r2, r3), down[...], products)
    partial[...] = dot(grads.T, products[...]).astype(BF16)


def place_blocks(total, outs):
    patches = total.shape[0] // 16
    for first, out in enumerate(outs):
        for second in range(4):
            place = (4 * second + first) * patches
            out[second * patches : (second + 1) * patches] = total[place : place + patches].astype(BF16)


def down_far_kernel(offsets, own, one, two, three, w_down, out, stack):
    part, span = own.shape[0], out.shape[0]
    for k, block in enumerate((own, one, two, three)):
        stack[pl.ds(pl.multiple_of(offsets[k], 16), part), :] = block[:, span:]
    out[...] = dot(stack[...].T, w_down[...]).astype(BF16)


def sum_near_kernel(
    offsets, own, one, two, three, w_down, other, r0, r1, r2, r3, down, products, grad_other, *rest
):
    stack = rest[-1]
    part, span = own.shape[0], other.shape[0]
    width = w_down.shape[1]
    for k, block in enumerate((own, one, two, three)):
        stack[pl.ds(pl.multiple_of(offsets[k], 16), part), :] = block[:, :span]
    grads = grad_rows((r0, r1, r2, r3), down[...], products)
    total = dot(grads.T, products[...]) + grad_other[...].astype(F32)
    place_blocks(total, [out.at[:, width:] for out in rest[:-1]])
    total = dot(stack[...].T, w_down[...]) + other[...].astype(F32)
    place_blocks(total, [out.at[:, :width] for out in rest[:-1]])


def add_kernel(own, one, two, three, *outs):
    total = (
        own[...].astype(F32) + one[...].astype(F32) + two[...].astype(F32) + three[...].astype(F32)
    )
    patches = own.shape[0] // 4
    for i, out in enumerate(outs):
        out[...] = total[i * patches : (i + 1) * patches].astype(out.dtype)


def decode_kernel(own, one, two, three, rep, back, weight, owners, partial, outgoing):
    width = rep.shape[1]
    total = own[...] + one[...].astype(F32) + two[...].astype(F32) + three[...].astype(F32)
    states = (total[:, :width] + rep[...].astype(F32)).astype(BF16)
    partial[:, : weight.shape[1]] = dot(states, weight[...]).astype(BF16)
    partial[:, weight.shape[1] :] = (total[:, width:] + back[...]).astype(BF16)
    count = rep.shape[0]
    own_row = jnp.broadcast_to(owners[...], (count, count))
    row = lax.broadcasted_iota(jnp.int32, (count, count), 0)
    column = lax.broadcasted_iota(jnp.int32, (count, count), 1)
    own_column = jnp.sum(jnp.where(row == column, own_row, 0), axis=1, keepdims=True)
    same = jnp.where((own_column == own_row) & (row < column), 1, 0)
    rank = jnp.sum(same, axis=0, keepdims=True)
    targets = 2 * owners[...] + rank
    slots = lax.broadcasted_iota(jnp.int32, (2 * count, count), 0)
    routing = jnp.where(slots == targets, 1.0, 0.0).astype(BF16)
    outgoing[...] = dot(routing, states).astype(BF16)


def finish_kernel(lengths, states, cots, own, one, two, three, out, grad):
    total = (
        own[...].astype(F32) + one[...].astype(F32) + two[...].astype(F32) + three[...].astype(F32)
    )
    pooling, size = membership(lengths[...], states.shape[0])
    width = states.shape[1]
    pick = (((0,), (0,)), ((), ()))
    for values, result, part in (
        (states, out, total[:, :width]),
        (cots, grad, total[:, width:] / size),
    ):
        high = part.astype(BF16)
        low = (part - high.astype(F32)).astype(BF16)
        spread = lax.dot_general(pooling, high, pick, preferred_element_type=F32)
        spread = spread + lax.dot_general(pooling, low, pick, preferred_element_type=F32)
        result[...] = (values[...].astype(F32) + spread).astype(BF16)


def on_device(
    byte_states, patch_lengths, patch_owner, w_enc, w_gate, w_lift, w_down, w_dec, byte_cot
):
    patches = patch_lengths.shape[1]
    width = byte_states.shape[1]
    latent = w_enc.shape[1]
    hid = w_gate.shape[1]
    part = hid // 4
    group = 16 * patches
    x, core = lax.axis_index("x"), lax.axis_index("c")
    step = jnp.where(core == 0, 1, 3)
    halving = (jnp.stack([x, x ^ step ^ 2, x ^ step, x ^ 2]) * part).astype(jnp.int32)
    offsets = (jnp.stack([x, x ^ 1, x ^ 2, x ^ 3]) * part).astype(jnp.int32)
    owners = patch_owner.reshape(1, patches)
    w_gate, w_lift = w_gate.T, w_lift.T

    def after(value, token):
        return lax.optimization_barrier((value, token))[0]

    def over(swap, own, *sends):
        sends = sends or (own,) * 3
        two, one, three = [swap(sends[k - 1], k) for k in (2, 1, 3)]
        return [own, one, two, three]

    def halve(keep, first):
        own, send = call(
            halve_kernel,
            [shape((keep.shape[0] // 2, width), F32), shape((keep.shape[0] // 2, width), BF16)],
            [keep, first],
            flops=2 * keep.size,
        )
        return own, swap_near(send, False)

    weights = [w_enc, w_gate, w_lift]
    keep, send = call(
        gate_product_kernel,
        [shape((4 * part, width), BF16)] * 2,
        weights,
        [halving],
        flops=4 * hid * width * latent,
        scratch=[pltpu.VMEM(w.shape, BF16) for w in weights]
        + [pltpu.VMEM((2 * hid, width), BF16), pltpu.SemaphoreType.DMA((3,))],
        outside=True,
    )
    first = swap_near(send, True)
    (pooled,) = call(
        pool_kernel,
        [shape((patches, 2 * width), BF16)],
        [patch_lengths, after(byte_states, send), byte_cot],
        flops=4 * patches * byte_states.size,
    )
    (rows,) = call(
        stack_kernel,
        [shape((4 * patches, 2 * width), BF16)],
        over(swap_first, pooled),
        flops=8 * patches * width,
    )
    near = over(swap_second, rows)
    far = [swap_core(block) for block in near]
    down_keep, down_send, patch_rep, back = call(
        down_product_kernel,
        [shape((2 * part, width), BF16)] * 2
        + [shape((patches, latent), BF16), shape((patches, width), F32)],
        [w_down, w_dec, w_enc, pooled],
        [halving],
        flops=2 * hid * width * latent,
        scratch=[pltpu.VMEM((hid, width), BF16)],
    )
    own, second = halve(keep, first)
    down_first = swap_near(after(down_send, first), True)
    flops = 4 * group * width * part
    products, near_hidden = call(
        near_kernel,
        [
            shape((2 * part, width), BF16),
            shape((part, group), BF16),
        ],
        [*near, after(own, down_send), second],
        flops=flops,
    )
    (hidden,) = call(
        far_kernel,
        [shape((part, 2 * group), BF16)],
        [*far, products, near_hidden],
        flops=flops,
    )
    hiddens = over(swap_x, hidden)
    down_own, down_second = halve(down_keep, down_first)
    down, far_partial = call(
        grad_far_kernel,
        [shape((part, width), BF16), shape((group, width), BF16)],
        [*far, down_own, down_second, products],
        flops=flops,
    )
    (far_rows,) = call(
        down_far_kernel,
        [shape((group, latent), BF16)],
        [*hiddens, w_down],
        [offsets],
        flops=2 * group * latent * hid,
        scratch=[pltpu.VMEM((hid, group), BF16)],
    )
    terms = call(
        sum_near_kernel,
        [shape((4 * patches, latent + width), BF16)] * 4,
        [
            *hiddens,
            w_down,
            swap_core(far_rows),
            *near,
            down,
            products,
            swap_core(far_partial),
        ],
        [offsets],
        flops=2 * group * latent * hid + flops,
        scratch=[pltpu.VMEM((hid, group), BF16)],
    )
    own, *sends = call(
        add_kernel,
        [shape((patches, latent + width), F32)] + [shape((patches, latent + width), BF16)] * 3,
        over(swap_first, *terms),
        flops=32 * patches * width,
    )
    partial, outgoing = call(
        decode_kernel,
        [shape((patches, 2 * width), BF16), shape((2 * patches, latent), BF16)],
        [*over(swap_second, own, *sends), patch_rep, back, w_dec, owners],
        flops=2 * patches * width * latent,
    )
    latent_states = lax.all_to_all(outgoing, SEQ, split_axis=0, concat_axis=0, tiled=True)
    partials = over(swap_x, partial)
    byte_out, byte_grad = call(
        finish_kernel,
        [shape(byte_states.shape, BF16), shape(byte_cot.shape, BF16)],
        [patch_lengths, byte_states, byte_cot, *partials],
        flops=16 * patches * byte_states.size,
    )
    return byte_out, byte_grad, latent_states


def solution(mesh):
    fine = Mesh(mesh.devices.reshape(4, 4, 2, 4), ("y", "z", "c", "x"))
    return jax.shard_map(
        on_device,
        mesh=fine,
        in_specs=(
            P(SEQ, None),
            P(SEQ, None),
            P(SEQ, None),
            P(None, "x"),
            P("x", SEQ),
            P("x", SEQ),
            P(SEQ, "x"),
            P("x", None),
            P(SEQ, None),
        ),
        out_specs=(P(SEQ, None), P(SEQ, None), P(SEQ, "x")),
        check_vma=False,
    )
```

time: 156 us -> 125 us (0.80)
  starting transfers between devices: 77.5 us -> 35.2 us
  blocking collectives: 0 us -> 14.8 us
  waiting for transfers between devices: 47.7 us -> 42.9 us
    ppermute x30 -> x12, starting transfers between devices: 38.4 us -> 15.9 us  [swap_first(): return lax.ppermute(value, SEQ, pairs)]
    ppermute x11 -> x6, starting transfers between devices: 23.8 us -> 7.41 us  [swap_core(): return lax.ppermute(value, 'c', [(0, 1), (1, 0)])]
    all_to_all x0 -> x1, blocking collectives: none -> 14.8 us  [on_device(): lax.all_to_all(outgoing, SEQ, split_axis=0, concat_axis=0, tiled=True)]
    ppermute x30 -> x12, waiting for transfers between devices: 40.3 us -> 30.4 us  [swap_first(): return lax.ppermute(value, SEQ, pairs)]
    ppermute x9 -> x6, waiting for transfers between devices: 2.23 us -> 8.2 us  [swap_x(): return lax.ppermute(value, 'x', [(i, i ^ k) for i in range(4)])]
    ppermute x9 -> x6, starting transfers between devices: 11.7 us -> 6.59 us  [swap_x(): return lax.ppermute(value, 'x', [(i, i ^ k) for i in range(4)])]
    ppermute x4, waiting for transfers between devices: 5.13 us -> 1.92 us  [swap_near(): lax.ppermute(value, ('c', 'x'), [(c * 4 + x, c * 4 + (x ^ steps[c])) for...]
    ppermute x11 -> x6, waiting for transfers between devices: 0.03 us -> 2.3 us  [swap_core(): return lax.ppermute(value, 'c', [(0, 1), (1, 0)])]
  transfers between devices with their start and end apart: 54 -> 28, of which waited for: 19 -> 12; matrix products, arithmetic and copies ran while one was open for 0% -> 0% of each run, Pallas kernels for 11% -> 9%
where the time goes in v4:
time: 125 us
  waiting for transfers between devices  42.9 us (34%)
  starting transfers between devices  35.2 us (28%)
  Pallas kernels  22.5 us (18%)
  blocking collectives  14.8 us (12%)
  local copies, waits for them, and re-layouts  7.62 us (6%)
    ppermute x12, waiting for transfers between devices, swap_first(): return lax.ppermute(value, SEQ, pairs)  30.4 us
    pallas_call x14, Pallas kernels, call(): pl.pallas_call(body, out_shape=outs, in_specs=specs, out_specs=[pl.BlockS...  22.5 us
    ppermute x12, starting transfers between devices, swap_first(): return lax.ppermute(value, SEQ, pairs)  15.9 us
    all_to_all x1, blocking collectives, on_device(): lax.all_to_all(outgoing, SEQ, split_axis=0, concat_axis=0, tiled=True)  14.8 us
    ppermute x6, waiting for transfers between devices, swap_x(): return lax.ppermute(value, 'x', [(i, i ^ k) for i in range(4)])  8.2 us
    ppermute x6, starting transfers between devices, swap_core(): return lax.ppermute(value, 'c', [(0, 1), (1, 0)])  7.41 us
    unnamed x66, local copies, waits for them, and re-layouts  6.86 us
    ppermute x6, starting transfers between devices, swap_x(): return lax.ppermute(value, 'x', [(i, i ^ k) for i in range(4)])  6.59 us
  transfers between devices with their start and end apart: 28, of which 12 were waited for; matrix products, arithmetic and copies ran while one was open for 0% of the time, Pallas kernels for 9%

profile of v4, /device:TPU:1, one launch (start us, length us, event | category | flops | bytes accessed | tf_op | source)
XLA Modules:
  0.0 124.7 jit_solution(15654693093462670900)
XLA Ops:
  1.3 6.3 %shard_map.112 = (bf16[448,1024]{1,0:T(8,128)(2,1)}, bf16[448,1024]{1,0:T(8,128)(2,1)}) custom-call(s32[4]{0:T(128)} %add_multiply_fusion.1.offsets, bf16[1024,1024]{1,0:T(8,128)(2,1)} %w_enc.1, bf16[448,1024]{1,0:T(8,128)(2,1)} %bitcast.10, bf16[448,1024]{1,0:T(8,128)(2,1)} %bitcast.11), custom_call_target="tpu_custom_call" | custom-call | flops 1879048192 | bytes 5767168 | tf_op jit(solution)/shard_map/pallas_call | solution.py:56
  7.5 3.4 %collective-permute-start.10 = (bf16[448,1024]{1,0:T(8,128)(2,1)}, bf16[448,1024]{1,0:T(8,128)(2,1)S(1)}, u32[]{:S(2)}, u32[]{:S(2)}) collective-permute-start(bf16[448,1024]{1,0:T(8,128)(2,1)} %get-tuple-element.32), channel_id=1, source_target_pairs={{0,1},{1,0},{2,3},{3,2},{4,7},{5,6},{6,5},{7,4},{8,9},{9,8},{10,11... | collective-permute-start | bytes 2752520 | tf_op jit(solution)/shard_map/ppermute | solution.py:27
  11.3 2.8 %collective-permute-start.2 = (bf16[32,2048]{1,0:T(8,128)(2,1)S(1)}, bf16[32,2048]{1,0:T(8,128)(2,1)S(1)}, u32[]{:S(2)}, u32[]{:S(2)}) collective-permute-start(bf16[32,2048]{1,0:T(8,128)(2,1)S(1)} %shard_map.113.own.pooled), channel_id=1, source_target_pairs={{0,24},{4,100},{8,16},{12,108},{16,8},{20,116},{24,0},{28,124},{32... | collective-permute-start | bytes 393224 | tf_op jit(solution)/shard_map/ppermute | solution.py:37
  14.7 2.6 %collective-permute-done.2.three = bf16[32,2048]{1,0:T(8,128)(2,1)S(1)} collective-permute-done((bf16[32,2048]{1,0:T(8,128)(2,1)S(1)}, bf16[32,2048]{1,0:T(8,128)(2,1)S(1)}, u32[]{:S(2)}, u32[]{:S(2)}) %collective-permute-start.2) | collective-permute-done | bytes 131104 | tf_op jit(solution)/shard_map/ppermute | solution.py:37
  17.4 2.0 %collective-permute-done.1.two = bf16[32,2048]{1,0:T(8,128)(2,1)S(1)} collective-permute-done((bf16[32,2048]{1,0:T(8,128)(2,1)S(1)}, bf16[32,2048]{1,0:T(8,128)(2,1)S(1)}, u32[]{:S(2)}, u32[]{:S(2)}) %collective-permute-start.1) | collective-permute-done | bytes 131104 | tf_op jit(solution)/shard_map/ppermute | solution.py:37
  19.4 3.8 %collective-permute-start.8 = (bf16[128,2048]{1,0:T(8,128)(2,1)S(1)}, bf16[128,2048]{1,0:T(8,128)(2,1)S(1)}, u32[]{:S(2)}, u32[]{:S(2)}) collective-permute-start(bf16[128,2048]{1,0:T(8,128)(2,1)S(1)} %shard_map.114.r0), channel_id=1, source_target_pairs={{0,96},{4,28},{8,104},{12,20},{16,112},{20,12},{24,120},{28,4},{32... | collective-permute-start | bytes 1572872 | tf_op jit(solution)/shard_map/ppermute | solution.py:37
  25.4 3.9 %collective-permute-start.3 = (bf16[128,2048]{1,0:T(8,128)(2,1)S(1)}, bf16[128,2048]{1,0:T(8,128)(2,1)S(1)}, u32[]{:S(2)}, u32[]{:S(2)}) collective-permute-start(bf16[128,2048]{1,0:T(8,128)(2,1)S(1)} %shard_map.114.r0), channel_id=1, source_target_pairs={{0,4},{4,0},{1,5},{5,1},{2,6},{6,2},{3,7},{7,3},{8,12},{12,8},{9,1... | collective-permute-start | bytes 1572872 | tf_op jit(solution)/shard_map/ppermute | solution.py:18
  29.3 6.5 %collective-permute-done.8.r3 = bf16[128,2048]{1,0:T(8,128)(2,1)S(1)} collective-permute-done((bf16[128,2048]{1,0:T(8,128)(2,1)S(1)}, bf16[128,2048]{1,0:T(8,128)(2,1)S(1)}, u32[]{:S(2)}, u32[]{:S(2)}) %collective-permute-start.8) | collective-permute-done | bytes 524320 | tf_op jit(solution)/shard_map/ppermute | solution.py:37
  35.7 1.9 %collective-permute-start.9 = (bf16[128,2048]{1,0:T(8,128)(2,1)S(1)}, bf16[128,2048]{1,0:T(8,128)(2,1)S(1)}, u32[]{:S(2)}, u32[]{:S(2)}) collective-permute-start(bf16[128,2048]{1,0:T(8,128)(2,1)S(1)} %collective-permute-done.8.r3), channel_id=1, source_target_pairs={{0,4},{4,0},{1,5},{5,1},{2,6},{6,2},{3,7},{7,3},{8,12},{12,8},{9,1... | collective-permute-start | bytes 1572872 | tf_op jit(solution)/shard_map/ppermute | solution.py:18
  40.2 3.2 %shard_map.116 = (bf16[224,1024]{1,0:T(8,128)(2,1)S(1)}, bf16[224,1024]{1,0:T(8,128)(2,1)S(1)}, bf16[32,1024]{1,0:T(8,128)(2,1)S(1)}, f32[32,1024]{1,0:T(8,128)S(1)}) custom-call(s32[4]{0:T(128)S(1)} %copy-done.31, bf16[448,1024]{1,0:T(8,128)(2,1)S(1)} %copy-done.1, bf16[1024,1024]{1,0:T(8,128)(2,1)S(1)} %copy-done, bf16[1024,1024]{1,0:T(8,128)(2,1)S(1)} %copy-done.4, ...), custom_call_target="tpu_custom_call" | custom-call | flops 939524096 | bytes 6356992 | tf_op jit(solution)/shard_map/pallas_call | solution.py:56
  52.5 1.9 %collective-permute-done.16.first = bf16[224,1024]{1,0:T(8,128)(2,1)S(1)} collective-permute-done((bf16[224,1024]{1,0:T(8,128)(2,1)S(1)}, bf16[224,1024]{1,0:T(8,128)(2,1)S(1)}, u32[]{:S(2)}, u32[]{:S(2)}) %collective-permute-start.16) | collective-permute-done | bytes 458784 | tf_op jit(solution)/shard_map/ppermute | solution.py:27
  56.0 8.2 %collective-permute-done.14.three = bf16[112,1024]{1,0:T(8,128)(2,1)} collective-permute-done((bf16[112,1024]{1,0:T(8,128)(2,1)}, bf16[112,1024]{1,0:T(8,128)(2,1)}, u32[]{:S(2)}, u32[]{:S(2)}) %collective-permute-start.14) | collective-permute-done | bytes 229408 | tf_op jit(solution)/shard_map/ppermute | solution.py:22
  64.2 2.1 %shard_map.119 = bf16[512,1024]{1,0:T(8,128)(2,1)S(1)} custom-call(s32[4]{0:T(128)S(1)} %add_multiply_fusion.offsets, bf16[112,1024]{1,0:T(8,128)(2,1)} %shard_map.118.own, bf16[112,1024]{1,0:T(8,128)(2,1)} %collective-permute-done.12.one, bf16[112,1024]{1,0:T(8,128)(2,1)} %collective-permute-done.13.two, bf16[112,1024]{1,0:T(8,128)(2,1)} %collective-permute-done.14.three, ...), custom_call_target="tpu_custom_call" | custom-call | flops 469762048 | bytes 2883584 | tf_op jit(solution)/shard_map/pallas_call | solution.py:56
  67.6 2.2 %shard_map.121 = (bf16[112,1024]{1,0:T(8,128)(2,1)S(1)}, bf16[512,1024]{1,0:T(8,128)(2,1)S(1)}) custom-call(bf16[128,2048]{1,0:T(8,128)(2,1)S(1)} %copy-done.10, bf16[128,2048]{1,0:T(8,128)(2,1)S(1)} %copy-done.16, bf16[128,2048]{1,0:T(8,128)(2,1)S(1)} %copy-done.14, bf16[128,2048]{1,0:T(8,128)(2,1)S(1)} %copy-done.12, f32[112,1024]{1,0:T(8,128)S(1)} %copy-done.25, ...), custom_call_target="tpu_custom_call" | custom-call | flops 234881024 | bytes 4521984 | tf_op jit(solution)/shard_map/pallas_call | solution.py:56
  70.5 2.3 %collective-permute-done.18.grad_other = bf16[512,1024]{1,0:T(8,128)(2,1)S(1)} collective-permute-done((bf16[512,1024]{1,0:T(8,128)(2,1)S(1)}, bf16[512,1024]{1,0:T(8,128)(2,1)S(1)}, u32[]{:S(2)}, u32[]{:S(2)}) %collective-permute-start.18) | collective-permute-done | bytes 1048608 | tf_op jit(solution)/shard_map/ppermute | solution.py:18
  72.8 3.2 %shard_map.122 = (bf16[128,2048]{1,0:T(8,128)(2,1)S(1)}, bf16[128,2048]{1,0:T(8,128)(2,1)S(1)}, bf16[128,2048]{1,0:T(8,128)(2,1)S(1)}, bf16[128,2048]{1,0:T(8,128)(2,1)S(1)}) custom-call(s32[4]{0:T(128)S(1)} %add_multiply_fusion.offsets, bf16[112,1024]{1,0:T(8,128)(2,1)} %shard_map.118.own, bf16[112,1024]{1,0:T(8,128)(2,1)} %collective-permute-done.12.one, ...), custom_call_target="tpu_custom_call" | custom-call | flops 704643072 | bytes 8814592 | tf_op jit(solution)/shard_map/pallas_call | solution.py:56
  77.4 2.6 %collective-permute-start.20 = (bf16[128,2048]{1,0:T(8,128)(2,1)S(1)}, bf16[128,2048]{1,0:T(8,128)(2,1)S(1)}, u32[]{:S(2)}, u32[]{:S(2)}) collective-permute-start(bf16[128,2048]{1,0:T(8,128)(2,1)S(1)} %get-tuple-element.49), channel_id=1, source_target_pairs={{0,16},{4,68},{8,24},{12,76},{16,0},{20,84},{24,8},{28,92},{32,48}... | collective-permute-start | bytes 1572872 | tf_op jit(solution)/shard_map/ppermute | solution.py:37
  80.0 4.4 %collective-permute-done.19.one = bf16[128,2048]{1,0:T(8,128)(2,1)S(1)} collective-permute-done((bf16[128,2048]{1,0:T(8,128)(2,1)S(1)}, bf16[128,2048]{1,0:T(8,128)(2,1)S(1)}, u32[]{:S(2)}, u32[]{:S(2)}) %collective-permute-start.19) | collective-permute-done | bytes 524320 | tf_op jit(solution)/shard_map/ppermute | solution.py:37
  84.4 7.9 %collective-permute-done.20.two = bf16[128,2048]{1,0:T(8,128)(2,1)S(1)} collective-permute-done((bf16[128,2048]{1,0:T(8,128)(2,1)S(1)}, bf16[128,2048]{1,0:T(8,128)(2,1)S(1)}, u32[]{:S(2)}, u32[]{:S(2)}) %collective-permute-start.20) | collective-permute-done | bytes 524320 | tf_op jit(solution)/shard_map/ppermute | solution.py:37
  92.3 2.9 %collective-permute-done.21.three = bf16[128,2048]{1,0:T(8,128)(2,1)S(1)} collective-permute-done((bf16[128,2048]{1,0:T(8,128)(2,1)S(1)}, bf16[128,2048]{1,0:T(8,128)(2,1)S(1)}, u32[]{:S(2)}, u32[]{:S(2)}) %collective-permute-start.21) | collective-permute-done | bytes 524320 | tf_op jit(solution)/shard_map/ppermute | solution.py:37
  95.5 2.6 %collective-permute-start.23 = (bf16[32,2048]{1,0:T(8,128)(2,1)S(1)}, bf16[32,2048]{1,0:T(8,128)(2,1)S(1)}, u32[]{:S(2)}, u32[]{:S(2)}) collective-permute-start(bf16[32,2048]{1,0:T(8,128)(2,1)S(1)} %get-tuple-element.53), channel_id=1, source_target_pairs={{0,64},{4,20},{8,72},{12,28},{16,80},{20,4},{24,88},{28,12},{32,96... | collective-permute-start | bytes 393224 | tf_op jit(solution)/shard_map/ppermute | solution.py:37
  99.6 2.2 %collective-permute-done.23.two = bf16[32,2048]{1,0:T(8,128)(2,1)S(1)} collective-permute-done((bf16[32,2048]{1,0:T(8,128)(2,1)S(1)}, bf16[32,2048]{1,0:T(8,128)(2,1)S(1)}, u32[]{:S(2)}, u32[]{:S(2)}) %collective-permute-start.23) | collective-permute-done | bytes 131104 | tf_op jit(solution)/shard_map/ppermute | solution.py:37
  104.1 2.1 %collective-permute-start.27 = (bf16[32,2048]{1,0:T(8,128)(2,1)S(1)}, bf16[32,2048]{1,0:T(8,128)(2,1)S(1)}, u32[]{:S(2)}, u32[]{:S(2)}) collective-permute-start(bf16[32,2048]{1,0:T(8,128)(2,1)S(1)} %get-tuple-element.57.own), channel_id=1, source_target_pairs={{0,3},{1,2},{2,1},{3,0},{4,7},{5,6},{6,5},{7,4},{8,11},{9,10},{10,... | collective-permute-start | bytes 393224 | tf_op jit(solution)/shard_map/ppermute | solution.py:22
  107.5 14.8 %all_to_all.12 = bf16[32,2,1024]{2,1,0:T(2,128)(2,1)S(1)} all-to-all(bf16[32,2,1024]{2,1,0:T(2,128)(2,1)S(1)} %all_to_all.8), channel_id=1, replica_groups=mesh['y'=4,'z'=4,'c'=2,'x'=4] {'y','z','c'}, dimensions={0} | all-to-all | bytes 262144 | tf_op jit(solution)/shard_map/all_to_all | solution.py:390
  (117 shorter events, 27.9 us)
Async XLA Ops:
  7.5 16.4 %collective-permute-start.10 = (bf16[448,1024]{1,0:T(8,128)(2,1)}, bf16[448,1024]{1,0:T(8,128)(2,1)S(1)}, u32[]{:S(2)}, u32[]{:S(2)}) collective-permute-start(bf16[448,1024]{1,0:T(8,128)(2,1)} %get-tuple-element.32), channel_id=1, source_target_pairs={{0,1},{1,0},{2,3},{3,2},{4,7},{5,6},{6,5},{7,4},{8,9},{9,8},{10,11... | collective-permute-start | bytes 2752520 | tf_op jit(solution)/shard_map/ppermute | solution.py:27
  11.3 6.1 %collective-permute-start.2 = (bf16[32,2048]{1,0:T(8,128)(2,1)S(1)}, bf16[32,2048]{1,0:T(8,128)(2,1)S(1)}, u32[]{:S(2)}, u32[]{:S(2)}) collective-permute-start(bf16[32,2048]{1,0:T(8,128)(2,1)S(1)} %shard_map.113.own.pooled), channel_id=1, source_target_pairs={{0,24},{4,100},{8,16},{12,108},{16,8},{20,116},{24,0},{28,124},{32... | collective-permute-start | bytes 393224 | tf_op jit(solution)/shard_map/ppermute | solution.py:37
  14.1 5.3 %collective-permute-start.1 = (bf16[32,2048]{1,0:T(8,128)(2,1)S(1)}, bf16[32,2048]{1,0:T(8,128)(2,1)S(1)}, u32[]{:S(2)}, u32[]{:S(2)}) collective-permute-start(bf16[32,2048]{1,0:T(8,128)(2,1)S(1)} %shard_map.113.own.pooled), channel_id=1, source_target_pairs={{0,16},{4,68},{8,24},{12,76},{16,0},{20,84},{24,8},{28,92},{32,48}... | collective-permute-start | bytes 393224 | tf_op jit(solution)/shard_map/ppermute | solution.py:37
  19.4 16.3 %collective-permute-start.8 = (bf16[128,2048]{1,0:T(8,128)(2,1)S(1)}, bf16[128,2048]{1,0:T(8,128)(2,1)S(1)}, u32[]{:S(2)}, u32[]{:S(2)}) collective-permute-start(bf16[128,2048]{1,0:T(8,128)(2,1)S(1)} %shard_map.114.r0), channel_id=1, source_target_pairs={{0,96},{4,28},{8,104},{12,20},{16,112},{20,12},{24,120},{28,4},{32... | collective-permute-start | bytes 1572872 | tf_op jit(solution)/shard_map/ppermute | solution.py:37
  23.3 14.4 %collective-permute-start.6 = (bf16[128,2048]{1,0:T(8,128)(2,1)S(1)}, bf16[128,2048]{1,0:T(8,128)(2,1)S(1)}, u32[]{:S(2)}, u32[]{:S(2)}) collective-permute-start(bf16[128,2048]{1,0:T(8,128)(2,1)S(1)} %shard_map.114.r0), channel_id=1, source_target_pairs={{0,64},{4,20},{8,72},{12,28},{16,80},{20,4},{24,88},{28,12},{32,96... | collective-permute-start | bytes 1572872 | tf_op jit(solution)/shard_map/ppermute | solution.py:37
  23.3 14.5 %collective-permute-start.4 = (bf16[128,2048]{1,0:T(8,128)(2,1)S(1)}, bf16[128,2048]{1,0:T(8,128)(2,1)S(1)}, u32[]{:S(2)}, u32[]{:S(2)}) collective-permute-start(bf16[128,2048]{1,0:T(8,128)(2,1)S(1)} %shard_map.114.r0), channel_id=1, source_target_pairs={{0,32},{4,12},{8,40},{12,4},{16,48},{20,28},{24,56},{28,20},{32,0}... | collective-permute-start | bytes 1572872 | tf_op jit(solution)/shard_map/ppermute | solution.py:37
  25.3 19.4 %collective-permute-start.11 = (bf16[224,1024]{1,0:T(8,128)(2,1)S(1)}, bf16[224,1024]{1,0:T(8,128)(2,1)S(1)}, u32[]{:S(2)}, u32[]{:S(2)}) collective-permute-start(bf16[224,1024]{1,0:T(8,128)(2,1)S(1)} %get-tuple-element.38), channel_id=1, source_target_pairs={{0,3},{1,2},{2,1},{3,0},{4,5},{5,4},{6,7},{7,6},{8,11},{9,10},{10,... | collective-permute-start | bytes 1376264 | tf_op jit(solution)/shard_map/ppermute | solution.py:27
  25.4 21.6 %collective-permute-start.3 = (bf16[128,2048]{1,0:T(8,128)(2,1)S(1)}, bf16[128,2048]{1,0:T(8,128)(2,1)S(1)}, u32[]{:S(2)}, u32[]{:S(2)}) collective-permute-start(bf16[128,2048]{1,0:T(8,128)(2,1)S(1)} %shard_map.114.r0), channel_id=1, source_target_pairs={{0,4},{4,0},{1,5},{5,1},{2,6},{6,2},{3,7},{7,3},{8,12},{12,8},{9,1... | collective-permute-start | bytes 1572872 | tf_op jit(solution)/shard_map/ppermute | solution.py:18
  35.7 11.3 %collective-permute-start.9 = (bf16[128,2048]{1,0:T(8,128)(2,1)S(1)}, bf16[128,2048]{1,0:T(8,128)(2,1)S(1)}, u32[]{:S(2)}, u32[]{:S(2)}) collective-permute-start(bf16[128,2048]{1,0:T(8,128)(2,1)S(1)} %collective-permute-done.8.r3), channel_id=1, source_target_pairs={{0,4},{4,0},{1,5},{5,1},{2,6},{6,2},{3,7},{7,3},{8,12},{12,8},{9,1... | collective-permute-start | bytes 1572872 | tf_op jit(solution)/shard_map/ppermute | solution.py:18
  37.7 9.4 %collective-permute-start.7 = (bf16[128,2048]{1,0:T(8,128)(2,1)S(1)}, bf16[128,2048]{1,0:T(8,128)(2,1)S(1)}, u32[]{:S(2)}, u32[]{:S(2)}) collective-permute-start(bf16[128,2048]{1,0:T(8,128)(2,1)S(1)} %collective-permute-done.6.r2), channel_id=1, source_target_pairs={{0,4},{4,0},{1,5},{5,1},{2,6},{6,2},{3,7},{7,3},{8,12},{12,8},{9,1... | collective-permute-start | bytes 1572872 | tf_op jit(solution)/shard_map/ppermute | solution.py:18
  37.8 9.4 %collective-permute-start.5 = (bf16[128,2048]{1,0:T(8,128)(2,1)S(1)}, bf16[128,2048]{1,0:T(8,128)(2,1)S(1)}, u32[]{:S(2)}, u32[]{:S(2)}) collective-permute-start(bf16[128,2048]{1,0:T(8,128)(2,1)S(1)} %collective-permute-done.4.r1), channel_id=1, source_target_pairs={{0,4},{4,0},{1,5},{5,1},{2,6},{6,2},{3,7},{7,3},{8,12},{12,8},{9,1... | collective-permute-start | bytes 1572872 | tf_op jit(solution)/shard_map/ppermute | solution.py:18
  44.7 9.7 %collective-permute-start.16 = (bf16[224,1024]{1,0:T(8,128)(2,1)S(1)}, bf16[224,1024]{1,0:T(8,128)(2,1)S(1)}, u32[]{:S(2)}, u32[]{:S(2)}) collective-permute-start(bf16[224,1024]{1,0:T(8,128)(2,1)S(1)} %get-tuple-element.42), channel_id=1, source_target_pairs={{0,1},{1,0},{2,3},{3,2},{4,7},{5,6},{6,5},{7,4},{8,9},{9,8},{10,11... | collective-permute-start | bytes 1376264 | tf_op jit(solution)/shard_map/ppermute | solution.py:27
  49.2 15.0 %collective-permute-start.14 = (bf16[112,1024]{1,0:T(8,128)(2,1)}, bf16[112,1024]{1,0:T(8,128)(2,1)}, u32[]{:S(2)}, u32[]{:S(2)}) collective-permute-start(bf16[112,1024]{1,0:T(8,128)(2,1)} %shard_map.118.own), channel_id=1, source_target_pairs={{0,3},{1,2},{2,1},{3,0},{4,7},{5,6},{6,5},{7,4},{8,11},{9,10},{10,... | collective-permute-start | bytes 688136 | tf_op jit(solution)/shard_map/ppermute | solution.py:22
  50.1 14.1 %collective-permute-start.13 = (bf16[112,1024]{1,0:T(8,128)(2,1)}, bf16[112,1024]{1,0:T(8,128)(2,1)}, u32[]{:S(2)}, u32[]{:S(2)}) collective-permute-start(bf16[112,1024]{1,0:T(8,128)(2,1)} %shard_map.118.own), channel_id=1, source_target_pairs={{0,2},{1,3},{2,0},{3,1},{4,6},{5,7},{6,4},{7,5},{8,10},{9,11},{10,... | collective-permute-start | bytes 688136 | tf_op jit(solution)/shard_map/ppermute | solution.py:22
  51.3 12.9 %collective-permute-start.12 = (bf16[112,1024]{1,0:T(8,128)(2,1)}, bf16[112,1024]{1,0:T(8,128)(2,1)}, u32[]{:S(2)}, u32[]{:S(2)}) collective-permute-start(bf16[112,1024]{1,0:T(8,128)(2,1)} %shard_map.118.own), channel_id=1, source_target_pairs={{0,1},{1,0},{2,3},{3,2},{4,5},{5,4},{6,7},{7,6},{8,9},{9,8},{10,11... | collective-permute-start | bytes 688136 | tf_op jit(solution)/shard_map/ppermute | solution.py:22
  55.9 10.5 %collective-permute-start.17 = (bf16[112,1024]{1,0:T(8,128)(2,1)}, bf16[112,1024]{1,0:T(8,128)(2,1)}, u32[]{:S(2)}, u32[]{:S(2)}) collective-permute-start(bf16[112,1024]{1,0:T(8,128)(2,1)} %get-tuple-element.44), channel_id=1, source_target_pairs={{0,3},{1,2},{2,1},{3,0},{4,5},{5,4},{6,7},{7,6},{8,11},{9,10},{10,... | collective-permute-start | bytes 688136 | tf_op jit(solution)/shard_map/ppermute | solution.py:27
  76.0 8.4 %collective-permute-start.19 = (bf16[128,2048]{1,0:T(8,128)(2,1)S(1)}, bf16[128,2048]{1,0:T(8,128)(2,1)S(1)}, u32[]{:S(2)}, u32[]{:S(2)}) collective-permute-start(bf16[128,2048]{1,0:T(8,128)(2,1)S(1)} %get-tuple-element.48), channel_id=1, source_target_pairs={{0,8},{4,36},{8,0},{12,44},{16,24},{20,52},{24,16},{28,60},{32,40}... | collective-permute-start | bytes 1572872 | tf_op jit(solution)/shard_map/ppermute | solution.py:37
  77.4 14.9 %collective-permute-start.20 = (bf16[128,2048]{1,0:T(8,128)(2,1)S(1)}, bf16[128,2048]{1,0:T(8,128)(2,1)S(1)}, u32[]{:S(2)}, u32[]{:S(2)}) collective-permute-start(bf16[128,2048]{1,0:T(8,128)(2,1)S(1)} %get-tuple-element.49), channel_id=1, source_target_pairs={{0,16},{4,68},{8,24},{12,76},{16,0},{20,84},{24,8},{28,92},{32,48}... | collective-permute-start | bytes 1572872 | tf_op jit(solution)/shard_map/ppermute | solution.py:37
  80.0 15.2 %collective-permute-start.21 = (bf16[128,2048]{1,0:T(8,128)(2,1)S(1)}, bf16[128,2048]{1,0:T(8,128)(2,1)S(1)}, u32[]{:S(2)}, u32[]{:S(2)}) collective-permute-start(bf16[128,2048]{1,0:T(8,128)(2,1)S(1)} %get-tuple-element.50), channel_id=1, source_target_pairs={{0,24},{4,100},{8,16},{12,108},{16,8},{20,116},{24,0},{28,124},{32... | collective-permute-start | bytes 1572872 | tf_op jit(solution)/shard_map/ppermute | solution.py:37
  95.5 6.3 %collective-permute-start.23 = (bf16[32,2048]{1,0:T(8,128)(2,1)S(1)}, bf16[32,2048]{1,0:T(8,128)(2,1)S(1)}, u32[]{:S(2)}, u32[]{:S(2)}) collective-permute-start(bf16[32,2048]{1,0:T(8,128)(2,1)S(1)} %get-tuple-element.53), channel_id=1, source_target_pairs={{0,64},{4,20},{8,72},{12,28},{16,80},{20,4},{24,88},{28,12},{32,96... | collective-permute-start | bytes 393224 | tf_op jit(solution)/shard_map/ppermute | solution.py:37
  98.1 5.5 %collective-permute-start.24 = (bf16[32,2048]{1,0:T(8,128)(2,1)S(1)}, bf16[32,2048]{1,0:T(8,128)(2,1)S(1)}, u32[]{:S(2)}, u32[]{:S(2)}) collective-permute-start(bf16[32,2048]{1,0:T(8,128)(2,1)S(1)} %get-tuple-element.54), channel_id=1, source_target_pairs={{0,96},{4,28},{8,104},{12,20},{16,112},{20,12},{24,120},{28,4},{32... | collective-permute-start | bytes 393224 | tf_op jit(solution)/shard_map/ppermute | solution.py:37
  104.1 18.9 %collective-permute-start.27 = (bf16[32,2048]{1,0:T(8,128)(2,1)S(1)}, bf16[32,2048]{1,0:T(8,128)(2,1)S(1)}, u32[]{:S(2)}, u32[]{:S(2)}) collective-permute-start(bf16[32,2048]{1,0:T(8,128)(2,1)S(1)} %get-tuple-element.57.own), channel_id=1, source_target_pairs={{0,3},{1,2},{2,1},{3,0},{4,7},{5,6},{6,5},{7,4},{8,11},{9,10},{10,... | collective-permute-start | bytes 393224 | tf_op jit(solution)/shard_map/ppermute | solution.py:22
  106.2 16.8 %collective-permute-start.26 = (bf16[32,2048]{1,0:T(8,128)(2,1)S(1)}, bf16[32,2048]{1,0:T(8,128)(2,1)S(1)}, u32[]{:S(2)}, u32[]{:S(2)}) collective-permute-start(bf16[32,2048]{1,0:T(8,128)(2,1)S(1)} %get-tuple-element.57.own), channel_id=1, source_target_pairs={{0,2},{1,3},{2,0},{3,1},{4,6},{5,7},{6,4},{7,5},{8,10},{9,11},{10,... | collective-permute-start | bytes 393224 | tf_op jit(solution)/shard_map/ppermute | solution.py:22
  106.7 16.4 %collective-permute-start.25 = (bf16[32,2048]{1,0:T(8,128)(2,1)S(1)}, bf16[32,2048]{1,0:T(8,128)(2,1)S(1)}, u32[]{:S(2)}, u32[]{:S(2)}) collective-permute-start(bf16[32,2048]{1,0:T(8,128)(2,1)S(1)} %get-tuple-element.57.own), channel_id=1, source_target_pairs={{0,1},{1,0},{2,3},{3,2},{4,5},{5,4},{6,7},{7,6},{8,9},{9,8},{10,11... | collective-permute-start | bytes 393224 | tf_op jit(solution)/shard_map/ppermute | solution.py:22
  (37 other events, 403.9 us)

commit v5 on v4

--- a/solution.py
+++ b/solution.py
@@ -11,7 +11,7 @@
 F32 = jnp.float32
 BF16 = jnp.bfloat16
 SEQ = ("y", "z", "c")
-VMEM_LIMIT = 16 * 1024 * 1024
+VMEM_LIMIT = 32 * 1024 * 1024
 
 
 def swap_core(value):
@@ -109,14 +109,16 @@
             out[to : to + part] = whole[pl.ds(place, part), :]
 
 
-def gate_product_kernel(
-    offsets, enc_hbm, gate_hbm, lift_hbm, keep, send, w_enc, w_gate, w_lift, whole, sems
-):
+def product_kernel(offsets, *refs):
+    sources, (keep, send), (w_enc, w_gate, w_lift, w_down, w_dec, whole, sems) = (
+        refs[:5],
+        refs[5:7],
+        refs[7:],
+    )
+    targets = (w_enc, w_gate, w_lift, w_down, w_dec)
     copies = [
         pltpu.make_async_copy(source, target, sems.at[i])
-        for i, (source, target) in enumerate(
-            ((enc_hbm, w_enc), (gate_hbm, w_gate), (lift_hbm, w_lift))
-        )
+        for i, (source, target) in enumerate(zip(sources, targets))
     ]
     for copy in copies:
         copy.start()
@@ -125,13 +127,14 @@
     copies[1].wait()
     whole[:hid] = dot_t(w_gate[...], w_enc[...]).astype(BF16)
     copies[2].wait()
-    whole[hid:] = dot_t(w_lift[...], w_enc[...]).astype(BF16)
-    cut_products(2, offsets, whole, keep, send)
-
-
-def down_product_kernel(offsets, w_down, w_dec, w_enc, pooled, keep, send, rep, back, whole):
-    whole[...] = dot(w_down[...], w_dec[...]).astype(BF16)
-    cut_products(1, offsets, whole, keep, send)
+    whole[hid : 2 * hid] = dot_t(w_lift[...], w_enc[...]).astype(BF16)
+    copies[3].wait()
+    copies[4].wait()
+    whole[2 * hid :] = dot(w_down[...], w_dec[...]).astype(BF16)
+    cut_products(3, offsets, whole, keep, send)
+
+
+def encode_kernel(w_dec, w_enc, pooled, rep, back):
     width = w_enc.shape[0]
     rep[...] = dot(pooled[:, :width], w_enc[...]).astype(BF16)
     back[...] = dot_t(dot_t(pooled[:, width:], w_dec[...]).astype(BF16), w_enc[...])
@@ -145,8 +148,8 @@
 
 def gate_rows(rows, products):
     width = products.shape[1]
-    both = dot_t(products[...], jnp.concatenate([block[:, :width] for block in rows], axis=0))
-    part = both.shape[0] // 2
+    part = products.shape[0] // 3
+    both = dot_t(products[: 2 * part], jnp.concatenate([block[:, :width] for block in rows], axis=0))
     return both[:part], both[part:]
 
 
@@ -166,19 +169,21 @@
     hidden[:, half:] = hidden_rows((r0, r1, r2, r3), products)
 
 
-def grad_rows(rows, down, products):
-    width = down.shape[1]
-    grad_hidden = dot_t(down, jnp.concatenate([block[:, width:] for block in rows], axis=0))
+def grad_rows(rows, products):
+    width = products.shape[1]
+    part = products.shape[0] // 3
+    grad_hidden = dot_t(
+        products[2 * part :], jnp.concatenate([block[:, width:] for block in rows], axis=0)
+    )
     gate, lift = gate_rows(rows, products)
     sig = 1.0 / (1.0 + jnp.exp(-gate))
     grad_gate = grad_hidden * lift * sig * (1.0 + gate * (1.0 - sig))
-    return jnp.concatenate([grad_gate, grad_hidden * (gate * sig)], axis=0).astype(BF16)
-
-
-def grad_far_kernel(r0, r1, r2, r3, own, second, products, down, partial):
-    down[...] = (own[...] + second[...].astype(F32)).astype(BF16)
-    grads = grad_rows((r0, r1, r2, r3), down[...], products)
-    partial[...] = dot(grads.T, products[...]).astype(BF16)
+    grads = jnp.concatenate([grad_gate, grad_hidden * (gate * sig)], axis=0).astype(BF16)
+    return dot(grads.T, products[: 2 * part])
+
+
+def grad_far_kernel(r0, r1, r2, r3, products, partial):
+    partial[...] = grad_rows((r0, r1, r2, r3), products).astype(BF16)
 
 
 def place_blocks(total, outs):
@@ -197,15 +202,14 @@
 
 
 def sum_near_kernel(
-    offsets, own, one, two, three, w_down, other, r0, r1, r2, r3, down, products, grad_other, *rest
+    offsets, own, one, two, three, w_down, other, r0, r1, r2, r3, products, grad_other, *rest
 ):
     stack = rest[-1]
     part, span = own.shape[0], other.shape[0]
     width = w_down.shape[1]
     for k, block in enumerate((own, one, two, three)):
         stack[pl.ds(pl.multiple_of(offsets[k], 16), part), :] = block[:, :span]
-    grads = grad_rows((r0, r1, r2, r3), down[...], products)
-    total = dot(grads.T, products[...]) + grad_other[...].astype(F32)
+    total = grad_rows((r0, r1, r2, r3), products) + grad_other[...].astype(F32)
     place_blocks(total, [out.at[:, width:] for out in rest[:-1]])
     total = dot(stack[...].T, w_down[...]) + other[...].astype(F32)
     place_blocks(total, [out.at[:, :width] for out in rest[:-1]])
@@ -290,15 +294,15 @@
         )
         return own, swap_near(send, False)
 
-    weights = [w_enc, w_gate, w_lift]
+    weights = [w_enc, w_gate, w_lift, w_down, w_dec]
     keep, send = call(
-        gate_product_kernel,
-        [shape((4 * part, width), BF16)] * 2,
+        product_kernel,
+        [shape((6 * part, width), BF16)] * 2,
         weights,
         [halving],
-        flops=4 * hid * width * latent,
+        flops=6 * hid * width * latent,
         scratch=[pltpu.VMEM(w.shape, BF16) for w in weights]
-        + [pltpu.VMEM((2 * hid, width), BF16), pltpu.SemaphoreType.DMA((3,))],
+        + [pltpu.VMEM((3 * hid, width), BF16), pltpu.SemaphoreType.DMA((5,))],
         outside=True,
     )
     first = swap_near(send, True)
@@ -316,25 +320,15 @@
     )
     near = over(swap_second, rows)
     far = [swap_core(block) for block in near]
-    down_keep, down_send, patch_rep, back = call(
-        down_product_kernel,
-        [shape((2 * part, width), BF16)] * 2
-        + [shape((patches, latent), BF16), shape((patches, width), F32)],
-        [w_down, w_dec, w_enc, pooled],
-        [halving],
-        flops=2 * hid * width * latent,
-        scratch=[pltpu.VMEM((hid, width), BF16)],
-    )
     own, second = halve(keep, first)
-    down_first = swap_near(after(down_send, first), True)
     flops = 4 * group * width * part
     products, near_hidden = call(
         near_kernel,
         [
-            shape((2 * part, width), BF16),
+            shape((3 * part, width), BF16),
             shape((part, group), BF16),
         ],
-        [*near, after(own, down_send), second],
+        [*near, own, second],
         flops=flops,
     )
     (hidden,) = call(
@@ -344,17 +338,22 @@
         flops=flops,
     )
     hiddens = over(swap_x, hidden)
-    down_own, down_second = halve(down_keep, down_first)
-    down, far_partial = call(
+    (far_partial,) = call(
         grad_far_kernel,
-        [shape((part, width), BF16), shape((group, width), BF16)],
-        [*far, down_own, down_second, products],
+        [shape((group, width), BF16)],
+        [*far, products],
         flops=flops,
+    )
+    patch_rep, back = call(
+        encode_kernel,
+        [shape((patches, latent), BF16), shape((patches, width), F32)],
+        [w_dec, w_enc, pooled],
+        flops=6 * patches * width * latent,
     )
     (far_rows,) = call(
         down_far_kernel,
         [shape((group, latent), BF16)],
-        [*hiddens, w_down],
+        [*hiddens, after(w_down, (far_partial, back))],
         [offsets],
         flops=2 * group * latent * hid,
         scratch=[pltpu.VMEM((hid, group), BF16)],
@@ -367,7 +366,6 @@
             w_down,
             swap_core(far_rows),
             *near,
-            down,
             products,
             swap_core(far_partial),
         ],

time: 125 us -> 121 us (0.968)
  starting transfers between devices: 35.2 us -> 41.1 us
  waiting for transfers between devices: 42.9 us -> 37.1 us
  local copies, waits for them, and re-layouts: 7.62 us -> 3.6 us
  Pallas kernels: 22.5 us -> 19.7 us
  blocking collectives: 14.8 us -> 17.2 us
    ppermute x6, starting transfers between devices: 7.41 us -> 12.6 us  [swap_core(): return lax.ppermute(value, 'c', [(0, 1), (1, 0)])]
    unnamed x66 -> x52, local copies, waits for them, and re-layouts: 6.86 us -> 2.85 us
    ppermute x6, waiting for transfers between devices: 8.2 us -> 4.63 us  [swap_x(): return lax.ppermute(value, 'x', [(i, i ^ k) for i in range(4)])]
    pallas_call x14 -> x13, Pallas kernels: 22.5 us -> 19.7 us  [call(): pl.pallas_call(body, out_shape=outs, in_specs=specs, out_specs=[pl.BlockS...]
    ppermute x12, waiting for transfers between devices: 30.4 us -> 27.9 us  [swap_first(): return lax.ppermute(value, SEQ, pairs)]
    all_to_all x1, blocking collectives: 14.8 us -> 17.2 us  [on_device(): lax.all_to_all(outgoing, SEQ, split_axis=0, concat_axis=0, tiled=True)]
    ppermute x4 -> x2, starting transfers between devices: 5.29 us -> 3.95 us  [swap_near(): lax.ppermute(value, ('c', 'x'), [(c * 4 + x, c * 4 + (x ^ steps[c])) for...]
  transfers between devices with their start and end apart: 28 -> 26, of which waited for: 12 -> 15; matrix products, arithmetic and copies ran while one was open for 0% -> 0% of each run, Pallas kernels for 9% -> 5%
where the time goes in v5:
time: 121 us; the launch traced here: 120 us
  starting transfers between devices  41.1 us (34%)
  waiting for transfers between devices  37.1 us (31%)
  Pallas kernels  19.7 us (16%)
  blocking collectives  17.2 us (14%)
  local copies, waits for them, and re-layouts  3.6 us (3%)
    ppermute x12, waiting for transfers between devices, swap_first(): return lax.ppermute(value, SEQ, pairs)  27.9 us
    pallas_call x13, Pallas kernels, call(): pl.pallas_call(body, out_shape=outs, in_specs=specs, out_specs=[pl.BlockS...  19.7 us
    all_to_all x1, blocking collectives, on_device(): lax.all_to_all(outgoing, SEQ, split_axis=0, concat_axis=0, tiled=True)  17.2 us
    ppermute x12, starting transfers between devices, swap_first(): return lax.ppermute(value, SEQ, pairs)  16.8 us
    ppermute x6, starting transfers between devices, swap_core(): return lax.ppermute(value, 'c', [(0, 1), (1, 0)])  12.6 us
    ppermute x6, starting transfers between devices, swap_x(): return lax.ppermute(value, 'x', [(i, i ^ k) for i in range(4)])  7.79 us
    ppermute x6, waiting for transfers between devices, swap_x(): return lax.ppermute(value, 'x', [(i, i ^ k) for i in range(4)])  4.63 us
    ppermute x2, starting transfers between devices, swap_near(): lax.ppermute(value, ('c', 'x'), [(c * 4 + x, c * 4 + (x ^ steps[c])) for...  3.95 us
  transfers between devices with their start and end apart: 26, of which 15 were waited for; matrix products, arithmetic and copies ran while one was open for 0% of the time, Pallas kernels for 5%

profile of v5, /device:TPU:1, one launch (start us, length us, event | category | flops | bytes accessed | tf_op | source)
XLA Modules:
  0.0 120.3 jit_solution(3473509582471411887)
XLA Ops:
  1.2 7.7 %shard_map.112 = (bf16[672,1024]{1,0:T(8,128)(2,1)}, bf16[672,1024]{1,0:T(8,128)(2,1)}) custom-call(s32[4]{0:T(128)} %add_multiply_fusion.1.offsets, bf16[1024,1024]{1,0:T(8,128)(2,1)} %w_enc.1, bf16[448,1024]{1,0:T(8,128)(2,1)} %bitcast.10, bf16[448,1024]{1,0:T(8,128)(2,1)} %bitcast.11, bf16[448,1024]{1,0:T(8,128)(2,1)} %w_down.2, bf16[1024,1024]{1,0:T(8,128)(2,1)} %weight.1), custom_call_target="tpu_custom_call" | custom-call | flops 2818572288 | bytes 9699328 | tf_op jit(solution)/shard_map/pallas_call | solution.py:56
  8.9 3.4 %collective-permute-start.10 = (bf16[672,1024]{1,0:T(8,128)(2,1)}, bf16[672,1024]{1,0:T(8,128)(2,1)S(1)}, u32[]{:S(2)}, u32[]{:S(2)}) collective-permute-start(bf16[672,1024]{1,0:T(8,128)(2,1)} %get-tuple-element.25), channel_id=1, source_target_pairs={{0,1},{1,0},{2,3},{3,2},{4,7},{5,6},{6,5},{7,4},{8,9},{9,8},{10,11... | collective-permute-start | bytes 4128776 | tf_op jit(solution)/shard_map/ppermute | solution.py:27
  14.0 2.6 %collective-permute-start.1 = (bf16[32,2048]{1,0:T(8,128)(2,1)S(1)}, bf16[32,2048]{1,0:T(8,128)(2,1)S(1)}, u32[]{:S(2)}, u32[]{:S(2)}) collective-permute-start(bf16[32,2048]{1,0:T(8,128)(2,1)S(1)} %shard_map.113.own.pooled), channel_id=1, source_target_pairs={{0,16},{4,68},{8,24},{12,76},{16,0},{20,84},{24,8},{28,92},{32,48}... | collective-permute-start | bytes 393224 | tf_op jit(solution)/shard_map/ppermute | solution.py:37
  16.8 3.9 %collective-permute-done.1.two = bf16[32,2048]{1,0:T(8,128)(2,1)S(1)} collective-permute-done((bf16[32,2048]{1,0:T(8,128)(2,1)S(1)}, bf16[32,2048]{1,0:T(8,128)(2,1)S(1)}, u32[]{:S(2)}, u32[]{:S(2)}) %collective-permute-start.1) | collective-permute-done | bytes 131104 | tf_op jit(solution)/shard_map/ppermute | solution.py:37
  23.6 3.3 %collective-permute-start.6 = (bf16[128,2048]{1,0:T(8,128)(2,1)S(1)}, bf16[128,2048]{1,0:T(8,128)(2,1)S(1)}, u32[]{:S(2)}, u32[]{:S(2)}) collective-permute-start(bf16[128,2048]{1,0:T(8,128)(2,1)S(1)} %shard_map.114.r0), channel_id=1, source_target_pairs={{0,64},{4,20},{8,72},{12,28},{16,80},{20,4},{24,88},{28,12},{32,96... | collective-permute-start | bytes 1572872 | tf_op jit(solution)/shard_map/ppermute | solution.py:37
  29.1 3.1 %collective-permute-start.3 = (bf16[128,2048]{1,0:T(8,128)(2,1)S(1)}, bf16[128,2048]{1,0:T(8,128)(2,1)S(1)}, u32[]{:S(2)}, u32[]{:S(2)}) collective-permute-start(bf16[128,2048]{1,0:T(8,128)(2,1)S(1)} %shard_map.114.r0), channel_id=1, source_target_pairs={{0,4},{4,0},{1,5},{5,1},{2,6},{6,2},{3,7},{7,3},{8,12},{12,8},{9,1... | collective-permute-start | bytes 1572872 | tf_op jit(solution)/shard_map/ppermute | solution.py:18
  33.4 6.0 %collective-permute-done.6.r2 = bf16[128,2048]{1,0:T(8,128)(2,1)S(1)} collective-permute-done((bf16[128,2048]{1,0:T(8,128)(2,1)S(1)}, bf16[128,2048]{1,0:T(8,128)(2,1)S(1)}, u32[]{:S(2)}, u32[]{:S(2)}) %collective-permute-start.6) | collective-permute-done | bytes 524320 | tf_op jit(solution)/shard_map/ppermute | solution.py:37
  39.4 2.2 %collective-permute-start.7 = (bf16[128,2048]{1,0:T(8,128)(2,1)S(1)}, bf16[128,2048]{1,0:T(8,128)(2,1)S(1)}, u32[]{:S(2)}, u32[]{:S(2)}) collective-permute-start(bf16[128,2048]{1,0:T(8,128)(2,1)S(1)} %collective-permute-done.6.r2), channel_id=1, source_target_pairs={{0,4},{4,0},{1,5},{5,1},{2,6},{6,2},{3,7},{7,3},{8,12},{12,8},{9,1... | collective-permute-start | bytes 1572872 | tf_op jit(solution)/shard_map/ppermute | solution.py:18
  42.0 2.7 %collective-permute-start.9 = (bf16[128,2048]{1,0:T(8,128)(2,1)S(1)}, bf16[128,2048]{1,0:T(8,128)(2,1)S(1)}, u32[]{:S(2)}, u32[]{:S(2)}) collective-permute-start(bf16[128,2048]{1,0:T(8,128)(2,1)S(1)} %collective-permute-done.8.r3), channel_id=1, source_target_pairs={{0,4},{4,0},{1,5},{5,1},{2,6},{6,2},{3,7},{7,3},{8,12},{12,8},{9,1... | collective-permute-start | bytes 1572872 | tf_op jit(solution)/shard_map/ppermute | solution.py:18
  47.3 2.7 %collective-permute-start.13 = (bf16[112,1024]{1,0:T(8,128)(2,1)S(1)}, bf16[112,1024]{1,0:T(8,128)(2,1)}, u32[]{:S(2)}, u32[]{:S(2)}) collective-permute-start(bf16[112,1024]{1,0:T(8,128)(2,1)S(1)} %shard_map.117.own), channel_id=1, source_target_pairs={{0,2},{1,3},{2,0},{3,1},{4,6},{5,7},{6,4},{7,5},{8,10},{9,11},{10,... | collective-permute-start | bytes 688136 | tf_op jit(solution)/shard_map/ppermute | solution.py:22
  57.8 2.6 %collective-permute-done.13.two = bf16[112,1024]{1,0:T(8,128)(2,1)} collective-permute-done((bf16[112,1024]{1,0:T(8,128)(2,1)S(1)}, bf16[112,1024]{1,0:T(8,128)(2,1)}, u32[]{:S(2)}, u32[]{:S(2)}) %collective-permute-start.13) | collective-permute-done | bytes 229408 | tf_op jit(solution)/shard_map/ppermute | solution.py:22
  60.4 2.0 %collective-permute-done.14.three = bf16[112,1024]{1,0:T(8,128)(2,1)} collective-permute-done((bf16[112,1024]{1,0:T(8,128)(2,1)S(1)}, bf16[112,1024]{1,0:T(8,128)(2,1)}, u32[]{:S(2)}, u32[]{:S(2)}) %collective-permute-start.14) | collective-permute-done | bytes 229408 | tf_op jit(solution)/shard_map/ppermute | solution.py:22
  62.4 1.9 %shard_map.120 = bf16[512,1024]{1,0:T(8,128)(2,1)S(1)} custom-call(s32[4]{0:T(128)S(1)} %add_multiply_fusion.offsets, bf16[112,1024]{1,0:T(8,128)(2,1)S(1)} %shard_map.117.own, bf16[112,1024]{1,0:T(8,128)(2,1)} %collective-permute-done.12.one, bf16[112,1024]{1,0:T(8,128)(2,1)} %collective-permute-done.13.two, ...), custom_call_target="tpu_custom_call" | custom-call | flops 469762048 | bytes 2883584 | tf_op jit(solution)/shard_map/pallas_call | solution.py:56
  64.4 2.1 %collective-permute-start.15 = (bf16[512,1024]{1,0:T(8,128)(2,1)S(1)}, bf16[512,1024]{1,0:T(8,128)(2,1)S(1)}, u32[]{:S(2)}, u32[]{:S(2)}) collective-permute-start(bf16[512,1024]{1,0:T(8,128)(2,1)S(1)} %shard_map.120), channel_id=1, source_target_pairs={{0,4},{4,0},{1,5},{5,1},{2,6},{6,2},{3,7},{7,3},{8,12},{12,8},{9,1... | collective-permute-start | bytes 3145736 | tf_op jit(solution)/shard_map/ppermute | solution.py:18
  66.5 2.3 %collective-permute-done.15.other = bf16[512,1024]{1,0:T(8,128)(2,1)S(1)} collective-permute-done((bf16[512,1024]{1,0:T(8,128)(2,1)S(1)}, bf16[512,1024]{1,0:T(8,128)(2,1)S(1)}, u32[]{:S(2)}, u32[]{:S(2)}) %collective-permute-start.15) | collective-permute-done | bytes 1048608 | tf_op jit(solution)/shard_map/ppermute | solution.py:18
  68.8 3.0 %shard_map.121 = (bf16[128,2048]{1,0:T(8,128)(2,1)S(1)}, bf16[128,2048]{1,0:T(8,128)(2,1)S(1)}, bf16[128,2048]{1,0:T(8,128)(2,1)S(1)}, bf16[128,2048]{1,0:T(8,128)(2,1)S(1)}) custom-call(s32[4]{0:T(128)S(1)} %add_multiply_fusion.offsets, bf16[112,1024]{1,0:T(8,128)(2,1)S(1)} %shard_map.117.own, bf16[112,1024]{1,0:T(8,128)(2,1)} %collective-permute-done.12.one, ...), custom_call_target="tpu_custom_call" | custom-call | flops 704643072 | bytes 8814592 | tf_op jit(solution)/shard_map/pallas_call | solution.py:56
  73.1 2.7 %collective-permute-start.19 = (bf16[128,2048]{1,0:T(8,128)(2,1)S(1)}, bf16[128,2048]{1,0:T(8,128)(2,1)S(1)}, u32[]{:S(2)}, u32[]{:S(2)}) collective-permute-start(bf16[128,2048]{1,0:T(8,128)(2,1)S(1)} %get-tuple-element.37), channel_id=1, source_target_pairs={{0,24},{4,100},{8,16},{12,108},{16,8},{20,116},{24,0},{28,124},{32... | collective-permute-start | bytes 1572872 | tf_op jit(solution)/shard_map/ppermute | solution.py:37
  75.8 4.5 %collective-permute-done.17.one = bf16[128,2048]{1,0:T(8,128)(2,1)S(1)} collective-permute-done((bf16[128,2048]{1,0:T(8,128)(2,1)S(1)}, bf16[128,2048]{1,0:T(8,128)(2,1)S(1)}, u32[]{:S(2)}, u32[]{:S(2)}) %collective-permute-start.17) | collective-permute-done | bytes 524320 | tf_op jit(solution)/shard_map/ppermute | solution.py:37
  80.3 5.3 %collective-permute-done.18.two = bf16[128,2048]{1,0:T(8,128)(2,1)S(1)} collective-permute-done((bf16[128,2048]{1,0:T(8,128)(2,1)S(1)}, bf16[128,2048]{1,0:T(8,128)(2,1)S(1)}, u32[]{:S(2)}, u32[]{:S(2)}) %collective-permute-start.18) | collective-permute-done | bytes 524320 | tf_op jit(solution)/shard_map/ppermute | solution.py:37
  85.6 2.7 %collective-permute-done.19.three = bf16[128,2048]{1,0:T(8,128)(2,1)S(1)} collective-permute-done((bf16[128,2048]{1,0:T(8,128)(2,1)S(1)}, bf16[128,2048]{1,0:T(8,128)(2,1)S(1)}, u32[]{:S(2)}, u32[]{:S(2)}) %collective-permute-start.19) | collective-permute-done | bytes 524320 | tf_op jit(solution)/shard_map/ppermute | solution.py:37
  88.6 2.2 %collective-permute-start.21 = (bf16[32,2048]{1,0:T(8,128)(2,1)S(1)}, bf16[32,2048]{1,0:T(8,128)(2,1)S(1)}, u32[]{:S(2)}, u32[]{:S(2)}) collective-permute-start(bf16[32,2048]{1,0:T(8,128)(2,1)S(1)} %get-tuple-element.40), channel_id=1, source_target_pairs={{0,64},{4,20},{8,72},{12,28},{16,80},{20,4},{24,88},{28,12},{32,96... | collective-permute-start | bytes 393224 | tf_op jit(solution)/shard_map/ppermute | solution.py:37
  92.5 2.1 %collective-permute-done.21.two = bf16[32,2048]{1,0:T(8,128)(2,1)S(1)} collective-permute-done((bf16[32,2048]{1,0:T(8,128)(2,1)S(1)}, bf16[32,2048]{1,0:T(8,128)(2,1)S(1)}, u32[]{:S(2)}, u32[]{:S(2)}) %collective-permute-start.21) | collective-permute-done | bytes 131104 | tf_op jit(solution)/shard_map/ppermute | solution.py:37
  98.4 2.3 %collective-permute-start.25 = (bf16[32,2048]{1,0:T(8,128)(2,1)S(1)}, bf16[32,2048]{1,0:T(8,128)(2,1)S(1)}, u32[]{:S(2)}, u32[]{:S(2)}) collective-permute-start(bf16[32,2048]{1,0:T(8,128)(2,1)S(1)} %get-tuple-element.43.own), channel_id=1, source_target_pairs={{0,3},{1,2},{2,1},{3,0},{4,7},{5,6},{6,5},{7,4},{8,11},{9,10},{10,... | collective-permute-start | bytes 393224 | tf_op jit(solution)/shard_map/ppermute | solution.py:22
  100.8 17.2 %all_to_all.12 = bf16[32,2,1024]{2,1,0:T(2,128)(2,1)S(1)} all-to-all(bf16[32,2,1024]{2,1,0:T(2,128)(2,1)S(1)} %all_to_all.8), channel_id=1, replica_groups=mesh['y'=4,'z'=4,'c'=2,'x'=4] {'y','z','c'}, dimensions={0} | all-to-all | bytes 262144 | tf_op jit(solution)/shard_map/all_to_all | solution.py:388
  (98 shorter events, 28.9 us)
Async XLA Ops:
  8.9 19.3 %collective-permute-start.10 = (bf16[672,1024]{1,0:T(8,128)(2,1)}, bf16[672,1024]{1,0:T(8,128)(2,1)S(1)}, u32[]{:S(2)}, u32[]{:S(2)}) collective-permute-start(bf16[672,1024]{1,0:T(8,128)(2,1)} %get-tuple-element.25), channel_id=1, source_target_pairs={{0,1},{1,0},{2,3},{3,2},{4,7},{5,6},{6,5},{7,4},{8,9},{9,8},{10,11... | collective-permute-start | bytes 4128776 | tf_op jit(solution)/shard_map/ppermute | solution.py:27
  14.0 6.7 %collective-permute-start.1 = (bf16[32,2048]{1,0:T(8,128)(2,1)S(1)}, bf16[32,2048]{1,0:T(8,128)(2,1)S(1)}, u32[]{:S(2)}, u32[]{:S(2)}) collective-permute-start(bf16[32,2048]{1,0:T(8,128)(2,1)S(1)} %shard_map.113.own.pooled), channel_id=1, source_target_pairs={{0,16},{4,68},{8,24},{12,76},{16,0},{20,84},{24,8},{28,92},{32,48}... | collective-permute-start | bytes 393224 | tf_op jit(solution)/shard_map/ppermute | solution.py:37
  16.6 5.2 %collective-permute-start.2 = (bf16[32,2048]{1,0:T(8,128)(2,1)S(1)}, bf16[32,2048]{1,0:T(8,128)(2,1)S(1)}, u32[]{:S(2)}, u32[]{:S(2)}) collective-permute-start(bf16[32,2048]{1,0:T(8,128)(2,1)S(1)} %shard_map.113.own.pooled), channel_id=1, source_target_pairs={{0,24},{4,100},{8,16},{12,108},{16,8},{20,116},{24,0},{28,124},{32... | collective-permute-start | bytes 393224 | tf_op jit(solution)/shard_map/ppermute | solution.py:37
  21.9 10.3 %collective-permute-start.4 = (bf16[128,2048]{1,0:T(8,128)(2,1)S(1)}, bf16[128,2048]{1,0:T(8,128)(2,1)S(1)}, u32[]{:S(2)}, u32[]{:S(2)}) collective-permute-start(bf16[128,2048]{1,0:T(8,128)(2,1)S(1)} %shard_map.114.r0), channel_id=1, source_target_pairs={{0,32},{4,12},{8,40},{12,4},{16,48},{20,28},{24,56},{28,20},{32,0}... | collective-permute-start | bytes 1572872 | tf_op jit(solution)/shard_map/ppermute | solution.py:37
  23.6 15.8 %collective-permute-start.6 = (bf16[128,2048]{1,0:T(8,128)(2,1)S(1)}, bf16[128,2048]{1,0:T(8,128)(2,1)S(1)}, u32[]{:S(2)}, u32[]{:S(2)}) collective-permute-start(bf16[128,2048]{1,0:T(8,128)(2,1)S(1)} %shard_map.114.r0), channel_id=1, source_target_pairs={{0,64},{4,20},{8,72},{12,28},{16,80},{20,4},{24,88},{28,12},{32,96... | collective-permute-start | bytes 1572872 | tf_op jit(solution)/shard_map/ppermute | solution.py:37
  26.9 15.2 %collective-permute-start.8 = (bf16[128,2048]{1,0:T(8,128)(2,1)S(1)}, bf16[128,2048]{1,0:T(8,128)(2,1)S(1)}, u32[]{:S(2)}, u32[]{:S(2)}) collective-permute-start(bf16[128,2048]{1,0:T(8,128)(2,1)S(1)} %shard_map.114.r0), channel_id=1, source_target_pairs={{0,96},{4,28},{8,104},{12,20},{16,112},{20,12},{24,120},{28,4},{32... | collective-permute-start | bytes 1572872 | tf_op jit(solution)/shard_map/ppermute | solution.py:37
  28.5 16.2 %collective-permute-start.11 = (bf16[336,1024]{1,0:T(8,128)(2,1)S(1)}, bf16[336,1024]{1,0:T(8,128)(2,1)S(1)}, u32[]{:S(2)}, u32[]{:S(2)}) collective-permute-start(bf16[336,1024]{1,0:T(8,128)(2,1)S(1)} %get-tuple-element.29), channel_id=1, source_target_pairs={{0,3},{1,2},{2,1},{3,0},{4,5},{5,4},{6,7},{7,6},{8,11},{9,10},{10,... | collective-permute-start | bytes 2064392 | tf_op jit(solution)/shard_map/ppermute | solution.py:27
  29.1 16.2 %collective-permute-start.3 = (bf16[128,2048]{1,0:T(8,128)(2,1)S(1)}, bf16[128,2048]{1,0:T(8,128)(2,1)S(1)}, u32[]{:S(2)}, u32[]{:S(2)}) collective-permute-start(bf16[128,2048]{1,0:T(8,128)(2,1)S(1)} %shard_map.114.r0), channel_id=1, source_target_pairs={{0,4},{4,0},{1,5},{5,1},{2,6},{6,2},{3,7},{7,3},{8,12},{12,8},{9,1... | collective-permute-start | bytes 1572872 | tf_op jit(solution)/shard_map/ppermute | solution.py:18
  32.2 13.1 %collective-permute-start.5 = (bf16[128,2048]{1,0:T(8,128)(2,1)S(1)}, bf16[128,2048]{1,0:T(8,128)(2,1)S(1)}, u32[]{:S(2)}, u32[]{:S(2)}) collective-permute-start(bf16[128,2048]{1,0:T(8,128)(2,1)S(1)} %collective-permute-done.4.r1), channel_id=1, source_target_pairs={{0,4},{4,0},{1,5},{5,1},{2,6},{6,2},{3,7},{7,3},{8,12},{12,8},{9,1... | collective-permute-start | bytes 1572872 | tf_op jit(solution)/shard_map/ppermute | solution.py:18
  39.4 6.0 %collective-permute-start.7 = (bf16[128,2048]{1,0:T(8,128)(2,1)S(1)}, bf16[128,2048]{1,0:T(8,128)(2,1)S(1)}, u32[]{:S(2)}, u32[]{:S(2)}) collective-permute-start(bf16[128,2048]{1,0:T(8,128)(2,1)S(1)} %collective-permute-done.6.r2), channel_id=1, source_target_pairs={{0,4},{4,0},{1,5},{5,1},{2,6},{6,2},{3,7},{7,3},{8,12},{12,8},{9,1... | collective-permute-start | bytes 1572872 | tf_op jit(solution)/shard_map/ppermute | solution.py:18
  42.0 4.2 %collective-permute-start.9 = (bf16[128,2048]{1,0:T(8,128)(2,1)S(1)}, bf16[128,2048]{1,0:T(8,128)(2,1)S(1)}, u32[]{:S(2)}, u32[]{:S(2)}) collective-permute-start(bf16[128,2048]{1,0:T(8,128)(2,1)S(1)} %collective-permute-done.8.r3), channel_id=1, source_target_pairs={{0,4},{4,0},{1,5},{5,1},{2,6},{6,2},{3,7},{7,3},{8,12},{12,8},{9,1... | collective-permute-start | bytes 1572872 | tf_op jit(solution)/shard_map/ppermute | solution.py:18
  47.0 10.8 %collective-permute-start.12 = (bf16[112,1024]{1,0:T(8,128)(2,1)S(1)}, bf16[112,1024]{1,0:T(8,128)(2,1)}, u32[]{:S(2)}, u32[]{:S(2)}) collective-permute-start(bf16[112,1024]{1,0:T(8,128)(2,1)S(1)} %shard_map.117.own), channel_id=1, source_target_pairs={{0,1},{1,0},{2,3},{3,2},{4,5},{5,4},{6,7},{7,6},{8,9},{9,8},{10,11... | collective-permute-start | bytes 688136 | tf_op jit(solution)/shard_map/ppermute | solution.py:22
  47.3 13.2 %collective-permute-start.13 = (bf16[112,1024]{1,0:T(8,128)(2,1)S(1)}, bf16[112,1024]{1,0:T(8,128)(2,1)}, u32[]{:S(2)}, u32[]{:S(2)}) collective-permute-start(bf16[112,1024]{1,0:T(8,128)(2,1)S(1)} %shard_map.117.own), channel_id=1, source_target_pairs={{0,2},{1,3},{2,0},{3,1},{4,6},{5,7},{6,4},{7,5},{8,10},{9,11},{10,... | collective-permute-start | bytes 688136 | tf_op jit(solution)/shard_map/ppermute | solution.py:22
  50.0 12.4 %collective-permute-start.14 = (bf16[112,1024]{1,0:T(8,128)(2,1)S(1)}, bf16[112,1024]{1,0:T(8,128)(2,1)}, u32[]{:S(2)}, u32[]{:S(2)}) collective-permute-start(bf16[112,1024]{1,0:T(8,128)(2,1)S(1)} %shard_map.117.own), channel_id=1, source_target_pairs={{0,3},{1,2},{2,1},{3,0},{4,7},{5,6},{6,5},{7,4},{8,11},{9,10},{10,... | collective-permute-start | bytes 688136 | tf_op jit(solution)/shard_map/ppermute | solution.py:22
  56.5 10.0 %collective-permute-start.16 = (bf16[512,1024]{1,0:T(8,128)(2,1)S(1)}, bf16[512,1024]{1,0:T(8,128)(2,1)S(1)}, u32[]{:S(2)}, u32[]{:S(2)}) collective-permute-start(bf16[512,1024]{1,0:T(8,128)(2,1)S(1)} %shard_map.118), channel_id=1, source_target_pairs={{0,4},{4,0},{1,5},{5,1},{2,6},{6,2},{3,7},{7,3},{8,12},{12,8},{9,1... | collective-permute-start | bytes 3145736 | tf_op jit(solution)/shard_map/ppermute | solution.py:18
  64.4 4.4 %collective-permute-start.15 = (bf16[512,1024]{1,0:T(8,128)(2,1)S(1)}, bf16[512,1024]{1,0:T(8,128)(2,1)S(1)}, u32[]{:S(2)}, u32[]{:S(2)}) collective-permute-start(bf16[512,1024]{1,0:T(8,128)(2,1)S(1)} %shard_map.120), channel_id=1, source_target_pairs={{0,4},{4,0},{1,5},{5,1},{2,6},{6,2},{3,7},{7,3},{8,12},{12,8},{9,1... | collective-permute-start | bytes 3145736 | tf_op jit(solution)/shard_map/ppermute | solution.py:18
  71.9 8.4 %collective-permute-start.17 = (bf16[128,2048]{1,0:T(8,128)(2,1)S(1)}, bf16[128,2048]{1,0:T(8,128)(2,1)S(1)}, u32[]{:S(2)}, u32[]{:S(2)}) collective-permute-start(bf16[128,2048]{1,0:T(8,128)(2,1)S(1)} %get-tuple-element.35), channel_id=1, source_target_pairs={{0,8},{4,36},{8,0},{12,44},{16,24},{20,52},{24,16},{28,60},{32,40}... | collective-permute-start | bytes 1572872 | tf_op jit(solution)/shard_map/ppermute | solution.py:37
  72.0 13.6 %collective-permute-start.18 = (bf16[128,2048]{1,0:T(8,128)(2,1)S(1)}, bf16[128,2048]{1,0:T(8,128)(2,1)S(1)}, u32[]{:S(2)}, u32[]{:S(2)}) collective-permute-start(bf16[128,2048]{1,0:T(8,128)(2,1)S(1)} %get-tuple-element.36), channel_id=1, source_target_pairs={{0,16},{4,68},{8,24},{12,76},{16,0},{20,84},{24,8},{28,92},{32,48}... | collective-permute-start | bytes 1572872 | tf_op jit(solution)/shard_map/ppermute | solution.py:37
  73.1 15.2 %collective-permute-start.19 = (bf16[128,2048]{1,0:T(8,128)(2,1)S(1)}, bf16[128,2048]{1,0:T(8,128)(2,1)S(1)}, u32[]{:S(2)}, u32[]{:S(2)}) collective-permute-start(bf16[128,2048]{1,0:T(8,128)(2,1)S(1)} %get-tuple-element.37), channel_id=1, source_target_pairs={{0,24},{4,100},{8,16},{12,108},{16,8},{20,116},{24,0},{28,124},{32... | collective-permute-start | bytes 1572872 | tf_op jit(solution)/shard_map/ppermute | solution.py:37
  88.6 5.9 %collective-permute-start.21 = (bf16[32,2048]{1,0:T(8,128)(2,1)S(1)}, bf16[32,2048]{1,0:T(8,128)(2,1)S(1)}, u32[]{:S(2)}, u32[]{:S(2)}) collective-permute-start(bf16[32,2048]{1,0:T(8,128)(2,1)S(1)} %get-tuple-element.40), channel_id=1, source_target_pairs={{0,64},{4,20},{8,72},{12,28},{16,80},{20,4},{24,88},{28,12},{32,96... | collective-permute-start | bytes 393224 | tf_op jit(solution)/shard_map/ppermute | solution.py:37
  90.8 5.5 %collective-permute-start.22 = (bf16[32,2048]{1,0:T(8,128)(2,1)S(1)}, bf16[32,2048]{1,0:T(8,128)(2,1)S(1)}, u32[]{:S(2)}, u32[]{:S(2)}) collective-permute-start(bf16[32,2048]{1,0:T(8,128)(2,1)S(1)} %get-tuple-element.41), channel_id=1, source_target_pairs={{0,96},{4,28},{8,104},{12,20},{16,112},{20,12},{24,120},{28,4},{32... | collective-permute-start | bytes 393224 | tf_op jit(solution)/shard_map/ppermute | solution.py:37
  96.8 21.9 %collective-permute-start.23 = (bf16[32,2048]{1,0:T(8,128)(2,1)S(1)}, bf16[32,2048]{1,0:T(8,128)(2,1)S(1)}, u32[]{:S(2)}, u32[]{:S(2)}) collective-permute-start(bf16[32,2048]{1,0:T(8,128)(2,1)S(1)} %get-tuple-element.43.own), channel_id=1, source_target_pairs={{0,1},{1,0},{2,3},{3,2},{4,5},{5,4},{6,7},{7,6},{8,9},{9,8},{10,11... | collective-permute-start | bytes 393224 | tf_op jit(solution)/shard_map/ppermute | solution.py:22
  96.9 21.8 %collective-permute-start.24 = (bf16[32,2048]{1,0:T(8,128)(2,1)S(1)}, bf16[32,2048]{1,0:T(8,128)(2,1)S(1)}, u32[]{:S(2)}, u32[]{:S(2)}) collective-permute-start(bf16[32,2048]{1,0:T(8,128)(2,1)S(1)} %get-tuple-element.43.own), channel_id=1, source_target_pairs={{0,2},{1,3},{2,0},{3,1},{4,6},{5,7},{6,4},{7,5},{8,10},{9,11},{10,... | collective-permute-start | bytes 393224 | tf_op jit(solution)/shard_map/ppermute | solution.py:22
  98.4 20.3 %collective-permute-start.25 = (bf16[32,2048]{1,0:T(8,128)(2,1)S(1)}, bf16[32,2048]{1,0:T(8,128)(2,1)S(1)}, u32[]{:S(2)}, u32[]{:S(2)}) collective-permute-start(bf16[32,2048]{1,0:T(8,128)(2,1)S(1)} %get-tuple-element.43.own), channel_id=1, source_target_pairs={{0,3},{1,2},{2,1},{3,0},{4,7},{5,6},{6,5},{7,4},{8,11},{9,10},{10,... | collective-permute-start | bytes 393224 | tf_op jit(solution)/shard_map/ppermute | solution.py:22
  (28 other events, 227.7 us)

commit v6 on v5

--- a/solution.py
+++ b/solution.py
@@ -146,44 +146,31 @@
     send[...] = (keep[half:].astype(F32) + first[half:].astype(F32)).astype(BF16)
 
 
-def gate_rows(rows, products):
+def hidden_rows(rows, products):
     width = products.shape[1]
     part = products.shape[0] // 3
-    both = dot_t(products[: 2 * part], jnp.concatenate([block[:, :width] for block in rows], axis=0))
-    return both[:part], both[part:]
-
-
-def hidden_rows(rows, products):
-    gate, lift = gate_rows(rows, products)
-    return (gate * (1.0 / (1.0 + jnp.exp(-gate))) * lift).astype(BF16)
-
-
-def near_kernel(r0, r1, r2, r3, own, second, products, hidden):
+    stacked = [block[...] for block in rows]
+    stacked = jnp.concatenate(stacked, axis=0)
+    both = dot_t(products[: 2 * part], stacked[:, :width])
+    grad_hidden = dot_t(products[2 * part :], stacked[:, width:])
+    gate, lift = both[:part], both[part:]
+    sig = 1.0 / (1.0 + jnp.exp(-gate))
+    silu = gate * sig
+    grad_gate = grad_hidden * lift * sig * (1.0 + gate * (1.0 - sig))
+    grads = jnp.concatenate([grad_gate, grad_hidden * silu], axis=0).astype(BF16)
+    return (silu * lift).astype(BF16), dot(grads.T, products[: 2 * part])
+
+
+def near_kernel(r0, r1, r2, r3, own, second, products, hidden, partial):
     products[...] = (own[...] + second[...].astype(F32)).astype(BF16)
-    hidden[...] = hidden_rows((r0, r1, r2, r3), products)
-
-
-def far_kernel(r0, r1, r2, r3, products, near_hidden, hidden):
+    hidden[...], partial[...] = hidden_rows((r0, r1, r2, r3), products)
+
+
+def far_kernel(r0, r1, r2, r3, products, near_hidden, hidden, partial):
     half = near_hidden.shape[1]
     hidden[:, :half] = near_hidden[...]
-    hidden[:, half:] = hidden_rows((r0, r1, r2, r3), products)
-
-
-def grad_rows(rows, products):
-    width = products.shape[1]
-    part = products.shape[0] // 3
-    grad_hidden = dot_t(
-        products[2 * part :], jnp.concatenate([block[:, width:] for block in rows], axis=0)
-    )
-    gate, lift = gate_rows(rows, products)
-    sig = 1.0 / (1.0 + jnp.exp(-gate))
-    grad_gate = grad_hidden * lift * sig * (1.0 + gate * (1.0 - sig))
-    grads = jnp.concatenate([grad_gate, grad_hidden * (gate * sig)], axis=0).astype(BF16)
-    return dot(grads.T, products[: 2 * part])
-
-
-def grad_far_kernel(r0, r1, r2, r3, products, partial):
-    partial[...] = grad_rows((r0, r1, r2, r3), products).astype(BF16)
+    hidden[:, half:], terms = hidden_rows((r0, r1, r2, r3), products)
+    partial[...] = terms.astype(BF16)
 
 
 def place_blocks(total, outs):
@@ -201,27 +188,26 @@
     out[...] = dot(stack[...].T, w_down[...]).astype(BF16)
 
 
-def sum_near_kernel(
-    offsets, own, one, two, three, w_down, other, r0, r1, r2, r3, products, grad_other, *rest
-):
+def grad_near_kernel(partial, other, *outs):
+    place_blocks(partial[...] + other[...].astype(F32), outs)
+
+
+def down_near_kernel(offsets, own, one, two, three, w_down, other, *rest):
     stack = rest[-1]
     part, span = own.shape[0], other.shape[0]
-    width = w_down.shape[1]
     for k, block in enumerate((own, one, two, three)):
         stack[pl.ds(pl.multiple_of(offsets[k], 16), part), :] = block[:, :span]
-    total = grad_rows((r0, r1, r2, r3), products) + grad_other[...].astype(F32)
-    place_blocks(total, [out.at[:, width:] for out in rest[:-1]])
-    total = dot(stack[...].T, w_down[...]) + other[...].astype(F32)
-    place_blocks(total, [out.at[:, :width] for out in rest[:-1]])
-
-
-def add_kernel(own, one, two, three, *outs):
-    total = (
-        own[...].astype(F32) + one[...].astype(F32) + two[...].astype(F32) + three[...].astype(F32)
-    )
-    patches = own.shape[0] // 4
-    for i, out in enumerate(outs):
-        out[...] = total[i * patches : (i + 1) * patches].astype(out.dtype)
+    place_blocks(dot(stack[...].T, w_down[...]) + other[...].astype(F32), rest[:-1])
+
+
+def add_kernel(*refs):
+    terms, outs = refs[:8], refs[8:]
+    patches, width = terms[0].shape[0] // 4, terms[0].shape[1]
+    for i in range(2):
+        total = sum(term[...].astype(F32) for term in terms[4 * i : 4 * i + 4])
+        for k, out in enumerate(outs):
+            rows = total[k * patches : (k + 1) * patches]
+            out[:, i * width : (i + 1) * width] = rows.astype(out.dtype)
 
 
 def decode_kernel(own, one, two, three, rep, back, weight, owners, partial, outgoing):
@@ -322,28 +308,30 @@
     far = [swap_core(block) for block in near]
     own, second = halve(keep, first)
     flops = 4 * group * width * part
-    products, near_hidden = call(
+    products, near_hidden, near_partial = call(
         near_kernel,
         [
             shape((3 * part, width), BF16),
             shape((part, group), BF16),
+            shape((group, width), F32),
         ],
         [*near, own, second],
-        flops=flops,
-    )
-    (hidden,) = call(
+        flops=3 * flops,
+    )
+    hidden, far_partial = call(
         far_kernel,
-        [shape((part, 2 * group), BF16)],
+        [shape((part, 2 * group), BF16), shape((group, width), BF16)],
         [*far, products, near_hidden],
-        flops=flops,
+        flops=3 * flops,
     )
     hiddens = over(swap_x, hidden)
-    (far_partial,) = call(
-        grad_far_kernel,
-        [shape((group, width), BF16)],
-        [*far, products],
-        flops=flops,
-    )
+    grad_terms = call(
+        grad_near_kernel,
+        [shape((4 * patches, width), BF16)] * 4,
+        [near_partial, swap_core(far_partial)],
+        flops=near_partial.size,
+    )
+    grad_first = over(swap_first, *grad_terms)
     patch_rep, back = call(
         encode_kernel,
         [shape((patches, latent), BF16), shape((patches, width), F32)],
@@ -353,30 +341,23 @@
     (far_rows,) = call(
         down_far_kernel,
         [shape((group, latent), BF16)],
-        [*hiddens, after(w_down, (far_partial, back))],
+        [*hiddens, after(w_down, (*grad_terms, back))],
         [offsets],
         flops=2 * group * latent * hid,
         scratch=[pltpu.VMEM((hid, group), BF16)],
     )
     terms = call(
-        sum_near_kernel,
-        [shape((4 * patches, latent + width), BF16)] * 4,
-        [
-            *hiddens,
-            w_down,
-            swap_core(far_rows),
-            *near,
-            products,
-            swap_core(far_partial),
-        ],
+        down_near_kernel,
+        [shape((4 * patches, latent), BF16)] * 4,
+        [*hiddens, w_down, swap_core(far_rows)],
         [offsets],
-        flops=2 * group * latent * hid + flops,
+        flops=2 * group * latent * hid,
         scratch=[pltpu.VMEM((hid, group), BF16)],
     )
     own, *sends = call(
         add_kernel,
         [shape((patches, latent + width), F32)] + [shape((patches, latent + width), BF16)] * 3,
-        over(swap_first, *terms),
+        over(swap_first, *terms) + grad_first,
         flops=32 * patches * width,
     )
     partial, outgoing = call(

time: 121 us -> 117 us (0.967)
  waiting for transfers between devices: 37.1 us -> 32.5 us
  starting transfers between devices: 41.1 us -> 44.4 us
  blocking collectives: 17.2 us -> 14.9 us
  Pallas kernels: 19.7 us -> 21.2 us
  local copies, waits for them, and re-layouts: 3.6 us -> 2.39 us
    ppermute x12 -> x15, starting transfers between devices: 16.8 us -> 21.4 us  [swap_first(): return lax.ppermute(value, SEQ, pairs)]
    ppermute x12 -> x15, waiting for transfers between devices: 27.9 us -> 24 us  [swap_first(): return lax.ppermute(value, SEQ, pairs)]
    ppermute x6, waiting for transfers between devices: 3.16 us -> 0.24 us  [swap_core(): return lax.ppermute(value, 'c', [(0, 1), (1, 0)])]
    all_to_all x1, blocking collectives: 17.2 us -> 14.9 us  [on_device(): lax.all_to_all(outgoing, SEQ, split_axis=0, concat_axis=0, tiled=True)]
    ppermute x6, waiting for transfers between devices: 4.63 us -> 6.93 us  [swap_x(): return lax.ppermute(value, 'x', [(i, i ^ k) for i in range(4)])]
    pallas_call x13, Pallas kernels: 19.7 us -> 21.2 us  [call(): pl.pallas_call(body, out_shape=outs, in_specs=specs, out_specs=[pl.BlockS...]
    ppermute x6, starting transfers between devices: 12.6 us -> 11.2 us  [swap_core(): return lax.ppermute(value, 'c', [(0, 1), (1, 0)])]
    unnamed x52 -> x20, local copies, waits for them, and re-layouts: 2.85 us -> 1.63 us
  transfers between devices with their start and end apart: 26 -> 29, of which waited for: 15 -> 15; matrix products, arithmetic and copies ran while one was open for 0% -> 0% of each run, Pallas kernels for 5% -> 6%
where the time goes in v6:
time: 117 us
  starting transfers between devices  44.4 us (38%)
  waiting for transfers between devices  32.5 us (28%)
  Pallas kernels  21.2 us (18%)
  blocking collectives  14.9 us (13%)
  local copies, waits for them, and re-layouts  2.39 us (2%)
    ppermute x15, waiting for transfers between devices, swap_first(): return lax.ppermute(value, SEQ, pairs)  24 us
    ppermute x15, starting transfers between devices, swap_first(): return lax.ppermute(value, SEQ, pairs)  21.4 us
    pallas_call x13, Pallas kernels, call(): pl.pallas_call(body, out_shape=outs, in_specs=specs, out_specs=[pl.BlockS...  21.2 us
    all_to_all x1, blocking collectives, on_device(): lax.all_to_all(outgoing, SEQ, split_axis=0, concat_axis=0, tiled=True)  14.9 us
    ppermute x6, starting transfers between devices, swap_core(): return lax.ppermute(value, 'c', [(0, 1), (1, 0)])  11.2 us
    ppermute x6, starting transfers between devices, swap_x(): return lax.ppermute(value, 'x', [(i, i ^ k) for i in range(4)])  7.79 us
    ppermute x6, waiting for transfers between devices, swap_x(): return lax.ppermute(value, 'x', [(i, i ^ k) for i in range(4)])  6.93 us
    ppermute x2, starting transfers between devices, swap_near(): lax.ppermute(value, ('c', 'x'), [(c * 4 + x, c * 4 + (x ^ steps[c])) for...  3.96 us
  transfers between devices with their start and end apart: 29, of which 15 were waited for; matrix products, arithmetic and copies ran while one was open for 0% of the time, Pallas kernels for 6%

profile of v6, /device:TPU:1, one launch (start us, length us, event | category | flops | bytes accessed | tf_op | source)
XLA Modules:
  0.0 116.9 jit_solution(16827361569331890000)
XLA Ops:
  1.2 7.7 %shard_map.112 = (bf16[672,1024]{1,0:T(8,128)(2,1)}, bf16[672,1024]{1,0:T(8,128)(2,1)}) custom-call(s32[4]{0:T(128)} %add_multiply_fusion.1.offsets, bf16[1024,1024]{1,0:T(8,128)(2,1)} %w_enc.1, bf16[448,1024]{1,0:T(8,128)(2,1)} %bitcast.10, bf16[448,1024]{1,0:T(8,128)(2,1)} %bitcast.11, bf16[448,1024]{1,0:T(8,128)(2,1)} %w_down.2, bf16[1024,1024]{1,0:T(8,128)(2,1)} %weight.1), custom_call_target="tpu_custom_call" | custom-call | flops 2818572288 | bytes 9699328 | tf_op jit(solution)/shard_map/pallas_call | solution.py:56
  8.9 3.4 %collective-permute-start.10 = (bf16[672,1024]{1,0:T(8,128)(2,1)}, bf16[672,1024]{1,0:T(8,128)(2,1)S(1)}, u32[]{:S(2)}, u32[]{:S(2)}) collective-permute-start(bf16[672,1024]{1,0:T(8,128)(2,1)} %get-tuple-element.32), channel_id=1, source_target_pairs={{0,1},{1,0},{2,3},{3,2},{4,7},{5,6},{6,5},{7,4},{8,9},{9,8},{10,11... | collective-permute-start | bytes 4128776 | tf_op jit(solution)/shard_map/ppermute | solution.py:27
  14.0 2.6 %collective-permute-start.1 = (bf16[32,2048]{1,0:T(8,128)(2,1)S(1)}, bf16[32,2048]{1,0:T(8,128)(2,1)S(1)}, u32[]{:S(2)}, u32[]{:S(2)}) collective-permute-start(bf16[32,2048]{1,0:T(8,128)(2,1)S(1)} %shard_map.113.own.pooled), channel_id=1, source_target_pairs={{0,16},{4,68},{8,24},{12,76},{16,0},{20,84},{24,8},{28,92},{32,48}... | collective-permute-start | bytes 393224 | tf_op jit(solution)/shard_map/ppermute | solution.py:37
  16.8 3.9 %collective-permute-done.1.two = bf16[32,2048]{1,0:T(8,128)(2,1)S(1)} collective-permute-done((bf16[32,2048]{1,0:T(8,128)(2,1)S(1)}, bf16[32,2048]{1,0:T(8,128)(2,1)S(1)}, u32[]{:S(2)}, u32[]{:S(2)}) %collective-permute-start.1) | collective-permute-done | bytes 131104 | tf_op jit(solution)/shard_map/ppermute | solution.py:37
  23.5 3.3 %collective-permute-start.6 = (bf16[128,2048]{1,0:T(8,128)(2,1)S(1)}, bf16[128,2048]{1,0:T(8,128)(2,1)S(1)}, u32[]{:S(2)}, u32[]{:S(2)}) collective-permute-start(bf16[128,2048]{1,0:T(8,128)(2,1)S(1)} %shard_map.114.r0), channel_id=1, source_target_pairs={{0,64},{4,20},{8,72},{12,28},{16,80},{20,4},{24,88},{28,12},{32,96... | collective-permute-start | bytes 1572872 | tf_op jit(solution)/shard_map/ppermute | solution.py:37
  29.1 3.1 %collective-permute-start.3 = (bf16[128,2048]{1,0:T(8,128)(2,1)S(1)}, bf16[128,2048]{1,0:T(8,128)(2,1)S(1)}, u32[]{:S(2)}, u32[]{:S(2)}) collective-permute-start(bf16[128,2048]{1,0:T(8,128)(2,1)S(1)} %shard_map.114.r0), channel_id=1, source_target_pairs={{0,4},{4,0},{1,5},{5,1},{2,6},{6,2},{3,7},{7,3},{8,12},{12,8},{9,1... | collective-permute-start | bytes 1572872 | tf_op jit(solution)/shard_map/ppermute | solution.py:18
  33.4 6.0 %collective-permute-done.6.r2 = bf16[128,2048]{1,0:T(8,128)(2,1)S(1)} collective-permute-done((bf16[128,2048]{1,0:T(8,128)(2,1)S(1)}, bf16[128,2048]{1,0:T(8,128)(2,1)S(1)}, u32[]{:S(2)}, u32[]{:S(2)}) %collective-permute-start.6) | collective-permute-done | bytes 524320 | tf_op jit(solution)/shard_map/ppermute | solution.py:37
  39.3 2.2 %collective-permute-start.7 = (bf16[128,2048]{1,0:T(8,128)(2,1)S(1)}, bf16[128,2048]{1,0:T(8,128)(2,1)S(1)}, u32[]{:S(2)}, u32[]{:S(2)}) collective-permute-start(bf16[128,2048]{1,0:T(8,128)(2,1)S(1)} %collective-permute-done.6.r2), channel_id=1, source_target_pairs={{0,4},{4,0},{1,5},{5,1},{2,6},{6,2},{3,7},{7,3},{8,12},{12,8},{9,1... | collective-permute-start | bytes 1572872 | tf_op jit(solution)/shard_map/ppermute | solution.py:18
  42.0 2.7 %collective-permute-start.9 = (bf16[128,2048]{1,0:T(8,128)(2,1)S(1)}, bf16[128,2048]{1,0:T(8,128)(2,1)S(1)}, u32[]{:S(2)}, u32[]{:S(2)}) collective-permute-start(bf16[128,2048]{1,0:T(8,128)(2,1)S(1)} %collective-permute-done.8.r3), channel_id=1, source_target_pairs={{0,4},{4,0},{1,5},{5,1},{2,6},{6,2},{3,7},{7,3},{8,12},{12,8},{9,1... | collective-permute-start | bytes 1572872 | tf_op jit(solution)/shard_map/ppermute | solution.py:18
  46.2 2.2 %shard_map.117 = (bf16[112,1024]{1,0:T(8,128)(2,1)S(1)}, bf16[512,1024]{1,0:T(8,128)(2,1)}) custom-call(bf16[128,2048]{1,0:T(8,128)(2,1)S(1)} %collective-permute-done.3.r0, bf16[128,2048]{1,0:T(8,128)(2,1)S(1)} %collective-permute-done.5.r1, bf16[128,2048]{1,0:T(8,128)(2,1)S(1)} %collective-permute-done.7.r2, ...), custom_call_target="tpu_custom_call" | custom-call | flops 704643072 | bytes 4177920 | tf_op jit(solution)/shard_map/pallas_call | solution.py:56
  49.1 2.7 %collective-permute-start.13 = (bf16[112,1024]{1,0:T(8,128)(2,1)S(1)}, bf16[112,1024]{1,0:T(8,128)(2,1)}, u32[]{:S(2)}, u32[]{:S(2)}) collective-permute-start(bf16[112,1024]{1,0:T(8,128)(2,1)S(1)} %get-tuple-element.39.own), channel_id=1, source_target_pairs={{0,2},{1,3},{2,0},{3,1},{4,6},{5,7},{6,4},{7,5},{8,10},{9,11},{10,... | collective-permute-start | bytes 688136 | tf_op jit(solution)/shard_map/ppermute | solution.py:22
  57.5 4.9 %collective-permute-done.13.two = bf16[112,1024]{1,0:T(8,128)(2,1)} collective-permute-done((bf16[112,1024]{1,0:T(8,128)(2,1)S(1)}, bf16[112,1024]{1,0:T(8,128)(2,1)}, u32[]{:S(2)}, u32[]{:S(2)}) %collective-permute-start.13) | collective-permute-done | bytes 229408 | tf_op jit(solution)/shard_map/ppermute | solution.py:22
  62.5 2.0 %collective-permute-done.14.three = bf16[112,1024]{1,0:T(8,128)(2,1)} collective-permute-done((bf16[112,1024]{1,0:T(8,128)(2,1)S(1)}, bf16[112,1024]{1,0:T(8,128)(2,1)}, u32[]{:S(2)}, u32[]{:S(2)}) %collective-permute-start.14) | collective-permute-done | bytes 229408 | tf_op jit(solution)/shard_map/ppermute | solution.py:22
  64.5 1.9 %shard_map.120 = bf16[512,1024]{1,0:T(8,128)(2,1)S(1)} custom-call(s32[4]{0:T(128)S(1)} %add_multiply_fusion.offsets, bf16[112,1024]{1,0:T(8,128)(2,1)S(1)} %get-tuple-element.39.own, bf16[112,1024]{1,0:T(8,128)(2,1)} %collective-permute-done.12.one, bf16[112,1024]{1,0:T(8,128)(2,1)} %collective-permute-done.13.two, ...), custom_call_target="tpu_custom_call" | custom-call | flops 469762048 | bytes 2883584 | tf_op jit(solution)/shard_map/pallas_call | solution.py:56
  69.2 2.7 %collective-permute-start.22 = (bf16[128,1024]{1,0:T(8,128)(2,1)S(1)}, bf16[128,1024]{1,0:T(8,128)(2,1)S(1)}, u32[]{:S(2)}, u32[]{:S(2)}) collective-permute-start(bf16[128,1024]{1,0:T(8,128)(2,1)S(1)} %get-tuple-element.45), channel_id=1, source_target_pairs={{0,24},{4,100},{8,16},{12,108},{16,8},{20,116},{24,0},{28,124},{32... | collective-permute-start | bytes 786440 | tf_op jit(solution)/shard_map/ppermute | solution.py:37
  71.9 1.9 %shard_map.121 = (bf16[128,1024]{1,0:T(8,128)(2,1)S(1)}, bf16[128,1024]{1,0:T(8,128)(2,1)S(1)}, bf16[128,1024]{1,0:T(8,128)(2,1)S(1)}, bf16[128,1024]{1,0:T(8,128)(2,1)S(1)}) custom-call(s32[4]{0:T(128)S(1)} %add_multiply_fusion.offsets, bf16[112,1024]{1,0:T(8,128)(2,1)S(1)} %get-tuple-element.39.own, bf16[112,1024]{1,0:T(8,128)(2,1)} %collective-permute-done.12.one, ...), custom_call_target="tpu_custom_call" | custom-call | flops 469762048 | bytes 3932160 | tf_op jit(solution)/shard_map/pallas_call | solution.py:56
  75.2 2.7 %collective-permute-start.19 = (bf16[128,1024]{1,0:T(8,128)(2,1)S(1)}, bf16[128,1024]{1,0:T(8,128)(2,1)S(1)}, u32[]{:S(2)}, u32[]{:S(2)}) collective-permute-start(bf16[128,1024]{1,0:T(8,128)(2,1)S(1)} %get-tuple-element.51), channel_id=1, source_target_pairs={{0,24},{4,100},{8,16},{12,108},{16,8},{20,116},{24,0},{28,124},{32... | collective-permute-start | bytes 786440 | tf_op jit(solution)/shard_map/ppermute | solution.py:37
  79.5 2.6 %collective-permute-done.18.refs_2_ = bf16[128,1024]{1,0:T(8,128)(2,1)S(1)} collective-permute-done((bf16[128,1024]{1,0:T(8,128)(2,1)S(1)}, bf16[128,1024]{1,0:T(8,128)(2,1)S(1)}, u32[]{:S(2)}, u32[]{:S(2)}) %collective-permute-start.18) | collective-permute-done | bytes 262176 | tf_op jit(solution)/shard_map/ppermute | solution.py:37
  82.1 2.6 %collective-permute-done.19.refs_3_ = bf16[128,1024]{1,0:T(8,128)(2,1)S(1)} collective-permute-done((bf16[128,1024]{1,0:T(8,128)(2,1)S(1)}, bf16[128,1024]{1,0:T(8,128)(2,1)S(1)}, u32[]{:S(2)}, u32[]{:S(2)}) %collective-permute-start.19) | collective-permute-done | bytes 262176 | tf_op jit(solution)/shard_map/ppermute | solution.py:37
  86.1 3.6 %collective-permute-start.24 = (bf16[32,2048]{1,0:T(8,128)(2,1)S(1)}, bf16[32,2048]{1,0:T(8,128)(2,1)S(1)}, u32[]{:S(2)}, u32[]{:S(2)}) collective-permute-start(bf16[32,2048]{1,0:T(8,128)(2,1)S(1)} %get-tuple-element.54), channel_id=1, source_target_pairs={{0,64},{4,20},{8,72},{12,28},{16,80},{20,4},{24,88},{28,12},{32,96... | collective-permute-start | bytes 393224 | tf_op jit(solution)/shard_map/ppermute | solution.py:37
  89.7 3.8 %collective-permute-done.24.two = bf16[32,2048]{1,0:T(8,128)(2,1)S(1)} collective-permute-done((bf16[32,2048]{1,0:T(8,128)(2,1)S(1)}, bf16[32,2048]{1,0:T(8,128)(2,1)S(1)}, u32[]{:S(2)}, u32[]{:S(2)}) %collective-permute-start.24) | collective-permute-done | bytes 131104 | tf_op jit(solution)/shard_map/ppermute | solution.py:37
  93.5 1.7 %collective-permute-done.25.three = bf16[32,2048]{1,0:T(8,128)(2,1)S(1)} collective-permute-done((bf16[32,2048]{1,0:T(8,128)(2,1)S(1)}, bf16[32,2048]{1,0:T(8,128)(2,1)S(1)}, u32[]{:S(2)}, u32[]{:S(2)}) %collective-permute-start.25) | collective-permute-done | bytes 131104 | tf_op jit(solution)/shard_map/ppermute | solution.py:37
  97.1 2.5 %collective-permute-start.28 = (bf16[32,2048]{1,0:T(8,128)(2,1)S(1)}, bf16[32,2048]{1,0:T(8,128)(2,1)S(1)}, u32[]{:S(2)}, u32[]{:S(2)}) collective-permute-start(bf16[32,2048]{1,0:T(8,128)(2,1)S(1)} %get-tuple-element.57.own), channel_id=1, source_target_pairs={{0,3},{1,2},{2,1},{3,0},{4,7},{5,6},{6,5},{7,4},{8,11},{9,10},{10,... | collective-permute-start | bytes 393224 | tf_op jit(solution)/shard_map/ppermute | solution.py:22
  99.7 14.9 %all_to_all.12 = bf16[32,2,1024]{2,1,0:T(2,128)(2,1)S(1)} all-to-all(bf16[32,2,1024]{2,1,0:T(2,128)(2,1)S(1)} %all_to_all.8), channel_id=1, replica_groups=mesh['y'=4,'z'=4,'c'=2,'x'=4] {'y','z','c'}, dimensions={0} | all-to-all | bytes 262144 | tf_op jit(solution)/shard_map/all_to_all | solution.py:369
  (72 shorter events, 28.5 us)
Async XLA Ops:
  8.9 19.3 %collective-permute-start.10 = (bf16[672,1024]{1,0:T(8,128)(2,1)}, bf16[672,1024]{1,0:T(8,128)(2,1)S(1)}, u32[]{:S(2)}, u32[]{:S(2)}) collective-permute-start(bf16[672,1024]{1,0:T(8,128)(2,1)} %get-tuple-element.32), channel_id=1, source_target_pairs={{0,1},{1,0},{2,3},{3,2},{4,7},{5,6},{6,5},{7,4},{8,9},{9,8},{10,11... | collective-permute-start | bytes 4128776 | tf_op jit(solution)/shard_map/ppermute | solution.py:27
  14.0 6.7 %collective-permute-start.1 = (bf16[32,2048]{1,0:T(8,128)(2,1)S(1)}, bf16[32,2048]{1,0:T(8,128)(2,1)S(1)}, u32[]{:S(2)}, u32[]{:S(2)}) collective-permute-start(bf16[32,2048]{1,0:T(8,128)(2,1)S(1)} %shard_map.113.own.pooled), channel_id=1, source_target_pairs={{0,16},{4,68},{8,24},{12,76},{16,0},{20,84},{24,8},{28,92},{32,48}... | collective-permute-start | bytes 393224 | tf_op jit(solution)/shard_map/ppermute | solution.py:37
  21.9 10.3 %collective-permute-start.4 = (bf16[128,2048]{1,0:T(8,128)(2,1)S(1)}, bf16[128,2048]{1,0:T(8,128)(2,1)S(1)}, u32[]{:S(2)}, u32[]{:S(2)}) collective-permute-start(bf16[128,2048]{1,0:T(8,128)(2,1)S(1)} %shard_map.114.r0), channel_id=1, source_target_pairs={{0,32},{4,12},{8,40},{12,4},{16,48},{20,28},{24,56},{28,20},{32,0}... | collective-permute-start | bytes 1572872 | tf_op jit(solution)/shard_map/ppermute | solution.py:37
  23.5 15.8 %collective-permute-start.6 = (bf16[128,2048]{1,0:T(8,128)(2,1)S(1)}, bf16[128,2048]{1,0:T(8,128)(2,1)S(1)}, u32[]{:S(2)}, u32[]{:S(2)}) collective-permute-start(bf16[128,2048]{1,0:T(8,128)(2,1)S(1)} %shard_map.114.r0), channel_id=1, source_target_pairs={{0,64},{4,20},{8,72},{12,28},{16,80},{20,4},{24,88},{28,12},{32,96... | collective-permute-start | bytes 1572872 | tf_op jit(solution)/shard_map/ppermute | solution.py:37
  26.8 15.2 %collective-permute-start.8 = (bf16[128,2048]{1,0:T(8,128)(2,1)S(1)}, bf16[128,2048]{1,0:T(8,128)(2,1)S(1)}, u32[]{:S(2)}, u32[]{:S(2)}) collective-permute-start(bf16[128,2048]{1,0:T(8,128)(2,1)S(1)} %shard_map.114.r0), channel_id=1, source_target_pairs={{0,96},{4,28},{8,104},{12,20},{16,112},{20,12},{24,120},{28,4},{32... | collective-permute-start | bytes 1572872 | tf_op jit(solution)/shard_map/ppermute | solution.py:37
  28.5 16.2 %collective-permute-start.11 = (bf16[336,1024]{1,0:T(8,128)(2,1)S(1)}, bf16[336,1024]{1,0:T(8,128)(2,1)S(1)}, u32[]{:S(2)}, u32[]{:S(2)}) collective-permute-start(bf16[336,1024]{1,0:T(8,128)(2,1)S(1)} %get-tuple-element.36), channel_id=1, source_target_pairs={{0,3},{1,2},{2,1},{3,0},{4,5},{5,4},{6,7},{7,6},{8,11},{9,10},{10,... | collective-permute-start | bytes 2064392 | tf_op jit(solution)/shard_map/ppermute | solution.py:27
  29.1 16.9 %collective-permute-start.3 = (bf16[128,2048]{1,0:T(8,128)(2,1)S(1)}, bf16[128,2048]{1,0:T(8,128)(2,1)S(1)}, u32[]{:S(2)}, u32[]{:S(2)}) collective-permute-start(bf16[128,2048]{1,0:T(8,128)(2,1)S(1)} %shard_map.114.r0), channel_id=1, source_target_pairs={{0,4},{4,0},{1,5},{5,1},{2,6},{6,2},{3,7},{7,3},{8,12},{12,8},{9,1... | collective-permute-start | bytes 1572872 | tf_op jit(solution)/shard_map/ppermute | solution.py:18
  32.1 13.8 %collective-permute-start.5 = (bf16[128,2048]{1,0:T(8,128)(2,1)S(1)}, bf16[128,2048]{1,0:T(8,128)(2,1)S(1)}, u32[]{:S(2)}, u32[]{:S(2)}) collective-permute-start(bf16[128,2048]{1,0:T(8,128)(2,1)S(1)} %collective-permute-done.4.r1), channel_id=1, source_target_pairs={{0,4},{4,0},{1,5},{5,1},{2,6},{6,2},{3,7},{7,3},{8,12},{12,8},{9,1... | collective-permute-start | bytes 1572872 | tf_op jit(solution)/shard_map/ppermute | solution.py:18
  39.3 6.6 %collective-permute-start.7 = (bf16[128,2048]{1,0:T(8,128)(2,1)S(1)}, bf16[128,2048]{1,0:T(8,128)(2,1)S(1)}, u32[]{:S(2)}, u32[]{:S(2)}) collective-permute-start(bf16[128,2048]{1,0:T(8,128)(2,1)S(1)} %collective-permute-done.6.r2), channel_id=1, source_target_pairs={{0,4},{4,0},{1,5},{5,1},{2,6},{6,2},{3,7},{7,3},{8,12},{12,8},{9,1... | collective-permute-start | bytes 1572872 | tf_op jit(solution)/shard_map/ppermute | solution.py:18
  48.4 7.6 %collective-permute-start.15 = (bf16[512,1024]{1,0:T(8,128)(2,1)}, bf16[512,1024]{1,0:T(8,128)(2,1)}, u32[]{:S(2)}, u32[]{:S(2)}) collective-permute-start(bf16[512,1024]{1,0:T(8,128)(2,1)} %get-tuple-element.41), channel_id=1, source_target_pairs={{0,4},{4,0},{1,5},{5,1},{2,6},{6,2},{3,7},{7,3},{8,12},{12,8},{9,1... | collective-permute-start | bytes 3145736 | tf_op jit(solution)/shard_map/ppermute | solution.py:18
  48.8 8.7 %collective-permute-start.12 = (bf16[112,1024]{1,0:T(8,128)(2,1)S(1)}, bf16[112,1024]{1,0:T(8,128)(2,1)}, u32[]{:S(2)}, u32[]{:S(2)}) collective-permute-start(bf16[112,1024]{1,0:T(8,128)(2,1)S(1)} %get-tuple-element.39.own), channel_id=1, source_target_pairs={{0,1},{1,0},{2,3},{3,2},{4,5},{5,4},{6,7},{7,6},{8,9},{9,8},{10,11... | collective-permute-start | bytes 688136 | tf_op jit(solution)/shard_map/ppermute | solution.py:22
  49.1 13.4 %collective-permute-start.13 = (bf16[112,1024]{1,0:T(8,128)(2,1)S(1)}, bf16[112,1024]{1,0:T(8,128)(2,1)}, u32[]{:S(2)}, u32[]{:S(2)}) collective-permute-start(bf16[112,1024]{1,0:T(8,128)(2,1)S(1)} %get-tuple-element.39.own), channel_id=1, source_target_pairs={{0,2},{1,3},{2,0},{3,1},{4,6},{5,7},{6,4},{7,5},{8,10},{9,11},{10,... | collective-permute-start | bytes 688136 | tf_op jit(solution)/shard_map/ppermute | solution.py:22
  51.8 12.7 %collective-permute-start.14 = (bf16[112,1024]{1,0:T(8,128)(2,1)S(1)}, bf16[112,1024]{1,0:T(8,128)(2,1)}, u32[]{:S(2)}, u32[]{:S(2)}) collective-permute-start(bf16[112,1024]{1,0:T(8,128)(2,1)S(1)} %get-tuple-element.39.own), channel_id=1, source_target_pairs={{0,3},{1,2},{2,1},{3,0},{4,7},{5,6},{6,5},{7,4},{8,11},{9,10},{10,... | collective-permute-start | bytes 688136 | tf_op jit(solution)/shard_map/ppermute | solution.py:22
  66.4 5.5 %collective-permute-start.16 = (bf16[512,1024]{1,0:T(8,128)(2,1)S(1)}, bf16[512,1024]{1,0:T(8,128)(2,1)S(1)}, u32[]{:S(2)}, u32[]{:S(2)}) collective-permute-start(bf16[512,1024]{1,0:T(8,128)(2,1)S(1)} %shard_map.120), channel_id=1, source_target_pairs={{0,4},{4,0},{1,5},{5,1},{2,6},{6,2},{3,7},{7,3},{8,12},{12,8},{9,1... | collective-permute-start | bytes 3145736 | tf_op jit(solution)/shard_map/ppermute | solution.py:18
  68.1 7.1 %collective-permute-start.20 = (bf16[128,1024]{1,0:T(8,128)(2,1)S(1)}, bf16[128,1024]{1,0:T(8,128)(2,1)S(1)}, u32[]{:S(2)}, u32[]{:S(2)}) collective-permute-start(bf16[128,1024]{1,0:T(8,128)(2,1)S(1)} %get-tuple-element.43), channel_id=1, source_target_pairs={{0,8},{4,36},{8,0},{12,44},{16,24},{20,52},{24,16},{28,60},{32,40}... | collective-permute-start | bytes 786440 | tf_op jit(solution)/shard_map/ppermute | solution.py:37
  68.1 9.8 %collective-permute-start.21 = (bf16[128,1024]{1,0:T(8,128)(2,1)S(1)}, bf16[128,1024]{1,0:T(8,128)(2,1)S(1)}, u32[]{:S(2)}, u32[]{:S(2)}) collective-permute-start(bf16[128,1024]{1,0:T(8,128)(2,1)S(1)} %get-tuple-element.44), channel_id=1, source_target_pairs={{0,16},{4,68},{8,24},{12,76},{16,0},{20,84},{24,8},{28,92},{32,48}... | collective-permute-start | bytes 786440 | tf_op jit(solution)/shard_map/ppermute | solution.py:37
  69.2 9.6 %collective-permute-start.22 = (bf16[128,1024]{1,0:T(8,128)(2,1)S(1)}, bf16[128,1024]{1,0:T(8,128)(2,1)S(1)}, u32[]{:S(2)}, u32[]{:S(2)}) collective-permute-start(bf16[128,1024]{1,0:T(8,128)(2,1)S(1)} %get-tuple-element.45), channel_id=1, source_target_pairs={{0,24},{4,100},{8,16},{12,108},{16,8},{20,116},{24,0},{28,124},{32... | collective-permute-start | bytes 786440 | tf_op jit(solution)/shard_map/ppermute | solution.py:37
  73.9 5.6 %collective-permute-start.17 = (bf16[128,1024]{1,0:T(8,128)(2,1)S(1)}, bf16[128,1024]{1,0:T(8,128)(2,1)S(1)}, u32[]{:S(2)}, u32[]{:S(2)}) collective-permute-start(bf16[128,1024]{1,0:T(8,128)(2,1)S(1)} %get-tuple-element.49), channel_id=1, source_target_pairs={{0,8},{4,36},{8,0},{12,44},{16,24},{20,52},{24,16},{28,60},{32,40}... | collective-permute-start | bytes 786440 | tf_op jit(solution)/shard_map/ppermute | solution.py:37
  74.0 8.1 %collective-permute-start.18 = (bf16[128,1024]{1,0:T(8,128)(2,1)S(1)}, bf16[128,1024]{1,0:T(8,128)(2,1)S(1)}, u32[]{:S(2)}, u32[]{:S(2)}) collective-permute-start(bf16[128,1024]{1,0:T(8,128)(2,1)S(1)} %get-tuple-element.50), channel_id=1, source_target_pairs={{0,16},{4,68},{8,24},{12,76},{16,0},{20,84},{24,8},{28,92},{32,48}... | collective-permute-start | bytes 786440 | tf_op jit(solution)/shard_map/ppermute | solution.py:37
  75.2 9.5 %collective-permute-start.19 = (bf16[128,1024]{1,0:T(8,128)(2,1)S(1)}, bf16[128,1024]{1,0:T(8,128)(2,1)S(1)}, u32[]{:S(2)}, u32[]{:S(2)}) collective-permute-start(bf16[128,1024]{1,0:T(8,128)(2,1)S(1)} %get-tuple-element.51), channel_id=1, source_target_pairs={{0,24},{4,100},{8,16},{12,108},{16,8},{20,116},{24,0},{28,124},{32... | collective-permute-start | bytes 786440 | tf_op jit(solution)/shard_map/ppermute | solution.py:37
  86.1 7.4 %collective-permute-start.24 = (bf16[32,2048]{1,0:T(8,128)(2,1)S(1)}, bf16[32,2048]{1,0:T(8,128)(2,1)S(1)}, u32[]{:S(2)}, u32[]{:S(2)}) collective-permute-start(bf16[32,2048]{1,0:T(8,128)(2,1)S(1)} %get-tuple-element.54), channel_id=1, source_target_pairs={{0,64},{4,20},{8,72},{12,28},{16,80},{20,4},{24,88},{28,12},{32,96... | collective-permute-start | bytes 393224 | tf_op jit(solution)/shard_map/ppermute | solution.py:37
  95.7 19.6 %collective-permute-start.26 = (bf16[32,2048]{1,0:T(8,128)(2,1)S(1)}, bf16[32,2048]{1,0:T(8,128)(2,1)S(1)}, u32[]{:S(2)}, u32[]{:S(2)}) collective-permute-start(bf16[32,2048]{1,0:T(8,128)(2,1)S(1)} %get-tuple-element.57.own), channel_id=1, source_target_pairs={{0,1},{1,0},{2,3},{3,2},{4,5},{5,4},{6,7},{7,6},{8,9},{9,8},{10,11... | collective-permute-start | bytes 393224 | tf_op jit(solution)/shard_map/ppermute | solution.py:22
  95.8 19.5 %collective-permute-start.27 = (bf16[32,2048]{1,0:T(8,128)(2,1)S(1)}, bf16[32,2048]{1,0:T(8,128)(2,1)S(1)}, u32[]{:S(2)}, u32[]{:S(2)}) collective-permute-start(bf16[32,2048]{1,0:T(8,128)(2,1)S(1)} %get-tuple-element.57.own), channel_id=1, source_target_pairs={{0,2},{1,3},{2,0},{3,1},{4,6},{5,7},{6,4},{7,5},{8,10},{9,11},{10,... | collective-permute-start | bytes 393224 | tf_op jit(solution)/shard_map/ppermute | solution.py:22
  97.1 18.1 %collective-permute-start.28 = (bf16[32,2048]{1,0:T(8,128)(2,1)S(1)}, bf16[32,2048]{1,0:T(8,128)(2,1)S(1)}, u32[]{:S(2)}, u32[]{:S(2)}) collective-permute-start(bf16[32,2048]{1,0:T(8,128)(2,1)S(1)} %get-tuple-element.57.own), channel_id=1, source_target_pairs={{0,3},{1,2},{2,1},{3,0},{4,7},{5,6},{6,5},{7,4},{8,11},{9,10},{10,... | collective-permute-start | bytes 393224 | tf_op jit(solution)/shard_map/ppermute | solution.py:22
  (15 other events, 118.4 us)

commit v7 on v6

--- a/solution.py
+++ b/solution.py
@@ -181,10 +181,22 @@
             out[second * patches : (second + 1) * patches] = total[place : place + patches].astype(BF16)
 
 
-def down_far_kernel(offsets, own, one, two, three, w_down, out, stack):
-    part, span = own.shape[0], out.shape[0]
-    for k, block in enumerate((own, one, two, three)):
-        stack[pl.ds(pl.multiple_of(offsets[k], 16), part), :] = block[:, span:]
+def pair_kernel(own, second, out):
+    part = own.shape[0]
+    out[:part] = own[...]
+    out[part:] = second[...]
+
+
+def stack_hidden(offsets, own, second, others, low, stack):
+    part, span = own.shape[0], stack.shape[1]
+    blocks = (own, second, others.at[:part], others.at[part:])
+    for k, block in enumerate(blocks):
+        place = pl.multiple_of(offsets[k], 16)
+        stack[pl.ds(place, part), :] = block[:, low : low + span]
+
+
+def down_far_kernel(offsets, own, second, others, w_down, out, stack):
+    stack_hidden(offsets, own, second, others, out.shape[0], stack)
     out[...] = dot(stack[...].T, w_down[...]).astype(BF16)
 
 
@@ -192,11 +204,9 @@
     place_blocks(partial[...] + other[...].astype(F32), outs)
 
 
-def down_near_kernel(offsets, own, one, two, three, w_down, other, *rest):
+def down_near_kernel(offsets, own, second, others, w_down, other, *rest):
     stack = rest[-1]
-    part, span = own.shape[0], other.shape[0]
-    for k, block in enumerate((own, one, two, three)):
-        stack[pl.ds(pl.multiple_of(offsets[k], 16), part), :] = block[:, :span]
+    stack_hidden(offsets, own, second, others, 0, stack)
     place_blocks(dot(stack[...].T, w_down[...]) + other[...].astype(F32), rest[:-1])
 
 
@@ -236,14 +246,15 @@
     pooling, size = membership(lengths[...], states.shape[0])
     width = states.shape[1]
     pick = (((0,), (0,)), ((), ()))
+    twice = jnp.concatenate([pooling, pooling], axis=0)
     for values, result, part in (
         (states, out, total[:, :width]),
         (cots, grad, total[:, width:] / size),
     ):
         high = part.astype(BF16)
         low = (part - high.astype(F32)).astype(BF16)
-        spread = lax.dot_general(pooling, high, pick, preferred_element_type=F32)
-        spread = spread + lax.dot_general(pooling, low, pick, preferred_element_type=F32)
+        both = jnp.concatenate([high, low], axis=0)
+        spread = lax.dot_general(twice, both, pick, preferred_element_type=F32)
         result[...] = (values[...].astype(F32) + spread).astype(BF16)
 
 
@@ -259,7 +270,6 @@
     x, core = lax.axis_index("x"), lax.axis_index("c")
     step = jnp.where(core == 0, 1, 3)
     halving = (jnp.stack([x, x ^ step ^ 2, x ^ step, x ^ 2]) * part).astype(jnp.int32)
-    offsets = (jnp.stack([x, x ^ 1, x ^ 2, x ^ 3]) * part).astype(jnp.int32)
     owners = patch_owner.reshape(1, patches)
     w_gate, w_lift = w_gate.T, w_lift.T
 
@@ -324,7 +334,9 @@
         [*far, products, near_hidden],
         flops=3 * flops,
     )
-    hiddens = over(swap_x, hidden)
+    hidden_second = swap_near(hidden, False)
+    (pair,) = call(pair_kernel, [shape((2 * part, 2 * group), BF16)], [hidden, hidden_second])
+    hiddens = [hidden, hidden_second, swap_near(pair, True)]
     grad_terms = call(
         grad_near_kernel,
         [shape((4 * patches, width), BF16)] * 4,
@@ -342,7 +354,7 @@
         down_far_kernel,
         [shape((group, latent), BF16)],
         [*hiddens, after(w_down, (*grad_terms, back))],
-        [offsets],
+        [halving],
         flops=2 * group * latent * hid,
         scratch=[pltpu.VMEM((hid, group), BF16)],
     )
@@ -350,7 +362,7 @@
         down_near_kernel,
         [shape((4 * patches, latent), BF16)] * 4,
         [*hiddens, w_down, swap_core(far_rows)],
-        [offsets],
+        [halving],
         flops=2 * group * latent * hid,
         scratch=[pltpu.VMEM((hid, group), BF16)],
     )

time: 117 us -> 113 us (0.966)
  Pallas kernels: 21.2 us -> 17.5 us
  waiting for transfers between devices: 32.5 us -> 35.7 us
  starting transfers between devices: 44.4 us -> 42.6 us
  local copies, waits for them, and re-layouts: 2.39 us -> 0.8 us
    ppermute x2 -> x4, waiting for transfers between devices: 1.38 us -> 11.1 us  [swap_near(): lax.ppermute(value, ('c', 'x'), [(c * 4 + x, c * 4 + (x ^ steps[c])) for...]
    ppermute x6 -> x3, waiting for transfers between devices: 6.93 us -> 0.01 us  [swap_x(): return lax.ppermute(value, 'x', [(i, i ^ k) for i in range(4)])]
    ppermute x6 -> x3, starting transfers between devices: 7.79 us -> 3.93 us  [swap_x(): return lax.ppermute(value, 'x', [(i, i ^ k) for i in range(4)])]
    pallas_call x13 -> x14, Pallas kernels: 21.2 us -> 17.5 us  [call(): pl.pallas_call(body, out_shape=outs, in_specs=specs, out_specs=[pl.BlockS...]
    ppermute x2 -> x4, starting transfers between devices: 3.96 us -> 6.1 us  [swap_near(): lax.ppermute(value, ('c', 'x'), [(c * 4 + x, c * 4 + (x ^ steps[c])) for...]
    unnamed x20 -> x18, local copies, waits for them, and re-layouts: 1.63 us -> 0.04 us
  transfers between devices with their start and end apart: 29 -> 28, of which waited for: 15 -> 15; matrix products, arithmetic and copies ran while one was open for 0% -> 0% of each run, Pallas kernels for 6% -> 4%
where the time goes in v7:
time: 113 us
  starting transfers between devices  42.6 us (38%)
  waiting for transfers between devices  35.7 us (32%)
  Pallas kernels  17.5 us (15%)
  blocking collectives  15.3 us (14%)
    ppermute x15, waiting for transfers between devices, swap_first(): return lax.ppermute(value, SEQ, pairs)  24.3 us
    ppermute x15, starting transfers between devices, swap_first(): return lax.ppermute(value, SEQ, pairs)  20.7 us
    pallas_call x14, Pallas kernels, call(): pl.pallas_call(body, out_shape=outs, in_specs=specs, out_specs=[pl.BlockS...  17.5 us
    all_to_all x1, blocking collectives, on_device(): lax.all_to_all(outgoing, SEQ, split_axis=0, concat_axis=0, tiled=True)  15.3 us
    ppermute x6, starting transfers between devices, swap_core(): return lax.ppermute(value, 'c', [(0, 1), (1, 0)])  11.8 us
    ppermute x4, waiting for transfers between devices, swap_near(): lax.ppermute(value, ('c', 'x'), [(c * 4 + x, c * 4 + (x ^ steps[c])) for...  11.1 us
    ppermute x4, starting transfers between devices, swap_near(): lax.ppermute(value, ('c', 'x'), [(c * 4 + x, c * 4 + (x ^ steps[c])) for...  6.1 us
    ppermute x3, starting transfers between devices, swap_x(): return lax.ppermute(value, 'x', [(i, i ^ k) for i in range(4)])  3.93 us
  transfers between devices with their start and end apart: 28, of which 15 were waited for; matrix products, arithmetic and copies ran while one was open for 0% of the time, Pallas kernels for 4%

profile of v7, /device:TPU:1, one launch (start us, length us, event | category | flops | bytes accessed | tf_op | source)
XLA Modules:
  0.0 113.2 jit_solution(14889706072762076471)
XLA Ops:
  1.3 7.7 %shard_map.112 = (bf16[672,1024]{1,0:T(8,128)(2,1)}, bf16[672,1024]{1,0:T(8,128)(2,1)}) custom-call(s32[4]{0:T(128)} %add_multiply_fusion.offsets, bf16[1024,1024]{1,0:T(8,128)(2,1)} %w_enc.1, bf16[448,1024]{1,0:T(8,128)(2,1)} %bitcast.8, bf16[448,1024]{1,0:T(8,128)(2,1)} %bitcast.9, bf16[448,1024]{1,0:T(8,128)(2,1)} %w_down.2, bf16[1024,1024]{1,0:T(8,128)(2,1)} %weight.1), custom_call_target="tpu_custom_call" | custom-call | flops 2818572288 | bytes 9699328 | tf_op jit(solution)/shard_map/pallas_call | solution.py:56
  9.0 3.4 %collective-permute-start.10 = (bf16[672,1024]{1,0:T(8,128)(2,1)}, bf16[672,1024]{1,0:T(8,128)(2,1)S(1)}, u32[]{:S(2)}, u32[]{:S(2)}) collective-permute-start(bf16[672,1024]{1,0:T(8,128)(2,1)} %get-tuple-element.32), channel_id=1, source_target_pairs={{0,1},{1,0},{2,3},{3,2},{4,7},{5,6},{6,5},{7,4},{8,9},{9,8},{10,11... | collective-permute-start | bytes 4128776 | tf_op jit(solution)/shard_map/ppermute | solution.py:27
  14.0 2.6 %collective-permute-start.1 = (bf16[32,2048]{1,0:T(8,128)(2,1)S(1)}, bf16[32,2048]{1,0:T(8,128)(2,1)S(1)}, u32[]{:S(2)}, u32[]{:S(2)}) collective-permute-start(bf16[32,2048]{1,0:T(8,128)(2,1)S(1)} %shard_map.113.own.pooled), channel_id=1, source_target_pairs={{0,16},{4,68},{8,24},{12,76},{16,0},{20,84},{24,8},{28,92},{32,48}... | collective-permute-start | bytes 393224 | tf_op jit(solution)/shard_map/ppermute | solution.py:37
  16.9 3.9 %collective-permute-done.1.two = bf16[32,2048]{1,0:T(8,128)(2,1)S(1)} collective-permute-done((bf16[32,2048]{1,0:T(8,128)(2,1)S(1)}, bf16[32,2048]{1,0:T(8,128)(2,1)S(1)}, u32[]{:S(2)}, u32[]{:S(2)}) %collective-permute-start.1) | collective-permute-done | bytes 131104 | tf_op jit(solution)/shard_map/ppermute | solution.py:37
  21.9 1.7 %collective-permute-start.4 = (bf16[128,2048]{1,0:T(8,128)(2,1)S(1)}, bf16[128,2048]{1,0:T(8,128)(2,1)S(1)}, u32[]{:S(2)}, u32[]{:S(2)}) collective-permute-start(bf16[128,2048]{1,0:T(8,128)(2,1)S(1)} %shard_map.114.r0), channel_id=1, source_target_pairs={{0,32},{4,12},{8,40},{12,4},{16,48},{20,28},{24,56},{28,20},{32,0}... | collective-permute-start | bytes 1572872 | tf_op jit(solution)/shard_map/ppermute | solution.py:37
  23.6 3.3 %collective-permute-start.6 = (bf16[128,2048]{1,0:T(8,128)(2,1)S(1)}, bf16[128,2048]{1,0:T(8,128)(2,1)S(1)}, u32[]{:S(2)}, u32[]{:S(2)}) collective-permute-start(bf16[128,2048]{1,0:T(8,128)(2,1)S(1)} %shard_map.114.r0), channel_id=1, source_target_pairs={{0,64},{4,20},{8,72},{12,28},{16,80},{20,4},{24,88},{28,12},{32,96... | collective-permute-start | bytes 1572872 | tf_op jit(solution)/shard_map/ppermute | solution.py:37
  29.1 3.1 %collective-permute-start.3 = (bf16[128,2048]{1,0:T(8,128)(2,1)S(1)}, bf16[128,2048]{1,0:T(8,128)(2,1)S(1)}, u32[]{:S(2)}, u32[]{:S(2)}) collective-permute-start(bf16[128,2048]{1,0:T(8,128)(2,1)S(1)} %shard_map.114.r0), channel_id=1, source_target_pairs={{0,4},{4,0},{1,5},{5,1},{2,6},{6,2},{3,7},{7,3},{8,12},{12,8},{9,1... | collective-permute-start | bytes 1572872 | tf_op jit(solution)/shard_map/ppermute | solution.py:18
  33.4 6.0 %collective-permute-done.6.r2 = bf16[128,2048]{1,0:T(8,128)(2,1)S(1)} collective-permute-done((bf16[128,2048]{1,0:T(8,128)(2,1)S(1)}, bf16[128,2048]{1,0:T(8,128)(2,1)S(1)}, u32[]{:S(2)}, u32[]{:S(2)}) %collective-permute-start.6) | collective-permute-done | bytes 524320 | tf_op jit(solution)/shard_map/ppermute | solution.py:37
  39.4 2.2 %collective-permute-start.7 = (bf16[128,2048]{1,0:T(8,128)(2,1)S(1)}, bf16[128,2048]{1,0:T(8,128)(2,1)S(1)}, u32[]{:S(2)}, u32[]{:S(2)}) collective-permute-start(bf16[128,2048]{1,0:T(8,128)(2,1)S(1)} %collective-permute-done.6.r2), channel_id=1, source_target_pairs={{0,4},{4,0},{1,5},{5,1},{2,6},{6,2},{3,7},{7,3},{8,12},{12,8},{9,1... | collective-permute-start | bytes 1572872 | tf_op jit(solution)/shard_map/ppermute | solution.py:18
  42.0 2.7 %collective-permute-start.9 = (bf16[128,2048]{1,0:T(8,128)(2,1)S(1)}, bf16[128,2048]{1,0:T(8,128)(2,1)S(1)}, u32[]{:S(2)}, u32[]{:S(2)}) collective-permute-start(bf16[128,2048]{1,0:T(8,128)(2,1)S(1)} %collective-permute-done.8.r3), channel_id=1, source_target_pairs={{0,4},{4,0},{1,5},{5,1},{2,6},{6,2},{3,7},{7,3},{8,12},{12,8},{9,1... | collective-permute-start | bytes 1572872 | tf_op jit(solution)/shard_map/ppermute | solution.py:18
  48.2 4.9 %collective-permute-done.12.second = bf16[112,1024]{1,0:T(8,128)(2,1)S(1)} collective-permute-done((bf16[112,1024]{1,0:T(8,128)(2,1)S(1)}, bf16[112,1024]{1,0:T(8,128)(2,1)S(1)}, u32[]{:S(2)}, u32[]{:S(2)}) %collective-permute-start.12) | collective-permute-done | bytes 229408 | tf_op jit(solution)/shard_map/ppermute | solution.py:27
  53.1 1.9 %collective-permute-start.13 = (bf16[224,1024]{1,0:T(8,128)(2,1)S(1)}, bf16[224,1024]{1,0:T(8,128)(2,1)S(1)}, u32[]{:S(2)}, u32[]{:S(2)}) collective-permute-start(bf16[224,1024]{1,0:T(8,128)(2,1)S(1)} %shard_map.118), channel_id=1, source_target_pairs={{0,1},{1,0},{2,3},{3,2},{4,7},{5,6},{6,5},{7,4},{8,9},{9,8},{10,11... | collective-permute-start | bytes 1376264 | tf_op jit(solution)/shard_map/ppermute | solution.py:27
  55.0 1.7 %shard_map.120 = (bf16[32,1024]{1,0:T(8,128)(2,1)S(1)}, f32[32,1024]{1,0:T(8,128)S(1)}) custom-call(bf16[1024,1024]{1,0:T(8,128)(2,1)S(1)} %copy-done, bf16[1024,1024]{1,0:T(8,128)(2,1)S(1)} %copy-done.2, bf16[32,2048]{1,0:T(8,128)(2,1)S(1)} %shard_map.113.own.pooled), custom_call_target="tpu_custom_call" | custom-call | flops 201326592 | bytes 4521984 | tf_op jit(solution)/shard_map/pallas_call | solution.py:56
  56.9 4.8 %collective-permute-done.13.others = bf16[224,1024]{1,0:T(8,128)(2,1)S(1)} collective-permute-done((bf16[224,1024]{1,0:T(8,128)(2,1)S(1)}, bf16[224,1024]{1,0:T(8,128)(2,1)S(1)}, u32[]{:S(2)}, u32[]{:S(2)}) %collective-permute-start.13) | collective-permute-done | bytes 458784 | tf_op jit(solution)/shard_map/ppermute | solution.py:27
  63.1 2.2 %collective-permute-start.15 = (bf16[512,1024]{1,0:T(8,128)(2,1)S(1)}, bf16[512,1024]{1,0:T(8,128)(2,1)S(1)}, u32[]{:S(2)}, u32[]{:S(2)}) collective-permute-start(bf16[512,1024]{1,0:T(8,128)(2,1)S(1)} %shard_map.121), channel_id=1, source_target_pairs={{0,4},{4,0},{1,5},{5,1},{2,6},{6,2},{3,7},{7,3},{8,12},{12,8},{9,1... | collective-permute-start | bytes 3145736 | tf_op jit(solution)/shard_map/ppermute | solution.py:18
  66.4 2.7 %collective-permute-start.21 = (bf16[128,1024]{1,0:T(8,128)(2,1)S(1)}, bf16[128,1024]{1,0:T(8,128)(2,1)S(1)}, u32[]{:S(2)}, u32[]{:S(2)}) collective-permute-start(bf16[128,1024]{1,0:T(8,128)(2,1)S(1)} %get-tuple-element.45), channel_id=1, source_target_pairs={{0,24},{4,100},{8,16},{12,108},{16,8},{20,116},{24,0},{28,124},{32... | collective-permute-start | bytes 786440 | tf_op jit(solution)/shard_map/ppermute | solution.py:37
  71.8 2.7 %collective-permute-start.18 = (bf16[128,1024]{1,0:T(8,128)(2,1)S(1)}, bf16[128,1024]{1,0:T(8,128)(2,1)S(1)}, u32[]{:S(2)}, u32[]{:S(2)}) collective-permute-start(bf16[128,1024]{1,0:T(8,128)(2,1)S(1)} %get-tuple-element.51), channel_id=1, source_target_pairs={{0,24},{4,100},{8,16},{12,108},{16,8},{20,116},{24,0},{28,124},{32... | collective-permute-start | bytes 786440 | tf_op jit(solution)/shard_map/ppermute | solution.py:37
  76.5 2.5 %collective-permute-done.17.refs_2_ = bf16[128,1024]{1,0:T(8,128)(2,1)S(1)} collective-permute-done((bf16[128,1024]{1,0:T(8,128)(2,1)S(1)}, bf16[128,1024]{1,0:T(8,128)(2,1)S(1)}, u32[]{:S(2)}, u32[]{:S(2)}) %collective-permute-start.17) | collective-permute-done | bytes 262176 | tf_op jit(solution)/shard_map/ppermute | solution.py:37
  79.0 2.6 %collective-permute-done.18.refs_3_ = bf16[128,1024]{1,0:T(8,128)(2,1)S(1)} collective-permute-done((bf16[128,1024]{1,0:T(8,128)(2,1)S(1)}, bf16[128,1024]{1,0:T(8,128)(2,1)S(1)}, u32[]{:S(2)}, u32[]{:S(2)}) %collective-permute-start.18) | collective-permute-done | bytes 262176 | tf_op jit(solution)/shard_map/ppermute | solution.py:37
  82.3 3.6 %collective-permute-start.23 = (bf16[32,2048]{1,0:T(8,128)(2,1)S(1)}, bf16[32,2048]{1,0:T(8,128)(2,1)S(1)}, u32[]{:S(2)}, u32[]{:S(2)}) collective-permute-start(bf16[32,2048]{1,0:T(8,128)(2,1)S(1)} %get-tuple-element.54), channel_id=1, source_target_pairs={{0,64},{4,20},{8,72},{12,28},{16,80},{20,4},{24,88},{28,12},{32,96... | collective-permute-start | bytes 393224 | tf_op jit(solution)/shard_map/ppermute | solution.py:37
  85.9 3.8 %collective-permute-done.23.two = bf16[32,2048]{1,0:T(8,128)(2,1)S(1)} collective-permute-done((bf16[32,2048]{1,0:T(8,128)(2,1)S(1)}, bf16[32,2048]{1,0:T(8,128)(2,1)S(1)}, u32[]{:S(2)}, u32[]{:S(2)}) %collective-permute-start.23) | collective-permute-done | bytes 131104 | tf_op jit(solution)/shard_map/ppermute | solution.py:37
  89.7 1.7 %collective-permute-done.24.three = bf16[32,2048]{1,0:T(8,128)(2,1)S(1)} collective-permute-done((bf16[32,2048]{1,0:T(8,128)(2,1)S(1)}, bf16[32,2048]{1,0:T(8,128)(2,1)S(1)}, u32[]{:S(2)}, u32[]{:S(2)}) %collective-permute-start.24) | collective-permute-done | bytes 131104 | tf_op jit(solution)/shard_map/ppermute | solution.py:37
  92.0 3.6 %collective-permute-start.26 = (bf16[32,2048]{1,0:T(8,128)(2,1)S(1)}, bf16[32,2048]{1,0:T(8,128)(2,1)S(1)}, u32[]{:S(2)}, u32[]{:S(2)}) collective-permute-start(bf16[32,2048]{1,0:T(8,128)(2,1)S(1)} %get-tuple-element.57.own), channel_id=1, source_target_pairs={{0,2},{1,3},{2,0},{3,1},{4,6},{5,7},{6,4},{7,5},{8,10},{9,11},{10,... | collective-permute-start | bytes 393224 | tf_op jit(solution)/shard_map/ppermute | solution.py:22
  95.9 15.3 %all_to_all.12 = bf16[32,2,1024]{2,1,0:T(2,128)(2,1)S(1)} all-to-all(bf16[32,2,1024]{2,1,0:T(2,128)(2,1)S(1)} %all_to_all.8), channel_id=1, replica_groups=mesh['y'=4,'z'=4,'c'=2,'x'=4] {'y','z','c'}, dimensions={0} | all-to-all | bytes 262144 | tf_op jit(solution)/shard_map/all_to_all | solution.py:381
  (68 shorter events, 21.9 us)
Async XLA Ops:
  9.0 19.3 %collective-permute-start.10 = (bf16[672,1024]{1,0:T(8,128)(2,1)}, bf16[672,1024]{1,0:T(8,128)(2,1)S(1)}, u32[]{:S(2)}, u32[]{:S(2)}) collective-permute-start(bf16[672,1024]{1,0:T(8,128)(2,1)} %get-tuple-element.32), channel_id=1, source_target_pairs={{0,1},{1,0},{2,3},{3,2},{4,7},{5,6},{6,5},{7,4},{8,9},{9,8},{10,11... | collective-permute-start | bytes 4128776 | tf_op jit(solution)/shard_map/ppermute | solution.py:27
  14.0 6.7 %collective-permute-start.1 = (bf16[32,2048]{1,0:T(8,128)(2,1)S(1)}, bf16[32,2048]{1,0:T(8,128)(2,1)S(1)}, u32[]{:S(2)}, u32[]{:S(2)}) collective-permute-start(bf16[32,2048]{1,0:T(8,128)(2,1)S(1)} %shard_map.113.own.pooled), channel_id=1, source_target_pairs={{0,16},{4,68},{8,24},{12,76},{16,0},{20,84},{24,8},{28,92},{32,48}... | collective-permute-start | bytes 393224 | tf_op jit(solution)/shard_map/ppermute | solution.py:37
  16.7 5.2 %collective-permute-start.2 = (bf16[32,2048]{1,0:T(8,128)(2,1)S(1)}, bf16[32,2048]{1,0:T(8,128)(2,1)S(1)}, u32[]{:S(2)}, u32[]{:S(2)}) collective-permute-start(bf16[32,2048]{1,0:T(8,128)(2,1)S(1)} %shard_map.113.own.pooled), channel_id=1, source_target_pairs={{0,24},{4,100},{8,16},{12,108},{16,8},{20,116},{24,0},{28,124},{32... | collective-permute-start | bytes 393224 | tf_op jit(solution)/shard_map/ppermute | solution.py:37
  21.9 10.3 %collective-permute-start.4 = (bf16[128,2048]{1,0:T(8,128)(2,1)S(1)}, bf16[128,2048]{1,0:T(8,128)(2,1)S(1)}, u32[]{:S(2)}, u32[]{:S(2)}) collective-permute-start(bf16[128,2048]{1,0:T(8,128)(2,1)S(1)} %shard_map.114.r0), channel_id=1, source_target_pairs={{0,32},{4,12},{8,40},{12,4},{16,48},{20,28},{24,56},{28,20},{32,0}... | collective-permute-start | bytes 1572872 | tf_op jit(solution)/shard_map/ppermute | solution.py:37
  23.6 15.8 %collective-permute-start.6 = (bf16[128,2048]{1,0:T(8,128)(2,1)S(1)}, bf16[128,2048]{1,0:T(8,128)(2,1)S(1)}, u32[]{:S(2)}, u32[]{:S(2)}) collective-permute-start(bf16[128,2048]{1,0:T(8,128)(2,1)S(1)} %shard_map.114.r0), channel_id=1, source_target_pairs={{0,64},{4,20},{8,72},{12,28},{16,80},{20,4},{24,88},{28,12},{32,96... | collective-permute-start | bytes 1572872 | tf_op jit(solution)/shard_map/ppermute | solution.py:37
  26.9 15.2 %collective-permute-start.8 = (bf16[128,2048]{1,0:T(8,128)(2,1)S(1)}, bf16[128,2048]{1,0:T(8,128)(2,1)S(1)}, u32[]{:S(2)}, u32[]{:S(2)}) collective-permute-start(bf16[128,2048]{1,0:T(8,128)(2,1)S(1)} %shard_map.114.r0), channel_id=1, source_target_pairs={{0,96},{4,28},{8,104},{12,20},{16,112},{20,12},{24,120},{28,4},{32... | collective-permute-start | bytes 1572872 | tf_op jit(solution)/shard_map/ppermute | solution.py:37
  28.5 16.2 %collective-permute-start.11 = (bf16[336,1024]{1,0:T(8,128)(2,1)S(1)}, bf16[336,1024]{1,0:T(8,128)(2,1)S(1)}, u32[]{:S(2)}, u32[]{:S(2)}) collective-permute-start(bf16[336,1024]{1,0:T(8,128)(2,1)S(1)} %get-tuple-element.36), channel_id=1, source_target_pairs={{0,3},{1,2},{2,1},{3,0},{4,5},{5,4},{6,7},{7,6},{8,11},{9,10},{10,... | collective-permute-start | bytes 2064392 | tf_op jit(solution)/shard_map/ppermute | solution.py:27
  29.1 16.9 %collective-permute-start.3 = (bf16[128,2048]{1,0:T(8,128)(2,1)S(1)}, bf16[128,2048]{1,0:T(8,128)(2,1)S(1)}, u32[]{:S(2)}, u32[]{:S(2)}) collective-permute-start(bf16[128,2048]{1,0:T(8,128)(2,1)S(1)} %shard_map.114.r0), channel_id=1, source_target_pairs={{0,4},{4,0},{1,5},{5,1},{2,6},{6,2},{3,7},{7,3},{8,12},{12,8},{9,1... | collective-permute-start | bytes 1572872 | tf_op jit(solution)/shard_map/ppermute | solution.py:18
  32.2 13.8 %collective-permute-start.5 = (bf16[128,2048]{1,0:T(8,128)(2,1)S(1)}, bf16[128,2048]{1,0:T(8,128)(2,1)S(1)}, u32[]{:S(2)}, u32[]{:S(2)}) collective-permute-start(bf16[128,2048]{1,0:T(8,128)(2,1)S(1)} %collective-permute-done.4.r1), channel_id=1, source_target_pairs={{0,4},{4,0},{1,5},{5,1},{2,6},{6,2},{3,7},{7,3},{8,12},{12,8},{9,1... | collective-permute-start | bytes 1572872 | tf_op jit(solution)/shard_map/ppermute | solution.py:18
  39.4 6.6 %collective-permute-start.7 = (bf16[128,2048]{1,0:T(8,128)(2,1)S(1)}, bf16[128,2048]{1,0:T(8,128)(2,1)S(1)}, u32[]{:S(2)}, u32[]{:S(2)}) collective-permute-start(bf16[128,2048]{1,0:T(8,128)(2,1)S(1)} %collective-permute-done.6.r2), channel_id=1, source_target_pairs={{0,4},{4,0},{1,5},{5,1},{2,6},{6,2},{3,7},{7,3},{8,12},{12,8},{9,1... | collective-permute-start | bytes 1572872 | tf_op jit(solution)/shard_map/ppermute | solution.py:18
  47.5 9.2 %collective-permute-start.14 = (bf16[512,1024]{1,0:T(8,128)(2,1)S(1)}, bf16[512,1024]{1,0:T(8,128)(2,1)S(1)}, u32[]{:S(2)}, u32[]{:S(2)}) collective-permute-start(bf16[512,1024]{1,0:T(8,128)(2,1)S(1)} %get-tuple-element.41), channel_id=1, source_target_pairs={{0,4},{4,0},{1,5},{5,1},{2,6},{6,2},{3,7},{7,3},{8,12},{12,8},{9,1... | collective-permute-start | bytes 3145736 | tf_op jit(solution)/shard_map/ppermute | solution.py:18
  53.1 8.6 %collective-permute-start.13 = (bf16[224,1024]{1,0:T(8,128)(2,1)S(1)}, bf16[224,1024]{1,0:T(8,128)(2,1)S(1)}, u32[]{:S(2)}, u32[]{:S(2)}) collective-permute-start(bf16[224,1024]{1,0:T(8,128)(2,1)S(1)} %shard_map.118), channel_id=1, source_target_pairs={{0,1},{1,0},{2,3},{3,2},{4,7},{5,6},{6,5},{7,4},{8,9},{9,8},{10,11... | collective-permute-start | bytes 1376264 | tf_op jit(solution)/shard_map/ppermute | solution.py:27
  63.1 6.1 %collective-permute-start.15 = (bf16[512,1024]{1,0:T(8,128)(2,1)S(1)}, bf16[512,1024]{1,0:T(8,128)(2,1)S(1)}, u32[]{:S(2)}, u32[]{:S(2)}) collective-permute-start(bf16[512,1024]{1,0:T(8,128)(2,1)S(1)} %shard_map.121), channel_id=1, source_target_pairs={{0,4},{4,0},{1,5},{5,1},{2,6},{6,2},{3,7},{7,3},{8,12},{12,8},{9,1... | collective-permute-start | bytes 3145736 | tf_op jit(solution)/shard_map/ppermute | solution.py:18
  65.3 6.5 %collective-permute-start.19 = (bf16[128,1024]{1,0:T(8,128)(2,1)S(1)}, bf16[128,1024]{1,0:T(8,128)(2,1)S(1)}, u32[]{:S(2)}, u32[]{:S(2)}) collective-permute-start(bf16[128,1024]{1,0:T(8,128)(2,1)S(1)} %get-tuple-element.43), channel_id=1, source_target_pairs={{0,8},{4,36},{8,0},{12,44},{16,24},{20,52},{24,16},{28,60},{32,40}... | collective-permute-start | bytes 786440 | tf_op jit(solution)/shard_map/ppermute | solution.py:37
  65.3 9.1 %collective-permute-start.20 = (bf16[128,1024]{1,0:T(8,128)(2,1)S(1)}, bf16[128,1024]{1,0:T(8,128)(2,1)S(1)}, u32[]{:S(2)}, u32[]{:S(2)}) collective-permute-start(bf16[128,1024]{1,0:T(8,128)(2,1)S(1)} %get-tuple-element.44), channel_id=1, source_target_pairs={{0,16},{4,68},{8,24},{12,76},{16,0},{20,84},{24,8},{28,92},{32,48}... | collective-permute-start | bytes 786440 | tf_op jit(solution)/shard_map/ppermute | solution.py:37
  66.4 9.6 %collective-permute-start.21 = (bf16[128,1024]{1,0:T(8,128)(2,1)S(1)}, bf16[128,1024]{1,0:T(8,128)(2,1)S(1)}, u32[]{:S(2)}, u32[]{:S(2)}) collective-permute-start(bf16[128,1024]{1,0:T(8,128)(2,1)S(1)} %get-tuple-element.45), channel_id=1, source_target_pairs={{0,24},{4,100},{8,16},{12,108},{16,8},{20,116},{24,0},{28,124},{32... | collective-permute-start | bytes 786440 | tf_op jit(solution)/shard_map/ppermute | solution.py:37
  70.5 6.0 %collective-permute-start.16 = (bf16[128,1024]{1,0:T(8,128)(2,1)S(1)}, bf16[128,1024]{1,0:T(8,128)(2,1)S(1)}, u32[]{:S(2)}, u32[]{:S(2)}) collective-permute-start(bf16[128,1024]{1,0:T(8,128)(2,1)S(1)} %get-tuple-element.49), channel_id=1, source_target_pairs={{0,8},{4,36},{8,0},{12,44},{16,24},{20,52},{24,16},{28,60},{32,40}... | collective-permute-start | bytes 786440 | tf_op jit(solution)/shard_map/ppermute | solution.py:37
  70.6 8.4 %collective-permute-start.17 = (bf16[128,1024]{1,0:T(8,128)(2,1)S(1)}, bf16[128,1024]{1,0:T(8,128)(2,1)S(1)}, u32[]{:S(2)}, u32[]{:S(2)}) collective-permute-start(bf16[128,1024]{1,0:T(8,128)(2,1)S(1)} %get-tuple-element.50), channel_id=1, source_target_pairs={{0,16},{4,68},{8,24},{12,76},{16,0},{20,84},{24,8},{28,92},{32,48}... | collective-permute-start | bytes 786440 | tf_op jit(solution)/shard_map/ppermute | solution.py:37
  71.8 9.9 %collective-permute-start.18 = (bf16[128,1024]{1,0:T(8,128)(2,1)S(1)}, bf16[128,1024]{1,0:T(8,128)(2,1)S(1)}, u32[]{:S(2)}, u32[]{:S(2)}) collective-permute-start(bf16[128,1024]{1,0:T(8,128)(2,1)S(1)} %get-tuple-element.51), channel_id=1, source_target_pairs={{0,24},{4,100},{8,16},{12,108},{16,8},{20,116},{24,0},{28,124},{32... | collective-permute-start | bytes 786440 | tf_op jit(solution)/shard_map/ppermute | solution.py:37
  82.3 7.4 %collective-permute-start.23 = (bf16[32,2048]{1,0:T(8,128)(2,1)S(1)}, bf16[32,2048]{1,0:T(8,128)(2,1)S(1)}, u32[]{:S(2)}, u32[]{:S(2)}) collective-permute-start(bf16[32,2048]{1,0:T(8,128)(2,1)S(1)} %get-tuple-element.54), channel_id=1, source_target_pairs={{0,64},{4,20},{8,72},{12,28},{16,80},{20,4},{24,88},{28,12},{32,96... | collective-permute-start | bytes 393224 | tf_op jit(solution)/shard_map/ppermute | solution.py:37
  85.9 5.5 %collective-permute-start.24 = (bf16[32,2048]{1,0:T(8,128)(2,1)S(1)}, bf16[32,2048]{1,0:T(8,128)(2,1)S(1)}, u32[]{:S(2)}, u32[]{:S(2)}) collective-permute-start(bf16[32,2048]{1,0:T(8,128)(2,1)S(1)} %get-tuple-element.55), channel_id=1, source_target_pairs={{0,96},{4,28},{8,104},{12,20},{16,112},{20,12},{24,120},{28,4},{32... | collective-permute-start | bytes 393224 | tf_op jit(solution)/shard_map/ppermute | solution.py:37
  91.9 20.0 %collective-permute-start.25 = (bf16[32,2048]{1,0:T(8,128)(2,1)S(1)}, bf16[32,2048]{1,0:T(8,128)(2,1)S(1)}, u32[]{:S(2)}, u32[]{:S(2)}) collective-permute-start(bf16[32,2048]{1,0:T(8,128)(2,1)S(1)} %get-tuple-element.57.own), channel_id=1, source_target_pairs={{0,1},{1,0},{2,3},{3,2},{4,5},{5,4},{6,7},{7,6},{8,9},{9,8},{10,11... | collective-permute-start | bytes 393224 | tf_op jit(solution)/shard_map/ppermute | solution.py:22
  92.0 19.9 %collective-permute-start.26 = (bf16[32,2048]{1,0:T(8,128)(2,1)S(1)}, bf16[32,2048]{1,0:T(8,128)(2,1)S(1)}, u32[]{:S(2)}, u32[]{:S(2)}) collective-permute-start(bf16[32,2048]{1,0:T(8,128)(2,1)S(1)} %get-tuple-element.57.own), channel_id=1, source_target_pairs={{0,2},{1,3},{2,0},{3,1},{4,6},{5,7},{6,4},{7,5},{8,10},{9,11},{10,... | collective-permute-start | bytes 393224 | tf_op jit(solution)/shard_map/ppermute | solution.py:22
  95.6 16.2 %collective-permute-start.27 = (bf16[32,2048]{1,0:T(8,128)(2,1)S(1)}, bf16[32,2048]{1,0:T(8,128)(2,1)S(1)}, u32[]{:S(2)}, u32[]{:S(2)}) collective-permute-start(bf16[32,2048]{1,0:T(8,128)(2,1)S(1)} %get-tuple-element.57.own), channel_id=1, source_target_pairs={{0,3},{1,2},{2,1},{3,0},{4,7},{5,6},{6,5},{7,4},{8,11},{9,10},{10,... | collective-permute-start | bytes 393224 | tf_op jit(solution)/shard_map/ppermute | solution.py:22
  (13 other events, 120.2 us)

commit v8 on v7

--- a/solution.py
+++ b/solution.py
@@ -353,7 +353,7 @@
     (far_rows,) = call(
         down_far_kernel,
         [shape((group, latent), BF16)],
-        [*hiddens, after(w_down, (*grad_terms, back))],
+        [*hiddens, after(w_down, (grad_first[1], back))],
         [halving],
         flops=2 * group * latent * hid,
         scratch=[pltpu.VMEM((hid, group), BF16)],

time: 113 us -> 111 us (0.982)
  starting transfers between devices: 42.6 us -> 39.8 us
  local copies, waits for them, and re-layouts: 0.8 us -> 2.08 us
    ppermute x4, waiting for transfers between devices: 11.1 us -> 7.22 us  [swap_near(): lax.ppermute(value, ('c', 'x'), [(c * 4 + x, c * 4 + (x ^ steps[c])) for...]
    ppermute x15, waiting for transfers between devices: 24.3 us -> 27.1 us  [swap_first(): return lax.ppermute(value, SEQ, pairs)]
    ppermute x15, starting transfers between devices: 20.7 us -> 18 us  [swap_first(): return lax.ppermute(value, SEQ, pairs)]
    unnamed x18, local copies, waits for them, and re-layouts: 0.04 us -> 1.32 us
    ppermute x6, waiting for transfers between devices: 0.25 us -> 1.5 us  [swap_core(): return lax.ppermute(value, 'c', [(0, 1), (1, 0)])]
  transfers between devices with their start and end apart: 28 -> 28, of which waited for: 15 -> 16; matrix products, arithmetic and copies ran while one was open for 0% -> 0% of each run, Pallas kernels for 4% -> 5%
where the time goes in v8:
time: 111 us
  starting transfers between devices  39.8 us (36%)
  waiting for transfers between devices  35.9 us (32%)
  Pallas kernels  17.5 us (16%)
  blocking collectives  14.5 us (13%)
  local copies, waits for them, and re-layouts  2.08 us (2%)
    ppermute x15, waiting for transfers between devices, swap_first(): return lax.ppermute(value, SEQ, pairs)  27.1 us
    ppermute x15, starting transfers between devices, swap_first(): return lax.ppermute(value, SEQ, pairs)  18 us
    pallas_call x14, Pallas kernels, call(): pl.pallas_call(body, out_shape=outs, in_specs=specs, out_specs=[pl.BlockS...  17.5 us
    all_to_all x1, blocking collectives, on_device(): lax.all_to_all(outgoing, SEQ, split_axis=0, concat_axis=0, tiled=True)  14.5 us
    ppermute x6, starting transfers between devices, swap_core(): return lax.ppermute(value, 'c', [(0, 1), (1, 0)])  11.8 us
    ppermute x4, waiting for transfers between devices, swap_near(): lax.ppermute(value, ('c', 'x'), [(c * 4 + x, c * 4 + (x ^ steps[c])) for...  7.22 us
    ppermute x4, starting transfers between devices, swap_near(): lax.ppermute(value, ('c', 'x'), [(c * 4 + x, c * 4 + (x ^ steps[c])) for...  6.1 us
    ppermute x3, starting transfers between devices, swap_x(): return lax.ppermute(value, 'x', [(i, i ^ k) for i in range(4)])  3.93 us
  transfers between devices with their start and end apart: 28, of which 16 were waited for; matrix products, arithmetic and copies ran while one was open for 0% of the time, Pallas kernels for 5%

profile of v8, /device:TPU:1, one launch (start us, length us, event | category | flops | bytes accessed | tf_op | source)
XLA Modules:
  0.0 111.1 jit_solution(8316189033388173403)
XLA Ops:
  1.3 7.7 %shard_map.112 = (bf16[672,1024]{1,0:T(8,128)(2,1)}, bf16[672,1024]{1,0:T(8,128)(2,1)}) custom-call(s32[4]{0:T(128)} %add_multiply_fusion.offsets, bf16[1024,1024]{1,0:T(8,128)(2,1)} %w_enc.1, bf16[448,1024]{1,0:T(8,128)(2,1)} %bitcast.8, bf16[448,1024]{1,0:T(8,128)(2,1)} %bitcast.9, bf16[448,1024]{1,0:T(8,128)(2,1)} %w_down.2, bf16[1024,1024]{1,0:T(8,128)(2,1)} %weight.1), custom_call_target="tpu_custom_call" | custom-call | flops 2818572288 | bytes 9699328 | tf_op jit(solution)/shard_map/pallas_call | solution.py:56
  9.0 3.4 %collective-permute-start.10 = (bf16[672,1024]{1,0:T(8,128)(2,1)}, bf16[672,1024]{1,0:T(8,128)(2,1)S(1)}, u32[]{:S(2)}, u32[]{:S(2)}) collective-permute-start(bf16[672,1024]{1,0:T(8,128)(2,1)} %get-tuple-element.32), channel_id=1, source_target_pairs={{0,1},{1,0},{2,3},{3,2},{4,7},{5,6},{6,5},{7,4},{8,9},{9,8},{10,11... | collective-permute-start | bytes 4128776 | tf_op jit(solution)/shard_map/ppermute | solution.py:27
  14.0 2.6 %collective-permute-start.1 = (bf16[32,2048]{1,0:T(8,128)(2,1)S(1)}, bf16[32,2048]{1,0:T(8,128)(2,1)S(1)}, u32[]{:S(2)}, u32[]{:S(2)}) collective-permute-start(bf16[32,2048]{1,0:T(8,128)(2,1)S(1)} %shard_map.113.own.pooled), channel_id=1, source_target_pairs={{0,16},{4,68},{8,24},{12,76},{16,0},{20,84},{24,8},{28,92},{32,48}... | collective-permute-start | bytes 393224 | tf_op jit(solution)/shard_map/ppermute | solution.py:37
  16.9 3.9 %collective-permute-done.1.two = bf16[32,2048]{1,0:T(8,128)(2,1)S(1)} collective-permute-done((bf16[32,2048]{1,0:T(8,128)(2,1)S(1)}, bf16[32,2048]{1,0:T(8,128)(2,1)S(1)}, u32[]{:S(2)}, u32[]{:S(2)}) %collective-permute-start.1) | collective-permute-done | bytes 131104 | tf_op jit(solution)/shard_map/ppermute | solution.py:37
  21.9 1.7 %collective-permute-start.4 = (bf16[128,2048]{1,0:T(8,128)(2,1)S(1)}, bf16[128,2048]{1,0:T(8,128)(2,1)S(1)}, u32[]{:S(2)}, u32[]{:S(2)}) collective-permute-start(bf16[128,2048]{1,0:T(8,128)(2,1)S(1)} %shard_map.114.r0), channel_id=1, source_target_pairs={{0,32},{4,12},{8,40},{12,4},{16,48},{20,28},{24,56},{28,20},{32,0}... | collective-permute-start | bytes 1572872 | tf_op jit(solution)/shard_map/ppermute | solution.py:37
  23.6 3.3 %collective-permute-start.6 = (bf16[128,2048]{1,0:T(8,128)(2,1)S(1)}, bf16[128,2048]{1,0:T(8,128)(2,1)S(1)}, u32[]{:S(2)}, u32[]{:S(2)}) collective-permute-start(bf16[128,2048]{1,0:T(8,128)(2,1)S(1)} %shard_map.114.r0), channel_id=1, source_target_pairs={{0,64},{4,20},{8,72},{12,28},{16,80},{20,4},{24,88},{28,12},{32,96... | collective-permute-start | bytes 1572872 | tf_op jit(solution)/shard_map/ppermute | solution.py:37
  29.1 3.1 %collective-permute-start.3 = (bf16[128,2048]{1,0:T(8,128)(2,1)S(1)}, bf16[128,2048]{1,0:T(8,128)(2,1)S(1)}, u32[]{:S(2)}, u32[]{:S(2)}) collective-permute-start(bf16[128,2048]{1,0:T(8,128)(2,1)S(1)} %shard_map.114.r0), channel_id=1, source_target_pairs={{0,4},{4,0},{1,5},{5,1},{2,6},{6,2},{3,7},{7,3},{8,12},{12,8},{9,1... | collective-permute-start | bytes 1572872 | tf_op jit(solution)/shard_map/ppermute | solution.py:18
  33.4 6.0 %collective-permute-done.6.r2 = bf16[128,2048]{1,0:T(8,128)(2,1)S(1)} collective-permute-done((bf16[128,2048]{1,0:T(8,128)(2,1)S(1)}, bf16[128,2048]{1,0:T(8,128)(2,1)S(1)}, u32[]{:S(2)}, u32[]{:S(2)}) %collective-permute-start.6) | collective-permute-done | bytes 524320 | tf_op jit(solution)/shard_map/ppermute | solution.py:37
  39.4 2.2 %collective-permute-start.7 = (bf16[128,2048]{1,0:T(8,128)(2,1)S(1)}, bf16[128,2048]{1,0:T(8,128)(2,1)S(1)}, u32[]{:S(2)}, u32[]{:S(2)}) collective-permute-start(bf16[128,2048]{1,0:T(8,128)(2,1)S(1)} %collective-permute-done.6.r2), channel_id=1, source_target_pairs={{0,4},{4,0},{1,5},{5,1},{2,6},{6,2},{3,7},{7,3},{8,12},{12,8},{9,1... | collective-permute-start | bytes 1572872 | tf_op jit(solution)/shard_map/ppermute | solution.py:18
  42.0 2.7 %collective-permute-start.9 = (bf16[128,2048]{1,0:T(8,128)(2,1)S(1)}, bf16[128,2048]{1,0:T(8,128)(2,1)S(1)}, u32[]{:S(2)}, u32[]{:S(2)}) collective-permute-start(bf16[128,2048]{1,0:T(8,128)(2,1)S(1)} %collective-permute-done.8.r3), channel_id=1, source_target_pairs={{0,4},{4,0},{1,5},{5,1},{2,6},{6,2},{3,7},{7,3},{8,12},{12,8},{9,1... | collective-permute-start | bytes 1572872 | tf_op jit(solution)/shard_map/ppermute | solution.py:18
  48.2 4.9 %collective-permute-done.12.second = bf16[112,1024]{1,0:T(8,128)(2,1)S(1)} collective-permute-done((bf16[112,1024]{1,0:T(8,128)(2,1)S(1)}, bf16[112,1024]{1,0:T(8,128)(2,1)S(1)}, u32[]{:S(2)}, u32[]{:S(2)}) %collective-permute-start.12) | collective-permute-done | bytes 229408 | tf_op jit(solution)/shard_map/ppermute | solution.py:27
  53.1 1.9 %collective-permute-start.13 = (bf16[224,1024]{1,0:T(8,128)(2,1)S(1)}, bf16[224,1024]{1,0:T(8,128)(2,1)S(1)}, u32[]{:S(2)}, u32[]{:S(2)}) collective-permute-start(bf16[224,1024]{1,0:T(8,128)(2,1)S(1)} %shard_map.118), channel_id=1, source_target_pairs={{0,1},{1,0},{2,3},{3,2},{4,7},{5,6},{6,5},{7,4},{8,9},{9,8},{10,11... | collective-permute-start | bytes 1376264 | tf_op jit(solution)/shard_map/ppermute | solution.py:27
  56.6 1.7 %shard_map.120 = (bf16[32,1024]{1,0:T(8,128)(2,1)S(1)}, f32[32,1024]{1,0:T(8,128)S(1)}) custom-call(bf16[1024,1024]{1,0:T(8,128)(2,1)S(1)} %copy-done, bf16[1024,1024]{1,0:T(8,128)(2,1)S(1)} %copy-done.2, bf16[32,2048]{1,0:T(8,128)(2,1)S(1)} %shard_map.113.own.pooled), custom_call_target="tpu_custom_call" | custom-call | flops 201326592 | bytes 4521984 | tf_op jit(solution)/shard_map/pallas_call | solution.py:56
  58.3 2.5 %collective-permute-done.15.refs_5_ = bf16[128,1024]{1,0:T(8,128)(2,1)S(1)} collective-permute-done((bf16[128,1024]{1,0:T(8,128)(2,1)S(1)}, bf16[128,1024]{1,0:T(8,128)(2,1)S(1)}, u32[]{:S(2)}, u32[]{:S(2)}) %collective-permute-start.15) | collective-permute-done | bytes 262176 | tf_op jit(solution)/shard_map/ppermute | solution.py:37
  63.1 2.2 %collective-permute-start.16 = (bf16[512,1024]{1,0:T(8,128)(2,1)S(1)}, bf16[512,1024]{1,0:T(8,128)(2,1)S(1)}, u32[]{:S(2)}, u32[]{:S(2)}) collective-permute-start(bf16[512,1024]{1,0:T(8,128)(2,1)S(1)} %shard_map.121), channel_id=1, source_target_pairs={{0,4},{4,0},{1,5},{5,1},{2,6},{6,2},{3,7},{7,3},{8,12},{12,8},{9,1... | collective-permute-start | bytes 3145736 | tf_op jit(solution)/shard_map/ppermute | solution.py:18
  70.6 2.3 %collective-permute-start.19 = (bf16[128,1024]{1,0:T(8,128)(2,1)S(1)}, bf16[128,1024]{1,0:T(8,128)(2,1)S(1)}, u32[]{:S(2)}, u32[]{:S(2)}) collective-permute-start(bf16[128,1024]{1,0:T(8,128)(2,1)S(1)} %get-tuple-element.48), channel_id=1, source_target_pairs={{0,24},{4,100},{8,16},{12,108},{16,8},{20,116},{24,0},{28,124},{32... | collective-permute-start | bytes 786440 | tf_op jit(solution)/shard_map/ppermute | solution.py:37
  72.9 2.0 %collective-permute-done.21.refs_7_ = bf16[128,1024]{1,0:T(8,128)(2,1)S(1)} collective-permute-done((bf16[128,1024]{1,0:T(8,128)(2,1)S(1)}, bf16[128,1024]{1,0:T(8,128)(2,1)S(1)}, u32[]{:S(2)}, u32[]{:S(2)}) %collective-permute-start.21) | collective-permute-done | bytes 262176 | tf_op jit(solution)/shard_map/ppermute | solution.py:37
  74.8 3.2 %collective-permute-done.18.refs_2_ = bf16[128,1024]{1,0:T(8,128)(2,1)S(1)} collective-permute-done((bf16[128,1024]{1,0:T(8,128)(2,1)S(1)}, bf16[128,1024]{1,0:T(8,128)(2,1)S(1)}, u32[]{:S(2)}, u32[]{:S(2)}) %collective-permute-start.18) | collective-permute-done | bytes 262176 | tf_op jit(solution)/shard_map/ppermute | solution.py:37
  78.0 2.4 %collective-permute-done.19.refs_3_ = bf16[128,1024]{1,0:T(8,128)(2,1)S(1)} collective-permute-done((bf16[128,1024]{1,0:T(8,128)(2,1)S(1)}, bf16[128,1024]{1,0:T(8,128)(2,1)S(1)}, u32[]{:S(2)}, u32[]{:S(2)}) %collective-permute-start.19) | collective-permute-done | bytes 262176 | tf_op jit(solution)/shard_map/ppermute | solution.py:37
  81.0 3.6 %collective-permute-start.23 = (bf16[32,2048]{1,0:T(8,128)(2,1)S(1)}, bf16[32,2048]{1,0:T(8,128)(2,1)S(1)}, u32[]{:S(2)}, u32[]{:S(2)}) collective-permute-start(bf16[32,2048]{1,0:T(8,128)(2,1)S(1)} %get-tuple-element.54), channel_id=1, source_target_pairs={{0,64},{4,20},{8,72},{12,28},{16,80},{20,4},{24,88},{28,12},{32,96... | collective-permute-start | bytes 393224 | tf_op jit(solution)/shard_map/ppermute | solution.py:37
  84.7 3.7 %collective-permute-done.23.two = bf16[32,2048]{1,0:T(8,128)(2,1)S(1)} collective-permute-done((bf16[32,2048]{1,0:T(8,128)(2,1)S(1)}, bf16[32,2048]{1,0:T(8,128)(2,1)S(1)}, u32[]{:S(2)}, u32[]{:S(2)}) %collective-permute-start.23) | collective-permute-done | bytes 131104 | tf_op jit(solution)/shard_map/ppermute | solution.py:37
  88.3 1.7 %collective-permute-done.24.three = bf16[32,2048]{1,0:T(8,128)(2,1)S(1)} collective-permute-done((bf16[32,2048]{1,0:T(8,128)(2,1)S(1)}, bf16[32,2048]{1,0:T(8,128)(2,1)S(1)}, u32[]{:S(2)}, u32[]{:S(2)}) %collective-permute-start.24) | collective-permute-done | bytes 131104 | tf_op jit(solution)/shard_map/ppermute | solution.py:37
  90.6 3.4 %collective-permute-start.26 = (bf16[32,2048]{1,0:T(8,128)(2,1)S(1)}, bf16[32,2048]{1,0:T(8,128)(2,1)S(1)}, u32[]{:S(2)}, u32[]{:S(2)}) collective-permute-start(bf16[32,2048]{1,0:T(8,128)(2,1)S(1)} %get-tuple-element.57.own), channel_id=1, source_target_pairs={{0,2},{1,3},{2,0},{3,1},{4,6},{5,7},{6,4},{7,5},{8,10},{9,11},{10,... | collective-permute-start | bytes 393224 | tf_op jit(solution)/shard_map/ppermute | solution.py:22
  94.5 14.5 %all_to_all.12 = bf16[32,2,1024]{2,1,0:T(2,128)(2,1)S(1)} all-to-all(bf16[32,2,1024]{2,1,0:T(2,128)(2,1)S(1)} %all_to_all.8), channel_id=1, replica_groups=mesh['y'=4,'z'=4,'c'=2,'x'=4] {'y','z','c'}, dimensions={0} | all-to-all | bytes 262144 | tf_op jit(solution)/shard_map/all_to_all | solution.py:381
  (68 shorter events, 24.0 us)
Async XLA Ops:
  9.0 19.3 %collective-permute-start.10 = (bf16[672,1024]{1,0:T(8,128)(2,1)}, bf16[672,1024]{1,0:T(8,128)(2,1)S(1)}, u32[]{:S(2)}, u32[]{:S(2)}) collective-permute-start(bf16[672,1024]{1,0:T(8,128)(2,1)} %get-tuple-element.32), channel_id=1, source_target_pairs={{0,1},{1,0},{2,3},{3,2},{4,7},{5,6},{6,5},{7,4},{8,9},{9,8},{10,11... | collective-permute-start | bytes 4128776 | tf_op jit(solution)/shard_map/ppermute | solution.py:27
  14.0 6.7 %collective-permute-start.1 = (bf16[32,2048]{1,0:T(8,128)(2,1)S(1)}, bf16[32,2048]{1,0:T(8,128)(2,1)S(1)}, u32[]{:S(2)}, u32[]{:S(2)}) collective-permute-start(bf16[32,2048]{1,0:T(8,128)(2,1)S(1)} %shard_map.113.own.pooled), channel_id=1, source_target_pairs={{0,16},{4,68},{8,24},{12,76},{16,0},{20,84},{24,8},{28,92},{32,48}... | collective-permute-start | bytes 393224 | tf_op jit(solution)/shard_map/ppermute | solution.py:37
  16.7 5.2 %collective-permute-start.2 = (bf16[32,2048]{1,0:T(8,128)(2,1)S(1)}, bf16[32,2048]{1,0:T(8,128)(2,1)S(1)}, u32[]{:S(2)}, u32[]{:S(2)}) collective-permute-start(bf16[32,2048]{1,0:T(8,128)(2,1)S(1)} %shard_map.113.own.pooled), channel_id=1, source_target_pairs={{0,24},{4,100},{8,16},{12,108},{16,8},{20,116},{24,0},{28,124},{32... | collective-permute-start | bytes 393224 | tf_op jit(solution)/shard_map/ppermute | solution.py:37
  21.9 10.3 %collective-permute-start.4 = (bf16[128,2048]{1,0:T(8,128)(2,1)S(1)}, bf16[128,2048]{1,0:T(8,128)(2,1)S(1)}, u32[]{:S(2)}, u32[]{:S(2)}) collective-permute-start(bf16[128,2048]{1,0:T(8,128)(2,1)S(1)} %shard_map.114.r0), channel_id=1, source_target_pairs={{0,32},{4,12},{8,40},{12,4},{16,48},{20,28},{24,56},{28,20},{32,0}... | collective-permute-start | bytes 1572872 | tf_op jit(solution)/shard_map/ppermute | solution.py:37
  23.6 15.8 %collective-permute-start.6 = (bf16[128,2048]{1,0:T(8,128)(2,1)S(1)}, bf16[128,2048]{1,0:T(8,128)(2,1)S(1)}, u32[]{:S(2)}, u32[]{:S(2)}) collective-permute-start(bf16[128,2048]{1,0:T(8,128)(2,1)S(1)} %shard_map.114.r0), channel_id=1, source_target_pairs={{0,64},{4,20},{8,72},{12,28},{16,80},{20,4},{24,88},{28,12},{32,96... | collective-permute-start | bytes 1572872 | tf_op jit(solution)/shard_map/ppermute | solution.py:37
  26.9 15.2 %collective-permute-start.8 = (bf16[128,2048]{1,0:T(8,128)(2,1)S(1)}, bf16[128,2048]{1,0:T(8,128)(2,1)S(1)}, u32[]{:S(2)}, u32[]{:S(2)}) collective-permute-start(bf16[128,2048]{1,0:T(8,128)(2,1)S(1)} %shard_map.114.r0), channel_id=1, source_target_pairs={{0,96},{4,28},{8,104},{12,20},{16,112},{20,12},{24,120},{28,4},{32... | collective-permute-start | bytes 1572872 | tf_op jit(solution)/shard_map/ppermute | solution.py:37
  28.5 16.2 %collective-permute-start.11 = (bf16[336,1024]{1,0:T(8,128)(2,1)S(1)}, bf16[336,1024]{1,0:T(8,128)(2,1)S(1)}, u32[]{:S(2)}, u32[]{:S(2)}) collective-permute-start(bf16[336,1024]{1,0:T(8,128)(2,1)S(1)} %get-tuple-element.36), channel_id=1, source_target_pairs={{0,3},{1,2},{2,1},{3,0},{4,5},{5,4},{6,7},{7,6},{8,11},{9,10},{10,... | collective-permute-start | bytes 2064392 | tf_op jit(solution)/shard_map/ppermute | solution.py:27
  29.1 16.9 %collective-permute-start.3 = (bf16[128,2048]{1,0:T(8,128)(2,1)S(1)}, bf16[128,2048]{1,0:T(8,128)(2,1)S(1)}, u32[]{:S(2)}, u32[]{:S(2)}) collective-permute-start(bf16[128,2048]{1,0:T(8,128)(2,1)S(1)} %shard_map.114.r0), channel_id=1, source_target_pairs={{0,4},{4,0},{1,5},{5,1},{2,6},{6,2},{3,7},{7,3},{8,12},{12,8},{9,1... | collective-permute-start | bytes 1572872 | tf_op jit(solution)/shard_map/ppermute | solution.py:18
  32.2 13.8 %collective-permute-start.5 = (bf16[128,2048]{1,0:T(8,128)(2,1)S(1)}, bf16[128,2048]{1,0:T(8,128)(2,1)S(1)}, u32[]{:S(2)}, u32[]{:S(2)}) collective-permute-start(bf16[128,2048]{1,0:T(8,128)(2,1)S(1)} %collective-permute-done.4.r1), channel_id=1, source_target_pairs={{0,4},{4,0},{1,5},{5,1},{2,6},{6,2},{3,7},{7,3},{8,12},{12,8},{9,1... | collective-permute-start | bytes 1572872 | tf_op jit(solution)/shard_map/ppermute | solution.py:18
  39.4 6.6 %collective-permute-start.7 = (bf16[128,2048]{1,0:T(8,128)(2,1)S(1)}, bf16[128,2048]{1,0:T(8,128)(2,1)S(1)}, u32[]{:S(2)}, u32[]{:S(2)}) collective-permute-start(bf16[128,2048]{1,0:T(8,128)(2,1)S(1)} %collective-permute-done.6.r2), channel_id=1, source_target_pairs={{0,4},{4,0},{1,5},{5,1},{2,6},{6,2},{3,7},{7,3},{8,12},{12,8},{9,1... | collective-permute-start | bytes 1572872 | tf_op jit(solution)/shard_map/ppermute | solution.py:18
  47.5 7.6 %collective-permute-start.14 = (bf16[512,1024]{1,0:T(8,128)(2,1)S(1)}, bf16[512,1024]{1,0:T(8,128)(2,1)S(1)}, u32[]{:S(2)}, u32[]{:S(2)}) collective-permute-start(bf16[512,1024]{1,0:T(8,128)(2,1)S(1)} %get-tuple-element.41), channel_id=1, source_target_pairs={{0,4},{4,0},{1,5},{5,1},{2,6},{6,2},{3,7},{7,3},{8,12},{12,8},{9,1... | collective-permute-start | bytes 3145736 | tf_op jit(solution)/shard_map/ppermute | solution.py:18
  47.9 5.2 %collective-permute-start.12 = (bf16[112,1024]{1,0:T(8,128)(2,1)S(1)}, bf16[112,1024]{1,0:T(8,128)(2,1)S(1)}, u32[]{:S(2)}, u32[]{:S(2)}) collective-permute-start(bf16[112,1024]{1,0:T(8,128)(2,1)S(1)} %get-tuple-element.39.own), channel_id=1, source_target_pairs={{0,3},{1,2},{2,1},{3,0},{4,5},{5,4},{6,7},{7,6},{8,11},{9,10},{10,... | collective-permute-start | bytes 688136 | tf_op jit(solution)/shard_map/ppermute | solution.py:27
  53.1 8.6 %collective-permute-start.13 = (bf16[224,1024]{1,0:T(8,128)(2,1)S(1)}, bf16[224,1024]{1,0:T(8,128)(2,1)S(1)}, u32[]{:S(2)}, u32[]{:S(2)}) collective-permute-start(bf16[224,1024]{1,0:T(8,128)(2,1)S(1)} %shard_map.118), channel_id=1, source_target_pairs={{0,1},{1,0},{2,3},{3,2},{4,7},{5,6},{6,5},{7,4},{8,9},{9,8},{10,11... | collective-permute-start | bytes 1376264 | tf_op jit(solution)/shard_map/ppermute | solution.py:27
  55.2 5.6 %collective-permute-start.15 = (bf16[128,1024]{1,0:T(8,128)(2,1)S(1)}, bf16[128,1024]{1,0:T(8,128)(2,1)S(1)}, u32[]{:S(2)}, u32[]{:S(2)}) collective-permute-start(bf16[128,1024]{1,0:T(8,128)(2,1)S(1)} %get-tuple-element.42), channel_id=1, source_target_pairs={{0,8},{4,36},{8,0},{12,44},{16,24},{20,52},{24,16},{28,60},{32,40}... | collective-permute-start | bytes 786440 | tf_op jit(solution)/shard_map/ppermute | solution.py:37
  65.3 7.6 %collective-permute-start.20 = (bf16[128,1024]{1,0:T(8,128)(2,1)S(1)}, bf16[128,1024]{1,0:T(8,128)(2,1)S(1)}, u32[]{:S(2)}, u32[]{:S(2)}) collective-permute-start(bf16[128,1024]{1,0:T(8,128)(2,1)S(1)} %get-tuple-element.50), channel_id=1, source_target_pairs={{0,16},{4,68},{8,24},{12,76},{16,0},{20,84},{24,8},{28,92},{32,48}... | collective-permute-start | bytes 786440 | tf_op jit(solution)/shard_map/ppermute | solution.py:37
  65.3 9.5 %collective-permute-start.21 = (bf16[128,1024]{1,0:T(8,128)(2,1)S(1)}, bf16[128,1024]{1,0:T(8,128)(2,1)S(1)}, u32[]{:S(2)}, u32[]{:S(2)}) collective-permute-start(bf16[128,1024]{1,0:T(8,128)(2,1)S(1)} %get-tuple-element.51), channel_id=1, source_target_pairs={{0,24},{4,100},{8,16},{12,108},{16,8},{20,116},{24,0},{28,124},{32... | collective-permute-start | bytes 786440 | tf_op jit(solution)/shard_map/ppermute | solution.py:37
  68.9 5.9 %collective-permute-start.17 = (bf16[128,1024]{1,0:T(8,128)(2,1)S(1)}, bf16[128,1024]{1,0:T(8,128)(2,1)S(1)}, u32[]{:S(2)}, u32[]{:S(2)}) collective-permute-start(bf16[128,1024]{1,0:T(8,128)(2,1)S(1)} %get-tuple-element.46), channel_id=1, source_target_pairs={{0,8},{4,36},{8,0},{12,44},{16,24},{20,52},{24,16},{28,60},{32,40}... | collective-permute-start | bytes 786440 | tf_op jit(solution)/shard_map/ppermute | solution.py:37
  69.4 8.7 %collective-permute-start.18 = (bf16[128,1024]{1,0:T(8,128)(2,1)S(1)}, bf16[128,1024]{1,0:T(8,128)(2,1)S(1)}, u32[]{:S(2)}, u32[]{:S(2)}) collective-permute-start(bf16[128,1024]{1,0:T(8,128)(2,1)S(1)} %get-tuple-element.47), channel_id=1, source_target_pairs={{0,16},{4,68},{8,24},{12,76},{16,0},{20,84},{24,8},{28,92},{32,48}... | collective-permute-start | bytes 786440 | tf_op jit(solution)/shard_map/ppermute | solution.py:37
  70.6 9.9 %collective-permute-start.19 = (bf16[128,1024]{1,0:T(8,128)(2,1)S(1)}, bf16[128,1024]{1,0:T(8,128)(2,1)S(1)}, u32[]{:S(2)}, u32[]{:S(2)}) collective-permute-start(bf16[128,1024]{1,0:T(8,128)(2,1)S(1)} %get-tuple-element.48), channel_id=1, source_target_pairs={{0,24},{4,100},{8,16},{12,108},{16,8},{20,116},{24,0},{28,124},{32... | collective-permute-start | bytes 786440 | tf_op jit(solution)/shard_map/ppermute | solution.py:37
  81.0 7.4 %collective-permute-start.23 = (bf16[32,2048]{1,0:T(8,128)(2,1)S(1)}, bf16[32,2048]{1,0:T(8,128)(2,1)S(1)}, u32[]{:S(2)}, u32[]{:S(2)}) collective-permute-start(bf16[32,2048]{1,0:T(8,128)(2,1)S(1)} %get-tuple-element.54), channel_id=1, source_target_pairs={{0,64},{4,20},{8,72},{12,28},{16,80},{20,4},{24,88},{28,12},{32,96... | collective-permute-start | bytes 393224 | tf_op jit(solution)/shard_map/ppermute | solution.py:37
  84.6 5.5 %collective-permute-start.24 = (bf16[32,2048]{1,0:T(8,128)(2,1)S(1)}, bf16[32,2048]{1,0:T(8,128)(2,1)S(1)}, u32[]{:S(2)}, u32[]{:S(2)}) collective-permute-start(bf16[32,2048]{1,0:T(8,128)(2,1)S(1)} %get-tuple-element.55), channel_id=1, source_target_pairs={{0,96},{4,28},{8,104},{12,20},{16,112},{20,12},{24,120},{28,4},{32... | collective-permute-start | bytes 393224 | tf_op jit(solution)/shard_map/ppermute | solution.py:37
  90.5 19.2 %collective-permute-start.25 = (bf16[32,2048]{1,0:T(8,128)(2,1)S(1)}, bf16[32,2048]{1,0:T(8,128)(2,1)S(1)}, u32[]{:S(2)}, u32[]{:S(2)}) collective-permute-start(bf16[32,2048]{1,0:T(8,128)(2,1)S(1)} %get-tuple-element.57.own), channel_id=1, source_target_pairs={{0,1},{1,0},{2,3},{3,2},{4,5},{5,4},{6,7},{7,6},{8,9},{9,8},{10,11... | collective-permute-start | bytes 393224 | tf_op jit(solution)/shard_map/ppermute | solution.py:22
  90.6 19.1 %collective-permute-start.26 = (bf16[32,2048]{1,0:T(8,128)(2,1)S(1)}, bf16[32,2048]{1,0:T(8,128)(2,1)S(1)}, u32[]{:S(2)}, u32[]{:S(2)}) collective-permute-start(bf16[32,2048]{1,0:T(8,128)(2,1)S(1)} %get-tuple-element.57.own), channel_id=1, source_target_pairs={{0,2},{1,3},{2,0},{3,1},{4,6},{5,7},{6,4},{7,5},{8,10},{9,11},{10,... | collective-permute-start | bytes 393224 | tf_op jit(solution)/shard_map/ppermute | solution.py:22
  94.0 15.7 %collective-permute-start.27 = (bf16[32,2048]{1,0:T(8,128)(2,1)S(1)}, bf16[32,2048]{1,0:T(8,128)(2,1)S(1)}, u32[]{:S(2)}, u32[]{:S(2)}) collective-permute-start(bf16[32,2048]{1,0:T(8,128)(2,1)S(1)} %get-tuple-element.57.own), channel_id=1, source_target_pairs={{0,3},{1,2},{2,1},{3,0},{4,7},{5,6},{6,5},{7,4},{8,11},{9,10},{10,... | collective-permute-start | bytes 393224 | tf_op jit(solution)/shard_map/ppermute | solution.py:22
  (13 other events, 114.3 us)

commit v9 on v8

--- a/solution.py
+++ b/solution.py
@@ -99,8 +99,15 @@
         out[k * span : (k + 1) * span] = block[...]
 
 
-def cut_products(count, offsets, whole, keep, send):
+def block_offsets(part):
+    x = lax.axis_index("x")
+    step = jnp.where(lax.axis_index("c") == 0, 1, 3)
+    return [x * part, (x ^ step ^ 2) * part, (x ^ step) * part, (x ^ 2) * part]
+
+
+def cut_products(count, whole, keep, send):
     part = keep.shape[0] // (2 * count)
+    offsets = block_offsets(part)
     for k in range(4):
         out = keep if k < 2 else send
         for i in range(count):
@@ -109,29 +116,36 @@
             out[to : to + part] = whole[pl.ds(place, part), :]
 
 
-def product_kernel(offsets, *refs):
+def product_kernel(*refs):
     sources, (keep, send), (w_enc, w_gate, w_lift, w_down, w_dec, whole, sems) = (
         refs[:5],
         refs[5:7],
         refs[7:],
     )
     targets = (w_enc, w_gate, w_lift, w_down, w_dec)
+    half = w_enc.shape[0] // 2
+    pairs = list(zip(sources[1:], targets[1:]))
+    pairs[1:1] = [
+        (sources[0].at[pl.ds(i * half, half)], w_enc.at[pl.ds(i * half, half)]) for i in range(2)
+    ]
     copies = [
         pltpu.make_async_copy(source, target, sems.at[i])
-        for i, (source, target) in enumerate(zip(sources, targets))
+        for i, (source, target) in enumerate(pairs)
     ]
     for copy in copies:
         copy.start()
     hid = w_gate.shape[0]
     copies[0].wait()
-    copies[1].wait()
-    whole[:hid] = dot_t(w_gate[...], w_enc[...]).astype(BF16)
-    copies[2].wait()
+    for i in range(2):
+        copies[1 + i].wait()
+        columns = slice(i * half, (i + 1) * half)
+        whole[:hid, columns] = dot_t(w_gate[...], w_enc[columns]).astype(BF16)
+    copies[3].wait()
     whole[hid : 2 * hid] = dot_t(w_lift[...], w_enc[...]).astype(BF16)
-    copies[3].wait()
     copies[4].wait()
+    copies[5].wait()
     whole[2 * hid :] = dot(w_down[...], w_dec[...]).astype(BF16)
-    cut_products(3, offsets, whole, keep, send)
+    cut_products(3, whole, keep, send)
 
 
 def encode_kernel(w_dec, w_enc, pooled, rep, back):
@@ -187,16 +201,17 @@
     out[part:] = second[...]
 
 
-def stack_hidden(offsets, own, second, others, low, stack):
+def stack_hidden(own, second, others, low, stack):
     part, span = own.shape[0], stack.shape[1]
     blocks = (own, second, others.at[:part], others.at[part:])
+    offsets = block_offsets(part)
     for k, block in enumerate(blocks):
         place = pl.multiple_of(offsets[k], 16)
         stack[pl.ds(place, part), :] = block[:, low : low + span]
 
 
-def down_far_kernel(offsets, own, second, others, w_down, out, stack):
-    stack_hidden(offsets, own, second, others, out.shape[0], stack)
+def down_far_kernel(own, second, others, w_down, out, stack):
+    stack_hidden(own, second, others, out.shape[0], stack)
     out[...] = dot(stack[...].T, w_down[...]).astype(BF16)
 
 
@@ -204,9 +219,9 @@
     place_blocks(partial[...] + other[...].astype(F32), outs)
 
 
-def down_near_kernel(offsets, own, second, others, w_down, other, *rest):
+def down_near_kernel(own, second, others, w_down, other, *rest):
     stack = rest[-1]
-    stack_hidden(offsets, own, second, others, 0, stack)
+    stack_hidden(own, second, others, 0, stack)
     place_blocks(dot(stack[...].T, w_down[...]) + other[...].astype(F32), rest[:-1])
 
 
@@ -267,9 +282,6 @@
     hid = w_gate.shape[1]
     part = hid // 4
     group = 16 * patches
-    x, core = lax.axis_index("x"), lax.axis_index("c")
-    step = jnp.where(core == 0, 1, 3)
-    halving = (jnp.stack([x, x ^ step ^ 2, x ^ step, x ^ 2]) * part).astype(jnp.int32)
     owners = patch_owner.reshape(1, patches)
     w_gate, w_lift = w_gate.T, w_lift.T
 
@@ -295,10 +307,9 @@
         product_kernel,
         [shape((6 * part, width), BF16)] * 2,
         weights,
-        [halving],
         flops=6 * hid * width * latent,
         scratch=[pltpu.VMEM(w.shape, BF16) for w in weights]
-        + [pltpu.VMEM((3 * hid, width), BF16), pltpu.SemaphoreType.DMA((5,))],
+        + [pltpu.VMEM((3 * hid, width), BF16), pltpu.SemaphoreType.DMA((6,))],
         outside=True,
     )
     first = swap_near(send, True)
@@ -353,8 +364,7 @@
     (far_rows,) = call(
         down_far_kernel,
         [shape((group, latent), BF16)],
-        [*hiddens, after(w_down, (grad_first[1], back))],
-        [halving],
+        [*hiddens, after(w_down, (grad_first[2], back))],
         flops=2 * group * latent * hid,
         scratch=[pltpu.VMEM((hid, group), BF16)],
     )
@@ -362,7 +372,6 @@
         down_near_kernel,
         [shape((4 * patches, latent), BF16)] * 4,
         [*hiddens, w_down, swap_core(far_rows)],
-        [halving],
         flops=2 * group * latent * hid,
         scratch=[pltpu.VMEM((hid, group), BF16)],
     )

time: 111 us -> 109 us (0.982)
  Pallas kernels: 17.5 us -> 15.6 us
  starting transfers between devices: 39.8 us -> 38.2 us
    pallas_call x14, Pallas kernels: 17.5 us -> 15.6 us  [call(): pl.pallas_call(body, out_shape=outs, in_specs=specs, out_specs=[pl.BlockS...]
  transfers between devices with their start and end apart: 28 -> 28, of which waited for: 16 -> 15; matrix products, arithmetic and copies ran while one was open for 0% -> 0% of each run, Pallas kernels for 5% -> 4%
where the time goes in v9:
time: 109 us
  starting transfers between devices  38.2 us (35%)
  waiting for transfers between devices  36.9 us (34%)
  Pallas kernels  15.6 us (14%)
  blocking collectives  15 us (14%)
  local copies, waits for them, and re-layouts  2.09 us (2%)
    ppermute x15, waiting for transfers between devices, swap_first(): return lax.ppermute(value, SEQ, pairs)  28.1 us
    ppermute x15, starting transfers between devices, swap_first(): return lax.ppermute(value, SEQ, pairs)  16.9 us
    pallas_call x14, Pallas kernels, call(): pl.pallas_call(body, out_shape=outs, in_specs=specs, out_specs=[pl.BlockS...  15.6 us
    all_to_all x1, blocking collectives, on_device(): lax.all_to_all(outgoing, SEQ, split_axis=0, concat_axis=0, tiled=True)  15 us
    ppermute x6, starting transfers between devices, swap_core(): return lax.ppermute(value, 'c', [(0, 1), (1, 0)])  11.2 us
    ppermute x4, waiting for transfers between devices, swap_near(): lax.ppermute(value, ('c', 'x'), [(c * 4 + x, c * 4 + (x ^ steps[c])) for...  6.3 us
    ppermute x4, starting transfers between devices, swap_near(): lax.ppermute(value, ('c', 'x'), [(c * 4 + x, c * 4 + (x ^ steps[c])) for...  6.09 us
    ppermute x3, starting transfers between devices, swap_x(): return lax.ppermute(value, 'x', [(i, i ^ k) for i in range(4)])  4.01 us
  transfers between devices with their start and end apart: 28, of which 15 were waited for; matrix products, arithmetic and copies ran while one was open for 0% of the time, Pallas kernels for 4%

profile of v9, /device:TPU:1, one launch (start us, length us, event | category | flops | bytes accessed | tf_op | source)
XLA Modules:
  0.0 108.6 jit_solution(18396276738829845064)
XLA Ops:
  0.7 6.9 %shard_map.112 = (bf16[672,1024]{1,0:T(8,128)(2,1)}, bf16[672,1024]{1,0:T(8,128)(2,1)}) custom-call(bf16[1024,1024]{1,0:T(8,128)(2,1)} %w_enc.1, bf16[448,1024]{1,0:T(8,128)(2,1)} %bitcast.4, bf16[448,1024]{1,0:T(8,128)(2,1)} %bitcast.5, bf16[448,1024]{1,0:T(8,128)(2,1)} %w_down.2, bf16[1024,1024]{1,0:T(8,128)(2,1)} %weight.1), custom_call_target="tpu_custom_call" | custom-call | flops 2818572288 | bytes 9699328 | tf_op jit(solution)/shard_map/pallas_call | solution.py:56
  7.6 3.4 %collective-permute-start.10 = (bf16[672,1024]{1,0:T(8,128)(2,1)}, bf16[672,1024]{1,0:T(8,128)(2,1)S(1)}, u32[]{:S(2)}, u32[]{:S(2)}) collective-permute-start(bf16[672,1024]{1,0:T(8,128)(2,1)} %get-tuple-element.32), channel_id=1, source_target_pairs={{0,1},{1,0},{2,3},{3,2},{4,7},{5,6},{6,5},{7,4},{8,9},{9,8},{10,11... | collective-permute-start | bytes 4128776 | tf_op jit(solution)/shard_map/ppermute | solution.py:27
  12.7 2.6 %collective-permute-start.1 = (bf16[32,2048]{1,0:T(8,128)(2,1)S(1)}, bf16[32,2048]{1,0:T(8,128)(2,1)S(1)}, u32[]{:S(2)}, u32[]{:S(2)}) collective-permute-start(bf16[32,2048]{1,0:T(8,128)(2,1)S(1)} %shard_map.113.own.pooled), channel_id=1, source_target_pairs={{0,16},{4,68},{8,24},{12,76},{16,0},{20,84},{24,8},{28,92},{32,48}... | collective-permute-start | bytes 393224 | tf_op jit(solution)/shard_map/ppermute | solution.py:37
  15.5 3.8 %collective-permute-done.1.two = bf16[32,2048]{1,0:T(8,128)(2,1)S(1)} collective-permute-done((bf16[32,2048]{1,0:T(8,128)(2,1)S(1)}, bf16[32,2048]{1,0:T(8,128)(2,1)S(1)}, u32[]{:S(2)}, u32[]{:S(2)}) %collective-permute-start.1) | collective-permute-done | bytes 131104 | tf_op jit(solution)/shard_map/ppermute | solution.py:37
  20.5 1.7 %collective-permute-start.4 = (bf16[128,2048]{1,0:T(8,128)(2,1)S(1)}, bf16[128,2048]{1,0:T(8,128)(2,1)S(1)}, u32[]{:S(2)}, u32[]{:S(2)}) collective-permute-start(bf16[128,2048]{1,0:T(8,128)(2,1)S(1)} %shard_map.114.r0), channel_id=1, source_target_pairs={{0,32},{4,12},{8,40},{12,4},{16,48},{20,28},{24,56},{28,20},{32,0}... | collective-permute-start | bytes 1572872 | tf_op jit(solution)/shard_map/ppermute | solution.py:37
  22.2 3.3 %collective-permute-start.6 = (bf16[128,2048]{1,0:T(8,128)(2,1)S(1)}, bf16[128,2048]{1,0:T(8,128)(2,1)S(1)}, u32[]{:S(2)}, u32[]{:S(2)}) collective-permute-start(bf16[128,2048]{1,0:T(8,128)(2,1)S(1)} %shard_map.114.r0), channel_id=1, source_target_pairs={{0,64},{4,20},{8,72},{12,28},{16,80},{20,4},{24,88},{28,12},{32,96... | collective-permute-start | bytes 1572872 | tf_op jit(solution)/shard_map/ppermute | solution.py:37
  27.7 3.1 %collective-permute-start.3 = (bf16[128,2048]{1,0:T(8,128)(2,1)S(1)}, bf16[128,2048]{1,0:T(8,128)(2,1)S(1)}, u32[]{:S(2)}, u32[]{:S(2)}) collective-permute-start(bf16[128,2048]{1,0:T(8,128)(2,1)S(1)} %shard_map.114.r0), channel_id=1, source_target_pairs={{0,4},{4,0},{1,5},{5,1},{2,6},{6,2},{3,7},{7,3},{8,12},{12,8},{9,1... | collective-permute-start | bytes 1572872 | tf_op jit(solution)/shard_map/ppermute | solution.py:18
  32.0 6.0 %collective-permute-done.6.r2 = bf16[128,2048]{1,0:T(8,128)(2,1)S(1)} collective-permute-done((bf16[128,2048]{1,0:T(8,128)(2,1)S(1)}, bf16[128,2048]{1,0:T(8,128)(2,1)S(1)}, u32[]{:S(2)}, u32[]{:S(2)}) %collective-permute-start.6) | collective-permute-done | bytes 524320 | tf_op jit(solution)/shard_map/ppermute | solution.py:37
  38.0 2.2 %collective-permute-start.7 = (bf16[128,2048]{1,0:T(8,128)(2,1)S(1)}, bf16[128,2048]{1,0:T(8,128)(2,1)S(1)}, u32[]{:S(2)}, u32[]{:S(2)}) collective-permute-start(bf16[128,2048]{1,0:T(8,128)(2,1)S(1)} %collective-permute-done.6.r2), channel_id=1, source_target_pairs={{0,4},{4,0},{1,5},{5,1},{2,6},{6,2},{3,7},{7,3},{8,12},{12,8},{9,1... | collective-permute-start | bytes 1572872 | tf_op jit(solution)/shard_map/ppermute | solution.py:18
  40.7 2.7 %collective-permute-start.9 = (bf16[128,2048]{1,0:T(8,128)(2,1)S(1)}, bf16[128,2048]{1,0:T(8,128)(2,1)S(1)}, u32[]{:S(2)}, u32[]{:S(2)}) collective-permute-start(bf16[128,2048]{1,0:T(8,128)(2,1)S(1)} %collective-permute-done.8.r3), channel_id=1, source_target_pairs={{0,4},{4,0},{1,5},{5,1},{2,6},{6,2},{3,7},{7,3},{8,12},{12,8},{9,1... | collective-permute-start | bytes 1572872 | tf_op jit(solution)/shard_map/ppermute | solution.py:18
  46.8 4.9 %collective-permute-done.12.second = bf16[112,1024]{1,0:T(8,128)(2,1)S(1)} collective-permute-done((bf16[112,1024]{1,0:T(8,128)(2,1)S(1)}, bf16[112,1024]{1,0:T(8,128)(2,1)S(1)}, u32[]{:S(2)}, u32[]{:S(2)}) %collective-permute-start.12) | collective-permute-done | bytes 229408 | tf_op jit(solution)/shard_map/ppermute | solution.py:27
  51.8 1.9 %collective-permute-start.13 = (bf16[224,1024]{1,0:T(8,128)(2,1)S(1)}, bf16[224,1024]{1,0:T(8,128)(2,1)S(1)}, u32[]{:S(2)}, u32[]{:S(2)}) collective-permute-start(bf16[224,1024]{1,0:T(8,128)(2,1)S(1)} %shard_map.118), channel_id=1, source_target_pairs={{0,1},{1,0},{2,3},{3,2},{4,7},{5,6},{6,5},{7,4},{8,9},{9,8},{10,11... | collective-permute-start | bytes 1376264 | tf_op jit(solution)/shard_map/ppermute | solution.py:27
  55.2 1.7 %shard_map.120 = (bf16[32,1024]{1,0:T(8,128)(2,1)S(1)}, f32[32,1024]{1,0:T(8,128)S(1)}) custom-call(bf16[1024,1024]{1,0:T(8,128)(2,1)S(1)} %copy-done, bf16[1024,1024]{1,0:T(8,128)(2,1)S(1)} %copy-done.2, bf16[32,2048]{1,0:T(8,128)(2,1)S(1)} %shard_map.113.own.pooled), custom_call_target="tpu_custom_call" | custom-call | flops 201326592 | bytes 4521984 | tf_op jit(solution)/shard_map/pallas_call | solution.py:56
  56.9 4.0 %collective-permute-done.15.refs_6_ = bf16[128,1024]{1,0:T(8,128)(2,1)S(1)} collective-permute-done((bf16[128,1024]{1,0:T(8,128)(2,1)S(1)}, bf16[128,1024]{1,0:T(8,128)(2,1)S(1)}, u32[]{:S(2)}, u32[]{:S(2)}) %collective-permute-start.15) | collective-permute-done | bytes 262176 | tf_op jit(solution)/shard_map/ppermute | solution.py:37
  63.4 2.3 %collective-permute-done.16.other = bf16[512,1024]{1,0:T(8,128)(2,1)S(1)} collective-permute-done((bf16[512,1024]{1,0:T(8,128)(2,1)S(1)}, bf16[512,1024]{1,0:T(8,128)(2,1)S(1)}, u32[]{:S(2)}, u32[]{:S(2)}) %collective-permute-start.16) | collective-permute-done | bytes 1048608 | tf_op jit(solution)/shard_map/ppermute | solution.py:18
  68.1 2.3 %collective-permute-start.19 = (bf16[128,1024]{1,0:T(8,128)(2,1)S(1)}, bf16[128,1024]{1,0:T(8,128)(2,1)S(1)}, u32[]{:S(2)}, u32[]{:S(2)}) collective-permute-start(bf16[128,1024]{1,0:T(8,128)(2,1)S(1)} %get-tuple-element.48), channel_id=1, source_target_pairs={{0,24},{4,100},{8,16},{12,108},{16,8},{20,116},{24,0},{28,124},{32... | collective-permute-start | bytes 786440 | tf_op jit(solution)/shard_map/ppermute | solution.py:37
  70.4 1.7 %collective-permute-done.17.refs_1_ = bf16[128,1024]{1,0:T(8,128)(2,1)S(1)} collective-permute-done((bf16[128,1024]{1,0:T(8,128)(2,1)S(1)}, bf16[128,1024]{1,0:T(8,128)(2,1)S(1)}, u32[]{:S(2)}, u32[]{:S(2)}) %collective-permute-start.17) | collective-permute-done | bytes 262176 | tf_op jit(solution)/shard_map/ppermute | solution.py:37
  72.1 3.0 %collective-permute-done.18.refs_2_ = bf16[128,1024]{1,0:T(8,128)(2,1)S(1)} collective-permute-done((bf16[128,1024]{1,0:T(8,128)(2,1)S(1)}, bf16[128,1024]{1,0:T(8,128)(2,1)S(1)}, u32[]{:S(2)}, u32[]{:S(2)}) %collective-permute-start.18) | collective-permute-done | bytes 262176 | tf_op jit(solution)/shard_map/ppermute | solution.py:37
  75.0 2.6 %collective-permute-done.19.refs_3_ = bf16[128,1024]{1,0:T(8,128)(2,1)S(1)} collective-permute-done((bf16[128,1024]{1,0:T(8,128)(2,1)S(1)}, bf16[128,1024]{1,0:T(8,128)(2,1)S(1)}, u32[]{:S(2)}, u32[]{:S(2)}) %collective-permute-start.19) | collective-permute-done | bytes 262176 | tf_op jit(solution)/shard_map/ppermute | solution.py:37
  78.0 3.5 %collective-permute-start.23 = (bf16[32,2048]{1,0:T(8,128)(2,1)S(1)}, bf16[32,2048]{1,0:T(8,128)(2,1)S(1)}, u32[]{:S(2)}, u32[]{:S(2)}) collective-permute-start(bf16[32,2048]{1,0:T(8,128)(2,1)S(1)} %get-tuple-element.54), channel_id=1, source_target_pairs={{0,64},{4,20},{8,72},{12,28},{16,80},{20,4},{24,88},{28,12},{32,96... | collective-permute-start | bytes 393224 | tf_op jit(solution)/shard_map/ppermute | solution.py:37
  81.9 3.4 %collective-permute-done.23.two = bf16[32,2048]{1,0:T(8,128)(2,1)S(1)} collective-permute-done((bf16[32,2048]{1,0:T(8,128)(2,1)S(1)}, bf16[32,2048]{1,0:T(8,128)(2,1)S(1)}, u32[]{:S(2)}, u32[]{:S(2)}) %collective-permute-start.23) | collective-permute-done | bytes 131104 | tf_op jit(solution)/shard_map/ppermute | solution.py:37
  85.3 1.7 %collective-permute-done.24.three = bf16[32,2048]{1,0:T(8,128)(2,1)S(1)} collective-permute-done((bf16[32,2048]{1,0:T(8,128)(2,1)S(1)}, bf16[32,2048]{1,0:T(8,128)(2,1)S(1)}, u32[]{:S(2)}, u32[]{:S(2)}) %collective-permute-start.24) | collective-permute-done | bytes 131104 | tf_op jit(solution)/shard_map/ppermute | solution.py:37
  89.0 2.3 %collective-permute-start.26 = (bf16[32,2048]{1,0:T(8,128)(2,1)S(1)}, bf16[32,2048]{1,0:T(8,128)(2,1)S(1)}, u32[]{:S(2)}, u32[]{:S(2)}) collective-permute-start(bf16[32,2048]{1,0:T(8,128)(2,1)S(1)} %get-tuple-element.57.own), channel_id=1, source_target_pairs={{0,2},{1,3},{2,0},{3,1},{4,6},{5,7},{6,4},{7,5},{8,10},{9,11},{10,... | collective-permute-start | bytes 393224 | tf_op jit(solution)/shard_map/ppermute | solution.py:22
  91.6 15.0 %all_to_all.12 = bf16[32,2,1024]{2,1,0:T(2,128)(2,1)S(1)} all-to-all(bf16[32,2,1024]{2,1,0:T(2,128)(2,1)S(1)} %all_to_all.8), channel_id=1, replica_groups=mesh['y'=4,'z'=4,'c'=2,'x'=4] {'y','z','c'}, dimensions={0} | all-to-all | bytes 262144 | tf_op jit(solution)/shard_map/all_to_all | solution.py:390
  (65 shorter events, 22.0 us)
Async XLA Ops:
  7.6 19.3 %collective-permute-start.10 = (bf16[672,1024]{1,0:T(8,128)(2,1)}, bf16[672,1024]{1,0:T(8,128)(2,1)S(1)}, u32[]{:S(2)}, u32[]{:S(2)}) collective-permute-start(bf16[672,1024]{1,0:T(8,128)(2,1)} %get-tuple-element.32), channel_id=1, source_target_pairs={{0,1},{1,0},{2,3},{3,2},{4,7},{5,6},{6,5},{7,4},{8,9},{9,8},{10,11... | collective-permute-start | bytes 4128776 | tf_op jit(solution)/shard_map/ppermute | solution.py:27
  12.7 6.7 %collective-permute-start.1 = (bf16[32,2048]{1,0:T(8,128)(2,1)S(1)}, bf16[32,2048]{1,0:T(8,128)(2,1)S(1)}, u32[]{:S(2)}, u32[]{:S(2)}) collective-permute-start(bf16[32,2048]{1,0:T(8,128)(2,1)S(1)} %shard_map.113.own.pooled), channel_id=1, source_target_pairs={{0,16},{4,68},{8,24},{12,76},{16,0},{20,84},{24,8},{28,92},{32,48}... | collective-permute-start | bytes 393224 | tf_op jit(solution)/shard_map/ppermute | solution.py:37
  15.3 5.2 %collective-permute-start.2 = (bf16[32,2048]{1,0:T(8,128)(2,1)S(1)}, bf16[32,2048]{1,0:T(8,128)(2,1)S(1)}, u32[]{:S(2)}, u32[]{:S(2)}) collective-permute-start(bf16[32,2048]{1,0:T(8,128)(2,1)S(1)} %shard_map.113.own.pooled), channel_id=1, source_target_pairs={{0,24},{4,100},{8,16},{12,108},{16,8},{20,116},{24,0},{28,124},{32... | collective-permute-start | bytes 393224 | tf_op jit(solution)/shard_map/ppermute | solution.py:37
  20.5 10.3 %collective-permute-start.4 = (bf16[128,2048]{1,0:T(8,128)(2,1)S(1)}, bf16[128,2048]{1,0:T(8,128)(2,1)S(1)}, u32[]{:S(2)}, u32[]{:S(2)}) collective-permute-start(bf16[128,2048]{1,0:T(8,128)(2,1)S(1)} %shard_map.114.r0), channel_id=1, source_target_pairs={{0,32},{4,12},{8,40},{12,4},{16,48},{20,28},{24,56},{28,20},{32,0}... | collective-permute-start | bytes 1572872 | tf_op jit(solution)/shard_map/ppermute | solution.py:37
  22.2 15.8 %collective-permute-start.6 = (bf16[128,2048]{1,0:T(8,128)(2,1)S(1)}, bf16[128,2048]{1,0:T(8,128)(2,1)S(1)}, u32[]{:S(2)}, u32[]{:S(2)}) collective-permute-start(bf16[128,2048]{1,0:T(8,128)(2,1)S(1)} %shard_map.114.r0), channel_id=1, source_target_pairs={{0,64},{4,20},{8,72},{12,28},{16,80},{20,4},{24,88},{28,12},{32,96... | collective-permute-start | bytes 1572872 | tf_op jit(solution)/shard_map/ppermute | solution.py:37
  25.5 15.2 %collective-permute-start.8 = (bf16[128,2048]{1,0:T(8,128)(2,1)S(1)}, bf16[128,2048]{1,0:T(8,128)(2,1)S(1)}, u32[]{:S(2)}, u32[]{:S(2)}) collective-permute-start(bf16[128,2048]{1,0:T(8,128)(2,1)S(1)} %shard_map.114.r0), channel_id=1, source_target_pairs={{0,96},{4,28},{8,104},{12,20},{16,112},{20,12},{24,120},{28,4},{32... | collective-permute-start | bytes 1572872 | tf_op jit(solution)/shard_map/ppermute | solution.py:37
  27.2 16.1 %collective-permute-start.11 = (bf16[336,1024]{1,0:T(8,128)(2,1)S(1)}, bf16[336,1024]{1,0:T(8,128)(2,1)S(1)}, u32[]{:S(2)}, u32[]{:S(2)}) collective-permute-start(bf16[336,1024]{1,0:T(8,128)(2,1)S(1)} %get-tuple-element.36), channel_id=1, source_target_pairs={{0,3},{1,2},{2,1},{3,0},{4,5},{5,4},{6,7},{7,6},{8,11},{9,10},{10,... | collective-permute-start | bytes 2064392 | tf_op jit(solution)/shard_map/ppermute | solution.py:27
  27.7 16.9 %collective-permute-start.3 = (bf16[128,2048]{1,0:T(8,128)(2,1)S(1)}, bf16[128,2048]{1,0:T(8,128)(2,1)S(1)}, u32[]{:S(2)}, u32[]{:S(2)}) collective-permute-start(bf16[128,2048]{1,0:T(8,128)(2,1)S(1)} %shard_map.114.r0), channel_id=1, source_target_pairs={{0,4},{4,0},{1,5},{5,1},{2,6},{6,2},{3,7},{7,3},{8,12},{12,8},{9,1... | collective-permute-start | bytes 1572872 | tf_op jit(solution)/shard_map/ppermute | solution.py:18
  30.8 13.8 %collective-permute-start.5 = (bf16[128,2048]{1,0:T(8,128)(2,1)S(1)}, bf16[128,2048]{1,0:T(8,128)(2,1)S(1)}, u32[]{:S(2)}, u32[]{:S(2)}) collective-permute-start(bf16[128,2048]{1,0:T(8,128)(2,1)S(1)} %collective-permute-done.4.r1), channel_id=1, source_target_pairs={{0,4},{4,0},{1,5},{5,1},{2,6},{6,2},{3,7},{7,3},{8,12},{12,8},{9,1... | collective-permute-start | bytes 1572872 | tf_op jit(solution)/shard_map/ppermute | solution.py:18
  38.0 6.6 %collective-permute-start.7 = (bf16[128,2048]{1,0:T(8,128)(2,1)S(1)}, bf16[128,2048]{1,0:T(8,128)(2,1)S(1)}, u32[]{:S(2)}, u32[]{:S(2)}) collective-permute-start(bf16[128,2048]{1,0:T(8,128)(2,1)S(1)} %collective-permute-done.6.r2), channel_id=1, source_target_pairs={{0,4},{4,0},{1,5},{5,1},{2,6},{6,2},{3,7},{7,3},{8,12},{12,8},{9,1... | collective-permute-start | bytes 1572872 | tf_op jit(solution)/shard_map/ppermute | solution.py:18
  46.1 7.5 %collective-permute-start.14 = (bf16[512,1024]{1,0:T(8,128)(2,1)S(1)}, bf16[512,1024]{1,0:T(8,128)(2,1)S(1)}, u32[]{:S(2)}, u32[]{:S(2)}) collective-permute-start(bf16[512,1024]{1,0:T(8,128)(2,1)S(1)} %get-tuple-element.41), channel_id=1, source_target_pairs={{0,4},{4,0},{1,5},{5,1},{2,6},{6,2},{3,7},{7,3},{8,12},{12,8},{9,1... | collective-permute-start | bytes 3145736 | tf_op jit(solution)/shard_map/ppermute | solution.py:18
  46.6 5.2 %collective-permute-start.12 = (bf16[112,1024]{1,0:T(8,128)(2,1)S(1)}, bf16[112,1024]{1,0:T(8,128)(2,1)S(1)}, u32[]{:S(2)}, u32[]{:S(2)}) collective-permute-start(bf16[112,1024]{1,0:T(8,128)(2,1)S(1)} %get-tuple-element.39.own), channel_id=1, source_target_pairs={{0,3},{1,2},{2,1},{3,0},{4,5},{5,4},{6,7},{7,6},{8,11},{9,10},{10,... | collective-permute-start | bytes 688136 | tf_op jit(solution)/shard_map/ppermute | solution.py:27
  51.8 9.2 %collective-permute-start.13 = (bf16[224,1024]{1,0:T(8,128)(2,1)S(1)}, bf16[224,1024]{1,0:T(8,128)(2,1)S(1)}, u32[]{:S(2)}, u32[]{:S(2)}) collective-permute-start(bf16[224,1024]{1,0:T(8,128)(2,1)S(1)} %shard_map.118), channel_id=1, source_target_pairs={{0,1},{1,0},{2,3},{3,2},{4,7},{5,6},{6,5},{7,4},{8,9},{9,8},{10,11... | collective-permute-start | bytes 1376264 | tf_op jit(solution)/shard_map/ppermute | solution.py:27
  53.8 7.1 %collective-permute-start.15 = (bf16[128,1024]{1,0:T(8,128)(2,1)S(1)}, bf16[128,1024]{1,0:T(8,128)(2,1)S(1)}, u32[]{:S(2)}, u32[]{:S(2)}) collective-permute-start(bf16[128,1024]{1,0:T(8,128)(2,1)S(1)} %get-tuple-element.42), channel_id=1, source_target_pairs={{0,16},{4,68},{8,24},{12,76},{16,0},{20,84},{24,8},{28,92},{32,48}... | collective-permute-start | bytes 786440 | tf_op jit(solution)/shard_map/ppermute | solution.py:37
  63.4 7.0 %collective-permute-start.20 = (bf16[128,1024]{1,0:T(8,128)(2,1)S(1)}, bf16[128,1024]{1,0:T(8,128)(2,1)S(1)}, u32[]{:S(2)}, u32[]{:S(2)}) collective-permute-start(bf16[128,1024]{1,0:T(8,128)(2,1)S(1)} %get-tuple-element.50), channel_id=1, source_target_pairs={{0,8},{4,36},{8,0},{12,44},{16,24},{20,52},{24,16},{28,60},{32,40}... | collective-permute-start | bytes 786440 | tf_op jit(solution)/shard_map/ppermute | solution.py:37
  63.4 7.0 %collective-permute-start.21 = (bf16[128,1024]{1,0:T(8,128)(2,1)S(1)}, bf16[128,1024]{1,0:T(8,128)(2,1)S(1)}, u32[]{:S(2)}, u32[]{:S(2)}) collective-permute-start(bf16[128,1024]{1,0:T(8,128)(2,1)S(1)} %get-tuple-element.51), channel_id=1, source_target_pairs={{0,24},{4,100},{8,16},{12,108},{16,8},{20,116},{24,0},{28,124},{32... | collective-permute-start | bytes 786440 | tf_op jit(solution)/shard_map/ppermute | solution.py:37
  66.5 5.6 %collective-permute-start.17 = (bf16[128,1024]{1,0:T(8,128)(2,1)S(1)}, bf16[128,1024]{1,0:T(8,128)(2,1)S(1)}, u32[]{:S(2)}, u32[]{:S(2)}) collective-permute-start(bf16[128,1024]{1,0:T(8,128)(2,1)S(1)} %get-tuple-element.46), channel_id=1, source_target_pairs={{0,8},{4,36},{8,0},{12,44},{16,24},{20,52},{24,16},{28,60},{32,40}... | collective-permute-start | bytes 786440 | tf_op jit(solution)/shard_map/ppermute | solution.py:37
  66.6 8.5 %collective-permute-start.18 = (bf16[128,1024]{1,0:T(8,128)(2,1)S(1)}, bf16[128,1024]{1,0:T(8,128)(2,1)S(1)}, u32[]{:S(2)}, u32[]{:S(2)}) collective-permute-start(bf16[128,1024]{1,0:T(8,128)(2,1)S(1)} %get-tuple-element.47), channel_id=1, source_target_pairs={{0,16},{4,68},{8,24},{12,76},{16,0},{20,84},{24,8},{28,92},{32,48}... | collective-permute-start | bytes 786440 | tf_op jit(solution)/shard_map/ppermute | solution.py:37
  68.1 9.5 %collective-permute-start.19 = (bf16[128,1024]{1,0:T(8,128)(2,1)S(1)}, bf16[128,1024]{1,0:T(8,128)(2,1)S(1)}, u32[]{:S(2)}, u32[]{:S(2)}) collective-permute-start(bf16[128,1024]{1,0:T(8,128)(2,1)S(1)} %get-tuple-element.48), channel_id=1, source_target_pairs={{0,24},{4,100},{8,16},{12,108},{16,8},{20,116},{24,0},{28,124},{32... | collective-permute-start | bytes 786440 | tf_op jit(solution)/shard_map/ppermute | solution.py:37
  78.0 7.3 %collective-permute-start.23 = (bf16[32,2048]{1,0:T(8,128)(2,1)S(1)}, bf16[32,2048]{1,0:T(8,128)(2,1)S(1)}, u32[]{:S(2)}, u32[]{:S(2)}) collective-permute-start(bf16[32,2048]{1,0:T(8,128)(2,1)S(1)} %get-tuple-element.54), channel_id=1, source_target_pairs={{0,64},{4,20},{8,72},{12,28},{16,80},{20,4},{24,88},{28,12},{32,96... | collective-permute-start | bytes 393224 | tf_op jit(solution)/shard_map/ppermute | solution.py:37
  81.5 5.5 %collective-permute-start.24 = (bf16[32,2048]{1,0:T(8,128)(2,1)S(1)}, bf16[32,2048]{1,0:T(8,128)(2,1)S(1)}, u32[]{:S(2)}, u32[]{:S(2)}) collective-permute-start(bf16[32,2048]{1,0:T(8,128)(2,1)S(1)} %get-tuple-element.55), channel_id=1, source_target_pairs={{0,96},{4,28},{8,104},{12,20},{16,112},{20,12},{24,120},{28,4},{32... | collective-permute-start | bytes 393224 | tf_op jit(solution)/shard_map/ppermute | solution.py:37
  87.5 19.7 %collective-permute-start.25 = (bf16[32,2048]{1,0:T(8,128)(2,1)S(1)}, bf16[32,2048]{1,0:T(8,128)(2,1)S(1)}, u32[]{:S(2)}, u32[]{:S(2)}) collective-permute-start(bf16[32,2048]{1,0:T(8,128)(2,1)S(1)} %get-tuple-element.57.own), channel_id=1, source_target_pairs={{0,1},{1,0},{2,3},{3,2},{4,5},{5,4},{6,7},{7,6},{8,9},{9,8},{10,11... | collective-permute-start | bytes 393224 | tf_op jit(solution)/shard_map/ppermute | solution.py:22
  89.0 18.2 %collective-permute-start.26 = (bf16[32,2048]{1,0:T(8,128)(2,1)S(1)}, bf16[32,2048]{1,0:T(8,128)(2,1)S(1)}, u32[]{:S(2)}, u32[]{:S(2)}) collective-permute-start(bf16[32,2048]{1,0:T(8,128)(2,1)S(1)} %get-tuple-element.57.own), channel_id=1, source_target_pairs={{0,2},{1,3},{2,0},{3,1},{4,6},{5,7},{6,4},{7,5},{8,10},{9,11},{10,... | collective-permute-start | bytes 393224 | tf_op jit(solution)/shard_map/ppermute | solution.py:22
  91.3 15.9 %collective-permute-start.27 = (bf16[32,2048]{1,0:T(8,128)(2,1)S(1)}, bf16[32,2048]{1,0:T(8,128)(2,1)S(1)}, u32[]{:S(2)}, u32[]{:S(2)}) collective-permute-start(bf16[32,2048]{1,0:T(8,128)(2,1)S(1)} %get-tuple-element.57.own), channel_id=1, source_target_pairs={{0,3},{1,2},{2,1},{3,0},{4,7},{5,6},{6,5},{7,4},{8,11},{9,10},{10,... | collective-permute-start | bytes 393224 | tf_op jit(solution)/shard_map/ppermute | solution.py:22
  (12 other events, 104.9 us)
